TPU v7x, 32 devices: a whole 2x2x4 slice. The times are simulated.
32 devices in a mesh: row: 4 (over y, x), col: 8 (over z, core).
Axes of the slice: x: 2, y: 2, z: 4, core: 2. Of those that a mesh axis runs over, the one named last changes fastest.
Arguments:
- field_real: float32 [4096, 4096], P('row', 'col'), may hold values from -6 to 6
- field_imag: float32 [4096, 4096], P('row', 'col'), may hold values from -6 to 6
Outputs:
- slm_real: float32 [4096, 4096], P('row', 'col')
- slm_imag: float32 [4096, 4096], P('row', 'col')
All inputs are finite; a program needn't handle non-finite values.
Results may differ from a plain program's by a relative error of at most 0.0003.
Values sent between devices are 32-bit elements; how exact they have to be, the bound alone decides.
No kernel may reach another device: no remote copies, remote signals or barrier semaphores. Data moves between devices by JAX's collectives and lax.ppermute only.
A program may use at most 128 MiB of HBM per device.

v0:
```python
from functools import partial
import math

import jax
import jax.numpy as jnp
from jax import lax
from jax.sharding import PartitionSpec as P

N = 4096


wavelength = 5.2e-07
distance = 0.2


def optics(padded_side):
    pitch = 2e-06 * math.sqrt(8192.0 / padded_side)
    extent = padded_side * pitch
    ratio_sq = (wavelength / extent) ** 2
    band_limit = extent / (wavelength * math.sqrt((2.0 * distance / extent) ** 2 + 1.0))
    return (ratio_sq, band_limit)


def factor_pair(length):
    bit_count = length.bit_length() - 1
    inner_size = 2 ** ((bit_count + 1) // 2)
    return (length // inner_size, inner_size)


def signed_index(index_ids, modulus):
    return jnp.where(index_ids >= modulus // 2, index_ids - modulus, index_ids)


def transfer(row_signed, col_signed, ratio_sq, band_limit):
    square = row_signed[:, None] * row_signed[:, None] + col_signed[None, :] * col_signed[None, :]
    scaled = ratio_sq * square
    phase_angle = -2.0 * math.pi * distance / wavelength * scaled / (1.0 + jnp.sqrt(1.0 - scaled))
    gauss_gain = jnp.exp(square * (-2.0 / (band_limit * band_limit)))
    inside = (jnp.abs(row_signed)[:, None] < band_limit) & (
        jnp.abs(col_signed)[None, :] < band_limit
    )
    total_gain = jnp.where(inside, gauss_gain, 0.0)
    return (total_gain * jnp.cos(phase_angle), total_gain * jnp.sin(phase_angle))


def encode(near_real, near_imag, amplitude, peak, even_cell):
    amp_level = 0.8 * amplitude / peak
    amp_floor = jnp.maximum(amplitude, 0.05 * peak)
    unit_real = near_real / amp_floor
    unit_imag = near_imag / amp_floor
    lift_part = jnp.sqrt(1.0 - amp_level * amp_level)
    cell_sign = jnp.where(even_cell, 1.0, -1.0)
    out_real = unit_real * amp_level + cell_sign * unit_imag * lift_part
    out_imag = unit_imag * amp_level - cell_sign * unit_real * lift_part
    return (out_real, out_imag)


def index_range(range_start, id_count):
    return jnp.arange(id_count, dtype=jnp.int32) + range_start


def phase_table(first_ids, second_ids, modulus, exponent_sign):
    product = first_ids[:, None] * second_ids[None, :] % modulus
    phase_arg = exponent_sign * 2.0 * math.pi / modulus * product.astype(jnp.float32)
    return (jnp.cos(phase_arg), jnp.sin(phase_arg))


def complex_einsum(form, left_real, left_imag, right_real, right_imag):
    real_dot = partial(jnp.einsum, form, precision=lax.Precision.HIGHEST)
    out_real = real_dot(left_real, right_real) - real_dot(left_imag, right_imag)
    out_imag = real_dot(left_real, right_imag) + real_dot(left_imag, right_real)
    return (out_real, out_imag)


def transform_last(values_real, values_imag, exponent_sign, in_start, out_start, out_count, length):
    outer_size, inner_size = factor_pair(length)
    row_count = values_real.shape[0]
    blocks_in = values_real.shape[1] // inner_size
    first_block = in_start // inner_size
    cube_real = values_real.reshape(row_count, blocks_in, inner_size)
    cube_imag = values_imag.reshape(row_count, blocks_in, inner_size)
    step_real, step_imag = phase_table(
        index_range(first_block, blocks_in), index_range(0, outer_size), outer_size, exponent_sign
    )
    mid_real, mid_imag = complex_einsum("rnq,nk->rkq", cube_real, cube_imag, step_real, step_imag)
    twist_real, twist_imag = phase_table(
        index_range(0, outer_size), index_range(0, inner_size), length, exponent_sign
    )
    mid_real, mid_imag = (
        mid_real * twist_real - mid_imag * twist_imag,
        mid_real * twist_imag + mid_imag * twist_real,
    )
    blocks_out = out_count // outer_size
    second_block = out_start // outer_size
    last_real, last_imag = phase_table(
        index_range(0, inner_size), index_range(second_block, blocks_out), inner_size, exponent_sign
    )
    done_real, done_imag = complex_einsum("rkq,qj->rjk", mid_real, mid_imag, last_real, last_imag)
    return (
        done_real.reshape(row_count, blocks_out * outer_size),
        done_imag.reshape(row_count, blocks_out * outer_size),
    )


def body(field_real, field_imag):
    padded = 2 * N
    quarter = padded // 4
    col_total = lax.axis_size("col")
    device = lax.axis_index("row") * col_total + lax.axis_index("col")
    strip_real, strip_imag = (
        lax.all_to_all(field_real, "col", split_axis=0, concat_axis=1, tiled=True),
        lax.all_to_all(field_imag, "col", split_axis=0, concat_axis=1, tiled=True),
    )
    wide_real, wide_imag = transform_last(strip_real, strip_imag, -1.0, quarter, 0, padded, padded)
    ratio_sq, band_limit = optics(padded)
    pick_real, pick_imag = (wide_real, wide_imag)
    freq_start = 0
    column_real, column_imag = (
        lax.all_to_all(pick_real, ("row", "col"), split_axis=1, concat_axis=0, tiled=True),
        lax.all_to_all(pick_imag, ("row", "col"), split_axis=1, concat_axis=0, tiled=True),
    )
    col_width = column_real.shape[1]
    turned_real = column_real.T
    turned_imag = column_imag.T
    spec_real, spec_imag = transform_last(
        turned_real, turned_imag, -1.0, quarter, freq_start, padded, padded
    )
    freq_ids = index_range(freq_start, padded)
    freq_signed = signed_index(freq_ids, padded).astype(jnp.float32)
    col_ids = device * col_width + jnp.arange(col_width, dtype=jnp.int32)
    col_signed = signed_index(col_ids, padded).astype(jnp.float32)
    gain_real, gain_imag = transfer(col_signed, freq_signed, ratio_sq, band_limit)
    mixed_real = spec_real * gain_real - spec_imag * gain_imag
    mixed_imag = spec_real * gain_imag + spec_imag * gain_real
    inv_real, inv_imag = transform_last(mixed_real, mixed_imag, 1.0, freq_start, quarter, N, padded)
    back_real = inv_real.T
    back_imag = inv_imag.T
    line_real, line_imag = (
        lax.all_to_all(back_real, ("row", "col"), split_axis=0, concat_axis=1, tiled=True),
        lax.all_to_all(back_imag, ("row", "col"), split_axis=0, concat_axis=1, tiled=True),
    )
    line_rows = line_real.shape[0]
    full_real, full_imag = (line_real, line_imag)
    near_real, near_imag = transform_last(full_real, full_imag, 1.0, 0, quarter, N, padded)
    amplitude = jnp.sqrt(near_real * near_real + near_imag * near_imag)
    peak = lax.pmax(jnp.max(amplitude), ("row", "col"))
    row_ids = device * line_rows + jnp.arange(line_rows, dtype=jnp.int32)
    col_all = jnp.arange(N, dtype=jnp.int32)
    even_cell = (row_ids[:, None] + col_all[None, :]) % 2 == 0
    slm_real, slm_imag = encode(near_real, near_imag, amplitude, peak, even_cell)
    tile_real, tile_imag = (
        lax.all_to_all(slm_real, "col", split_axis=1, concat_axis=0, tiled=True),
        lax.all_to_all(slm_imag, "col", split_axis=1, concat_axis=0, tiled=True),
    )
    return (tile_real, tile_imag)


def solution(mesh):
    in_specs = (P("row", "col"), P("row", "col"))
    out_specs = (P("row", "col"), P("row", "col"))
    return jax.shard_map(body, mesh=mesh, in_specs=in_specs, out_specs=out_specs, check_vma=False)
```

profile of v0, /device:TPU:0, one launch (start us, length us, event | category | flops | bytes accessed | tf_op | source)
XLA Modules:
  0.0 1018.3 jit_solution(6477746587708901937)
XLA Ops:
  0.6 55.4 %all_to_all.134 = f32[8,128,512]{2,1,0:T(8,128)S(1)} all-to-all(f32[8,128,512]{2,1,0:T(8,128)} %bitcast.243), channel_id=1, replica_groups=mesh['row'=4,'col'=8] {'col'}, dimensions={0} | all-to-all | bytes 4194304 | tf_op jit(solution)/shard_map/all_to_all | solution.py:111
  56.0 4.4 all-to-all-start.1
  60.6 2.5 copy.92
  64.7 5.3 fusion.144
  70.0 5.4 fusion.150
  75.4 34.1 %all-to-all-done.1 = f32[8,128,512]{2,1,0:T(8,128)} async-done(((f32[8,128,512]{2,1,0:T(8,128)}), f32[8,128,512]{2,1,0:T(8,128)}, u32[]{:S(2)}, u32[]{:S(2)}) %all-to-all-start.1) | async-done | bytes 2097184 | tf_op jit(solution)/shard_map/all_to_all | solution.py:112
  109.5 4.1 copy.93
  115.2 6.0 convolution_add_fusion.1
  121.2 5.0 subtract_bitcast_fusion.6
  126.2 6.0 fusion.42
  132.3 6.6 add_bitcast_fusion.5
  138.9 4.4 copy.101
  143.2 3.6 all-to-all-start.3
  146.9 9.1 fusion.44
  156.0 6.0 subtract_bitcast_fusion.5
  162.0 4.5 copy.96
  166.4 75.5 %all-to-all-done.3 = f32[128,32,256]{0,2,1:T(8,128)} async-done(((f32[128,32,256]{0,2,1:T(8,128)}), f32[128,32,256]{0,2,1:T(8,128)}, u32[]{:S(2)}, u32[]{:S(2)}) %all-to-all-start.3) | async-done | bytes 4194336 | tf_op jit(solution)/shard_map/all_to_all | solution.py:120
  241.9 3.8 all-to-all-start.2
  245.9 13.7 %fusion.28 = f32[64,256,128]{2,0,1:T(8,128)} fusion(f32[256,32,128]{2,0,1:T(8,128)} %bitcast.29, s32[32]{0:T(128)S(1)} %iota_add_fusion.1), kind=kOutput, calls=%fused_computation.49 | convolution fusion | flops 805335040 | bytes 12583040 | tf_op jit(solution)/shard_map/rnq,nk->rkq/dot_general | solution.py:70
  259.6 13.6 %fusion.26 = f32[64,256,128]{2,0,1:T(8,128)} fusion(f32[256,32,128]{2,0,1:T(8,128)} %bitcast.29, s32[32]{0:T(128)S(1)} %iota_add_fusion.1), kind=kOutput, calls=%fused_computation.47 | convolution fusion | flops 805335040 | bytes 12583040 | tf_op jit(solution)/shard_map/rnq,nk->rkq/dot_general | solution.py:71
  273.3 67.5 %all-to-all-done.2 = f32[128,32,256]{0,2,1:T(8,128)} async-done(((f32[128,32,256]{0,2,1:T(8,128)}), f32[128,32,256]{0,2,1:T(8,128)}, u32[]{:S(2)}, u32[]{:S(2)}) %all-to-all-start.2) | async-done | bytes 4194336 | tf_op jit(solution)/shard_map/all_to_all | solution.py:119
  340.7 13.9 %fusion.30 = f32[64,256,128]{2,0,1:T(8,128)} fusion(f32[256,32,128]{2,0,1:T(8,128)} %bitcast.26, s32[32]{0:T(128)S(1)} %iota_add_fusion.1), kind=kOutput, calls=%fused_computation.51 | convolution fusion | flops 805335040 | bytes 12583040 | tf_op jit(solution)/shard_map/rnq,nk->rkq/dot_general | solution.py:71
  354.6 21.1 %subtract_bitcast_fusion.2 = (f32[256,64,128]{2,1,0:T(8,128)}, f32[256,64,128]{2,1,0:T(8,128)}) fusion(f32[64,128]{1,0:T(8,128)S(1)} %get-tuple-element.16, f32[64,128]{1,0:T(8,128)S(1)} %get-tuple-element.17, f32[64,256,128]{2,0,1:T(8,128)} %fusion.30, f32[64,256,128]{2,0,1:T(8,128)} %fusion.26, f32[64,256,128]{2,0,1:T(8,128)} %fusion.28, ...), kind=kOutput, calls=%fused_computation.22 | convolution fusion | flops 822112256 | bytes 46203008 | tf_op jit(solution)/shard_map/rnq,nk->rkq/dot_general | solution.py:70
  375.7 16.3 %fusion.20 = f32[128,256,64]{1,0,2:T(8,128)S(1)} fusion(f32[256,64,128]{2,1,0:T(8,128)} %get-tuple-element.5), kind=kOutput, calls=%fused_computation.33 | convolution fusion | flops 3221454848 | bytes 16777216 | tf_op jit(solution)/shard_map/rkq,qj->rjk/dot_general | solution.py:70
  392.1 17.4 %fusion.18 = f32[128,256,64]{1,0,2:T(8,128)} fusion(f32[256,64,128]{2,1,0:T(8,128)S(1)} %copy-done.2), kind=kOutput, calls=%fused_computation.31 | convolution fusion | flops 3221454848 | bytes 16777216 | tf_op jit(solution)/shard_map/rkq,qj->rjk/dot_general | solution.py:71
  409.5 17.7 %subtract_bitcast_fusion.1 = f32[256,128,64]{0,1,2:T(8,128)} fusion(f32[128,256,64]{1,0,2:T(8,128)S(1)} %fusion.20, f32[256,64,128]{2,1,0:T(8,128)S(1)} %bitcast.231), kind=kOutput, calls=%fused_computation.20 | convolution fusion | flops 3223552000 | bytes 25165824 | tf_op jit(solution)/shard_map/rkq,qj->rjk/dot_general | solution.py:70
  427.2 8.2 copy.106
  435.4 19.8 %add_bitcast_fusion.1 = f32[256,128,64]{0,1,2:T(8,128)} fusion(f32[128,256,64]{1,0,2:T(8,128)} %fusion.18, f32[256,64,128]{2,1,0:T(8,128)S(1)} %bitcast.231), kind=kOutput, calls=%fused_computation.19 | convolution fusion | flops 3223552000 | bytes 25165824 | tf_op jit(solution)/shard_map/rkq,qj->rjk/dot_general | solution.py:71
  455.2 8.2 copy.109
  463.5 40.8 %fusion.9 = (f32[256,64,128]{0,2,1:T(8,128)}, f32[256,64,128]{0,2,1:T(8,128)}) fusion(f32[64,128]{1,0:T(8,128)S(1)} %fusion.119, f32[256]{0:T(256)S(1)} %fusion.186, pred[64,128]{1,0:T(8,128)(4,1)S(1)} %abs_compare_fusion, pred[256]{0:T(512)(128)(4,1)S(1)} %abs_compare_fusion.1, f32[256,64,128]{0,2,1:T(8,128)S(1)} %bitcast.233, f32[256,64,128]{0,2,1:T(8,128)S(1)} %bitcast.232), kind=kLoop, calls=%fused_computation.14 | loop fusion | flops 35651584 | bytes 33596672 | tf_op jit(solution)/shard_map/add | solution.py:134
  504.3 8.7 copy.111
  513.0 12.7 %fusion.106 = f32[64,256,128]{2,0,1:T(8,128)} fusion(f32[256,64,128]{2,1,0:T(8,128)} %copy.111), kind=kOutput, calls=%fused_computation.144 | convolution fusion | flops 1610670080 | bytes 16777216 | tf_op jit(solution)/shard_map/rnq,nk->rkq/dot_general | solution.py:70
  525.8 9.9 fusion.111
  535.7 8.7 copy.110
  544.4 11.9 %fusion.104 = f32[64,256,128]{2,0,1:T(8,128)} fusion(f32[256,64,128]{2,1,0:T(8,128)} %copy.110), kind=kOutput, calls=%fused_computation.142 | convolution fusion | flops 1610670080 | bytes 16777216 | tf_op jit(solution)/shard_map/rnq,nk->rkq/dot_general | solution.py:71
  556.3 19.7 %subtract_bitcast_fusion = (f32[256,64,128]{2,1,0:T(8,128)}, f32[256,64,128]{2,1,0:T(8,128)}) fusion(f32[64,128]{1,0:T(8,128)S(1)} %get-tuple-element.18, f32[64,128]{1,0:T(8,128)S(1)} %get-tuple-element.19, f32[64,256,128]{2,0,1:T(8,128)} %fusion.104, f32[64,256,128]{2,0,1:T(8,128)} %fusion.111, f32[64,256,128]{2,0,1:T(8,128)} %fusion.106, ...), kind=kOutput, calls=%fused_computation.18 | convolution fusion | flops 1627447296 | bytes 50397184 | tf_op jit(solution)/shard_map/rnq,nk->rkq/dot_general | solution.py:70
  576.0 17.5 %fusion.12 = f32[64,256,64]{1,0,2:T(8,128)S(1)} fusion(f32[256,64,128]{2,1,0:T(8,128)} %get-tuple-element.3, s32[64]{0:T(128)S(1)} %iota_add_fusion.2), kind=kOutput, calls=%fused_computation.25 | convolution fusion | flops 1610727424 | bytes 12583168 | tf_op jit(solution)/shard_map/rkq,qj->rjk/dot_general | solution.py:70
  593.6 13.5 %subtract_bitcast_fusion.4 = f32[256,64,64]{0,1,2:T(8,128)S(1)} fusion(f32[64,256,64]{1,0,2:T(8,128)S(1)} %fusion.12, f32[256,64,128]{2,1,0:T(8,128)S(1)} %copy-done, s32[64]{0:T(128)S(1)} %iota_add_fusion.2), kind=kOutput, calls=%fused_computation.42 | convolution fusion | flops 1611776000 | bytes 16777472 | tf_op jit(solution)/shard_map/rkq,qj->rjk/dot_general | solution.py:70
  607.0 4.6 copy.116
  611.6 3.6 all-to-all-start.4
  615.2 16.6 %fusion.10 = f32[64,256,64]{1,0,2:T(8,128)S(1)} fusion(f32[256,64,128]{2,1,0:T(8,128)} %get-tuple-element.3, s32[64]{0:T(128)S(1)} %iota_add_fusion.2), kind=kOutput, calls=%fused_computation.23 | convolution fusion | flops 1610727424 | bytes 12583168 | tf_op jit(solution)/shard_map/rkq,qj->rjk/dot_general | solution.py:71
  631.8 17.2 %add_bitcast_fusion.4 = f32[256,64,64]{0,1,2:T(8,128)S(1)} fusion(f32[64,256,64]{1,0,2:T(8,128)S(1)} %fusion.10, f32[256,64,128]{2,1,0:T(8,128)} %get-tuple-element.2, s32[64]{0:T(128)S(1)} %iota_add_fusion.2), kind=kOutput, calls=%fused_computation.41 | convolution fusion | flops 1611776000 | bytes 16777472 | tf_op jit(solution)/shard_map/rkq,qj->rjk/dot_general | solution.py:71
  649.1 4.5 copy.120
  653.5 56.7 %all-to-all-done.4 = f32[32,128,256]{2,1,0:T(8,128)} async-done(((f32[32,128,256]{2,1,0:T(8,128)}), f32[32,128,256]{2,1,0:T(8,128)}, u32[]{:S(2)}, u32[]{:S(2)}) %all-to-all-start.4) | async-done | bytes 4194336 | tf_op jit(solution)/shard_map/all_to_all | solution.py:139
  710.3 4.0 all-to-all-start.5
  714.3 6.6 copy.117
  720.8 4.7 reshape.255
  725.5 8.1 fusion.101
  733.7 5.5 fusion.109
  739.1 70.2 %all-to-all-done.5 = f32[32,128,256]{2,1,0:T(8,128)} async-done(((f32[32,128,256]{2,1,0:T(8,128)}), f32[32,128,256]{2,1,0:T(8,128)}, u32[]{:S(2)}, u32[]{:S(2)}) %all-to-all-start.5) | async-done | bytes 4194336 | tf_op jit(solution)/shard_map/all_to_all | solution.py:140
  809.3 6.6 copy.121
  815.9 4.9 reshape.257
  820.8 8.0 convolution_add_fusion
  828.9 5.4 subtract_bitcast_fusion.3
  834.3 7.1 fusion.36
  841.4 6.7 fusion.34
  848.1 6.9 subtract_bitcast_fusion.7
  856.3 7.8 sqrt_reduce_fusion
  866.6 37.1 %pmax.7 = f32[]{:T(128)} all-reduce(f32[]{:T(128)} %get-tuple-element.14), channel_id=1, replica_groups=mesh['row'=4,'col'=8] {'row','col'}, use_global_device_ids=true, to_apply=%region_1.2 | all-reduce | flops 1 | bytes 8 | tf_op jit(solution)/shard_map/pmax | solution.py:146
  904.3 6.2 fusion.65
  910.5 53.2 %all_to_all.135 = f32[128,8,512]{0,2,1:T(8,128)} all-to-all(f32[128,8,512]{0,2,1:T(8,128)S(1)} %get-tuple-element.13), channel_id=1, replica_groups=mesh['row'=4,'col'=8] {'col'}, dimensions={1} | all-to-all | bytes 4194304 | tf_op jit(solution)/shard_map/all_to_all | solution.py:152
  963.7 3.6 all-to-all-start.7
  967.3 2.9 copy.128
  970.2 46.1 %all-to-all-done.7 = f32[128,8,512]{0,2,1:T(8,128)S(1)} async-done(((f32[128,8,512]{0,2,1:T(8,128)}), f32[128,8,512]{0,2,1:T(8,128)S(1)}, u32[]{:S(2)}, u32[]{:S(2)}) %all-to-all-start.7) | async-done | bytes 2097184 | tf_op jit(solution)/shard_map/all_to_all | solution.py:153
  (40 shorter events, 9.2 us)
Async XLA Ops:
  56.0 53.4 %all-to-all-start.1 = ((f32[8,128,512]{2,1,0:T(8,128)}), f32[8,128,512]{2,1,0:T(8,128)}, u32[]{:S(2)}, u32[]{:S(2)}) async-start(f32[8,128,512]{2,1,0:T(8,128)} %bitcast.244), calls=%async_computation.1 | async-start | bytes 4194304 | tf_op jit(solution)/shard_map/all_to_all | solution.py:112
  115.2 6.0 copy-start.9
  126.2 6.0 copy-start.7
  126.2 6.0 copy-start.4
  143.2 98.7 %all-to-all-start.3 = ((f32[128,32,256]{0,2,1:T(8,128)}), f32[128,32,256]{0,2,1:T(8,128)}, u32[]{:S(2)}, u32[]{:S(2)}) async-start(f32[128,32,256]{0,2,1:T(8,128)} %bitcast.236), calls=%async_computation.3 | async-start | bytes 8388608 | tf_op jit(solution)/shard_map/all_to_all | solution.py:120
  146.9 9.1 copy-start.5
  241.9 98.8 %all-to-all-start.2 = ((f32[128,32,256]{0,2,1:T(8,128)}), f32[128,32,256]{0,2,1:T(8,128)}, u32[]{:S(2)}, u32[]{:S(2)}) async-start(f32[128,32,256]{0,2,1:T(8,128)} %bitcast.234), calls=%async_computation.2 | async-start | bytes 8388608 | tf_op jit(solution)/shard_map/all_to_all | solution.py:119
  375.7 16.4 %copy-start.2 = (f32[256,64,128]{2,1,0:T(8,128)S(1)}, f32[256,64,128]{2,1,0:T(8,128)}, u32[]{:S(2)}) copy-start(f32[256,64,128]{2,1,0:T(8,128)} %get-tuple-element.5) | copy-start | bytes 25165828
  375.7 33.8 %slice-start = ((s8[8388608]{0:T(1024)(128)(4,1)}), s8[4194304]{0:T(1024)(128)(4,1)S(1)}, s32[]{:S(2)}) async-start(s8[8388608]{0:T(1024)(128)(4,1)} %bitcast.230), calls=%async_computation.8 | async-start | bytes 8388608
  392.1 17.4 %slice-start.1 = ((s8[8388608]{0:T(1024)(128)(4,1)}), s8[4194304]{0:T(1024)(128)(4,1)S(1)}, s32[]{:S(2)}) async-start(s8[8388608]{0:T(1024)(128)(4,1)} %bitcast.230), calls=%async_computation.9 | async-start | bytes 8388608
  513.0 12.7 %copy-start.1 = (f32[256,64,128]{2,1,0:T(8,128)S(1)}, f32[256,64,128]{2,1,0:T(8,128)}, u32[]{:S(2)}) copy-start(f32[256,64,128]{2,1,0:T(8,128)} %copy.111) | copy-start | bytes 25165828
  576.0 17.5 %copy-start = (f32[256,64,128]{2,1,0:T(8,128)S(1)}, f32[256,64,128]{2,1,0:T(8,128)}, u32[]{:S(2)}) copy-start(f32[256,64,128]{2,1,0:T(8,128)} %get-tuple-element.2) | copy-start | bytes 25165828
  611.6 98.7 %all-to-all-start.4 = ((f32[32,128,256]{2,1,0:T(8,128)}), f32[32,128,256]{2,1,0:T(8,128)}, u32[]{:S(2)}, u32[]{:S(2)}) async-start(f32[32,128,256]{2,1,0:T(8,128)} %bitcast.237), calls=%async_computation.4 | async-start | bytes 8388608 | tf_op jit(solution)/shard_map/all_to_all | solution.py:139
  710.3 99.0 %all-to-all-start.5 = ((f32[32,128,256]{2,1,0:T(8,128)}), f32[32,128,256]{2,1,0:T(8,128)}, u32[]{:S(2)}, u32[]{:S(2)}) async-start(f32[32,128,256]{2,1,0:T(8,128)} %bitcast.235), calls=%async_computation.5 | async-start | bytes 8388608 | tf_op jit(solution)/shard_map/all_to_all | solution.py:140
  725.5 8.1 copy-start.6
  820.8 8.0 copy-start.3
  820.8 8.0 copy-start.8
  963.7 52.6 %all-to-all-start.7 = ((f32[128,8,512]{0,2,1:T(8,128)}), f32[128,8,512]{0,2,1:T(8,128)S(1)}, u32[]{:S(2)}, u32[]{:S(2)}) async-start(f32[128,8,512]{0,2,1:T(8,128)} %get-tuple-element.12), calls=%async_computation.7 | async-start | bytes 4194304 | tf_op jit(solution)/shard_map/all_to_all | solution.py:153
where the time goes:
time: 1030 us; the launch traced here: 1020 us
  matrix products  357 us (35%)
  waiting for transfers between devices  350 us (34%)
  blocking collectives  146 us (14%)
  local copies, waits for them, and re-layouts  92.9 us (9%)
  other arithmetic  47.4 us (5%)
  starting transfers between devices  22.9 us (2%)
    dot_general x16, matrix products, complex_einsum(): out_real = real_dot(left_real, right_real) - real_dot(left_imag, right_imag)  183 us
    dot_general x16, matrix products, complex_einsum(): out_imag = real_dot(left_real, right_imag) + real_dot(left_imag, right_real)  175 us
    all_to_all x1, waiting for transfers between devices, body(): lax.all_to_all(pick_imag, ('row', 'col'), split_axis=1, concat_axis=0, ti...  75.5 us
    all_to_all x1, waiting for transfers between devices, body(): lax.all_to_all(back_imag, ('row', 'col'), split_axis=0, concat_axis=1, ti...  70.2 us
    all_to_all x1, waiting for transfers between devices, body(): lax.all_to_all(pick_real, ('row', 'col'), split_axis=1, concat_axis=0, ti...  67.5 us
    all_to_all x1, waiting for transfers between devices, body(): lax.all_to_all(back_real, ('row', 'col'), split_axis=0, concat_axis=1, ti...  56.7 us
    all_to_all x1, blocking collectives, body(): lax.all_to_all(field_real, 'col', split_axis=0, concat_axis=1, tiled=True)  55.4 us
    all_to_all x1, blocking collectives, body(): lax.all_to_all(slm_real, 'col', split_axis=1, concat_axis=0, tiled=True)  53.2 us
  transfers between devices with their start and end apart: 6, of which 6 were waited for; matrix products, arithmetic and copies ran while one was open for 13% of the time, Pallas kernels for 0%

commit v1 on v0

v1 whole, which is shorter than its diff:
```python
from functools import partial
import math

import jax
import jax.numpy as jnp
import ml_dtypes
import numpy as np
from jax import lax
from jax.experimental import pallas as pl
from jax.experimental.pallas import tpu as pltpu
from jax.sharding import PartitionSpec as P

N = 4096
PAD = 2 * N
wavelength = 5.2e-07
distance = 0.2
INNER = 256
SLABS = N // INNER
RES = PAD // INNER
HALF = 40
VMEM = 56 * 1024 * 1024


def optics(padded_side):
    pitch = 2e-06 * math.sqrt(8192.0 / padded_side)
    extent = padded_side * pitch
    ratio_sq = (wavelength / extent) ** 2
    band_limit = extent / (wavelength * math.sqrt((2.0 * distance / extent) ** 2 + 1.0))
    return (ratio_sq, band_limit)


RATIO_SQ, LIMIT = optics(PAD)
assert RES * HALF - RES // 2 + RES > LIMIT and RES * HALF + RES // 2 > LIMIT


def residue(u):
    return u if u < RES // 2 else u - RES


def split16(table):
    table = np.asarray(table, np.float64)
    high = table.astype(np.float32).astype(ml_dtypes.bfloat16)
    low = (table - high.astype(np.float64)).astype(np.float32).astype(ml_dtypes.bfloat16)
    return high, low


def row_order(groups):
    rows = []
    for group in range(groups):
        for part in range(2):
            for s in range(8):
                rows.append((part, group * 8 + s - HALF))
    return rows


def column_tables(groups):
    q = np.arange(INNER)
    rows = row_order(groups)
    forward = np.zeros((len(rows), 2 * INNER))
    inverse = np.zeros((2 * INNER, len(rows)))
    for at, (part, k1) in enumerate(rows):
        if abs(k1) > HALF:
            continue
        angle = 2.0 * np.pi * ((k1 * q) % INNER) / INNER
        c, s = np.cos(angle), np.sin(angle)
        if part == 0:
            forward[at, :INNER], forward[at, INNER:] = c, s
            inverse[:INNER, at], inverse[INNER:, at] = c, s
        else:
            forward[at, :INNER], forward[at, INNER:] = -s, c
            inverse[:INNER, at], inverse[INNER:, at] = -s, c
    return split16(forward) + split16(inverse)


def line_tables():
    q = np.arange(INNER)
    forward = np.zeros((2 * INNER, 256))
    inverse = np.zeros((256, 2 * INNER))
    for lane in range(2 * HALF + 1):
        angle = 2.0 * np.pi * (((lane - HALF) * q) % INNER) / INNER
        c, s = np.cos(angle), np.sin(angle)
        forward[:INNER, lane], forward[INNER:, lane] = c, s
        forward[:INNER, 128 + lane], forward[INNER:, 128 + lane] = -s, c
        inverse[lane, :INNER], inverse[lane, INNER:] = c, s
        inverse[128 + lane, :INNER], inverse[128 + lane, INNER:] = -s, c
    return split16(forward) + split16(inverse)


def twist_table():
    q = np.arange(INNER) + N // 2
    k0 = np.array([residue(u) for u in range(RES)])
    angle = 2.0 * np.pi * ((k0[:, None] * q[None, :]) % PAD) / PAD
    return np.cos(angle).astype(np.float32), (-np.sin(angle)).astype(np.float32)


def turn(value, num, den):
    re, im = value
    num = num % den
    eighth = 8 * num
    if num == 0:
        return re, im
    if 2 * num == den:
        return -re, -im
    if 4 * num == den:
        return -im, re
    if 4 * num == 3 * den:
        return im, -re
    if eighth % den == 0:
        root = np.float32(math.sqrt(0.5))
        kind = eighth // den
        if kind == 1:
            return (re - im) * root, (re + im) * root
        if kind == 3:
            return (re + im) * (-root), (re - im) * root
        if kind == 5:
            return (im - re) * root, (re + im) * (-root)
        return (re + im) * root, (im - re) * root
    c = np.float32(math.cos(2.0 * math.pi * num / den))
    s = np.float32(math.sin(2.0 * math.pi * num / den))
    return re * c - im * s, re * s + im * c


def small_dft(get, ids, sign):
    count = len(ids)
    if count == 1:
        return [get(ids[0])]
    even = small_dft(get, ids[0::2], sign)
    odd = small_dft(get, ids[1::2], sign)
    half = count // 2
    first, second = [], []
    for j in range(half):
        re, im = even[j]
        t_re, t_im = turn(odd[j], sign * j, count)
        first.append((re + t_re, im + t_im))
        second.append((re - t_re, im - t_im))
    return first + second


def forward_slabs(get, put):
    ids = list(range(SLABS))
    for v, value in enumerate(small_dft(get, ids, -1)):
        put(2 * v, value)
    for v, value in enumerate(small_dft(lambda n: turn(get(n), -n, RES), ids, -1)):
        put(2 * v + 1, value)


def inverse_slabs(get, put):
    even = small_dft(get, list(range(0, RES, 2)), 1)
    odd = small_dft(get, list(range(1, RES, 2)), 1)
    for n in range(SLABS):
        t_re, t_im = turn(odd[n], n, RES)
        put(n, (even[n][0] + t_re, even[n][1] + t_im))


def high_low(value):
    high = value.astype(jnp.bfloat16)
    low = (value - high.astype(jnp.float32)).astype(jnp.bfloat16)
    return high, low


def dot16(left, right):
    return jnp.dot(left, right, preferred_element_type=jnp.float32)


def column_forward_kernel(field, twist, mat_high, mat_low, out, high, low):
    width = field.shape[-1]
    per_source = field.shape[2] // INNER
    pair = high.shape[2] // width

    def step(t, carry):
        q0 = pl.multiple_of(t * 16, 16)

        def get(n):
            source, block = divmod(n, per_source)
            rows = pl.ds(block * INNER + q0, 16)
            return field[source, 0, rows, :], field[source, 1, rows, :]

        def put(u, value):
            re, im = value
            c = twist[pl.ds(q0, 16), u : u + 1]
            s = twist[pl.ds(q0, 16), RES + u : RES + u + 1]
            lanes = pl.ds((u % pair) * width, width)
            for part, item in enumerate((re * c - im * s, re * s + im * c)):
                rows = pl.ds(part * INNER + q0, 16)
                high[u // pair, rows, lanes], low[u // pair, rows, lanes] = high_low(item)

        forward_slabs(get, put)
        return carry

    lax.fori_loop(0, INNER // 16, step, 0)

    def product(p, carry):
        done = (
            dot16(mat_high[...], high[p])
            + dot16(mat_high[...], low[p])
            + dot16(mat_low[...], high[p])
        )
        for part in range(pair):
            out[p * pair + part] = done[:, part * width : (part + 1) * width]
        return carry

    lax.fori_loop(0, RES // pair, product, 0)


def column_inverse_kernel(lines, twist, mat_high, mat_low, out, top, back):
    width = lines.shape[-1]
    per_dest = out.shape[2] // INNER
    pair = 2 if width == 128 else 1

    def product(p, carry):
        blocks = [lines[p * pair + part] for part in range(pair)]
        high, low = high_low(jnp.concatenate(blocks, axis=1) if pair > 1 else blocks[0])
        done = (
            dot16(mat_high[...], high) + dot16(mat_high[...], low) + dot16(mat_low[...], high)
        )
        for part in range(pair):
            back[p * pair + part] = done[:, part * width : (part + 1) * width]
        return carry

    lax.fori_loop(0, RES // pair, product, 0)
    top[...] = jnp.zeros_like(top)

    def step(t, carry):
        q0 = pl.multiple_of(t * 8, 8)
        largest = []

        def get(u):
            re = back[u, pl.ds(q0, 8), :]
            im = back[u, pl.ds(INNER + q0, 8), :]
            c = twist[pl.ds(q0, 8), u : u + 1]
            s = twist[pl.ds(q0, 8), RES + u : RES + u + 1]
            return re * c + im * s, im * c - re * s

        def put(n, value):
            dest, block = divmod(n, per_dest)
            rows = pl.ds(block * INNER + q0, 8)
            out[dest, 0, rows, :], out[dest, 1, rows, :] = value
            largest.append(value[0] * value[0] + value[1] * value[1])

        inverse_slabs(get, put)
        while len(largest) > 1:
            largest = [jnp.maximum(a, b) for a, b in zip(largest[0::2], largest[1::2])]
        top[...] = jnp.maximum(top[...], largest[0])
        return carry

    lax.fori_loop(0, INNER // 8, step, 0)


def line_kernel(
    order, lines, gain_re, gain_im, twist, fwd_high, fwd_low, inv_high, inv_low, out, high, low, back
):
    for side in range(2):
        lanes = pl.ds(side * 128, 128)
        waiting = {}

        def get(m):
            block = order[2 * m + side]
            return lines[block, 0:8, :], lines[block, 8:16, :]

        def put(u, value):
            re, im = value
            c = twist[u : u + 1, lanes]
            s = twist[RES + u : RES + u + 1, lanes]
            waiting[u] = (re * c - im * s, re * s + im * c)
            v = (u + RES // 2) % RES
            if v in waiting:
                low_u = min(u, v)
                rows = pl.ds(low_u * 16, 16)
                for part in range(2):
                    item = jnp.concatenate([waiting[low_u][part], waiting[low_u + RES // 2][part]], axis=0)
                    at = pl.ds(part * INNER + side * 128, 128)
                    high[rows, at], low[rows, at] = high_low(item)

        forward_slabs(get, put)

    spec = (
        dot16(high[...], fwd_high[...]) + dot16(high[...], fwd_low[...]) + dot16(low[...], fwd_high[...])
    )
    spec_re, spec_im = spec[:, :128], spec[:, 128:]
    mixed = jnp.concatenate(
        [
            spec_re * gain_re[0] - spec_im * gain_im[0],
            spec_re * gain_im[0] + spec_im * gain_re[0],
        ],
        axis=1,
    )
    mixed_high, mixed_low = high_low(mixed)
    back[...] = (
        dot16(mixed_high, inv_high[...])
        + dot16(mixed_high, inv_low[...])
        + dot16(mixed_low, inv_high[...])
    )

    for side in range(2):
        lanes = pl.ds(side * 128, 128)

        def get(u):
            rows = pl.ds((u % (RES // 2)) * 16 + (u // (RES // 2)) * 8, 8)
            re = back[rows, pl.ds(side * 128, 128)]
            im = back[rows, pl.ds(INNER + side * 128, 128)]
            c = twist[u : u + 1, lanes]
            s = twist[RES + u : RES + u + 1, lanes]
            return re * c + im * s, im * c - re * s

        def put(m, value):
            block = order[2 * m + side]
            out[block, 0:8, :], out[block, 8:16, :] = value

        inverse_slabs(get, put)


def gain_kernel(place, gain_re, gain_im):
    k0 = place[0]
    group = place[1] + pl.program_id(0)
    down = lax.broadcasted_iota(jnp.int32, (8, 128), 0)
    across = lax.broadcasted_iota(jnp.int32, (8, 128), 1)
    row = (k0 + RES * (group * 8 + down - HALF)).astype(jnp.float32)
    row_sq = row * row
    row_in = jnp.abs(row) < LIMIT
    for u in range(RES):
        col = (residue(u) + RES * (across - HALF)).astype(jnp.float32)
        square = row_sq + col * col
        scaled = RATIO_SQ * square
        phase = -2.0 * math.pi * distance / wavelength * scaled / (1.0 + jnp.sqrt(1.0 - scaled))
        total = jnp.where(
            row_in & (jnp.abs(col) < LIMIT), jnp.exp(square * (-2.0 / (LIMIT * LIMIT))), 0.0
        )
        quarter = jnp.floor(phase * (2.0 / math.pi) + 0.5)
        left = phase - quarter * 1.5703125
        left = left - quarter * 4.837512969970703125e-4
        left = left - quarter * 7.549789954891882e-8
        sq = left * left
        sine = ((-1.9515295891e-4 * sq + 8.3321608736e-3) * sq - 1.6666654611e-1) * sq * left + left
        cosine = (
            (2.443315711809948e-5 * sq - 1.388731625493765e-3) * sq + 4.166664568298827e-2
        ) * sq * sq - 0.5 * sq + 1.0
        which = quarter.astype(jnp.int32) & 3
        swap = (which & 1) == 1
        cos_part = jnp.where(swap, sine, cosine)
        sin_part = jnp.where(swap, cosine, sine)
        cos_part = jnp.where((which == 1) | (which == 2), -cos_part, cos_part)
        sin_part = jnp.where(which >= 2, -sin_part, sin_part)
        at = (u % (RES // 2)) * 16 + (u // (RES // 2)) * 8
        gain_re[0, at : at + 8, :] = total * cos_part
        gain_im[0, at : at + 8, :] = total * sin_part


def encode(near_real, near_imag, peak, even_cell):
    amplitude = jnp.sqrt(near_real * near_real + near_imag * near_imag)
    amp_level = 0.8 * amplitude / peak
    amp_floor = jnp.maximum(amplitude, 0.05 * peak)
    unit_real = near_real / amp_floor
    unit_imag = near_imag / amp_floor
    lift_part = jnp.sqrt(1.0 - amp_level * amp_level)
    cell_sign = jnp.where(even_cell, 1.0, -1.0)
    out_real = unit_real * amp_level + cell_sign * unit_imag * lift_part
    out_imag = unit_imag * amp_level - cell_sign * unit_real * lift_part
    return (out_real, out_imag)


def encode_kernel(peak, near, slm_real, slm_imag):
    shape = slm_real.shape
    cell = lax.broadcasted_iota(jnp.int32, shape, 0) + lax.broadcasted_iota(jnp.int32, shape, 1)
    slm_real[...], slm_imag[...] = encode(near[0, 0], near[0, 1], peak[0], (cell & 1) == 0)


def params():
    return pltpu.CompilerParams(vmem_limit_bytes=VMEM)


def whole(memory=pltpu.VMEM):
    return pl.BlockSpec(memory_space=memory)


def body(field_real, field_imag):
    row_total, col_total = lax.axis_size("row"), lax.axis_size("col")
    devices = row_total * col_total
    device = lax.axis_index("row") * col_total + lax.axis_index("col")
    height, tile_width = field_real.shape
    width = tile_width // row_total
    parts = max(1, devices // RES)
    groups = -(-(2 * HALF + 1) // (8 * parts)) * parts
    own = groups // parts
    pair = 2 if width == 128 else 1

    fwd_high, fwd_low, inv_high, inv_low = column_tables(groups)
    line_fh, line_fl, line_ih, line_il = line_tables()
    twist_c, twist_s = twist_table()
    twist_line = np.concatenate([twist_c, twist_s], axis=0)
    twist_col = np.concatenate([twist_c, twist_s], axis=0).T.copy()
    twist_col = np.pad(twist_col, ((0, 0), (0, 128 - 2 * RES)))

    u = device // parts
    k0 = jnp.where(u >= RES // 2, u - RES, u)
    place = jnp.stack([k0, (device % parts) * own]).astype(jnp.int32)
    gain_shape = jax.ShapeDtypeStruct((own, RES * 8, 128), jnp.float32)
    gain_spec = pl.BlockSpec((1, RES * 8, 128), lambda g: (g, 0, 0))
    gain_re, gain_im = pl.pallas_call(
        gain_kernel,
        grid=(own,),
        in_specs=[whole(pltpu.SMEM)],
        out_specs=[gain_spec, gain_spec],
        out_shape=[gain_shape, gain_shape],
        compiler_params=params(),
        name="gain",
    )(place)

    packed = jnp.stack([field_real, field_imag])
    packed = packed.reshape(2, height, row_total, width).transpose(2, 0, 1, 3)
    columns = lax.all_to_all(packed, "row", split_axis=0, concat_axis=0, tiled=True)

    lines_shape = jax.ShapeDtypeStruct((RES, groups * 16, width), jnp.float32)
    slab = pltpu.VMEM((RES // pair, 2 * INNER, pair * width), jnp.bfloat16)
    lines = pl.pallas_call(
        column_forward_kernel,
        in_specs=[whole()] * 4,
        out_specs=whole(),
        out_shape=lines_shape,
        scratch_shapes=[slab, slab],
        compiler_params=params(),
        name="column_forward",
    )(columns, twist_col, fwd_high, fwd_low)

    lines = lines.reshape(devices, own * 16, width)
    lines = lax.all_to_all(lines, ("row", "col"), split_axis=0, concat_axis=0, tiled=True)
    if width == 128:
        order = tuple((b % row_total) * col_total + b // row_total for b in range(N // 128))
    else:
        order = tuple(range(N // 128))
        lines = lines.reshape(row_total, col_total, own * 16, width).transpose(2, 1, 0, 3)
        lines = lines.reshape(own * 16, N // 128, 128).transpose(1, 0, 2)

    lines_spec = pl.BlockSpec((N // 128, 16, 128), lambda g: (0, g, 0))
    gain_spec = pl.BlockSpec((1, RES * 8, 128), lambda g: (g, 0, 0))
    lines = pl.pallas_call(
        partial(line_kernel, order),
        grid=(own,),
        in_specs=[lines_spec, gain_spec, gain_spec] + [whole()] * 5,
        out_specs=lines_spec,
        out_shape=jax.ShapeDtypeStruct((N // 128, own * 16, 128), jnp.float32),
        scratch_shapes=[
            pltpu.VMEM((RES * 8, 2 * INNER), jnp.bfloat16),
            pltpu.VMEM((RES * 8, 2 * INNER), jnp.bfloat16),
            pltpu.VMEM((RES * 8, 2 * INNER), jnp.float32),
        ],
        compiler_params=params(),
        name="line",
    )(lines, gain_re, gain_im, twist_line, line_fh, line_fl, line_ih, line_il)

    if width != 128:
        lines = lines.transpose(1, 0, 2).reshape(own * 16, col_total, row_total, width)
        lines = lines.transpose(2, 1, 0, 3).reshape(devices, own * 16, width)
    lines = lax.all_to_all(lines, ("row", "col"), split_axis=0, concat_axis=0, tiled=True)
    lines = lines.reshape(RES, groups * 16, width)

    near, top = pl.pallas_call(
        column_inverse_kernel,
        in_specs=[whole()] * 4,
        out_specs=[whole(), whole()],
        out_shape=[
            jax.ShapeDtypeStruct((row_total, 2, height, width), jnp.float32),
            jax.ShapeDtypeStruct((8, width), jnp.float32),
        ],
        scratch_shapes=[pltpu.VMEM((RES, 2 * INNER, width), jnp.float32)],
        compiler_params=params(),
        name="column_inverse",
    )(lines, twist_col, inv_high, inv_low)

    peak = jnp.sqrt(lax.pmax(jnp.max(top), ("row", "col")))
    near = lax.all_to_all(near, "row", split_axis=0, concat_axis=0, tiled=True)
    if width != 128:
        near = near.transpose(1, 2, 0, 3).reshape(2, height, tile_width)
        even_cell = (jnp.arange(height)[:, None] + jnp.arange(tile_width)[None, :]) % 2 == 0
        return encode(near[0], near[1], peak, even_cell)
    rows = 256
    tile_spec = pl.BlockSpec((rows, width), lambda i, r: (i, r))
    tile_shape = jax.ShapeDtypeStruct((height, tile_width), jnp.float32)
    return pl.pallas_call(
        encode_kernel,
        grid=(height // rows, row_total),
        in_specs=[
            whole(pltpu.SMEM),
            pl.BlockSpec((1, 2, rows, width), lambda i, r: (r, 0, i, 0)),
        ],
        out_specs=[tile_spec, tile_spec],
        out_shape=[tile_shape, tile_shape],
        compiler_params=params(),
        name="encode",
    )(peak.reshape(1), near)


def solution(mesh):
    in_specs = (P("row", "col"), P("row", "col"))
    out_specs = (P("row", "col"), P("row", "col"))
    return jax.shard_map(body, mesh=mesh, in_specs=in_specs, out_specs=out_specs, check_vma=False)
```

time: 1030 us -> 352 us (0.34); the launches traced: 1020 us -> 351 us
  matrix products: 357 us -> 0 us
  waiting for transfers between devices: 350 us -> 59.7 us
  local copies, waits for them, and re-layouts: 92.9 us -> 9.11 us
  Pallas kernels: 0 us -> 65.5 us
  blocking collectives: 146 us -> 202 us
  other arithmetic: 47.4 us -> 3.77 us
  starting transfers between devices: 22.9 us -> 9.37 us
    dot_general x32 -> x0, matrix products: 357 us -> none  [the longest x16 183 us: complex_einsum(): out_real = real_dot(left_real, right_real) - real_dot(left_imag, right_imag)]
    all_to_all x6 -> x2, waiting for transfers between devices: 350 us -> 59.7 us  [the longest x1 59.7 us: body(): lax.all_to_all(lines, ('row', 'col'), split_axis=0, concat_axis=0, tiled=...]
    pallas_call x0 -> x5, Pallas kernels: none -> 65.5 us  [the longest x1 17 us: body(): pl.pallas_call(column_inverse_kernel, in_specs=[whole()] * 4, out_specs=[...]
    pmax x1, blocking collectives: 37.1 us -> 79.1 us  [body(): peak = jnp.sqrt(lax.pmax(jnp.max(top), ('row', 'col')))]
    add x5 -> x0, other arithmetic: 40.9 us -> none  [the longest x1 40.8 us: body(): mixed_imag = spec_real * gain_imag + spec_imag * gain_real]
    add x5 -> x0, local copies, waits for them, and re-layouts: 28.3 us -> none  [the longest x4 19.6 us: complex_einsum(): out_imag = real_dot(left_real, right_imag) + real_dot(left_imag, right_real)]
    sub x5 -> x0, local copies, waits for them, and re-layouts: 27.2 us -> none  [the longest x4 18.5 us: complex_einsum(): out_real = real_dot(left_real, right_real) - real_dot(left_imag, right_imag)]
    all_to_all x6 -> x0, local copies, waits for them, and re-layouts: 24.6 us -> none  [the longest x1 6.64 us: body(): lax.all_to_all(back_imag, ('row', 'col'), split_axis=0, concat_axis=1, ti...]
  transfers between devices with their start and end apart: 6 -> 2, of which waited for: 6 -> 1; matrix products, arithmetic and copies ran while one was open for 13% -> 0% of each run, Pallas kernels for 0% -> 2%
where the time goes in v1:
time: 352 us; the launch traced here: 351 us
  blocking collectives  202 us (57%)
  Pallas kernels  65.5 us (19%)
  waiting for transfers between devices  59.7 us (17%)
  starting transfers between devices  9.37 us (3%)
  local copies, waits for them, and re-layouts  9.11 us (3%)
  other arithmetic  3.77 us (1%)
    pmax x1, blocking collectives, body(): peak = jnp.sqrt(lax.pmax(jnp.max(top), ('row', 'col')))  79.1 us
    all_to_all x1, blocking collectives, body(): lax.all_to_all(lines, ('row', 'col'), split_axis=0, concat_axis=0, tiled=...  70.4 us
    all_to_all x1, waiting for transfers between devices, body(): lax.all_to_all(lines, ('row', 'col'), split_axis=0, concat_axis=0, tiled=...  59.7 us
    all_to_all x1, blocking collectives, body(): lax.all_to_all(packed, 'row', split_axis=0, concat_axis=0, tiled=True)  52.9 us
    pallas_call x1, Pallas kernels, body(): pl.pallas_call(column_inverse_kernel, in_specs=[whole()] * 4, out_specs=[...  17 us
    pallas_call x1, Pallas kernels, body(): pl.pallas_call(partial(line_kernel, order), grid=(own,), in_specs=[lines_...  16.9 us
    pallas_call x1, Pallas kernels, body(): pl.pallas_call(column_forward_kernel, in_specs=[whole()] * 4, out_specs=w...  13.9 us
    pallas_call x1, Pallas kernels, body(): pl.pallas_call(encode_kernel, grid=(height // rows, row_total), in_specs=...  11.1 us
  transfers between devices with their start and end apart: 2, of which 1 were waited for; matrix products, arithmetic and copies ran while one was open for 0% of the time, Pallas kernels for 2%

profile of v1, /device:TPU:0, one launch (start us, length us, event | category | flops | bytes accessed | tf_op | source)
XLA Modules:
  0.0 351.3 jit_solution(14797947444725510821)
XLA Ops:
  0.6 1.9 copy.14
  2.6 1.8 copy.16
  4.4 1.9 copy.15
  6.3 1.8 copy.17
  8.1 2.5 maximum_bitcast_fusion
  10.6 52.9 %all_to_all.20.field = f32[4,2,1024,128]{3,2,1,0:T(8,128)} all-to-all(f32[4,2,1024,128]{3,2,1,0:T(8,128)S(1)} %maximum_bitcast_fusion), channel_id=1, replica_groups=mesh['row'=4,'col'=8] {'row'}, dimensions={0} | all-to-all | bytes 8388608 | tf_op jit(solution)/shard_map/all_to_all | solution.py:410
  63.6 13.9 %column_forward.1 = f32[32,176,128]{2,1,0:T(8,128)} custom-call(f32[4,2,1024,128]{3,2,1,0:T(8,128)} %all_to_all.20.field, f32[256,128]{1,0:T(8,128)} %constant.60.clone.twist, bf16[176,512]{1,0:T(8,128)(2,1)} %constant.61.clone.mat_high, bf16[176,512]{1,0:T(8,128)(2,1)} %constant.62.clone.mat_low), custom_call_target="tpu_custom_call" | custom-call | tf_op jit(solution)/shard_map/column_forward/pallas_call | solution.py:414
  77.4 4.4 %all-to-all-start.1 = ((f32[32,176,128]{2,1,0:T(8,128)}), f32[32,176,128]{2,1,0:T(8,128)S(1)}, u32[]{:S(2)}, u32[]{:S(2)}) async-start(f32[32,176,128]{2,1,0:T(8,128)} %column_forward.1), calls=%async_computation.1 | async-start | bytes 5767168 | tf_op jit(solution)/shard_map/all_to_all | solution.py:425
  81.9 0.6 pad_add_fusion.place
  82.5 6.7 %gain.1 = (f32[11,256,128]{2,1,0:T(8,128)}, f32[11,256,128]{2,1,0:T(8,128)}) custom-call(s32[2]{0:T(128)} %pad_add_fusion.place), custom_call_target="tpu_custom_call" | custom-call | tf_op jit(solution)/shard_map/gain/pallas_call | solution.py:398
  89.2 59.7 %all-to-all-done.1.lines = f32[32,176,128]{2,1,0:T(8,128)S(1)} async-done(((f32[32,176,128]{2,1,0:T(8,128)}), f32[32,176,128]{2,1,0:T(8,128)S(1)}, u32[]{:S(2)}, u32[]{:S(2)}) %all-to-all-start.1) | async-done | bytes 2883616 | tf_op jit(solution)/shard_map/all_to_all | solution.py:425
  148.9 0.0 copy-start
  148.9 1.6 copy-done
  150.5 16.9 %line.1 = f32[32,176,128]{2,1,0:T(8,128)} custom-call(f32[32,176,128]{2,1,0:T(8,128)} %copy-done, f32[11,256,128]{2,1,0:T(8,128)} %get-tuple-element.6.gain_re, f32[11,256,128]{2,1,0:T(8,128)} %get-tuple-element.7.gain_im, f32[64,256]{1,0:T(8,128)} %constant.63.clone.twist, bf16[512,256]{1,0:T(8,128)(2,1)} %constant.64.clone.fwd_high, ...), custom_call_target="tpu_custom_call" | custom-call | tf_op jit(solution)/shard_map/line/pallas_call | solution.py:435
  167.4 70.4 %all_to_all.21.lines = f32[32,176,128]{2,1,0:T(8,128)} all-to-all(f32[32,176,128]{2,1,0:T(8,128)} %line.1), channel_id=1, replica_groups=mesh['row'=4,'col'=8] {'row','col'}, dimensions={0} | all-to-all | bytes 5767168 | tf_op jit(solution)/shard_map/all_to_all | solution.py:453
  237.8 17.0 %column_inverse.1 = (f32[4,2,1024,128]{3,2,1,0:T(8,128)}, f32[8,128]{1,0:T(8,128)}) custom-call(f32[32,176,128]{2,1,0:T(8,128)} %all_to_all.21.lines, f32[256,128]{1,0:T(8,128)} %constant.60.clone.twist, bf16[512,176]{1,0:T(8,128)(2,1)} %constant.68.clone.mat_high, bf16[512,176]{1,0:T(8,128)(2,1)} %constant.69.clone.mat_low), custom_call_target="tpu_custom_call" | custom-call | tf_op jit(solution)/shard_map/column_inverse/pallas_call | solution.py:456
  254.8 0.0 copy-start.1
  254.9 5.0 %all-to-all-start.3 = ((f32[4,2,1024,128]{3,2,1,0:T(8,128)}), f32[4,2,1024,128]{3,2,1,0:T(8,128)}, u32[]{:S(2)}, u32[]{:S(2)}) async-start(f32[4,2,1024,128]{3,2,1,0:T(8,128)} %get-tuple-element.9), calls=%async_computation.3 | async-start | bytes 8388608 | tf_op jit(solution)/shard_map/all_to_all | solution.py:470
  259.8 0.0 copy-done.1
  259.8 0.6 reduce_max.9
  260.4 79.1 %pmax.7 = f32[]{:T(128)} all-reduce(f32[]{:T(128)} %reduce_max.9), channel_id=1, replica_groups=mesh['row'=4,'col'=8] {'row','col'}, use_global_device_ids=true, to_apply=%region_1.2 | all-reduce | flops 1 | bytes 8 | tf_op jit(solution)/shard_map/pmax | solution.py:469
  340.2 0.0 all-to-all-done.3.near
  340.3 11.1 %encode.1 = (f32[1024,512]{1,0:T(8,128)}, f32[1024,512]{1,0:T(8,128)}) custom-call(f32[1]{0:T(128)} %bitcast.4.peak, f32[4,2,1024,128]{3,2,1,0:T(8,128)} %all-to-all-done.3.near), custom_call_target="tpu_custom_call" | custom-call | tf_op jit(solution)/shard_map/encode/pallas_call | solution.py:478
Async XLA Ops:
  77.4 71.4 %all-to-all-start.1 = ((f32[32,176,128]{2,1,0:T(8,128)}), f32[32,176,128]{2,1,0:T(8,128)S(1)}, u32[]{:S(2)}, u32[]{:S(2)}) async-start(f32[32,176,128]{2,1,0:T(8,128)} %column_forward.1), calls=%async_computation.1 | async-start | bytes 5767168 | tf_op jit(solution)/shard_map/all_to_all | solution.py:425
  148.9 1.6 copy-start
  254.8 5.0 %copy-start.1 = (f32[8,128]{1,0:T(8,128)S(1)}, f32[8,128]{1,0:T(8,128)}, u32[]{:S(2)}) copy-start(f32[8,128]{1,0:T(8,128)} %get-tuple-element.8) | copy-start | bytes 12292
  254.9 85.4 %all-to-all-start.3 = ((f32[4,2,1024,128]{3,2,1,0:T(8,128)}), f32[4,2,1024,128]{3,2,1,0:T(8,128)}, u32[]{:S(2)}, u32[]{:S(2)}) async-start(f32[4,2,1024,128]{3,2,1,0:T(8,128)} %get-tuple-element.9), calls=%async_computation.3 | async-start | bytes 8388608 | tf_op jit(solution)/shard_map/all_to_all | solution.py:470

commit v2 on v1

--- a/solution.py
+++ b/solution.py
@@ -69,7 +69,13 @@
         else:
             forward[at, :INNER], forward[at, INNER:] = -s, c
             inverse[:INNER, at], inverse[INNER:, at] = -s, c
-    return split16(forward) + split16(inverse)
+    chunk = INNER // 2
+    forward = forward.reshape(-1, 2, 2, chunk).transpose(2, 0, 1, 3).reshape(2, -1, 2 * chunk)
+    inverse = inverse.reshape(2, 2, chunk, -1).transpose(1, 0, 2, 3).reshape(2, 2 * chunk, -1)
+    return (
+        np.concatenate(split16(forward), axis=1),
+        np.concatenate(split16(inverse), axis=1),
+    )
 
 
 def line_tables():
@@ -162,18 +168,35 @@
     return jnp.dot(left, right, preferred_element_type=jnp.float32)
 
 
-def column_forward_kernel(field, twist, mat_high, mat_low, out, high, low):
+def three_left(stacked, count, high, low):
+    both = dot16(stacked[...], high)
+    return both[:count] + both[count:] + dot16(stacked[:count], low)
+
+
+def three_right(stacked, count, high, low):
+    both = dot16(stacked, high)
+    return both[:count] + both[count:] + dot16(stacked[:count], low)
+
+
+def column_forward_kernel(field, twist, matrix, out, high, low):
     width = field.shape[-1]
-    per_source = field.shape[2] // INNER
-    pair = high.shape[2] // width
-
-    def step(t, carry):
+    per_source = field.shape[2]
+    chunk = field.shape[3]
+    pair = high.shape[-1] // width
+    rows_out = out.shape[1]
+    tiles = chunk // 16
+    pairs = RES // pair
+    now = pl.program_id(0)
+    steps = INNER // chunk
+
+    def butterflies(t):
         q0 = pl.multiple_of(t * 16, 16)
+        slot = now % 2
 
         def get(n):
             source, block = divmod(n, per_source)
-            rows = pl.ds(block * INNER + q0, 16)
-            return field[source, 0, rows, :], field[source, 1, rows, :]
+            rows = pl.ds(q0, 16)
+            return field[source, 0, block, rows, :], field[source, 1, block, rows, :]
 
         def put(u, value):
             re, im = value
@@ -181,74 +204,132 @@
             s = twist[pl.ds(q0, 16), RES + u : RES + u + 1]
             lanes = pl.ds((u % pair) * width, width)
             for part, item in enumerate((re * c - im * s, re * s + im * c)):
-                rows = pl.ds(part * INNER + q0, 16)
-                high[u // pair, rows, lanes], low[u // pair, rows, lanes] = high_low(item)
+                rows = pl.ds(part * chunk + q0, 16)
+                at = (slot, u // pair, rows, lanes)
+                high[at], low[at] = high_low(item)
 
         forward_slabs(get, put)
-        return carry
-
-    lax.fori_loop(0, INNER // 16, step, 0)
-
-    def product(p, carry):
-        done = (
-            dot16(mat_high[...], high[p])
-            + dot16(mat_high[...], low[p])
-            + dot16(mat_low[...], high[p])
-        )
+
+    def product(p, first):
+        slot = (now + 1) % 2
+        done = three_left(matrix.at[0], rows_out, high[slot, p], low[slot, p])
         for part in range(pair):
-            out[p * pair + part] = done[:, part * width : (part + 1) * width]
-        return carry
-
-    lax.fori_loop(0, RES // pair, product, 0)
-
-
-def column_inverse_kernel(lines, twist, mat_high, mat_low, out, top, back):
+            item = done[:, part * width : (part + 1) * width]
+            at = p * pair + part
+            out[at] = item if first else out[at] + item
+
+    @pl.when(now == 0)
+    def _():
+        pl.loop(0, tiles)(butterflies)
+
+    for step in range(1, steps + 1):
+
+        @pl.when(now == step)
+        def _():
+            @pl.loop(0, tiles)
+            def _(t):
+                for part in range(pairs // tiles):
+                    product(t * (pairs // tiles) + part, step == 1)
+                if step < steps:
+                    butterflies(t)
+
+
+def column_inverse_kernel(lines, twist, matrix, out, top, high, low, back):
     width = lines.shape[-1]
-    per_dest = out.shape[2] // INNER
-    pair = 2 if width == 128 else 1
-
-    def product(p, carry):
-        blocks = [lines[p * pair + part] for part in range(pair)]
-        high, low = high_low(jnp.concatenate(blocks, axis=1) if pair > 1 else blocks[0])
-        done = (
-            dot16(mat_high[...], high) + dot16(mat_high[...], low) + dot16(mat_low[...], high)
-        )
+    per_dest = out.shape[2]
+    chunk = out.shape[3]
+    pair = high.shape[-1] // width
+    tiles = chunk // 8
+    pairs = RES // pair
+    now = pl.program_id(0)
+    steps = INNER // chunk
+
+    def product(p):
+        done = three_left(matrix.at[0], 2 * chunk, high[p], low[p])
+        slot = now % 2
         for part in range(pair):
-            back[p * pair + part] = done[:, part * width : (part + 1) * width]
-        return carry
-
-    lax.fori_loop(0, RES // pair, product, 0)
-    top[...] = jnp.zeros_like(top)
-
-    def step(t, carry):
+            back[slot, p * pair + part] = done[:, part * width : (part + 1) * width]
+
+    def butterflies(t):
         q0 = pl.multiple_of(t * 8, 8)
+        slot = (now + 1) % 2
         largest = []
 
         def get(u):
-            re = back[u, pl.ds(q0, 8), :]
-            im = back[u, pl.ds(INNER + q0, 8), :]
+            re = back[slot, u, pl.ds(q0, 8), :]
+            im = back[slot, u, pl.ds(chunk + q0, 8), :]
             c = twist[pl.ds(q0, 8), u : u + 1]
             s = twist[pl.ds(q0, 8), RES + u : RES + u + 1]
             return re * c + im * s, im * c - re * s
 
         def put(n, value):
             dest, block = divmod(n, per_dest)
-            rows = pl.ds(block * INNER + q0, 8)
-            out[dest, 0, rows, :], out[dest, 1, rows, :] = value
+            rows = pl.ds(q0, 8)
+            out[dest, 0, block, rows, :], out[dest, 1, block, rows, :] = value
             largest.append(value[0] * value[0] + value[1] * value[1])
 
         inverse_slabs(get, put)
         while len(largest) > 1:
             largest = [jnp.maximum(a, b) for a, b in zip(largest[0::2], largest[1::2])]
         top[...] = jnp.maximum(top[...], largest[0])
-        return carry
-
-    lax.fori_loop(0, INNER // 8, step, 0)
+
+    @pl.when(now == 0)
+    def _():
+        top[...] = jnp.zeros_like(top)
+
+        @pl.loop(0, pairs)
+        def _(p):
+            blocks = [lines[p * pair + part] for part in range(pair)]
+            joined = jnp.concatenate(blocks, axis=1) if pair > 1 else blocks[0]
+            high[p], low[p] = high_low(joined)
+            product(p)
+
+    for step in range(1, steps + 1):
+
+        @pl.when(now == step)
+        def _():
+            @pl.loop(0, tiles)
+            def _(t):
+                butterflies(t)
+                if step < steps:
+                    for part in range(pairs // tiles):
+                        product(t * (pairs // tiles) + part)
 
 
 def line_kernel(
-    order, lines, gain_re, gain_im, twist, fwd_high, fwd_low, inv_high, inv_low, out, high, low, back
+    order, lines, gain_re, gain_im, twist, fwd_high, fwd_low, inv_high, inv_low, out, stacked, back
 ):
+    half = RES * 8
+
+    for side in range(2):
+        lanes = pl.ds(side * 128, 128)
+
+        def get(u):
+            rows = pl.ds((u % (RES // 2)) * 16 + (u // (RES // 2)) * 8, 8)
+            re = back[rows, pl.ds(side * 128, 128)]
+            im = back[rows, pl.ds(INNER + side * 128, 128)]
+            c = twist[u : u + 1, lanes]
+            s = twist[RES + u : RES + u + 1, lanes]
+            return re * c + im * s, im * c - re * s
+
+        def put(m, value):
+            block = order[2 * m + side]
+            out[block, 0:8, :], out[block, 8:16, :] = value
+
+        inverse_slabs(get, put)
+
+    spec = three_right(stacked[...], half, fwd_high[...], fwd_low[...])
+    spec_re, spec_im = spec[:, :128], spec[:, 128:]
+    mixed = jnp.concatenate(
+        [
+            spec_re * gain_re[0] - spec_im * gain_im[0],
+            spec_re * gain_im[0] + spec_im * gain_re[0],
+        ],
+        axis=1,
+    )
+    mixed = jnp.concatenate(high_low(mixed), axis=0)
+    back[...] = three_right(mixed, half, inv_high[...], inv_low[...])
+
     for side in range(2):
         lanes = pl.ds(side * 128, 128)
         waiting = {}
@@ -264,49 +345,17 @@
             waiting[u] = (re * c - im * s, re * s + im * c)
             v = (u + RES // 2) % RES
             if v in waiting:
-                low_u = min(u, v)
-                rows = pl.ds(low_u * 16, 16)
+                first = min(u, v)
+                rows = pl.ds(first * 16, 16)
+                rows_low = pl.ds(half + first * 16, 16)
                 for part in range(2):
-                    item = jnp.concatenate([waiting[low_u][part], waiting[low_u + RES // 2][part]], axis=0)
+                    item = jnp.concatenate(
+                        [waiting[first][part], waiting[first + RES // 2][part]], axis=0
+                    )
                     at = pl.ds(part * INNER + side * 128, 128)
-                    high[rows, at], low[rows, at] = high_low(item)
+                    stacked[rows, at], stacked[rows_low, at] = high_low(item)
 
         forward_slabs(get, put)
-
-    spec = (
-        dot16(high[...], fwd_high[...]) + dot16(high[...], fwd_low[...]) + dot16(low[...], fwd_high[...])
-    )
-    spec_re, spec_im = spec[:, :128], spec[:, 128:]
-    mixed = jnp.concatenate(
-        [
-            spec_re * gain_re[0] - spec_im * gain_im[0],
-            spec_re * gain_im[0] + spec_im * gain_re[0],
-        ],
-        axis=1,
-    )
-    mixed_high, mixed_low = high_low(mixed)
-    back[...] = (
-        dot16(mixed_high, inv_high[...])
-        + dot16(mixed_high, inv_low[...])
-        + dot16(mixed_low, inv_high[...])
-    )
-
-    for side in range(2):
-        lanes = pl.ds(side * 128, 128)
-
-        def get(u):
-            rows = pl.ds((u % (RES // 2)) * 16 + (u // (RES // 2)) * 8, 8)
-            re = back[rows, pl.ds(side * 128, 128)]
-            im = back[rows, pl.ds(INNER + side * 128, 128)]
-            c = twist[u : u + 1, lanes]
-            s = twist[RES + u : RES + u + 1, lanes]
-            return re * c + im * s, im * c - re * s
-
-        def put(m, value):
-            block = order[2 * m + side]
-            out[block, 0:8, :], out[block, 8:16, :] = value
-
-        inverse_slabs(get, put)
 
 
 def gain_kernel(place, gain_re, gain_im):
@@ -345,23 +394,32 @@
         gain_im[0, at : at + 8, :] = total * sin_part
 
 
+def inverse_root(value):
+    root = lax.rsqrt(value)
+    return root * (1.5 - 0.5 * (value * root) * root)
+
+
 def encode(near_real, near_imag, peak, even_cell):
-    amplitude = jnp.sqrt(near_real * near_real + near_imag * near_imag)
-    amp_level = 0.8 * amplitude / peak
-    amp_floor = jnp.maximum(amplitude, 0.05 * peak)
-    unit_real = near_real / amp_floor
-    unit_imag = near_imag / amp_floor
-    lift_part = jnp.sqrt(1.0 - amp_level * amp_level)
-    cell_sign = jnp.where(even_cell, 1.0, -1.0)
-    out_real = unit_real * amp_level + cell_sign * unit_imag * lift_part
-    out_imag = unit_imag * amp_level - cell_sign * unit_real * lift_part
-    return (out_real, out_imag)
+    square = near_real * near_real + near_imag * near_imag
+    root = inverse_root(jnp.maximum(square, 1.2e-38))
+    amp_level = (square * root) * (0.8 / peak)
+    unit = jnp.minimum(root, 20.0 / peak)
+    rest = 1.0 - amp_level * amp_level
+    lift_part = rest * inverse_root(rest)
+    level = unit * amp_level
+    lift = jnp.where(even_cell, unit * lift_part, -(unit * lift_part))
+    return (near_real * level + near_imag * lift, near_imag * level - near_real * lift)
 
 
 def encode_kernel(peak, near, slm_real, slm_imag):
     shape = slm_real.shape
     cell = lax.broadcasted_iota(jnp.int32, shape, 0) + lax.broadcasted_iota(jnp.int32, shape, 1)
     slm_real[...], slm_imag[...] = encode(near[0, 0], near[0, 1], peak[0], (cell & 1) == 0)
+
+
+def pack_kernel(field_real, field_imag, packed):
+    packed[0, 0] = field_real[...]
+    packed[0, 1] = field_imag[...]
 
 
 def params():
@@ -383,7 +441,7 @@
     own = groups // parts
     pair = 2 if width == 128 else 1
 
-    fwd_high, fwd_low, inv_high, inv_low = column_tables(groups)
+    fwd_col, inv_col = column_tables(groups)
     line_fh, line_fl, line_ih, line_il = line_tables()
     twist_c, twist_s = twist_table()
     twist_line = np.concatenate([twist_c, twist_s], axis=0)
@@ -405,21 +463,42 @@
         name="gain",
     )(place)
 
-    packed = jnp.stack([field_real, field_imag])
-    packed = packed.reshape(2, height, row_total, width).transpose(2, 0, 1, 3)
+    if width == 128:
+        rows = min(height, 512)
+        packed = pl.pallas_call(
+            pack_kernel,
+            grid=(row_total, height // rows),
+            in_specs=[pl.BlockSpec((rows, width), lambda r, i: (i, r))] * 2,
+            out_specs=pl.BlockSpec((1, 2, rows, width), lambda r, i: (r, 0, i, 0)),
+            out_shape=jax.ShapeDtypeStruct((row_total, 2, height, width), jnp.float32),
+            compiler_params=params(),
+            name="pack",
+        )(field_real, field_imag)
+    else:
+        packed = jnp.stack([field_real, field_imag])
+        packed = packed.reshape(2, height, row_total, width).transpose(2, 0, 1, 3)
     columns = lax.all_to_all(packed, "row", split_axis=0, concat_axis=0, tiled=True)
 
-    lines_shape = jax.ShapeDtypeStruct((RES, groups * 16, width), jnp.float32)
-    slab = pltpu.VMEM((RES // pair, 2 * INNER, pair * width), jnp.bfloat16)
+    blocks = height // INNER
+    chunk = INNER // 2
+    steps = INNER // chunk
+    columns = columns.reshape(row_total, 2, blocks, INNER, width)
+    tall = (row_total, 2, blocks, chunk, width)
+    slab = pltpu.VMEM((2, RES // pair, 2 * chunk, pair * width), jnp.bfloat16)
     lines = pl.pallas_call(
         column_forward_kernel,
-        in_specs=[whole()] * 4,
+        grid=(steps + 1,),
+        in_specs=[
+            pl.BlockSpec(tall, lambda i: (0, 0, 0, jnp.minimum(i, steps - 1), 0)),
+            pl.BlockSpec((chunk, 128), lambda i: (jnp.minimum(i, steps - 1), 0)),
+            pl.BlockSpec((1, 2 * groups * 16, 2 * chunk), lambda i: (jnp.maximum(i - 1, 0), 0, 0)),
+        ],
         out_specs=whole(),
-        out_shape=lines_shape,
+        out_shape=jax.ShapeDtypeStruct((RES, groups * 16, width), jnp.float32),
         scratch_shapes=[slab, slab],
         compiler_params=params(),
         name="column_forward",
-    )(columns, twist_col, fwd_high, fwd_low)
+    )(columns, twist_col, fwd_col)
 
     lines = lines.reshape(devices, own * 16, width)
     lines = lax.all_to_all(lines, ("row", "col"), split_axis=0, concat_axis=0, tiled=True)
@@ -430,17 +509,19 @@
         lines = lines.reshape(row_total, col_total, own * 16, width).transpose(2, 1, 0, 3)
         lines = lines.reshape(own * 16, N // 128, 128).transpose(1, 0, 2)
 
-    lines_spec = pl.BlockSpec((N // 128, 16, 128), lambda g: (0, g, 0))
-    gain_spec = pl.BlockSpec((1, RES * 8, 128), lambda g: (g, 0, 0))
+    last = own - 1
+    line_grain = (N // 128, 16, 128)
+    gain_grain = (1, RES * 8, 128)
     lines = pl.pallas_call(
         partial(line_kernel, order),
-        grid=(own,),
-        in_specs=[lines_spec, gain_spec, gain_spec] + [whole()] * 5,
-        out_specs=lines_spec,
+        grid=(own + 2,),
+        in_specs=[pl.BlockSpec(line_grain, lambda i: (0, jnp.minimum(i, last), 0))]
+        + [pl.BlockSpec(gain_grain, lambda i: (jnp.clip(i - 1, 0, last), 0, 0))] * 2
+        + [whole()] * 5,
+        out_specs=pl.BlockSpec(line_grain, lambda i: (0, jnp.clip(i - 2, 0, last), 0)),
         out_shape=jax.ShapeDtypeStruct((N // 128, own * 16, 128), jnp.float32),
         scratch_shapes=[
-            pltpu.VMEM((RES * 8, 2 * INNER), jnp.bfloat16),
-            pltpu.VMEM((RES * 8, 2 * INNER), jnp.bfloat16),
+            pltpu.VMEM((2 * RES * 8, 2 * INNER), jnp.bfloat16),
             pltpu.VMEM((RES * 8, 2 * INNER), jnp.float32),
         ],
         compiler_params=params(),
@@ -453,26 +534,45 @@
     lines = lax.all_to_all(lines, ("row", "col"), split_axis=0, concat_axis=0, tiled=True)
     lines = lines.reshape(RES, groups * 16, width)
 
+    slab = pltpu.VMEM((RES // pair, groups * 16, pair * width), jnp.bfloat16)
     near, top = pl.pallas_call(
         column_inverse_kernel,
-        in_specs=[whole()] * 4,
-        out_specs=[whole(), whole()],
+        grid=(steps + 1,),
+        in_specs=[
+            whole(),
+            pl.BlockSpec((chunk, 128), lambda i: (jnp.maximum(i - 1, 0), 0)),
+            pl.BlockSpec(
+                (1, 4 * chunk, groups * 16), lambda i: (jnp.minimum(i, steps - 1), 0, 0)
+            ),
+        ],
+        out_specs=[
+            pl.BlockSpec(tall, lambda i: (0, 0, 0, jnp.maximum(i - 1, 0), 0)),
+            whole(),
+        ],
         out_shape=[
-            jax.ShapeDtypeStruct((row_total, 2, height, width), jnp.float32),
+            jax.ShapeDtypeStruct((row_total, 2, blocks, INNER, width), jnp.float32),
             jax.ShapeDtypeStruct((8, width), jnp.float32),
         ],
-        scratch_shapes=[pltpu.VMEM((RES, 2 * INNER, width), jnp.float32)],
+        scratch_shapes=[slab, slab, pltpu.VMEM((2, RES, 2 * chunk, width), jnp.float32)],
         compiler_params=params(),
         name="column_inverse",
-    )(lines, twist_col, inv_high, inv_low)
-
-    peak = jnp.sqrt(lax.pmax(jnp.max(top), ("row", "col")))
+    )(lines, twist_col, inv_col)
+
+    near = near.reshape(row_total, 2, height, width)
     near = lax.all_to_all(near, "row", split_axis=0, concat_axis=0, tiled=True)
+    peak = jnp.max(top)
+    for axis, total in (("row", row_total), ("col", col_total)):
+        shift = 1
+        while shift < total:
+            partner = [(i, i ^ shift) for i in range(total)]
+            peak = jnp.maximum(peak, lax.ppermute(peak, axis, partner))
+            shift *= 2
+    peak = jnp.sqrt(peak)
     if width != 128:
         near = near.transpose(1, 2, 0, 3).reshape(2, height, tile_width)
         even_cell = (jnp.arange(height)[:, None] + jnp.arange(tile_width)[None, :]) % 2 == 0
         return encode(near[0], near[1], peak, even_cell)
-    rows = 256
+    rows = min(height, 512)
     tile_spec = pl.BlockSpec((rows, width), lambda i, r: (i, r))
     tile_shape = jax.ShapeDtypeStruct((height, tile_width), jnp.float32)
     return pl.pallas_call(

time: 352 us -> 330 us (0.938)
  blocking collectives: 202 us -> 125 us
  waiting for transfers between devices: 59.7 us -> 111 us
  starting transfers between devices: 9.37 us -> 17.9 us
  local copies, waits for them, and re-layouts: 9.11 us -> 1.62 us
    pmax x1 -> x0, blocking collectives: 79.1 us -> none  [body(): peak = jnp.sqrt(lax.pmax(jnp.max(top), ('row', 'col')))]
    ppermute x0 -> x5, waiting for transfers between devices: none -> 51.2 us  [body(): peak = jnp.maximum(peak, lax.ppermute(peak, axis, partner))]
    ppermute x0 -> x5, starting transfers between devices: none -> 8.42 us  [body(): peak = jnp.maximum(peak, lax.ppermute(peak, axis, partner))]
    pallas_call x3 -> x4, Pallas kernels: 47.8 us -> 52.3 us  [the longest x1 18.8 us: body(): pl.pallas_call(partial(line_kernel, order), grid=(own + 2,), in_specs=[pl...]
    unnamed x6 -> x4, local copies, waits for them, and re-layouts: 5.49 us -> 1.62 us
    another operation x2 -> x0, local copies, waits for them, and re-layouts: 3.62 us -> none  [body(): packed = jnp.stack([field_real, field_imag])]
  transfers between devices with their start and end apart: 2 -> 7, of which waited for: 1 -> 6; matrix products, arithmetic and copies ran while one was open for 0% -> 0% of each run, Pallas kernels for 2% -> 2%
where the time goes in v2:
time: 330 us; the launch traced here: 329 us
  blocking collectives  125 us (38%)
  waiting for transfers between devices  111 us (34%)
  Pallas kernels  67.1 us (20%)
  starting transfers between devices  17.9 us (5%)
  between operations  4.49 us (1%)
    all_to_all x1, blocking collectives, body(): lax.all_to_all(lines, ('row', 'col'), split_axis=0, concat_axis=0, tiled=...  70.4 us
    all_to_all x1, waiting for transfers between devices, body(): lax.all_to_all(lines, ('row', 'col'), split_axis=0, concat_axis=0, tiled=...  59.7 us
    all_to_all x1, blocking collectives, body(): lax.all_to_all(packed, 'row', split_axis=0, concat_axis=0, tiled=True)  55.1 us
    ppermute x5, waiting for transfers between devices, body(): peak = jnp.maximum(peak, lax.ppermute(peak, axis, partner))  51.2 us
    pallas_call x1, Pallas kernels, body(): pl.pallas_call(partial(line_kernel, order), grid=(own + 2,), in_specs=[pl...  18.8 us
    pallas_call x1, Pallas kernels, body(): pl.pallas_call(column_inverse_kernel, grid=(steps + 1,), in_specs=[whole(...  15.5 us
    pallas_call x1, Pallas kernels, body(): pl.pallas_call(column_forward_kernel, grid=(steps + 1,), in_specs=[pl.Blo...  11.3 us
    ppermute x5, starting transfers between devices, body(): peak = jnp.maximum(peak, lax.ppermute(peak, axis, partner))  8.42 us
  transfers between devices with their start and end apart: 7, of which 6 were waited for; matrix products, arithmetic and copies ran while one was open for 0% of the time, Pallas kernels for 2%

profile of v2, /device:TPU:0, one launch (start us, length us, event | category | flops | bytes accessed | tf_op | source)
XLA Modules:
  0.0 328.7 jit_solution(1236050998583950715)
XLA Ops:
  0.6 6.6 %pack.1 = f32[4,2,1024,128]{3,2,1,0:T(8,128)} custom-call(f32[1024,512]{1,0:T(8,128)} %field_real.1, f32[1024,512]{1,0:T(8,128)} %field_imag.1), custom_call_target="tpu_custom_call" | custom-call | tf_op jit(solution)/shard_map/pack/pallas_call | solution.py:468
  7.3 55.1 %all_to_all.20 = f32[4,2,1024,128]{3,2,1,0:T(8,128)} all-to-all(f32[4,2,1024,128]{3,2,1,0:T(8,128)} %pack.1), channel_id=1, replica_groups=mesh['row'=4,'col'=8] {'row'}, dimensions={0} | all-to-all | bytes 8388608 | tf_op jit(solution)/shard_map/all_to_all | solution.py:480
  62.3 11.3 %column_forward.1 = f32[32,176,128]{2,1,0:T(8,128)} custom-call(f32[4,2,4,256,128]{4,3,2,1,0:T(8,128)} %bitcast.4, f32[256,128]{1,0:T(8,128)} %constant.56.clone.twist, bf16[2,352,256]{2,1,0:T(8,128)(2,1)} %constant.57.clone.matrix), custom_call_target="tpu_custom_call" | custom-call | tf_op jit(solution)/shard_map/column_forward/pallas_call | solution.py:488
  73.7 4.5 %all-to-all-start.1 = ((f32[32,176,128]{2,1,0:T(8,128)}), f32[32,176,128]{2,1,0:T(8,128)S(1)}, u32[]{:S(2)}, u32[]{:S(2)}) async-start(f32[32,176,128]{2,1,0:T(8,128)} %column_forward.1), calls=%async_computation.1 | async-start | bytes 5767168 | tf_op jit(solution)/shard_map/all_to_all | solution.py:504
  78.2 0.6 pad_add_fusion.place
  78.8 6.7 %gain.1 = (f32[11,256,128]{2,1,0:T(8,128)}, f32[11,256,128]{2,1,0:T(8,128)}) custom-call(s32[2]{0:T(128)} %pad_add_fusion.place), custom_call_target="tpu_custom_call" | custom-call | tf_op jit(solution)/shard_map/gain/pallas_call | solution.py:456
  85.4 59.7 %all-to-all-done.1.lines = f32[32,176,128]{2,1,0:T(8,128)S(1)} async-done(((f32[32,176,128]{2,1,0:T(8,128)}), f32[32,176,128]{2,1,0:T(8,128)S(1)}, u32[]{:S(2)}, u32[]{:S(2)}) %all-to-all-start.1) | async-done | bytes 2883616 | tf_op jit(solution)/shard_map/all_to_all | solution.py:504
  145.2 0.0 copy-start
  145.2 1.6 copy-done
  146.8 18.8 %line.1 = f32[32,176,128]{2,1,0:T(8,128)} custom-call(f32[32,176,128]{2,1,0:T(8,128)} %copy-done, f32[11,256,128]{2,1,0:T(8,128)} %get-tuple-element.6.gain_re, f32[11,256,128]{2,1,0:T(8,128)} %get-tuple-element.7.gain_im, f32[64,256]{1,0:T(8,128)} %constant.58.clone.twist, bf16[512,256]{1,0:T(8,128)(2,1)} %constant.59.clone.fwd_high, ...), custom_call_target="tpu_custom_call" | custom-call | tf_op jit(solution)/shard_map/line/pallas_call | solution.py:515
  165.6 70.4 %all_to_all.21.lines = f32[32,176,128]{2,1,0:T(8,128)} all-to-all(f32[32,176,128]{2,1,0:T(8,128)} %line.1), channel_id=1, replica_groups=mesh['row'=4,'col'=8] {'row','col'}, dimensions={0} | all-to-all | bytes 5767168 | tf_op jit(solution)/shard_map/all_to_all | solution.py:534
  236.0 15.5 %column_inverse.1 = (f32[4,2,4,256,128]{4,3,2,1,0:T(8,128)}, f32[8,128]{1,0:T(8,128)}) custom-call(f32[32,176,128]{2,1,0:T(8,128)} %all_to_all.21.lines, f32[256,128]{1,0:T(8,128)} %constant.56.clone.twist, bf16[2,512,176]{2,1,0:T(8,128)(2,1)} %constant.63.clone.matrix), custom_call_target="tpu_custom_call" | custom-call | tf_op jit(solution)/shard_map/column_inverse/pallas_call | solution.py:538
  251.5 0.0 copy-start.1
  251.5 5.0 %all-to-all-start.3 = ((f32[4,2,1024,128]{3,2,1,0:T(8,128)}), f32[4,2,1024,128]{3,2,1,0:T(8,128)}, u32[]{:S(2)}, u32[]{:S(2)}) async-start(f32[4,2,1024,128]{3,2,1,0:T(8,128)} %bitcast.5), calls=%async_computation.3 | async-start | bytes 8388608 | tf_op jit(solution)/shard_map/all_to_all | solution.py:562
  256.5 0.0 copy-done.1
  256.5 0.6 reduce_max.9
  257.1 2.0 collective-permute-start
  259.1 44.9 %collective-permute-done = f32[]{:T(128)} collective-permute-done((f32[]{:T(128)}, f32[]{:T(128)}, u32[]{:S(2)}, u32[]{:S(2)}) %collective-permute-start) | collective-permute-done | bytes 36 | tf_op jit(solution)/shard_map/ppermute | solution.py:568
  305.3 2.8 collective-permute-start.1
  308.1 0.7 collective-permute-done.1
  309.5 0.9 collective-permute-start.2
  310.4 0.3 collective-permute-done.2
  311.3 1.4 collective-permute-start.3
  312.6 2.2 collective-permute-done.3
  315.4 1.4 collective-permute-start.4
  316.8 3.1 collective-permute-done.4
  320.6 0.0 all-to-all-done.3.near
  320.6 8.1 %encode.1 = (f32[1024,512]{1,0:T(8,128)}, f32[1024,512]{1,0:T(8,128)}) custom-call(f32[1]{0:T(128)} %bitcast.2.peak, f32[4,2,1024,128]{3,2,1,0:T(8,128)} %all-to-all-done.3.near), custom_call_target="tpu_custom_call" | custom-call | tf_op jit(solution)/shard_map/encode/pallas_call | solution.py:578
Async XLA Ops:
  73.7 71.5 %all-to-all-start.1 = ((f32[32,176,128]{2,1,0:T(8,128)}), f32[32,176,128]{2,1,0:T(8,128)S(1)}, u32[]{:S(2)}, u32[]{:S(2)}) async-start(f32[32,176,128]{2,1,0:T(8,128)} %column_forward.1), calls=%async_computation.1 | async-start | bytes 5767168 | tf_op jit(solution)/shard_map/all_to_all | solution.py:504
  145.2 1.6 copy-start
  251.5 5.0 %copy-start.1 = (f32[8,128]{1,0:T(8,128)S(1)}, f32[8,128]{1,0:T(8,128)}, u32[]{:S(2)}) copy-start(f32[8,128]{1,0:T(8,128)} %get-tuple-element.8) | copy-start | bytes 12292
  251.5 69.0 %all-to-all-start.3 = ((f32[4,2,1024,128]{3,2,1,0:T(8,128)}), f32[4,2,1024,128]{3,2,1,0:T(8,128)}, u32[]{:S(2)}, u32[]{:S(2)}) async-start(f32[4,2,1024,128]{3,2,1,0:T(8,128)} %bitcast.5), calls=%async_computation.3 | async-start | bytes 8388608 | tf_op jit(solution)/shard_map/all_to_all | solution.py:562
  257.1 46.9 %collective-permute-start = (f32[]{:T(128)}, f32[]{:T(128)}, u32[]{:S(2)}, u32[]{:S(2)}) collective-permute-start(f32[]{:T(128)} %reduce_max.9), channel_id=1, source_target_pairs={{0,8},{8,0},{16,24},{24,16},{1,9},{9,1},{17,25},{25,17},{2,10},{10... | collective-permute-start | bytes 20 | tf_op jit(solution)/shard_map/ppermute | solution.py:568
  305.3 3.6 %collective-permute-start.1 = (f32[]{:T(128)}, f32[]{:T(128)}, u32[]{:S(2)}, u32[]{:S(2)}) collective-permute-start(f32[]{:T(128)} %max.15), channel_id=1, source_target_pairs={{0,16},{8,24},{16,0},{24,8},{1,17},{9,25},{17,1},{25,9},{2,18},{10... | collective-permute-start | bytes 20 | tf_op jit(solution)/shard_map/ppermute | solution.py:568
  309.5 1.2 collective-permute-start.2
  311.3 3.6 %collective-permute-start.3 = (f32[]{:T(128)}, f32[]{:T(128)}, u32[]{:S(2)}, u32[]{:S(2)}) collective-permute-start(f32[]{:T(128)} %max.17), channel_id=1, source_target_pairs={{0,2},{1,3},{2,0},{3,1},{4,6},{5,7},{6,4},{7,5},{8,10},{9,11},{10,... | collective-permute-start | bytes 20 | tf_op jit(solution)/shard_map/ppermute | solution.py:568
  315.4 4.5 %collective-permute-start.4 = (f32[]{:T(128)}, f32[]{:T(128)}, u32[]{:S(2)}, u32[]{:S(2)}) collective-permute-start(f32[]{:T(128)} %max.18), channel_id=1, source_target_pairs={{0,4},{1,5},{2,6},{3,7},{4,0},{5,1},{6,2},{7,3},{8,12},{9,13},{10,... | collective-permute-start | bytes 20 | tf_op jit(solution)/shard_map/ppermute | solution.py:568

commit v3 on v2

v3 whole, which is shorter than its diff:
```python
from functools import partial
import math

import jax
import jax.numpy as jnp
import ml_dtypes
import numpy as np
from jax import lax
from jax.experimental import pallas as pl
from jax.experimental.pallas import tpu as pltpu
from jax.sharding import PartitionSpec as P

N = 4096
PAD = 2 * N
wavelength = 5.2e-07
distance = 0.2
INNER = 256
SLABS = N // INNER
RES = PAD // INNER
HALF = 40
CHUNKS = 2
CHUNK = INNER // CHUNKS
VMEM = 56 * 1024 * 1024


def optics(padded_side):
    pitch = 2e-06 * math.sqrt(8192.0 / padded_side)
    extent = padded_side * pitch
    ratio_sq = (wavelength / extent) ** 2
    band_limit = extent / (wavelength * math.sqrt((2.0 * distance / extent) ** 2 + 1.0))
    return (ratio_sq, band_limit)


RATIO_SQ, LIMIT = optics(PAD)
assert RES * HALF - RES // 2 + RES > LIMIT and RES * HALF + RES // 2 > LIMIT


def residue(u):
    return u if u < RES // 2 else u - RES


def split16(table):
    table = np.asarray(table, np.float64)
    high = table.astype(np.float32).astype(ml_dtypes.bfloat16)
    low = (table - high.astype(np.float64)).astype(np.float32).astype(ml_dtypes.bfloat16)
    return high, low


def row_order(groups, tail):
    rows = []
    for group in range(groups):
        size = 4 if tail and group == groups - 1 else 8
        for part in range(2):
            for s in range(size):
                rows.append((part, group * 8 + s - HALF))
    return rows


def column_tables(groups, tail):
    q = np.arange(INNER)
    rows = row_order(groups, tail)
    forward = np.zeros((len(rows), 2, INNER))
    inverse = np.zeros((2, INNER, len(rows)))
    for at, (part, k1) in enumerate(rows):
        if abs(k1) > HALF:
            continue
        angle = 2.0 * np.pi * ((k1 * q) % INNER) / INNER
        c, s = np.cos(angle), np.sin(angle)
        forward[at] = (c, s) if part == 0 else (-s, c)
        inverse[:, :, at] = (c, s) if part == 0 else (-s, c)
    forward = forward.reshape(-1, 2, CHUNKS, CHUNK // 8, 8).transpose(2, 0, 3, 1, 4)
    forward = np.concatenate(split16(forward.reshape(CHUNKS, len(rows), 2 * CHUNK)), axis=1)
    inverse = inverse.reshape(2, CHUNKS, CHUNK, -1).transpose(1, 0, 2, 3)
    high, low = split16(inverse.reshape(CHUNKS, 2 * CHUNK, len(rows)))
    inverse = np.concatenate([high, high, low], axis=2)
    inverse = np.pad(inverse, ((0, 0), (0, 0), (0, -3 * len(rows) % 16)))
    return forward, inverse


def line_tables():
    q = np.arange(INNER)
    forward = np.zeros((2 * INNER, 256))
    inverse = np.zeros((256, 2 * INNER))
    for lane in range(2 * HALF + 1):
        angle = 2.0 * np.pi * (((lane - HALF) * q) % INNER) / INNER
        c, s = np.cos(angle), np.sin(angle)
        forward[:INNER, lane], forward[INNER:, lane] = c, s
        forward[:INNER, 128 + lane], forward[INNER:, 128 + lane] = -s, c
        inverse[lane, :INNER], inverse[lane, INNER:] = c, s
        inverse[128 + lane, :INNER], inverse[128 + lane, INNER:] = -s, c
    return split16(forward) + split16(inverse)


def twist_table():
    q = np.arange(INNER) + N // 2
    k0 = np.arange(RES // 2 + 1)
    angle = 2.0 * np.pi * ((k0[:, None] * q[None, :]) % PAD) / PAD
    return np.cos(angle).astype(np.float32), (-np.sin(angle)).astype(np.float32)


def turn(value, num, den):
    re, im = value
    num = num % den
    eighth = 8 * num
    if num == 0:
        return re, im
    if 2 * num == den:
        return -re, -im
    if 4 * num == den:
        return -im, re
    if 4 * num == 3 * den:
        return im, -re
    if eighth % den == 0:
        root = np.float32(math.sqrt(0.5))
        kind = eighth // den
        if kind == 1:
            return (re - im) * root, (re + im) * root
        if kind == 3:
            return (re + im) * (-root), (re - im) * root
        if kind == 5:
            return (im - re) * root, (re + im) * (-root)
        return (re + im) * root, (im - re) * root
    c = np.float32(math.cos(2.0 * math.pi * num / den))
    s = np.float32(math.sin(2.0 * math.pi * num / den))
    return re * c - im * s, re * s + im * c


def small_dft(get, ids, sign):
    count = len(ids)
    if count == 1:
        return [get(ids[0])]
    even = small_dft(get, ids[0::2], sign)
    odd = small_dft(get, ids[1::2], sign)
    half = count // 2
    first, second = [], []
    for j in range(half):
        re, im = even[j]
        t_re, t_im = turn(odd[j], sign * j, count)
        first.append((re + t_re, im + t_im))
        second.append((re - t_re, im - t_im))
    return first + second


def forward_slabs(get, put):
    ids = list(range(SLABS))
    for v, value in enumerate(small_dft(get, ids, -1)):
        put(2 * v, value)
    for v, value in enumerate(small_dft(lambda n: turn(get(n), -n, RES), ids, -1)):
        put(2 * v + 1, value)


def inverse_slabs(get, put):
    even = small_dft(get, list(range(0, RES, 2)), 1)
    odd = small_dft(get, list(range(1, RES, 2)), 1)
    for n in range(SLABS):
        t_re, t_im = turn(odd[n], n, RES)
        put(n, (even[n][0] + t_re, even[n][1] + t_im))


def twisted(value, u, sign, read):
    re, im = value
    k0 = residue(u)
    if k0 == 0:
        return value
    c, s = read(abs(k0))
    if (k0 < 0) == (sign > 0):
        return re * c + im * s, im * c - re * s
    return re * c - im * s, re * s + im * c


def high_low(value):
    high = value.astype(jnp.bfloat16)
    low = (value - high.astype(jnp.float32)).astype(jnp.bfloat16)
    return high, low


def dot16(left, right):
    return jnp.dot(left, right, preferred_element_type=jnp.float32)


def three_left(stacked, count, high, low):
    both = dot16(stacked[...], high)
    return both[:count] + both[count:] + dot16(stacked[:count], low)


def three_right(stacked, count, high, low):
    both = dot16(stacked, high)
    return both[:count] + both[count:] + dot16(stacked[:count], low)


def interleave(tiles, products, butterflies, product):
    steps = min(tiles, products)

    @pl.loop(0, steps)
    def _(t):
        if product is not None:
            for part in range(products // steps):
                product(t * (products // steps) + part)
        if butterflies is not None:
            for part in range(tiles // steps):
                butterflies(t * (tiles // steps) + part)


def column_twist(twist, q0):
    def read(k):
        rows = pl.ds(q0, 8)
        return twist[rows, k : k + 1], twist[rows, 64 + k : 65 + k]

    return read


def column_forward_kernel(field, twist, matrix, out, high, low):
    width = field.shape[-1]
    per_source = field.shape[2]
    many = high.shape[-1] // width
    rows_out = out.shape[1]
    now = pl.program_id(0)

    def butterflies(t):
        q0 = pl.multiple_of(t * 8, 8)
        slot = now % 2

        def get(n):
            source, block = divmod(n, per_source)
            rows = pl.ds(q0, 8)
            return field[source, 0, block, rows, :], field[source, 1, block, rows, :]

        def put(u, value):
            item = jnp.concatenate(twisted(value, u, 1, column_twist(twist, q0)), axis=0)
            at = (slot, u // many, pl.ds(pl.multiple_of(t * 16, 16), 16), pl.ds((u % many) * width, width))
            high[at], low[at] = high_low(item)

        forward_slabs(get, put)

    def product(p, first):
        slot = (now + 1) % 2
        done = three_left(matrix.at[0], rows_out, high[slot, p], low[slot, p])
        for part in range(many):
            item = done[:, part * width : (part + 1) * width]
            at = p * many + part
            out[at] = item if first else out[at] + item

    for step in range(CHUNKS + 1):

        @pl.when(now == step)
        def _():
            interleave(
                CHUNK // 8,
                RES // many,
                butterflies if step < CHUNKS else None,
                partial(product, first=step == 1) if step > 0 else None,
            )


def column_inverse_kernel(lines, twist, matrix, out, top, deep, back):
    width = lines.shape[-1]
    rows_in = lines.shape[1]
    per_dest = out.shape[2]
    many = deep.shape[-1] // width
    now = pl.program_id(0)

    def product(p):
        done = dot16(matrix[0], deep[p])
        slot = now % 2
        for part in range(many):
            back[slot, p * many + part] = done[:, part * width : (part + 1) * width]

    def prepare(p):
        blocks = [lines[p * many + part] for part in range(many)]
        joined = jnp.concatenate(blocks, axis=1) if many > 1 else blocks[0]
        high = joined.astype(jnp.bfloat16).astype(jnp.float32)
        parts = [high, joined - high, high]
        if deep.shape[1] > 3 * rows_in:
            parts.append(jnp.zeros((deep.shape[1] - 3 * rows_in, many * width), jnp.float32))
        deep[p] = jnp.concatenate(parts, axis=0).astype(jnp.bfloat16)
        product(p)

    def butterflies(t):
        q0 = pl.multiple_of(t * 8, 8)
        slot = (now + 1) % 2
        largest = []

        def get(u):
            re = back[slot, u, pl.ds(q0, 8), :]
            im = back[slot, u, pl.ds(CHUNK + q0, 8), :]
            return twisted((re, im), u, -1, column_twist(twist, q0))

        def put(n, value):
            dest, block = divmod(n, per_dest)
            rows = pl.ds(q0, 8)
            out[dest, 0, block, rows, :], out[dest, 1, block, rows, :] = value
            largest.append(value[0] * value[0] + value[1] * value[1])

        inverse_slabs(get, put)
        while len(largest) > 1:
            largest = [jnp.maximum(a, b) for a, b in zip(largest[0::2], largest[1::2])]
        top[...] = jnp.maximum(top[...], largest[0])

    @pl.when(now == 0)
    def _():
        top[...] = jnp.zeros_like(top)
        pl.loop(0, RES // many)(prepare)

    for step in range(1, CHUNKS + 1):

        @pl.when(now == step)
        def _():
            interleave(
                CHUNK // 8, RES // many, butterflies, product if step < CHUNKS else None
            )


def line_kernel(
    order, tail, lines, gain_re, gain_im, twist, fwd_high, fwd_low, inv_high, inv_low, out, *scratch
):
    half = RES * 8
    at_tail = pl.program_id(0) == pl.num_programs(0) - 1

    def line_twist(side):
        def read(k):
            lanes = pl.ds(side * 128, 128)
            return twist[0, k, :, lanes], twist[1, k, :, lanes]

        return read

    def forward(group, stacked):
        for side in range(2):
            waiting = {}

            def get(m):
                block = order[2 * m + side]
                at = group * 16
                return lines[block, at : at + 8, :], lines[block, at + 8 : at + 16, :]

            def put(u, value):
                waiting[u] = twisted(value, u, 1, line_twist(side))
                v = (u + RES // 2) % RES
                if v in waiting:
                    first = min(u, v)
                    rows = pl.ds(first * 16, 16)
                    rows_low = pl.ds(half + first * 16, 16)
                    for part in range(2):
                        item = jnp.concatenate(
                            [waiting[first][part], waiting[first + RES // 2][part]], axis=0
                        )
                        at = pl.ds(part * INNER + side * 128, 128)
                        stacked[rows, at], stacked[rows_low, at] = high_low(item)

            forward_slabs(get, put)

    def middle(group, stacked, back):
        spec = three_right(stacked[...], half, fwd_high[...], fwd_low[...])
        spec_re, spec_im = spec[:, :128], spec[:, 128:]
        g_re, g_im = gain_re[group], gain_im[group]
        mixed = jnp.concatenate(
            [spec_re * g_re - spec_im * g_im, spec_re * g_im + spec_im * g_re], axis=1
        )
        mixed = jnp.concatenate(high_low(mixed), axis=0)
        back[...] = three_right(mixed, half, inv_high[...], inv_low[...])

    def inverse(group, back):
        for side in range(2):

            def get(u):
                rows = pl.ds((u % (RES // 2)) * 16 + (u // (RES // 2)) * 8, 8)
                re = back[rows, pl.ds(side * 128, 128)]
                im = back[rows, pl.ds(INNER + side * 128, 128)]
                return twisted((re, im), u, -1, line_twist(side))

            def put(m, value):
                block = order[2 * m + side]
                at = group * 16
                out[block, at : at + 8, :], out[block, at + 8 : at + 16, :] = value

            inverse_slabs(get, put)

    if tail:

        @pl.when(at_tail)
        def _():
            for block in range(N // 128):
                lines[block, 8:12, :] = lines[block, 4:8, :]

    groups = len(scratch) // 2
    for group in range(groups):
        forward(group, scratch[group])
    for group in range(groups):
        middle(group, scratch[group], scratch[groups + group])
    for group in range(groups):
        inverse(group, scratch[groups + group])

    if tail:

        @pl.when(at_tail)
        def _():
            for block in range(N // 128):
                out[block, 4:8, :] = out[block, 8:12, :]


def gain_kernel(place, gain_re, gain_im):
    k0 = place[0]
    group = place[1] + pl.program_id(0)
    down = lax.broadcasted_iota(jnp.int32, (8, 128), 0)
    across = lax.broadcasted_iota(jnp.int32, (8, 128), 1)
    row = (k0 + RES * (group * 8 + down - HALF)).astype(jnp.float32)
    row_sq = row * row
    row_in = jnp.abs(row) < LIMIT
    for u in range(RES):
        col = (residue(u) + RES * (across - HALF)).astype(jnp.float32)
        square = row_sq + col * col
        scaled = RATIO_SQ * square
        phase = -2.0 * math.pi * distance / wavelength * scaled / (1.0 + jnp.sqrt(1.0 - scaled))
        total = jnp.where(
            row_in & (jnp.abs(col) < LIMIT), jnp.exp(square * (-2.0 / (LIMIT * LIMIT))), 0.0
        )
        quarter = jnp.floor(phase * (2.0 / math.pi) + 0.5)
        left = phase - quarter * 1.5703125
        left = left - quarter * 4.837512969970703125e-4
        left = left - quarter * 7.549789954891882e-8
        sq = left * left
        sine = ((-1.9515295891e-4 * sq + 8.3321608736e-3) * sq - 1.6666654611e-1) * sq * left + left
        cosine = (
            (2.443315711809948e-5 * sq - 1.388731625493765e-3) * sq + 4.166664568298827e-2
        ) * sq * sq - 0.5 * sq + 1.0
        which = quarter.astype(jnp.int32) & 3
        swap = (which & 1) == 1
        cos_part = jnp.where(swap, sine, cosine)
        sin_part = jnp.where(swap, cosine, sine)
        cos_part = jnp.where((which == 1) | (which == 2), -cos_part, cos_part)
        sin_part = jnp.where(which >= 2, -sin_part, sin_part)
        at = (u % (RES // 2)) * 16 + (u // (RES // 2)) * 8
        gain_re[0, at : at + 8, :] = total * cos_part
        gain_im[0, at : at + 8, :] = total * sin_part


def inverse_root(value):
    root = lax.rsqrt(value)
    return root * (1.5 - 0.5 * (value * root) * root)


def encode(near_real, near_imag, peak, even_cell):
    square = near_real * near_real + near_imag * near_imag
    root = inverse_root(jnp.maximum(square, 1.2e-38))
    amp_level = (square * root) * (0.8 / peak)
    unit = jnp.minimum(root, 20.0 / peak)
    rest = 1.0 - amp_level * amp_level
    lift_part = rest * inverse_root(rest)
    level = unit * amp_level
    lift = jnp.where(even_cell, unit * lift_part, -(unit * lift_part))
    return (near_real * level + near_imag * lift, near_imag * level - near_real * lift)


def encode_kernel(peak, near, slm_real, slm_imag):
    rows, width = near.shape[2:]
    cell = lax.broadcasted_iota(jnp.int32, (rows, width), 0)
    cell = cell + lax.broadcasted_iota(jnp.int32, (rows, width), 1)
    for r in range(near.shape[0]):
        lanes = pl.ds(r * width, width)
        slm_real[:, lanes], slm_imag[:, lanes] = encode(
            near[r, 0], near[r, 1], peak[0], (cell & 1) == 0
        )


def pack_kernel(field_real, field_imag, packed):
    width = packed.shape[-1]
    for r in range(packed.shape[0]):
        lanes = pl.ds(r * width, width)
        packed[r, 0] = field_real[:, lanes]
        packed[r, 1] = field_imag[:, lanes]


def params():
    return pltpu.CompilerParams(vmem_limit_bytes=VMEM)


def whole(memory=pltpu.VMEM):
    return pl.BlockSpec(memory_space=memory)


def body(field_real, field_imag):
    row_total, col_total = lax.axis_size("row"), lax.axis_size("col")
    devices = row_total * col_total
    device = lax.axis_index("row") * col_total + lax.axis_index("col")
    height, tile_width = field_real.shape
    width = tile_width // row_total
    parts = max(1, devices // RES)
    groups = -(-(2 * HALF + 1) // (8 * parts)) * parts
    own = groups // parts
    tail = parts == 1
    total_rows = groups * 16 - (8 if tail else 0)
    own_rows = total_rows // parts
    many = 4 if width == 128 else 1

    fwd_col, inv_col = column_tables(groups, tail)
    line_fh, line_fl, line_ih, line_il = line_tables()
    twist = np.stack(twist_table())
    twist_line = np.ascontiguousarray(np.broadcast_to(twist[:, :, None], twist.shape[:2] + (8, INNER)))
    twist_col = np.pad(twist, ((0, 0), (0, 64 - twist.shape[1]), (0, 0)))
    twist_col = twist_col.reshape(128, INNER).T.copy()

    u = device // parts
    k0 = jnp.where(u >= RES // 2, u - RES, u)
    place = jnp.stack([k0, (device % parts) * own]).astype(jnp.int32)
    gain_shape = jax.ShapeDtypeStruct((own, RES * 8, 128), jnp.float32)
    gain_spec = pl.BlockSpec((1, RES * 8, 128), lambda g: (g, 0, 0))
    gain_re, gain_im = pl.pallas_call(
        gain_kernel,
        grid=(own,),
        in_specs=[whole(pltpu.SMEM)],
        out_specs=[gain_spec, gain_spec],
        out_shape=[gain_shape, gain_shape],
        compiler_params=params(),
        name="gain",
    )(place)

    pack_rows = min(height, 256)
    if width == 128:
        packed = pl.pallas_call(
            pack_kernel,
            grid=(height // pack_rows,),
            in_specs=[pl.BlockSpec((pack_rows, tile_width), lambda i: (i, 0))] * 2,
            out_specs=pl.BlockSpec((row_total, 2, pack_rows, width), lambda i: (0, 0, i, 0)),
            out_shape=jax.ShapeDtypeStruct((row_total, 2, height, width), jnp.float32),
            compiler_params=params(),
            name="pack",
        )(field_real, field_imag)
    else:
        packed = jnp.stack([field_real, field_imag])
        packed = packed.reshape(2, height, row_total, width).transpose(2, 0, 1, 3)
    columns = lax.all_to_all(packed, "row", split_axis=0, concat_axis=0, tiled=True)

    blocks = height // INNER
    columns = columns.reshape(row_total, 2, blocks, INNER, width)
    tall = (row_total, 2, blocks, CHUNK, width)
    slab = pltpu.VMEM((2, RES // many, 2 * CHUNK, many * width), jnp.bfloat16)
    lines = pl.pallas_call(
        column_forward_kernel,
        grid=(CHUNKS + 1,),
        in_specs=[
            pl.BlockSpec(tall, lambda i: (0, 0, 0, jnp.minimum(i, CHUNKS - 1), 0)),
            pl.BlockSpec((CHUNK, 128), lambda i: (jnp.minimum(i, CHUNKS - 1), 0)),
            pl.BlockSpec((1, 2 * total_rows, 2 * CHUNK), lambda i: (jnp.maximum(i - 1, 0), 0, 0)),
        ],
        out_specs=whole(),
        out_shape=jax.ShapeDtypeStruct((RES, total_rows, width), jnp.float32),
        scratch_shapes=[slab, slab],
        compiler_params=params(),
        name="column_forward",
    )(columns, twist_col, fwd_col)

    lines = lines.reshape(devices, own_rows, width)
    lines = lax.all_to_all(lines, ("row", "col"), split_axis=0, concat_axis=0, tiled=True)
    if width == 128:
        order = tuple((b % row_total) * col_total + b // row_total for b in range(N // 128))
    else:
        order = tuple(range(N // 128))
        lines = lines.reshape(row_total, col_total, own_rows, width).transpose(2, 1, 0, 3)
        lines = lines.reshape(own_rows, N // 128, 128).transpose(1, 0, 2)

    at_once = 2
    line_grain = pl.BlockSpec((N // 128, 16 * at_once, 128), lambda i: (0, i, 0))
    gain_grain = pl.BlockSpec((at_once, RES * 8, 128), lambda i: (i, 0, 0))
    lines = pl.pallas_call(
        partial(line_kernel, order, tail),
        grid=(-(-own // at_once),),
        in_specs=[line_grain, gain_grain, gain_grain] + [whole()] * 5,
        out_specs=line_grain,
        out_shape=jax.ShapeDtypeStruct((N // 128, own_rows, 128), jnp.float32),
        scratch_shapes=[pltpu.VMEM((2 * RES * 8, 2 * INNER), jnp.bfloat16)] * at_once
        + [pltpu.VMEM((RES * 8, 2 * INNER), jnp.float32)] * at_once,
        compiler_params=params(),
        name="line",
    )(lines, gain_re, gain_im, twist_line, line_fh, line_fl, line_ih, line_il)

    if width != 128:
        lines = lines.transpose(1, 0, 2).reshape(own_rows, col_total, row_total, width)
        lines = lines.transpose(2, 1, 0, 3).reshape(devices, own_rows, width)
    lines = lax.all_to_all(lines, ("row", "col"), split_axis=0, concat_axis=0, tiled=True)
    lines = lines.reshape(RES, total_rows, width)

    near, top = pl.pallas_call(
        column_inverse_kernel,
        grid=(CHUNKS + 1,),
        in_specs=[
            whole(),
            pl.BlockSpec((CHUNK, 128), lambda i: (jnp.maximum(i - 1, 0), 0)),
            pl.BlockSpec((1,) + inv_col.shape[1:], lambda i: (jnp.minimum(i, CHUNKS - 1), 0, 0)),
        ],
        out_specs=[
            pl.BlockSpec(tall, lambda i: (0, 0, 0, jnp.maximum(i - 1, 0), 0)),
            whole(),
        ],
        out_shape=[
            jax.ShapeDtypeStruct((row_total, 2, blocks, INNER, width), jnp.float32),
            jax.ShapeDtypeStruct((8, width), jnp.float32),
        ],
        scratch_shapes=[
            pltpu.VMEM((RES // many, inv_col.shape[2], many * width), jnp.bfloat16),
            pltpu.VMEM((2, RES, 2 * CHUNK, width), jnp.float32),
        ],
        compiler_params=params(),
        name="column_inverse",
    )(lines, twist_col, inv_col)

    near = near.reshape(row_total, 2, height, width)
    near = lax.all_to_all(near, "row", split_axis=0, concat_axis=0, tiled=True)
    peak = jnp.max(top)
    for axis, total in (("row", row_total), ("col", col_total)):
        shift = 1
        while shift < total:
            partner = [(i, i ^ shift) for i in range(total)]
            peak = jnp.maximum(peak, lax.ppermute(peak, axis, partner))
            shift *= 2
    peak = jnp.sqrt(peak)
    if width != 128:
        near = near.transpose(1, 2, 0, 3).reshape(2, height, tile_width)
        even_cell = (jnp.arange(height)[:, None] + jnp.arange(tile_width)[None, :]) % 2 == 0
        return encode(near[0], near[1], peak, even_cell)
    tile_spec = pl.BlockSpec((pack_rows, tile_width), lambda i: (i, 0))
    tile_shape = jax.ShapeDtypeStruct((height, tile_width), jnp.float32)
    return pl.pallas_call(
        encode_kernel,
        grid=(height // pack_rows,),
        in_specs=[
            whole(pltpu.SMEM),
            pl.BlockSpec((row_total, 2, pack_rows, width), lambda i: (0, 0, i, 0)),
        ],
        out_specs=[tile_spec, tile_spec],
        out_shape=[tile_shape, tile_shape],
        compiler_params=params(),
        name="encode",
    )(peak.reshape(1), near)


def solution(mesh):
    in_specs = (P("row", "col"), P("row", "col"))
    out_specs = (P("row", "col"), P("row", "col"))
    return jax.shard_map(body, mesh=mesh, in_specs=in_specs, out_specs=out_specs, check_vma=False)
```

time: 330 us -> 313 us (0.948)
  Pallas kernels: 67.1 us -> 56.1 us
    pallas_call x5, Pallas kernels: 60.4 us -> 49.5 us  [the longest x1 14.3 us: body(): pl.pallas_call(partial(line_kernel, order, tail), grid=(-(-own // at_once...]
where the time goes in v3:
time: 313 us; the launch traced here: 312 us
  blocking collectives  123 us (39%)
  waiting for transfers between devices  108 us (35%)
  Pallas kernels  56.1 us (18%)
  starting transfers between devices  17.9 us (6%)
  between operations  4.49 us (1%)
    all_to_all x1, blocking collectives, body(): lax.all_to_all(lines, ('row', 'col'), split_axis=0, concat_axis=0, tiled=...  67.6 us
    all_to_all x1, waiting for transfers between devices, body(): lax.all_to_all(lines, ('row', 'col'), split_axis=0, concat_axis=0, tiled=...  56.9 us
    all_to_all x1, blocking collectives, body(): lax.all_to_all(packed, 'row', split_axis=0, concat_axis=0, tiled=True)  55.1 us
    ppermute x5, waiting for transfers between devices, body(): peak = jnp.maximum(peak, lax.ppermute(peak, axis, partner))  51.3 us
    pallas_call x1, Pallas kernels, body(): pl.pallas_call(partial(line_kernel, order, tail), grid=(-(-own // at_once...  14.3 us
    pallas_call x1, Pallas kernels, body(): pl.pallas_call(column_inverse_kernel, grid=(CHUNKS + 1,), in_specs=[whole...  12.4 us
    pallas_call x1, Pallas kernels, body(): pl.pallas_call(column_forward_kernel, grid=(CHUNKS + 1,), in_specs=[pl.Bl...  11.5 us
    ppermute x5, starting transfers between devices, body(): peak = jnp.maximum(peak, lax.ppermute(peak, axis, partner))  8.42 us
  transfers between devices with their start and end apart: 7, of which 6 were waited for; matrix products, arithmetic and copies ran while one was open for 0% of the time, Pallas kernels for 2%

profile of v3, /device:TPU:0, one launch (start us, length us, event | category | flops | bytes accessed | tf_op | source)
XLA Modules:
  0.0 312.2 jit_solution(3275624436141911140)
XLA Ops:
  0.6 4.7 %pack.1 = f32[4,2,1024,128]{3,2,1,0:T(8,128)} custom-call(f32[1024,512]{1,0:T(8,128)} %field_real.1, f32[1024,512]{1,0:T(8,128)} %field_imag.1), custom_call_target="tpu_custom_call" | custom-call | tf_op jit(solution)/shard_map/pack/pallas_call | solution.py:518
  5.4 55.1 %all_to_all.20 = f32[4,2,1024,128]{3,2,1,0:T(8,128)} all-to-all(f32[4,2,1024,128]{3,2,1,0:T(8,128)} %pack.1), channel_id=1, replica_groups=mesh['row'=4,'col'=8] {'row'}, dimensions={0} | all-to-all | bytes 8388608 | tf_op jit(solution)/shard_map/all_to_all | solution.py:530
  60.4 11.5 %column_forward.1 = f32[32,168,128]{2,1,0:T(8,128)} custom-call(f32[4,2,4,256,128]{4,3,2,1,0:T(8,128)} %bitcast.4, f32[256,128]{1,0:T(8,128)} %constant.56.clone.twist, bf16[2,336,256]{2,1,0:T(8,128)(2,1)} %constant.57.clone.matrix), custom_call_target="tpu_custom_call" | custom-call | tf_op jit(solution)/shard_map/column_forward/pallas_call | solution.py:536
  71.9 4.5 %all-to-all-start.1 = ((f32[32,168,128]{2,1,0:T(8,128)}), f32[32,168,128]{2,1,0:T(8,128)S(1)}, u32[]{:S(2)}, u32[]{:S(2)}) async-start(f32[32,168,128]{2,1,0:T(8,128)} %column_forward.1), calls=%async_computation.1 | async-start | bytes 5505024 | tf_op jit(solution)/shard_map/all_to_all | solution.py:552
  76.4 0.6 pad_add_fusion.place
  77.1 6.7 %gain.1 = (f32[11,256,128]{2,1,0:T(8,128)}, f32[11,256,128]{2,1,0:T(8,128)}) custom-call(s32[2]{0:T(128)} %pad_add_fusion.place), custom_call_target="tpu_custom_call" | custom-call | tf_op jit(solution)/shard_map/gain/pallas_call | solution.py:506
  83.7 56.9 %all-to-all-done.1.lines = f32[32,168,128]{2,1,0:T(8,128)S(1)} async-done(((f32[32,168,128]{2,1,0:T(8,128)}), f32[32,168,128]{2,1,0:T(8,128)S(1)}, u32[]{:S(2)}, u32[]{:S(2)}) %all-to-all-start.1) | async-done | bytes 2752544 | tf_op jit(solution)/shard_map/all_to_all | solution.py:552
  140.6 0.0 copy-start
  140.6 1.6 copy-done
  142.2 14.3 %line.1 = f32[32,168,128]{2,1,0:T(8,128)} custom-call(f32[32,168,128]{2,1,0:T(8,128)} %copy-done, f32[11,256,128]{2,1,0:T(8,128)} %get-tuple-element.6.gain_re, f32[11,256,128]{2,1,0:T(8,128)} %get-tuple-element.7.gain_im, f32[2,17,8,256]{3,2,1,0:T(8,128)} %constant.58.clone.twist, bf16[512,256]{1,0:T(8,128)(2,1)} %constant.59.clone.fwd_high, ...), custom_call_target="tpu_custom_call" | custom-call | tf_op jit(solution)/shard_map/line/pallas_call | solution.py:563
  156.5 67.6 %all_to_all.21.lines = f32[32,168,128]{2,1,0:T(8,128)} all-to-all(f32[32,168,128]{2,1,0:T(8,128)} %line.1), channel_id=1, replica_groups=mesh['row'=4,'col'=8] {'row','col'}, dimensions={0} | all-to-all | bytes 5505024 | tf_op jit(solution)/shard_map/all_to_all | solution.py:578
  224.1 12.4 %column_inverse.1 = (f32[4,2,4,256,128]{4,3,2,1,0:T(8,128)}, f32[8,128]{1,0:T(8,128)}) custom-call(f32[32,168,128]{2,1,0:T(8,128)} %all_to_all.21.lines, f32[256,128]{1,0:T(8,128)} %constant.56.clone.twist, bf16[2,256,512]{2,1,0:T(8,128)(2,1)} %constant.63.clone.matrix), custom_call_target="tpu_custom_call" | custom-call | tf_op jit(solution)/shard_map/column_inverse/pallas_call | solution.py:581
  236.5 0.0 copy-start.1
  236.5 5.0 %all-to-all-start.3 = ((f32[4,2,1024,128]{3,2,1,0:T(8,128)}), f32[4,2,1024,128]{3,2,1,0:T(8,128)}, u32[]{:S(2)}, u32[]{:S(2)}) async-start(f32[4,2,1024,128]{3,2,1,0:T(8,128)} %bitcast.5), calls=%async_computation.3 | async-start | bytes 8388608 | tf_op jit(solution)/shard_map/all_to_all | solution.py:606
  241.5 0.0 copy-done.1
  241.5 0.6 reduce_max.9
  242.1 2.0 collective-permute-start
  244.1 45.0 %collective-permute-done = f32[]{:T(128)} collective-permute-done((f32[]{:T(128)}, f32[]{:T(128)}, u32[]{:S(2)}, u32[]{:S(2)}) %collective-permute-start) | collective-permute-done | bytes 36 | tf_op jit(solution)/shard_map/ppermute | solution.py:612
  290.4 2.8 collective-permute-start.1
  293.2 0.7 collective-permute-done.1
  294.5 0.9 collective-permute-start.2
  295.4 0.3 collective-permute-done.2
  296.3 1.4 collective-permute-start.3
  297.7 2.2 collective-permute-done.3
  300.5 1.4 collective-permute-start.4
  301.9 3.1 collective-permute-done.4
  305.6 0.0 all-to-all-done.3.near
  305.7 6.5 %encode.1 = (f32[1024,512]{1,0:T(8,128)}, f32[1024,512]{1,0:T(8,128)}) custom-call(f32[1]{0:T(128)} %bitcast.2.peak, f32[4,2,1024,128]{3,2,1,0:T(8,128)} %all-to-all-done.3.near), custom_call_target="tpu_custom_call" | custom-call | tf_op jit(solution)/shard_map/encode/pallas_call | solution.py:621
Async XLA Ops:
  71.9 68.7 %all-to-all-start.1 = ((f32[32,168,128]{2,1,0:T(8,128)}), f32[32,168,128]{2,1,0:T(8,128)S(1)}, u32[]{:S(2)}, u32[]{:S(2)}) async-start(f32[32,168,128]{2,1,0:T(8,128)} %column_forward.1), calls=%async_computation.1 | async-start | bytes 5505024 | tf_op jit(solution)/shard_map/all_to_all | solution.py:552
  140.6 1.6 copy-start
  236.5 5.0 %copy-start.1 = (f32[8,128]{1,0:T(8,128)S(1)}, f32[8,128]{1,0:T(8,128)}, u32[]{:S(2)}) copy-start(f32[8,128]{1,0:T(8,128)} %get-tuple-element.8) | copy-start | bytes 12292
  236.5 69.1 %all-to-all-start.3 = ((f32[4,2,1024,128]{3,2,1,0:T(8,128)}), f32[4,2,1024,128]{3,2,1,0:T(8,128)}, u32[]{:S(2)}, u32[]{:S(2)}) async-start(f32[4,2,1024,128]{3,2,1,0:T(8,128)} %bitcast.5), calls=%async_computation.3 | async-start | bytes 8388608 | tf_op jit(solution)/shard_map/all_to_all | solution.py:606
  242.1 47.0 %collective-permute-start = (f32[]{:T(128)}, f32[]{:T(128)}, u32[]{:S(2)}, u32[]{:S(2)}) collective-permute-start(f32[]{:T(128)} %reduce_max.9), channel_id=1, source_target_pairs={{0,8},{8,0},{16,24},{24,16},{1,9},{9,1},{17,25},{25,17},{2,10},{10... | collective-permute-start | bytes 20 | tf_op jit(solution)/shard_map/ppermute | solution.py:612
  290.4 3.6 %collective-permute-start.1 = (f32[]{:T(128)}, f32[]{:T(128)}, u32[]{:S(2)}, u32[]{:S(2)}) collective-permute-start(f32[]{:T(128)} %max.15), channel_id=1, source_target_pairs={{0,16},{8,24},{16,0},{24,8},{1,17},{9,25},{17,1},{25,9},{2,18},{10... | collective-permute-start | bytes 20 | tf_op jit(solution)/shard_map/ppermute | solution.py:612
  294.5 1.2 collective-permute-start.2
  296.3 3.6 %collective-permute-start.3 = (f32[]{:T(128)}, f32[]{:T(128)}, u32[]{:S(2)}, u32[]{:S(2)}) collective-permute-start(f32[]{:T(128)} %max.17), channel_id=1, source_target_pairs={{0,2},{1,3},{2,0},{3,1},{4,6},{5,7},{6,4},{7,5},{8,10},{9,11},{10,... | collective-permute-start | bytes 20 | tf_op jit(solution)/shard_map/ppermute | solution.py:612
  300.5 4.5 %collective-permute-start.4 = (f32[]{:T(128)}, f32[]{:T(128)}, u32[]{:S(2)}, u32[]{:S(2)}) collective-permute-start(f32[]{:T(128)} %max.18), channel_id=1, source_target_pairs={{0,4},{1,5},{2,6},{3,7},{4,0},{5,1},{6,2},{7,3},{8,12},{9,13},{10,... | collective-permute-start | bytes 20 | tf_op jit(solution)/shard_map/ppermute | solution.py:612

commit v4 on v3

--- a/solution.py
+++ b/solution.py
@@ -188,19 +188,6 @@
     return both[:count] + both[count:] + dot16(stacked[:count], low)
 
 
-def interleave(tiles, products, butterflies, product):
-    steps = min(tiles, products)
-
-    @pl.loop(0, steps)
-    def _(t):
-        if product is not None:
-            for part in range(products // steps):
-                product(t * (products // steps) + part)
-        if butterflies is not None:
-            for part in range(tiles // steps):
-                butterflies(t * (tiles // steps) + part)
-
-
 def column_twist(twist, q0):
     def read(k):
         rows = pl.ds(q0, 8)
@@ -209,16 +196,26 @@
     return read
 
 
-def column_forward_kernel(field, twist, matrix, out, high, low):
+def column_forward_kernel(count, place, twist, matrix, *refs):
+    pieces, refs = refs[:count], refs[count:]
+    before, (out, field, high, low, sems) = refs[:-5], refs[-5:]
     width = field.shape[-1]
     per_source = field.shape[2]
     many = high.shape[-1] // width
     rows_out = out.shape[1]
-    now = pl.program_id(0)
-
-    def butterflies(t):
+    copies = [
+        pltpu.make_async_copy(piece, field.at[place[0] ^ j], sems.at[j])
+        for j, piece in enumerate(pieces)
+    ]
+    copies += [pltpu.make_async_copy(item, out, sems.at[count]) for item in before]
+    for copy in copies:
+        copy.start()
+    for copy in copies[:count]:
+        copy.wait()
+
+    @pl.loop(0, CHUNK // 8)
+    def _(t):
         q0 = pl.multiple_of(t * 8, 8)
-        slot = now % 2
 
         def get(n):
             source, block = divmod(n, per_source)
@@ -227,45 +224,33 @@
 
         def put(u, value):
             item = jnp.concatenate(twisted(value, u, 1, column_twist(twist, q0)), axis=0)
-            at = (slot, u // many, pl.ds(pl.multiple_of(t * 16, 16), 16), pl.ds((u % many) * width, width))
+            rows = pl.ds(pl.multiple_of(t * 16, 16), 16)
+            at = (u // many, rows, pl.ds((u % many) * width, width))
             high[at], low[at] = high_low(item)
 
         forward_slabs(get, put)
 
-    def product(p, first):
-        slot = (now + 1) % 2
-        done = three_left(matrix.at[0], rows_out, high[slot, p], low[slot, p])
+    for copy in copies[count:]:
+        copy.wait()
+
+    @pl.loop(0, RES // many)
+    def _(p):
+        done = three_left(matrix, rows_out, high[p], low[p])
         for part in range(many):
             item = done[:, part * width : (part + 1) * width]
             at = p * many + part
-            out[at] = item if first else out[at] + item
-
-    for step in range(CHUNKS + 1):
-
-        @pl.when(now == step)
-        def _():
-            interleave(
-                CHUNK // 8,
-                RES // many,
-                butterflies if step < CHUNKS else None,
-                partial(product, first=step == 1) if step > 0 else None,
-            )
-
-
-def column_inverse_kernel(lines, twist, matrix, out, top, deep, back):
+            out[at] = out[at] + item if before else item
+
+
+def column_inverse_kernel(count, place, lines, twist, matrix, *refs):
+    pieces, (top, near, deep, back, sems) = refs[:count], refs[count:]
     width = lines.shape[-1]
     rows_in = lines.shape[1]
-    per_dest = out.shape[2]
+    per_dest = near.shape[2]
     many = deep.shape[-1] // width
-    now = pl.program_id(0)
-
-    def product(p):
-        done = dot16(matrix[0], deep[p])
-        slot = now % 2
-        for part in range(many):
-            back[slot, p * many + part] = done[:, part * width : (part + 1) * width]
-
-    def prepare(p):
+
+    @pl.loop(0, RES // many)
+    def _(p):
         blocks = [lines[p * many + part] for part in range(many)]
         joined = jnp.concatenate(blocks, axis=1) if many > 1 else blocks[0]
         high = joined.astype(jnp.bfloat16).astype(jnp.float32)
@@ -273,22 +258,26 @@
         if deep.shape[1] > 3 * rows_in:
             parts.append(jnp.zeros((deep.shape[1] - 3 * rows_in, many * width), jnp.float32))
         deep[p] = jnp.concatenate(parts, axis=0).astype(jnp.bfloat16)
-        product(p)
-
-    def butterflies(t):
+        done = dot16(matrix[...], deep[p])
+        for part in range(many):
+            back[p * many + part] = done[:, part * width : (part + 1) * width]
+
+    top[...] = jnp.zeros_like(top)
+
+    @pl.loop(0, CHUNK // 8)
+    def _(t):
         q0 = pl.multiple_of(t * 8, 8)
-        slot = (now + 1) % 2
         largest = []
 
         def get(u):
-            re = back[slot, u, pl.ds(q0, 8), :]
-            im = back[slot, u, pl.ds(CHUNK + q0, 8), :]
+            re = back[u, pl.ds(q0, 8), :]
+            im = back[u, pl.ds(CHUNK + q0, 8), :]
             return twisted((re, im), u, -1, column_twist(twist, q0))
 
         def put(n, value):
             dest, block = divmod(n, per_dest)
             rows = pl.ds(q0, 8)
-            out[dest, 0, block, rows, :], out[dest, 1, block, rows, :] = value
+            near[dest, 0, block, rows, :], near[dest, 1, block, rows, :] = value
             largest.append(value[0] * value[0] + value[1] * value[1])
 
         inverse_slabs(get, put)
@@ -296,18 +285,14 @@
             largest = [jnp.maximum(a, b) for a, b in zip(largest[0::2], largest[1::2])]
         top[...] = jnp.maximum(top[...], largest[0])
 
-    @pl.when(now == 0)
-    def _():
-        top[...] = jnp.zeros_like(top)
-        pl.loop(0, RES // many)(prepare)
-
-    for step in range(1, CHUNKS + 1):
-
-        @pl.when(now == step)
-        def _():
-            interleave(
-                CHUNK // 8, RES // many, butterflies, product if step < CHUNKS else None
-            )
+    copies = [
+        pltpu.make_async_copy(near.at[place[0] ^ j], piece, sems.at[j])
+        for j, piece in enumerate(pieces)
+    ]
+    for copy in copies:
+        copy.start()
+    for copy in copies:
+        copy.wait()
 
 
 def line_kernel(
@@ -450,27 +435,42 @@
     return (near_real * level + near_imag * lift, near_imag * level - near_real * lift)
 
 
-def encode_kernel(peak, near, slm_real, slm_imag):
-    rows, width = near.shape[2:]
-    cell = lax.broadcasted_iota(jnp.int32, (rows, width), 0)
-    cell = cell + lax.broadcasted_iota(jnp.int32, (rows, width), 1)
-    for r in range(near.shape[0]):
-        lanes = pl.ds(r * width, width)
-        slm_real[:, lanes], slm_imag[:, lanes] = encode(
-            near[r, 0], near[r, 1], peak[0], (cell & 1) == 0
+def encode_kernel(place, peak, *refs):
+    pieces, (slm_real, slm_imag) = refs[:-2], refs[-2:]
+    width = pieces[0].shape[-1]
+    count = len(pieces) // CHUNKS
+    cell = lax.broadcasted_iota(jnp.int32, (CHUNK, width), 0)
+    cell = cell + lax.broadcasted_iota(jnp.int32, (CHUNK, width), 1)
+    for at, piece in enumerate(pieces):
+        chunk, j = divmod(at, count)
+        rows = pl.ds(chunk * CHUNK, CHUNK)
+        lanes = pl.ds(pl.multiple_of((place[0] ^ j) * width, width), width)
+        slm_real[rows, lanes], slm_imag[rows, lanes] = encode(
+            piece[0, 0], piece[1, 0], peak[0], (cell & 1) == 0
         )
 
 
-def pack_kernel(field_real, field_imag, packed):
-    width = packed.shape[-1]
-    for r in range(packed.shape[0]):
-        lanes = pl.ds(r * width, width)
-        packed[r, 0] = field_real[:, lanes]
-        packed[r, 1] = field_imag[:, lanes]
+def pack_kernel(place, field_real, field_imag, *pieces):
+    width = pieces[0].shape[-1]
+    for j, piece in enumerate(pieces):
+        lanes = pl.ds(pl.multiple_of((place[0] ^ j) * width, width), width)
+        piece[0, 0] = field_real[:, lanes]
+        piece[1, 0] = field_imag[:, lanes]
+
+
+def exchange(pieces, axis):
+    total = len(pieces)
+    return [pieces[0]] + [
+        lax.ppermute(pieces[j], axis, [(i, i ^ j) for i in range(total)]) for j in range(1, total)
+    ]
 
 
 def params():
     return pltpu.CompilerParams(vmem_limit_bytes=VMEM)
+
+
+def cost(megabytes):
+    return pl.CostEstimate(flops=0, bytes_accessed=megabytes << 20, transcendentals=0)
 
 
 def whole(memory=pltpu.VMEM):
@@ -513,40 +513,52 @@
         name="gain",
     )(place)
 
-    pack_rows = min(height, 256)
-    if width == 128:
-        packed = pl.pallas_call(
-            pack_kernel,
-            grid=(height // pack_rows,),
-            in_specs=[pl.BlockSpec((pack_rows, tile_width), lambda i: (i, 0))] * 2,
-            out_specs=pl.BlockSpec((row_total, 2, pack_rows, width), lambda i: (0, 0, i, 0)),
-            out_shape=jax.ShapeDtypeStruct((row_total, 2, height, width), jnp.float32),
-            compiler_params=params(),
-            name="pack",
-        )(field_real, field_imag)
-    else:
+    place_row = lax.axis_index("row").reshape(1).astype(jnp.int32)
+    blocks = height // INNER
+    piece = (2, blocks, CHUNK, width)
+    piece_shape = jax.ShapeDtypeStruct(piece, jnp.float32)
+    anywhere = whole(pl.ANY)
+    if width != 128:
         packed = jnp.stack([field_real, field_imag])
-        packed = packed.reshape(2, height, row_total, width).transpose(2, 0, 1, 3)
-    columns = lax.all_to_all(packed, "row", split_axis=0, concat_axis=0, tiled=True)
-
-    blocks = height // INNER
-    columns = columns.reshape(row_total, 2, blocks, INNER, width)
-    tall = (row_total, 2, blocks, CHUNK, width)
-    slab = pltpu.VMEM((2, RES // many, 2 * CHUNK, many * width), jnp.bfloat16)
-    lines = pl.pallas_call(
-        column_forward_kernel,
-        grid=(CHUNKS + 1,),
-        in_specs=[
-            pl.BlockSpec(tall, lambda i: (0, 0, 0, jnp.minimum(i, CHUNKS - 1), 0)),
-            pl.BlockSpec((CHUNK, 128), lambda i: (jnp.minimum(i, CHUNKS - 1), 0)),
-            pl.BlockSpec((1, 2 * total_rows, 2 * CHUNK), lambda i: (jnp.maximum(i - 1, 0), 0, 0)),
-        ],
-        out_specs=whole(),
-        out_shape=jax.ShapeDtypeStruct((RES, total_rows, width), jnp.float32),
-        scratch_shapes=[slab, slab],
-        compiler_params=params(),
-        name="column_forward",
-    )(columns, twist_col, fwd_col)
+        packed = packed.reshape(2, blocks, CHUNKS, CHUNK, row_total, width).transpose(2, 4, 0, 1, 3, 5)
+        packed = jnp.take(packed, jnp.arange(row_total) ^ place_row[0], axis=1)
+    lines = []
+    for chunk in range(CHUNKS):
+        if width == 128:
+            pieces = pl.pallas_call(
+                pack_kernel,
+                grid=(blocks,),
+                in_specs=[whole(pltpu.SMEM)]
+                + [pl.BlockSpec((CHUNK, tile_width), lambda i: (i * CHUNKS + chunk, 0))] * 2,
+                out_specs=[pl.BlockSpec((2, 1, CHUNK, width), lambda i: (0, i, 0, 0))] * row_total,
+                out_shape=[piece_shape] * row_total,
+                compiler_params=params(),
+                cost_estimate=cost(4),
+                name="pack",
+            )(place_row, field_real, field_imag)
+        else:
+            pieces = [packed[chunk, j] for j in range(row_total)]
+        pieces = exchange(pieces, "row")
+        rows = slice(chunk * CHUNK, (chunk + 1) * CHUNK)
+        slab = pltpu.VMEM((RES // many, 2 * CHUNK, many * width), jnp.bfloat16)
+        lines = [
+            pl.pallas_call(
+                partial(column_forward_kernel, row_total),
+                in_specs=[whole(pltpu.SMEM)] + [whole()] * 2 + [anywhere] * (row_total + len(lines)),
+                out_specs=whole(),
+                out_shape=jax.ShapeDtypeStruct((RES, total_rows, width), jnp.float32),
+                scratch_shapes=[
+                    pltpu.VMEM((row_total,) + piece, jnp.float32),
+                    slab,
+                    slab,
+                    pltpu.SemaphoreType.DMA((row_total + 1,)),
+                ],
+                compiler_params=params(),
+                cost_estimate=cost(20),
+                name="column_forward",
+            )(place_row, twist_col[rows], fwd_col[chunk], *pieces, *lines)
+        ]
+    (lines,) = lines
 
     lines = lines.reshape(devices, own_rows, width)
     lines = lax.all_to_all(lines, ("row", "col"), split_axis=0, concat_axis=0, tiled=True)
@@ -578,58 +590,49 @@
     lines = lax.all_to_all(lines, ("row", "col"), split_axis=0, concat_axis=0, tiled=True)
     lines = lines.reshape(RES, total_rows, width)
 
-    near, top = pl.pallas_call(
-        column_inverse_kernel,
-        grid=(CHUNKS + 1,),
-        in_specs=[
-            whole(),
-            pl.BlockSpec((CHUNK, 128), lambda i: (jnp.maximum(i - 1, 0), 0)),
-            pl.BlockSpec((1,) + inv_col.shape[1:], lambda i: (jnp.minimum(i, CHUNKS - 1), 0, 0)),
-        ],
-        out_specs=[
-            pl.BlockSpec(tall, lambda i: (0, 0, 0, jnp.maximum(i - 1, 0), 0)),
-            whole(),
-        ],
-        out_shape=[
-            jax.ShapeDtypeStruct((row_total, 2, blocks, INNER, width), jnp.float32),
-            jax.ShapeDtypeStruct((8, width), jnp.float32),
-        ],
-        scratch_shapes=[
-            pltpu.VMEM((RES // many, inv_col.shape[2], many * width), jnp.bfloat16),
-            pltpu.VMEM((2, RES, 2 * CHUNK, width), jnp.float32),
-        ],
-        compiler_params=params(),
-        name="column_inverse",
-    )(lines, twist_col, inv_col)
-
-    near = near.reshape(row_total, 2, height, width)
-    near = lax.all_to_all(near, "row", split_axis=0, concat_axis=0, tiled=True)
-    peak = jnp.max(top)
+    near, tops = [], []
+    for chunk in range(CHUNKS):
+        rows = slice(chunk * CHUNK, (chunk + 1) * CHUNK)
+        *pieces, top = pl.pallas_call(
+            partial(column_inverse_kernel, row_total),
+            in_specs=[whole(pltpu.SMEM)] + [whole()] * 3,
+            out_specs=[anywhere] * row_total + [whole()],
+            out_shape=[piece_shape] * row_total + [jax.ShapeDtypeStruct((8, width), jnp.float32)],
+            scratch_shapes=[
+                pltpu.VMEM((row_total,) + piece, jnp.float32),
+                pltpu.VMEM((RES // many, inv_col.shape[2], many * width), jnp.bfloat16),
+                pltpu.VMEM((RES, 2 * CHUNK, width), jnp.float32),
+                pltpu.SemaphoreType.DMA((row_total,)),
+            ],
+            compiler_params=params(),
+            cost_estimate=cost(20),
+            name="column_inverse",
+        )(place_row, lines, twist_col[rows], inv_col[chunk])
+        near += exchange(pieces, "row")
+        tops.append(top)
+    peak = jnp.max(jnp.stack(tops))
     for axis, total in (("row", row_total), ("col", col_total)):
-        shift = 1
-        while shift < total:
-            partner = [(i, i ^ shift) for i in range(total)]
-            peak = jnp.maximum(peak, lax.ppermute(peak, axis, partner))
-            shift *= 2
+        peak = jnp.max(jnp.stack(exchange([peak] * total, axis)))
     peak = jnp.sqrt(peak)
+
     if width != 128:
-        near = near.transpose(1, 2, 0, 3).reshape(2, height, tile_width)
+        near = jnp.stack(near).reshape((CHUNKS, row_total) + piece)
+        near = jnp.take(near, jnp.arange(row_total) ^ place_row[0], axis=1)
+        near = near.transpose(2, 3, 0, 4, 1, 5).reshape(2, height, tile_width)
         even_cell = (jnp.arange(height)[:, None] + jnp.arange(tile_width)[None, :]) % 2 == 0
         return encode(near[0], near[1], peak, even_cell)
-    tile_spec = pl.BlockSpec((pack_rows, tile_width), lambda i: (i, 0))
+    tile_spec = pl.BlockSpec((INNER, tile_width), lambda i: (i, 0))
     tile_shape = jax.ShapeDtypeStruct((height, tile_width), jnp.float32)
     return pl.pallas_call(
         encode_kernel,
-        grid=(height // pack_rows,),
-        in_specs=[
-            whole(pltpu.SMEM),
-            pl.BlockSpec((row_total, 2, pack_rows, width), lambda i: (0, 0, i, 0)),
-        ],
+        grid=(blocks,),
+        in_specs=[whole(pltpu.SMEM)] * 2
+        + [pl.BlockSpec((2, 1, CHUNK, width), lambda i: (0, i, 0, 0))] * len(near),
         out_specs=[tile_spec, tile_spec],
         out_shape=[tile_shape, tile_shape],
         compiler_params=params(),
         name="encode",
-    )(peak.reshape(1), near)
+    )(place_row, peak.reshape(1), *near)
 
 
 def solution(mesh):

time: 313 us -> 314 us (level)
  blocking collectives: 123 us -> 67.6 us
  starting transfers between devices: 17.9 us -> 38.9 us
  Pallas kernels: 56.1 us -> 72.6 us
  waiting for transfers between devices: 108 us -> 118 us
  between operations: 4.49 us -> 8.45 us
    all_to_all x1 -> x0, blocking collectives: 55.1 us -> none  [body(): lax.all_to_all(packed, 'row', split_axis=0, concat_axis=0, tiled=True)]
    ppermute x5 -> x22, starting transfers between devices: 8.42 us -> 34 us  [exchange(): lax.ppermute(pieces[j], axis, [(i, i ^ j) for i in range(total)])]
    pallas_call x4 -> x7, Pallas kernels: 35.2 us -> 51.6 us  [the longest x2 19.2 us: body(): pl.pallas_call(partial(column_forward_kernel, row_total), in_specs=[whole...]
    ppermute x5 -> x22, waiting for transfers between devices: 51.3 us -> 61.3 us  [exchange(): lax.ppermute(pieces[j], axis, [(i, i ^ j) for i in range(total)])]
    all_to_all x1 -> x0, starting transfers between devices: 4.96 us -> none  [body(): near = lax.all_to_all(near, 'row', split_axis=0, concat_axis=0, tiled=True)]
  transfers between devices with their start and end apart: 7 -> 23, of which waited for: 6 -> 13; matrix products, arithmetic and copies ran while one was open for 0% -> 1% of each run, Pallas kernels for 2% -> 9%
where the time goes in v4:
time: 314 us; the launch traced here: 313 us
  waiting for transfers between devices  118 us (38%)
  Pallas kernels  72.6 us (23%)
  blocking collectives  67.6 us (22%)
  starting transfers between devices  38.9 us (12%)
  between operations  8.45 us (3%)
  local copies, waits for them, and re-layouts  4.46 us (1%)
    all_to_all x1, blocking collectives, body(): lax.all_to_all(lines, ('row', 'col'), split_axis=0, concat_axis=0, tiled=...  67.6 us
    ppermute x22, waiting for transfers between devices, exchange(): lax.ppermute(pieces[j], axis, [(i, i ^ j) for i in range(total)])  61.3 us
    all_to_all x1, waiting for transfers between devices, body(): lax.all_to_all(lines, ('row', 'col'), split_axis=0, concat_axis=0, tiled=...  56.8 us
    ppermute x22, starting transfers between devices, exchange(): lax.ppermute(pieces[j], axis, [(i, i ^ j) for i in range(total)])  34 us
    pallas_call x2, Pallas kernels, body(): pl.pallas_call(partial(column_forward_kernel, row_total), in_specs=[whole...  19.2 us
    pallas_call x2, Pallas kernels, body(): pl.pallas_call(partial(column_inverse_kernel, row_total), in_specs=[whole...  18.7 us
    pallas_call x1, Pallas kernels, body(): pl.pallas_call(partial(line_kernel, order, tail), grid=(-(-own // at_once...  14.3 us
    pallas_call x2, Pallas kernels, body(): pl.pallas_call(pack_kernel, grid=(blocks,), in_specs=[whole(pltpu.SMEM)]...  7.62 us
  transfers between devices with their start and end apart: 23, of which 13 were waited for; matrix products, arithmetic and copies ran while one was open for 1% of the time, Pallas kernels for 9%

profile of v4, /device:TPU:0, one launch (start us, length us, event | category | flops | bytes accessed | tf_op | source)
XLA Modules:
  0.0 312.8 jit_solution(4695132708384900347)
XLA Ops:
  0.6 3.8 %pack.3 = (f32[2,4,128,128]{3,2,1,0:T(8,128)}, f32[2,4,128,128]{3,2,1,0:T(8,128)}, f32[2,4,128,128]{3,2,1,0:T(8,128)}, f32[2,4,128,128]{3,2,1,0:T(8,128)}) custom-call(s32[1]{0:T(128)} %bitcast.place, f32[1024,512]{1,0:T(8,128)} %field_real.3, f32[1024,512]{1,0:T(8,128)} %field_imag.3), custom_call_target="tpu_custom_call" | custom-call | bytes 4194304 | tf_op jit(solution)/shard_map/pack/pallas_call | solution.py:528
  4.5 2.9 collective-permute-start.3
  7.4 1.5 collective-permute-start.4
  8.9 0.0 collective-permute-start.5
  8.9 3.8 %pack.2 = (f32[2,4,128,128]{3,2,1,0:T(8,128)}, f32[2,4,128,128]{3,2,1,0:T(8,128)}, f32[2,4,128,128]{3,2,1,0:T(8,128)}, f32[2,4,128,128]{3,2,1,0:T(8,128)}) custom-call(s32[1]{0:T(128)} %bitcast.place, f32[1024,512]{1,0:T(8,128)} %field_real.3, f32[1024,512]{1,0:T(8,128)} %field_imag.3), custom_call_target="tpu_custom_call" | custom-call | bytes 4194304 | tf_op jit(solution)/shard_map/pack/pallas_call | solution.py:528
  12.7 2.0 collective-permute-start
  14.7 1.5 collective-permute-start.1
  16.2 4.2 %collective-permute-done.3.refs_1_ = f32[2,4,128,128]{3,2,1,0:T(8,128)S(1)} collective-permute-done((f32[2,4,128,128]{3,2,1,0:T(8,128)}, f32[2,4,128,128]{3,2,1,0:T(8,128)S(1)}, u32[]{:S(2)}, u32[]{:S(2)}) %collective-permute-start.3) | collective-permute-done | bytes 524320 | tf_op jit(solution)/shard_map/ppermute | solution.py:464
  20.4 3.0 collective-permute-start.2
  23.4 10.3 %collective-permute-done.4.refs_2_ = f32[2,4,128,128]{3,2,1,0:T(8,128)S(1)} collective-permute-done((f32[2,4,128,128]{3,2,1,0:T(8,128)}, f32[2,4,128,128]{3,2,1,0:T(8,128)S(1)}, u32[]{:S(2)}, u32[]{:S(2)}) %collective-permute-start.4) | collective-permute-done | bytes 524320 | tf_op jit(solution)/shard_map/ppermute | solution.py:464
  33.7 0.0 collective-permute-done.5.refs_3_
  33.7 0.8 copy-done.11
  34.6 0.2 copy-done.12
  34.7 9.5 %column_forward.2.refs_4_ = f32[32,168,128]{2,1,0:T(8,128)} custom-call(s32[1]{0:T(128)} %bitcast.place, f32[128,128]{1,0:T(8,128)} %constant.62.clone.twist, bf16[336,256]{1,0:T(8,128)(2,1)} %constant.63.clone.matrix, f32[2,4,128,128]{3,2,1,0:T(8,128)} %get-tuple-element.26.refs_0_, f32[2,4,128,128]{3,2,1,0:T(8,128)} %copy-done.10, ...), custom_call_target="tpu_custom_call" | custom-call | bytes 20971520 | tf_op jit(solution)/shard_map/column_forward/pallas_call | solution.py:545
  44.3 0.0 collective-permute-done.refs_1_
  44.3 0.0 copy-start.7
  44.3 10.4 %collective-permute-done.1.refs_2_ = f32[2,4,128,128]{3,2,1,0:T(8,128)S(1)} collective-permute-done((f32[2,4,128,128]{3,2,1,0:T(8,128)}, f32[2,4,128,128]{3,2,1,0:T(8,128)S(1)}, u32[]{:S(2)}, u32[]{:S(2)}) %collective-permute-start.1) | collective-permute-done | bytes 524320 | tf_op jit(solution)/shard_map/ppermute | solution.py:464
  54.7 0.0 collective-permute-done.2.refs_3_
  54.7 0.8 copy-done.8
  55.5 0.2 copy-done.9
  55.7 9.6 %column_forward.3 = f32[32,168,128]{2,1,0:T(8,128)} custom-call(s32[1]{0:T(128)} %bitcast.place, f32[128,128]{1,0:T(8,128)} %constant.64.clone.twist, bf16[336,256]{1,0:T(8,128)(2,1)} %constant.65.clone.matrix, f32[2,4,128,128]{3,2,1,0:T(8,128)} %get-tuple-element.22.refs_0_, f32[2,4,128,128]{3,2,1,0:T(8,128)} %copy-done.7, f32[2,4,128,128]{3,2,1,0:T(8,128)} %copy-done.8, ...), custom_call_target="tpu_custom_call" | custom-call | bytes 20971520 | tf_op jit(solution)/shard_map/column_forward/pallas_call | solution.py:545
  65.3 4.9 %all-to-all-start = ((f32[32,168,128]{2,1,0:T(8,128)}), f32[32,168,128]{2,1,0:T(8,128)S(1)}, u32[]{:S(2)}, u32[]{:S(2)}) async-start(f32[32,168,128]{2,1,0:T(8,128)} %column_forward.3), calls=%async_computation | async-start | bytes 5505024 | tf_op jit(solution)/shard_map/all_to_all | solution.py:564
  70.3 0.7 pad_add_fusion.place
  70.9 6.7 %gain.1 = (f32[11,256,128]{2,1,0:T(8,128)}, f32[11,256,128]{2,1,0:T(8,128)}) custom-call(s32[2]{0:T(128)} %pad_add_fusion.place), custom_call_target="tpu_custom_call" | custom-call | tf_op jit(solution)/shard_map/gain/pallas_call | solution.py:506
  77.6 56.8 %all-to-all-done.lines = f32[32,168,128]{2,1,0:T(8,128)S(1)} async-done(((f32[32,168,128]{2,1,0:T(8,128)}), f32[32,168,128]{2,1,0:T(8,128)S(1)}, u32[]{:S(2)}, u32[]{:S(2)}) %all-to-all-start) | async-done | bytes 2752544 | tf_op jit(solution)/shard_map/all_to_all | solution.py:564
  134.5 1.5 copy-done
  136.0 14.3 %line.1 = f32[32,168,128]{2,1,0:T(8,128)} custom-call(f32[32,168,128]{2,1,0:T(8,128)} %copy-done, f32[11,256,128]{2,1,0:T(8,128)} %get-tuple-element.30.gain_re, f32[11,256,128]{2,1,0:T(8,128)} %get-tuple-element.31.gain_im, f32[2,17,8,256]{3,2,1,0:T(8,128)} %constant.66.clone.twist, bf16[512,256]{1,0:T(8,128)(2,1)} %constant.67.clone.fwd_high, ...), custom_call_target="tpu_custom_call" | custom-call | tf_op jit(solution)/shard_map/line/pallas_call | solution.py:575
  150.3 67.6 %all_to_all.10.lines = f32[32,168,128]{2,1,0:T(8,128)} all-to-all(f32[32,168,128]{2,1,0:T(8,128)} %line.1), channel_id=1, replica_groups=mesh['row'=4,'col'=8] {'row','col'}, dimensions={0} | all-to-all | bytes 5505024 | tf_op jit(solution)/shard_map/all_to_all | solution.py:590
  217.9 9.4 %column_inverse.3 = (f32[2,4,128,128]{3,2,1,0:T(8,128)}, f32[2,4,128,128]{3,2,1,0:T(8,128)}, f32[2,4,128,128]{3,2,1,0:T(8,128)}, f32[2,4,128,128]{3,2,1,0:T(8,128)}, f32[8,128]{1,0:T(8,128)}) custom-call(s32[1]{0:T(128)} %bitcast.place, f32[32,168,128]{2,1,0:T(8,128)} %all_to_all.10.lines, f32[128,128]{1,0:T(8,128)} %constant.64.clone.twist, ...), custom_call_target="tpu_custom_call" | custom-call | bytes 20971520 | tf_op jit(solution)/shard_map/column_inverse/pallas_call | solution.py:596
  227.3 0.1 collective-permute-start.19
  227.4 9.3 %column_inverse.2 = (f32[2,4,128,128]{3,2,1,0:T(8,128)}, f32[2,4,128,128]{3,2,1,0:T(8,128)}, f32[2,4,128,128]{3,2,1,0:T(8,128)}, f32[2,4,128,128]{3,2,1,0:T(8,128)}, f32[8,128]{1,0:T(8,128)}) custom-call(s32[1]{0:T(128)} %bitcast.place, f32[32,168,128]{2,1,0:T(8,128)} %all_to_all.10.lines, f32[128,128]{1,0:T(8,128)} %constant.62.clone.twist, ...), custom_call_target="tpu_custom_call" | custom-call | bytes 20971520 | tf_op jit(solution)/shard_map/column_inverse/pallas_call | solution.py:596
  236.7 1.3 reduce_max.55
  238.1 0.7 reduce_max.56
  240.1 3.3 %collective-permute-start.8 = (f32[]{:T(128)}, f32[]{:T(128)}, u32[]{:S(2)}, u32[]{:S(2)}) collective-permute-start(f32[]{:T(128)} %reduce_max.57), channel_id=1, source_target_pairs={{0,24},{8,16},{16,8},{24,0},{1,25},{9,17},{17,9},{25,1},{2,26},{10... | collective-permute-start | bytes 20 | tf_op jit(solution)/shard_map/ppermute | solution.py:464
  243.4 2.8 collective-permute-start.7
  246.2 1.3 collective-permute-start.6
  247.5 1.1 collective-permute-start.20
  248.6 1.1 collective-permute-done.6
  249.7 1.3 collective-permute-start.21
  251.6 0.8 collective-permute-start.16
  253.6 1.4 collective-permute-start.15
  255.0 3.4 %collective-permute-done.15 = f32[]{:T(128)} collective-permute-done((f32[]{:T(128)}, f32[]{:T(128)}, u32[]{:S(2)}, u32[]{:S(2)}) %collective-permute-start.15) | collective-permute-done | bytes 36 | tf_op jit(solution)/shard_map/ppermute | solution.py:464
  258.4 2.2 collective-permute-start.14
  260.6 3.3 %collective-permute-done.14 = f32[]{:T(128)} collective-permute-done((f32[]{:T(128)}, f32[]{:T(128)}, u32[]{:S(2)}, u32[]{:S(2)}) %collective-permute-start.14) | collective-permute-done | bytes 36 | tf_op jit(solution)/shard_map/ppermute | solution.py:464
  263.9 1.3 collective-permute-start.13
  265.2 2.7 collective-permute-done.13
  267.8 1.3 collective-permute-start.12
  269.1 3.2 %collective-permute-done.12 = f32[]{:T(128)} collective-permute-done((f32[]{:T(128)}, f32[]{:T(128)}, u32[]{:S(2)}, u32[]{:S(2)}) %collective-permute-start.12) | collective-permute-done | bytes 36 | tf_op jit(solution)/shard_map/ppermute | solution.py:464
  272.4 1.3 collective-permute-start.11
  273.7 1.8 collective-permute-done.11
  275.4 1.3 collective-permute-start.10
  276.7 2.3 collective-permute-done.10
  279.1 0.8 collective-permute-start.9
  279.9 0.3 collective-permute-done.9
  280.2 1.5 collective-permute-start.17
  281.7 0.0 collective-permute-done.19.refs_5_
  281.7 1.3 collective-permute-start.18
  287.4 0.0 collective-permute-done.20.refs_6_
  287.4 0.0 collective-permute-done.21.refs_7_
  287.4 0.0 collective-permute-done.16.refs_1_
  287.5 18.2 %collective-permute-done.17.refs_2_ = f32[2,4,128,128]{3,2,1,0:T(8,128)S(1)} collective-permute-done((f32[2,4,128,128]{3,2,1,0:T(8,128)}, f32[2,4,128,128]{3,2,1,0:T(8,128)S(1)}, u32[]{:S(2)}, u32[]{:S(2)}) %collective-permute-start.17) | collective-permute-done | bytes 524320 | tf_op jit(solution)/shard_map/ppermute | solution.py:464
  305.7 0.7 copy-done.5
  306.5 0.2 copy-done.6
  306.7 6.1 %encode.1 = (f32[1024,512]{1,0:T(8,128)}, f32[1024,512]{1,0:T(8,128)}) custom-call(s32[1]{0:T(128)} %bitcast.place, f32[1]{0:T(128)} %bitcast.2.peak, f32[2,4,128,128]{3,2,1,0:T(8,128)} %get-tuple-element.34.refs_0_, f32[2,4,128,128]{3,2,1,0:T(8,128)} %copy-done.4, f32[2,4,128,128]{3,2,1,0:T(8,128)} %copy-done.5, f32[2,4,128,128]{3,2,1,0:T(8,128)} %copy-done.6, ...), custom_call_target="tpu_custom_call" | custom-call | tf_op jit(solution)/shard_map/encode/pallas_call | solution.py:626
  (23 shorter events, 0.0 us)
Async XLA Ops:
  4.5 15.9 %collective-permute-start.3 = (f32[2,4,128,128]{3,2,1,0:T(8,128)}, f32[2,4,128,128]{3,2,1,0:T(8,128)S(1)}, u32[]{:S(2)}, u32[]{:S(2)}) collective-permute-start(f32[2,4,128,128]{3,2,1,0:T(8,128)} %get-tuple-element.27), channel_id=1, source_target_pairs={{0,8},{8,0},{16,24},{24,16},{1,9},{9,1},{17,25},{25,17},{2,10},{10... | collective-permute-start | bytes 1572872 | tf_op jit(solution)/shard_map/ppermute | solution.py:464
  7.4 26.3 %collective-permute-start.4 = (f32[2,4,128,128]{3,2,1,0:T(8,128)}, f32[2,4,128,128]{3,2,1,0:T(8,128)S(1)}, u32[]{:S(2)}, u32[]{:S(2)}) collective-permute-start(f32[2,4,128,128]{3,2,1,0:T(8,128)} %get-tuple-element.28), channel_id=1, source_target_pairs={{0,16},{8,24},{16,0},{24,8},{1,17},{9,25},{17,1},{25,9},{2,18},{10... | collective-permute-start | bytes 1572872 | tf_op jit(solution)/shard_map/ppermute | solution.py:464
  8.9 24.8 %collective-permute-start.5 = (f32[2,4,128,128]{3,2,1,0:T(8,128)}, f32[2,4,128,128]{3,2,1,0:T(8,128)S(1)}, u32[]{:S(2)}, u32[]{:S(2)}) collective-permute-start(f32[2,4,128,128]{3,2,1,0:T(8,128)} %get-tuple-element.29), channel_id=1, source_target_pairs={{0,24},{8,16},{16,8},{24,0},{1,25},{9,17},{17,9},{25,1},{2,26},{10... | collective-permute-start | bytes 1572872 | tf_op jit(solution)/shard_map/ppermute | solution.py:464
  12.7 31.5 %collective-permute-start = (f32[2,4,128,128]{3,2,1,0:T(8,128)}, f32[2,4,128,128]{3,2,1,0:T(8,128)S(1)}, u32[]{:S(2)}, u32[]{:S(2)}) collective-permute-start(f32[2,4,128,128]{3,2,1,0:T(8,128)} %get-tuple-element.23), channel_id=1, source_target_pairs={{0,8},{8,0},{16,24},{24,16},{1,9},{9,1},{17,25},{25,17},{2,10},{10... | collective-permute-start | bytes 1572872 | tf_op jit(solution)/shard_map/ppermute | solution.py:464
  14.7 40.0 %collective-permute-start.1 = (f32[2,4,128,128]{3,2,1,0:T(8,128)}, f32[2,4,128,128]{3,2,1,0:T(8,128)S(1)}, u32[]{:S(2)}, u32[]{:S(2)}) collective-permute-start(f32[2,4,128,128]{3,2,1,0:T(8,128)} %get-tuple-element.24), channel_id=1, source_target_pairs={{0,16},{8,24},{16,0},{24,8},{1,17},{9,25},{17,1},{25,9},{2,18},{10... | collective-permute-start | bytes 1572872 | tf_op jit(solution)/shard_map/ppermute | solution.py:464
  20.4 13.3 %copy-start.10 = (f32[2,4,128,128]{3,2,1,0:T(8,128)}, f32[2,4,128,128]{3,2,1,0:T(8,128)S(1)}, u32[]{:S(2)}) copy-start(f32[2,4,128,128]{3,2,1,0:T(8,128)S(1)} %collective-permute-done.3.refs_1_) | copy-start | bytes 1572868
  20.4 34.3 %collective-permute-start.2 = (f32[2,4,128,128]{3,2,1,0:T(8,128)}, f32[2,4,128,128]{3,2,1,0:T(8,128)S(1)}, u32[]{:S(2)}, u32[]{:S(2)}) collective-permute-start(f32[2,4,128,128]{3,2,1,0:T(8,128)} %get-tuple-element.25), channel_id=1, source_target_pairs={{0,24},{8,16},{16,8},{24,0},{1,25},{9,17},{17,9},{25,1},{2,26},{10... | collective-permute-start | bytes 1572872 | tf_op jit(solution)/shard_map/ppermute | solution.py:464
  33.7 0.8 copy-start.11
  33.7 1.0 copy-start.12
  44.3 10.5 %copy-start.7 = (f32[2,4,128,128]{3,2,1,0:T(8,128)}, f32[2,4,128,128]{3,2,1,0:T(8,128)S(1)}, u32[]{:S(2)}) copy-start(f32[2,4,128,128]{3,2,1,0:T(8,128)S(1)} %collective-permute-done.refs_1_) | copy-start | bytes 1572868
  54.7 0.8 copy-start.8
  54.7 1.0 copy-start.9
  65.3 69.1 %all-to-all-start = ((f32[32,168,128]{2,1,0:T(8,128)}), f32[32,168,128]{2,1,0:T(8,128)S(1)}, u32[]{:S(2)}, u32[]{:S(2)}) async-start(f32[32,168,128]{2,1,0:T(8,128)} %column_forward.3), calls=%async_computation | async-start | bytes 5505024 | tf_op jit(solution)/shard_map/all_to_all | solution.py:564
  134.5 1.5 copy-start
  227.3 10.7 %copy-start.13 = (f32[8,128]{1,0:T(8,128)S(1)}, f32[8,128]{1,0:T(8,128)}, u32[]{:S(2)}) copy-start(f32[8,128]{1,0:T(8,128)} %get-tuple-element.33) | copy-start | bytes 12292
  227.3 54.4 %collective-permute-start.19 = (f32[2,4,128,128]{3,2,1,0:T(8,128)}, f32[2,4,128,128]{3,2,1,0:T(8,128)S(1)}, u32[]{:S(2)}, u32[]{:S(2)}) collective-permute-start(f32[2,4,128,128]{3,2,1,0:T(8,128)} %get-tuple-element.39), channel_id=1, source_target_pairs={{0,8},{8,0},{16,24},{24,16},{1,9},{9,1},{17,25},{25,17},{2,10},{10... | collective-permute-start | bytes 1572872 | tf_op jit(solution)/shard_map/ppermute | solution.py:464
  240.1 12.9 %collective-permute-start.8 = (f32[]{:T(128)}, f32[]{:T(128)}, u32[]{:S(2)}, u32[]{:S(2)}) collective-permute-start(f32[]{:T(128)} %reduce_max.57), channel_id=1, source_target_pairs={{0,24},{8,16},{16,8},{24,0},{1,25},{9,17},{17,9},{25,1},{2,26},{10... | collective-permute-start | bytes 20 | tf_op jit(solution)/shard_map/ppermute | solution.py:464
  243.4 8.2 %collective-permute-start.7 = (f32[]{:T(128)}, f32[]{:T(128)}, u32[]{:S(2)}, u32[]{:S(2)}) collective-permute-start(f32[]{:T(128)} %reduce_max.57), channel_id=1, source_target_pairs={{0,16},{8,24},{16,0},{24,8},{1,17},{9,25},{17,1},{25,9},{2,18},{10... | collective-permute-start | bytes 20 | tf_op jit(solution)/shard_map/ppermute | solution.py:464
  246.2 3.5 %collective-permute-start.6 = (f32[]{:T(128)}, f32[]{:T(128)}, u32[]{:S(2)}, u32[]{:S(2)}) collective-permute-start(f32[]{:T(128)} %reduce_max.57), channel_id=1, source_target_pairs={{0,8},{8,0},{16,24},{24,16},{1,9},{9,1},{17,25},{25,17},{2,10},{10... | collective-permute-start | bytes 20 | tf_op jit(solution)/shard_map/ppermute | solution.py:464
  247.5 39.9 %collective-permute-start.20 = (f32[2,4,128,128]{3,2,1,0:T(8,128)}, f32[2,4,128,128]{3,2,1,0:T(8,128)S(1)}, u32[]{:S(2)}, u32[]{:S(2)}) collective-permute-start(f32[2,4,128,128]{3,2,1,0:T(8,128)} %get-tuple-element.40), channel_id=1, source_target_pairs={{0,16},{8,24},{16,0},{24,8},{1,17},{9,25},{17,1},{25,9},{2,18},{10... | collective-permute-start | bytes 1572872 | tf_op jit(solution)/shard_map/ppermute | solution.py:464
  249.7 37.7 %collective-permute-start.21 = (f32[2,4,128,128]{3,2,1,0:T(8,128)}, f32[2,4,128,128]{3,2,1,0:T(8,128)S(1)}, u32[]{:S(2)}, u32[]{:S(2)}) collective-permute-start(f32[2,4,128,128]{3,2,1,0:T(8,128)} %get-tuple-element.41), channel_id=1, source_target_pairs={{0,24},{8,16},{16,8},{24,0},{1,25},{9,17},{17,9},{25,1},{2,26},{10... | collective-permute-start | bytes 1572872 | tf_op jit(solution)/shard_map/ppermute | solution.py:464
  251.6 35.8 %collective-permute-start.16 = (f32[2,4,128,128]{3,2,1,0:T(8,128)}, f32[2,4,128,128]{3,2,1,0:T(8,128)S(1)}, u32[]{:S(2)}, u32[]{:S(2)}) collective-permute-start(f32[2,4,128,128]{3,2,1,0:T(8,128)} %get-tuple-element.35), channel_id=1, source_target_pairs={{0,8},{8,0},{16,24},{24,16},{1,9},{9,1},{17,25},{25,17},{2,10},{10... | collective-permute-start | bytes 1572872 | tf_op jit(solution)/shard_map/ppermute | solution.py:464
  253.6 4.8 %collective-permute-start.15 = (f32[]{:T(128)}, f32[]{:T(128)}, u32[]{:S(2)}, u32[]{:S(2)}) collective-permute-start(f32[]{:T(128)} %reduce_max.60), channel_id=1, source_target_pairs={{0,7},{1,6},{2,5},{3,4},{4,3},{5,2},{6,1},{7,0},{8,15},{9,14},{10,... | collective-permute-start | bytes 20 | tf_op jit(solution)/shard_map/ppermute | solution.py:464
  258.4 5.4 %collective-permute-start.14 = (f32[]{:T(128)}, f32[]{:T(128)}, u32[]{:S(2)}, u32[]{:S(2)}) collective-permute-start(f32[]{:T(128)} %reduce_max.60), channel_id=1, source_target_pairs={{0,6},{1,7},{2,4},{3,5},{4,2},{5,3},{6,0},{7,1},{8,14},{9,15},{10,... | collective-permute-start | bytes 20 | tf_op jit(solution)/shard_map/ppermute | solution.py:464
  263.9 4.0 %collective-permute-start.13 = (f32[]{:T(128)}, f32[]{:T(128)}, u32[]{:S(2)}, u32[]{:S(2)}) collective-permute-start(f32[]{:T(128)} %reduce_max.60), channel_id=1, source_target_pairs={{0,5},{1,4},{2,7},{3,6},{4,1},{5,0},{6,3},{7,2},{8,13},{9,12},{10,... | collective-permute-start | bytes 20 | tf_op jit(solution)/shard_map/ppermute | solution.py:464
  267.8 4.5 %collective-permute-start.12 = (f32[]{:T(128)}, f32[]{:T(128)}, u32[]{:S(2)}, u32[]{:S(2)}) collective-permute-start(f32[]{:T(128)} %reduce_max.60), channel_id=1, source_target_pairs={{0,4},{1,5},{2,6},{3,7},{4,0},{5,1},{6,2},{7,3},{8,12},{9,13},{10,... | collective-permute-start | bytes 20 | tf_op jit(solution)/shard_map/ppermute | solution.py:464
  272.4 3.1 collective-permute-start.11
  275.4 3.6 %collective-permute-start.10 = (f32[]{:T(128)}, f32[]{:T(128)}, u32[]{:S(2)}, u32[]{:S(2)}) collective-permute-start(f32[]{:T(128)} %reduce_max.60), channel_id=1, source_target_pairs={{0,2},{1,3},{2,0},{3,1},{4,6},{5,7},{6,4},{7,5},{8,10},{9,11},{10,... | collective-permute-start | bytes 20 | tf_op jit(solution)/shard_map/ppermute | solution.py:464
  279.1 1.1 collective-permute-start.9
  280.2 25.5 %collective-permute-start.17 = (f32[2,4,128,128]{3,2,1,0:T(8,128)}, f32[2,4,128,128]{3,2,1,0:T(8,128)S(1)}, u32[]{:S(2)}, u32[]{:S(2)}) collective-permute-start(f32[2,4,128,128]{3,2,1,0:T(8,128)} %get-tuple-element.36), channel_id=1, source_target_pairs={{0,16},{8,24},{16,0},{24,8},{1,17},{9,25},{17,1},{25,9},{2,18},{10... | collective-permute-start | bytes 1572872 | tf_op jit(solution)/shard_map/ppermute | solution.py:464
  281.7 24.0 %copy-start.1 = (f32[2,4,128,128]{3,2,1,0:T(8,128)}, f32[2,4,128,128]{3,2,1,0:T(8,128)S(1)}, u32[]{:S(2)}) copy-start(f32[2,4,128,128]{3,2,1,0:T(8,128)S(1)} %collective-permute-done.19.refs_5_) | copy-start | bytes 1572868
  281.7 24.0 %collective-permute-start.18 = (f32[2,4,128,128]{3,2,1,0:T(8,128)}, f32[2,4,128,128]{3,2,1,0:T(8,128)S(1)}, u32[]{:S(2)}, u32[]{:S(2)}) collective-permute-start(f32[2,4,128,128]{3,2,1,0:T(8,128)} %get-tuple-element.37), channel_id=1, source_target_pairs={{0,24},{8,16},{16,8},{24,0},{1,25},{9,17},{17,9},{25,1},{2,26},{10... | collective-permute-start | bytes 1572872 | tf_op jit(solution)/shard_map/ppermute | solution.py:464
  287.4 18.3 %copy-start.2 = (f32[2,4,128,128]{3,2,1,0:T(8,128)}, f32[2,4,128,128]{3,2,1,0:T(8,128)S(1)}, u32[]{:S(2)}) copy-start(f32[2,4,128,128]{3,2,1,0:T(8,128)S(1)} %collective-permute-done.20.refs_6_) | copy-start | bytes 1572868
  287.4 18.3 %copy-start.3 = (f32[2,4,128,128]{3,2,1,0:T(8,128)}, f32[2,4,128,128]{3,2,1,0:T(8,128)S(1)}, u32[]{:S(2)}) copy-start(f32[2,4,128,128]{3,2,1,0:T(8,128)S(1)} %collective-permute-done.21.refs_7_) | copy-start | bytes 1572868
  287.4 18.3 %copy-start.4 = (f32[2,4,128,128]{3,2,1,0:T(8,128)}, f32[2,4,128,128]{3,2,1,0:T(8,128)S(1)}, u32[]{:S(2)}) copy-start(f32[2,4,128,128]{3,2,1,0:T(8,128)S(1)} %collective-permute-done.16.refs_1_) | copy-start | bytes 1572868
  305.7 0.8 copy-start.5
  305.7 1.0 copy-start.6

commit v5 on v4

--- a/solution.py
+++ b/solution.py
@@ -242,15 +242,33 @@
             out[at] = out[at] + item if before else item
 
 
-def column_inverse_kernel(count, place, lines, twist, matrix, *refs):
-    pieces, (top, near, deep, back, sems) = refs[:count], refs[count:]
+def interleave(tiles, products, butterflies, product):
+    steps = min(tiles, products)
+
+    @pl.loop(0, steps)
+    def _(t):
+        if product is not None:
+            for part in range(products // steps):
+                product(t * (products // steps) + part)
+        if butterflies is not None:
+            for part in range(tiles // steps):
+                butterflies(t * (tiles // steps) + part)
+
+
+def column_inverse_kernel(lines, twist, matrix, out, top, deep, back):
     width = lines.shape[-1]
     rows_in = lines.shape[1]
-    per_dest = near.shape[2]
+    per_dest = out.shape[2]
     many = deep.shape[-1] // width
-
-    @pl.loop(0, RES // many)
-    def _(p):
+    now = pl.program_id(0)
+
+    def product(p):
+        done = dot16(matrix[0], deep[p])
+        slot = now % 2
+        for part in range(many):
+            back[slot, p * many + part] = done[:, part * width : (part + 1) * width]
+
+    def prepare(p):
         blocks = [lines[p * many + part] for part in range(many)]
         joined = jnp.concatenate(blocks, axis=1) if many > 1 else blocks[0]
         high = joined.astype(jnp.bfloat16).astype(jnp.float32)
@@ -258,26 +276,22 @@
         if deep.shape[1] > 3 * rows_in:
             parts.append(jnp.zeros((deep.shape[1] - 3 * rows_in, many * width), jnp.float32))
         deep[p] = jnp.concatenate(parts, axis=0).astype(jnp.bfloat16)
-        done = dot16(matrix[...], deep[p])
-        for part in range(many):
-            back[p * many + part] = done[:, part * width : (part + 1) * width]
-
-    top[...] = jnp.zeros_like(top)
-
-    @pl.loop(0, CHUNK // 8)
-    def _(t):
+        product(p)
+
+    def butterflies(t):
         q0 = pl.multiple_of(t * 8, 8)
+        slot = (now + 1) % 2
         largest = []
 
         def get(u):
-            re = back[u, pl.ds(q0, 8), :]
-            im = back[u, pl.ds(CHUNK + q0, 8), :]
+            re = back[slot, u, pl.ds(q0, 8), :]
+            im = back[slot, u, pl.ds(CHUNK + q0, 8), :]
             return twisted((re, im), u, -1, column_twist(twist, q0))
 
         def put(n, value):
             dest, block = divmod(n, per_dest)
             rows = pl.ds(q0, 8)
-            near[dest, 0, block, rows, :], near[dest, 1, block, rows, :] = value
+            out[dest, 0, block, rows, :], out[dest, 1, block, rows, :] = value
             largest.append(value[0] * value[0] + value[1] * value[1])
 
         inverse_slabs(get, put)
@@ -285,14 +299,18 @@
             largest = [jnp.maximum(a, b) for a, b in zip(largest[0::2], largest[1::2])]
         top[...] = jnp.maximum(top[...], largest[0])
 
-    copies = [
-        pltpu.make_async_copy(near.at[place[0] ^ j], piece, sems.at[j])
-        for j, piece in enumerate(pieces)
-    ]
-    for copy in copies:
-        copy.start()
-    for copy in copies:
-        copy.wait()
+    @pl.when(now == 0)
+    def _():
+        top[...] = jnp.zeros_like(top)
+        pl.loop(0, RES // many)(prepare)
+
+    for step in range(1, CHUNKS + 1):
+
+        @pl.when(now == step)
+        def _():
+            interleave(
+                CHUNK // 8, RES // many, butterflies, product if step < CHUNKS else None
+            )
 
 
 def line_kernel(
@@ -435,18 +453,14 @@
     return (near_real * level + near_imag * lift, near_imag * level - near_real * lift)
 
 
-def encode_kernel(place, peak, *refs):
-    pieces, (slm_real, slm_imag) = refs[:-2], refs[-2:]
-    width = pieces[0].shape[-1]
-    count = len(pieces) // CHUNKS
-    cell = lax.broadcasted_iota(jnp.int32, (CHUNK, width), 0)
-    cell = cell + lax.broadcasted_iota(jnp.int32, (CHUNK, width), 1)
-    for at, piece in enumerate(pieces):
-        chunk, j = divmod(at, count)
-        rows = pl.ds(chunk * CHUNK, CHUNK)
-        lanes = pl.ds(pl.multiple_of((place[0] ^ j) * width, width), width)
-        slm_real[rows, lanes], slm_imag[rows, lanes] = encode(
-            piece[0, 0], piece[1, 0], peak[0], (cell & 1) == 0
+def encode_kernel(peak, near, slm_real, slm_imag):
+    rows, width = near.shape[2:]
+    cell = lax.broadcasted_iota(jnp.int32, (rows, width), 0)
+    cell = cell + lax.broadcasted_iota(jnp.int32, (rows, width), 1)
+    for r in range(near.shape[0]):
+        lanes = pl.ds(r * width, width)
+        slm_real[:, lanes], slm_imag[:, lanes] = encode(
+            near[r, 0], near[r, 1], peak[0], (cell & 1) == 0
         )
 
 
@@ -513,6 +527,8 @@
         name="gain",
     )(place)
 
+    pack_rows = min(height, 256)
+    tall = (row_total, 2, height // INNER, CHUNK, width)
     place_row = lax.axis_index("row").reshape(1).astype(jnp.int32)
     blocks = height // INNER
     piece = (2, blocks, CHUNK, width)
@@ -590,49 +606,59 @@
     lines = lax.all_to_all(lines, ("row", "col"), split_axis=0, concat_axis=0, tiled=True)
     lines = lines.reshape(RES, total_rows, width)
 
-    near, tops = [], []
-    for chunk in range(CHUNKS):
-        rows = slice(chunk * CHUNK, (chunk + 1) * CHUNK)
-        *pieces, top = pl.pallas_call(
-            partial(column_inverse_kernel, row_total),
-            in_specs=[whole(pltpu.SMEM)] + [whole()] * 3,
-            out_specs=[anywhere] * row_total + [whole()],
-            out_shape=[piece_shape] * row_total + [jax.ShapeDtypeStruct((8, width), jnp.float32)],
-            scratch_shapes=[
-                pltpu.VMEM((row_total,) + piece, jnp.float32),
-                pltpu.VMEM((RES // many, inv_col.shape[2], many * width), jnp.bfloat16),
-                pltpu.VMEM((RES, 2 * CHUNK, width), jnp.float32),
-                pltpu.SemaphoreType.DMA((row_total,)),
-            ],
-            compiler_params=params(),
-            cost_estimate=cost(20),
-            name="column_inverse",
-        )(place_row, lines, twist_col[rows], inv_col[chunk])
-        near += exchange(pieces, "row")
-        tops.append(top)
-    peak = jnp.max(jnp.stack(tops))
-    for axis, total in (("row", row_total), ("col", col_total)):
-        peak = jnp.max(jnp.stack(exchange([peak] * total, axis)))
+    near, top = pl.pallas_call(
+        column_inverse_kernel,
+        grid=(CHUNKS + 1,),
+        in_specs=[
+            whole(),
+            pl.BlockSpec((CHUNK, 128), lambda i: (jnp.maximum(i - 1, 0), 0)),
+            pl.BlockSpec((1,) + inv_col.shape[1:], lambda i: (jnp.minimum(i, CHUNKS - 1), 0, 0)),
+        ],
+        out_specs=[
+            pl.BlockSpec(tall, lambda i: (0, 0, 0, jnp.maximum(i - 1, 0), 0)),
+            whole(),
+        ],
+        out_shape=[
+            jax.ShapeDtypeStruct((row_total, 2, blocks, INNER, width), jnp.float32),
+            jax.ShapeDtypeStruct((8, width), jnp.float32),
+        ],
+        scratch_shapes=[
+            pltpu.VMEM((RES // many, inv_col.shape[2], many * width), jnp.bfloat16),
+            pltpu.VMEM((2, RES, 2 * CHUNK, width), jnp.float32),
+        ],
+        compiler_params=params(),
+        name="column_inverse",
+    )(lines, twist_col, inv_col)
+
+    near = near.reshape(row_total, 2, height, width)
+    near = lax.all_to_all(near, "row", split_axis=0, concat_axis=0, tiled=True)
+    peak = jnp.max(top)
+    shift = 1
+    while shift < col_total:
+        partner = [(i, i ^ shift) for i in range(col_total)]
+        peak = jnp.maximum(peak, lax.ppermute(peak, "col", partner))
+        shift *= 2
+    for item in exchange([peak] * row_total, "row")[1:]:
+        peak = jnp.maximum(peak, item)
     peak = jnp.sqrt(peak)
-
     if width != 128:
-        near = jnp.stack(near).reshape((CHUNKS, row_total) + piece)
-        near = jnp.take(near, jnp.arange(row_total) ^ place_row[0], axis=1)
-        near = near.transpose(2, 3, 0, 4, 1, 5).reshape(2, height, tile_width)
+        near = near.transpose(1, 2, 0, 3).reshape(2, height, tile_width)
         even_cell = (jnp.arange(height)[:, None] + jnp.arange(tile_width)[None, :]) % 2 == 0
         return encode(near[0], near[1], peak, even_cell)
-    tile_spec = pl.BlockSpec((INNER, tile_width), lambda i: (i, 0))
+    tile_spec = pl.BlockSpec((pack_rows, tile_width), lambda i: (i, 0))
     tile_shape = jax.ShapeDtypeStruct((height, tile_width), jnp.float32)
     return pl.pallas_call(
         encode_kernel,
-        grid=(blocks,),
-        in_specs=[whole(pltpu.SMEM)] * 2
-        + [pl.BlockSpec((2, 1, CHUNK, width), lambda i: (0, i, 0, 0))] * len(near),
+        grid=(height // pack_rows,),
+        in_specs=[
+            whole(pltpu.SMEM),
+            pl.BlockSpec((row_total, 2, pack_rows, width), lambda i: (0, 0, i, 0)),
+        ],
         out_specs=[tile_spec, tile_spec],
         out_shape=[tile_shape, tile_shape],
         compiler_params=params(),
         name="encode",
-    )(place_row, peak.reshape(1), *near)
+    )(peak.reshape(1), near)
 
 
 def solution(mesh):

time: 314 us -> 297 us (0.946)
  waiting for transfers between devices: 118 us -> 88.9 us
  starting transfers between devices: 38.9 us -> 62.4 us
  Pallas kernels: 72.6 us -> 66.8 us
  between operations: 8.45 us -> 5.27 us
    ppermute x22 -> x9, waiting for transfers between devices: 61.3 us -> 25.6 us  [exchange(): lax.ppermute(pieces[j], axis, [(i, i ^ j) for i in range(total)])]
    ppermute x22 -> x9, starting transfers between devices: 34 us -> 49.8 us  [exchange(): lax.ppermute(pieces[j], axis, [(i, i ^ j) for i in range(total)])]
    ppermute x0 -> x3, waiting for transfers between devices: none -> 6.51 us  [body(): peak = jnp.maximum(peak, lax.ppermute(peak, 'col', partner))]
    pallas_call x3 -> x2, Pallas kernels: 24.8 us -> 18.9 us  [the longest x1 12.4 us: body(): pl.pallas_call(column_inverse_kernel, grid=(CHUNKS + 1,), in_specs=[whole...]
    all_to_all x0 -> x1, starting transfers between devices: none -> 5.01 us  [body(): near = lax.all_to_all(near, 'row', split_axis=0, concat_axis=0, tiled=True)]
  transfers between devices with their start and end apart: 23 -> 14, of which waited for: 13 -> 8; matrix products, arithmetic and copies ran while one was open for 1% -> 0% of each run, Pallas kernels for 9% -> 7%
where the time goes in v5:
time: 297 us; the launch traced here: 296 us
  waiting for transfers between devices  88.9 us (30%)
  blocking collectives  67.6 us (23%)
  Pallas kernels  66.8 us (22%)
  starting transfers between devices  62.4 us (21%)
  between operations  5.27 us (2%)
  local copies, waits for them, and re-layouts  3.56 us (1%)
    all_to_all x1, blocking collectives, body(): lax.all_to_all(lines, ('row', 'col'), split_axis=0, concat_axis=0, tiled=...  67.6 us
    all_to_all x1, waiting for transfers between devices, body(): lax.all_to_all(lines, ('row', 'col'), split_axis=0, concat_axis=0, tiled=...  56.8 us
    ppermute x9, starting transfers between devices, exchange(): lax.ppermute(pieces[j], axis, [(i, i ^ j) for i in range(total)])  49.8 us
    ppermute x9, waiting for transfers between devices, exchange(): lax.ppermute(pieces[j], axis, [(i, i ^ j) for i in range(total)])  25.6 us
    pallas_call x2, Pallas kernels, body(): pl.pallas_call(partial(column_forward_kernel, row_total), in_specs=[whole...  19.2 us
    pallas_call x1, Pallas kernels, body(): pl.pallas_call(partial(line_kernel, order, tail), grid=(-(-own // at_once...  14.3 us
    pallas_call x1, Pallas kernels, body(): pl.pallas_call(column_inverse_kernel, grid=(CHUNKS + 1,), in_specs=[whole...  12.4 us
    pallas_call x2, Pallas kernels, body(): pl.pallas_call(pack_kernel, grid=(blocks,), in_specs=[whole(pltpu.SMEM)]...  7.69 us
  transfers between devices with their start and end apart: 14, of which 8 were waited for; matrix products, arithmetic and copies ran while one was open for 0% of the time, Pallas kernels for 7%

profile of v5, /device:TPU:0, one launch (start us, length us, event | category | flops | bytes accessed | tf_op | source)
XLA Modules:
  0.0 295.9 jit_solution(9065542873210433818)
XLA Ops:
  0.6 3.9 %pack.3 = (f32[2,4,128,128]{3,2,1,0:T(8,128)}, f32[2,4,128,128]{3,2,1,0:T(8,128)}, f32[2,4,128,128]{3,2,1,0:T(8,128)}, f32[2,4,128,128]{3,2,1,0:T(8,128)}) custom-call(s32[1]{0:T(128)} %bitcast.place, f32[1024,512]{1,0:T(8,128)} %field_real.3, f32[1024,512]{1,0:T(8,128)} %field_imag.3), custom_call_target="tpu_custom_call" | custom-call | bytes 4194304 | tf_op jit(solution)/shard_map/pack/pallas_call | solution.py:544
  4.5 2.9 collective-permute-start.3
  7.5 1.5 collective-permute-start.4
  9.0 0.0 collective-permute-start.5
  9.0 3.8 %pack.2 = (f32[2,4,128,128]{3,2,1,0:T(8,128)}, f32[2,4,128,128]{3,2,1,0:T(8,128)}, f32[2,4,128,128]{3,2,1,0:T(8,128)}, f32[2,4,128,128]{3,2,1,0:T(8,128)}) custom-call(s32[1]{0:T(128)} %bitcast.place, f32[1024,512]{1,0:T(8,128)} %field_real.3, f32[1024,512]{1,0:T(8,128)} %field_imag.3), custom_call_target="tpu_custom_call" | custom-call | bytes 4194304 | tf_op jit(solution)/shard_map/pack/pallas_call | solution.py:544
  12.8 2.0 collective-permute-start
  14.7 1.5 collective-permute-start.1
  16.3 4.2 %collective-permute-done.3.refs_1_ = f32[2,4,128,128]{3,2,1,0:T(8,128)S(1)} collective-permute-done((f32[2,4,128,128]{3,2,1,0:T(8,128)}, f32[2,4,128,128]{3,2,1,0:T(8,128)S(1)}, u32[]{:S(2)}, u32[]{:S(2)}) %collective-permute-start.3) | collective-permute-done | bytes 524320 | tf_op jit(solution)/shard_map/ppermute | solution.py:478
  20.4 0.0 copy-start.4
  20.4 3.0 %collective-permute-start.2 = (f32[2,4,128,128]{3,2,1,0:T(8,128)}, f32[2,4,128,128]{3,2,1,0:T(8,128)S(1)}, u32[]{:S(2)}, u32[]{:S(2)}) collective-permute-start(f32[2,4,128,128]{3,2,1,0:T(8,128)} %get-tuple-element.17), channel_id=1, source_target_pairs={{0,24},{8,16},{16,8},{24,0},{1,25},{9,17},{17,9},{25,1},{2,26},{10... | collective-permute-start | bytes 1572872 | tf_op jit(solution)/shard_map/ppermute | solution.py:478
  23.5 10.3 %collective-permute-done.4.refs_2_ = f32[2,4,128,128]{3,2,1,0:T(8,128)S(1)} collective-permute-done((f32[2,4,128,128]{3,2,1,0:T(8,128)}, f32[2,4,128,128]{3,2,1,0:T(8,128)S(1)}, u32[]{:S(2)}, u32[]{:S(2)}) %collective-permute-start.4) | collective-permute-done | bytes 524320 | tf_op jit(solution)/shard_map/ppermute | solution.py:478
  33.8 0.0 copy-start.5
  33.8 0.0 collective-permute-done.5.refs_3_
  33.8 0.0 copy-start.6
  33.8 0.0 copy-done.4
  33.8 0.8 copy-done.5
  34.6 0.2 copy-done.6
  34.8 9.6 %column_forward.2.refs_4_ = f32[32,168,128]{2,1,0:T(8,128)} custom-call(s32[1]{0:T(128)} %bitcast.place, f32[128,128]{1,0:T(8,128)} %constant.62.clone.twist, bf16[336,256]{1,0:T(8,128)(2,1)} %constant.63.clone.matrix, f32[2,4,128,128]{3,2,1,0:T(8,128)} %get-tuple-element.18.refs_0_, f32[2,4,128,128]{3,2,1,0:T(8,128)} %copy-done.4, ...), custom_call_target="tpu_custom_call" | custom-call | bytes 20971520 | tf_op jit(solution)/shard_map/column_forward/pallas_call | solution.py:561
  44.3 0.0 collective-permute-done.refs_1_
  44.4 0.0 copy-start.1
  44.4 10.4 %collective-permute-done.1.refs_2_ = f32[2,4,128,128]{3,2,1,0:T(8,128)S(1)} collective-permute-done((f32[2,4,128,128]{3,2,1,0:T(8,128)}, f32[2,4,128,128]{3,2,1,0:T(8,128)S(1)}, u32[]{:S(2)}, u32[]{:S(2)}) %collective-permute-start.1) | collective-permute-done | bytes 524320 | tf_op jit(solution)/shard_map/ppermute | solution.py:478
  54.8 0.0 copy-start.2
  54.8 0.0 collective-permute-done.2.refs_3_
  54.8 0.0 copy-start.3
  54.8 0.0 copy-done.1
  54.8 0.8 copy-done.2
  55.6 0.2 copy-done.3
  55.8 9.6 %column_forward.3 = f32[32,168,128]{2,1,0:T(8,128)} custom-call(s32[1]{0:T(128)} %bitcast.place, f32[128,128]{1,0:T(8,128)} %constant.64.clone.twist, bf16[336,256]{1,0:T(8,128)(2,1)} %constant.65.clone.matrix, f32[2,4,128,128]{3,2,1,0:T(8,128)} %get-tuple-element.14.refs_0_, f32[2,4,128,128]{3,2,1,0:T(8,128)} %copy-done.1, f32[2,4,128,128]{3,2,1,0:T(8,128)} %copy-done.2, ...), custom_call_target="tpu_custom_call" | custom-call | bytes 20971520 | tf_op jit(solution)/shard_map/column_forward/pallas_call | solution.py:561
  65.4 4.9 %all-to-all-start = ((f32[32,168,128]{2,1,0:T(8,128)}), f32[32,168,128]{2,1,0:T(8,128)S(1)}, u32[]{:S(2)}, u32[]{:S(2)}) async-start(f32[32,168,128]{2,1,0:T(8,128)} %column_forward.3), calls=%async_computation | async-start | bytes 5505024 | tf_op jit(solution)/shard_map/all_to_all | solution.py:580
  70.3 0.7 pad_add_fusion.place
  71.0 6.7 %gain.1 = (f32[11,256,128]{2,1,0:T(8,128)}, f32[11,256,128]{2,1,0:T(8,128)}) custom-call(s32[2]{0:T(128)} %pad_add_fusion.place), custom_call_target="tpu_custom_call" | custom-call | tf_op jit(solution)/shard_map/gain/pallas_call | solution.py:520
  77.7 56.8 %all-to-all-done.lines = f32[32,168,128]{2,1,0:T(8,128)S(1)} async-done(((f32[32,168,128]{2,1,0:T(8,128)}), f32[32,168,128]{2,1,0:T(8,128)S(1)}, u32[]{:S(2)}, u32[]{:S(2)}) %all-to-all-start) | async-done | bytes 2752544 | tf_op jit(solution)/shard_map/all_to_all | solution.py:580
  134.5 0.0 copy-start
  134.5 1.6 copy-done
  136.1 14.3 %line.1 = f32[32,168,128]{2,1,0:T(8,128)} custom-call(f32[32,168,128]{2,1,0:T(8,128)} %copy-done, f32[11,256,128]{2,1,0:T(8,128)} %get-tuple-element.22.gain_re, f32[11,256,128]{2,1,0:T(8,128)} %get-tuple-element.23.gain_im, f32[2,17,8,256]{3,2,1,0:T(8,128)} %constant.66.clone.twist, bf16[512,256]{1,0:T(8,128)(2,1)} %constant.67.clone.fwd_high, ...), custom_call_target="tpu_custom_call" | custom-call | tf_op jit(solution)/shard_map/line/pallas_call | solution.py:591
  150.4 67.6 %all_to_all.15.lines = f32[32,168,128]{2,1,0:T(8,128)} all-to-all(f32[32,168,128]{2,1,0:T(8,128)} %line.1), channel_id=1, replica_groups=mesh['row'=4,'col'=8] {'row','col'}, dimensions={0} | all-to-all | bytes 5505024 | tf_op jit(solution)/shard_map/all_to_all | solution.py:606
  218.0 12.4 %column_inverse.1 = (f32[4,2,4,256,128]{4,3,2,1,0:T(8,128)}, f32[8,128]{1,0:T(8,128)}) custom-call(f32[32,168,128]{2,1,0:T(8,128)} %all_to_all.15.lines, f32[256,128]{1,0:T(8,128)} %constant.71.clone.twist, bf16[2,256,512]{2,1,0:T(8,128)(2,1)} %constant.72.clone.matrix), custom_call_target="tpu_custom_call" | custom-call | tf_op jit(solution)/shard_map/column_inverse/pallas_call | solution.py:609
  230.4 0.0 copy-start.7
  230.4 5.0 %all-to-all-start.2 = ((f32[4,2,1024,128]{3,2,1,0:T(8,128)}), f32[4,2,1024,128]{3,2,1,0:T(8,128)}, u32[]{:S(2)}, u32[]{:S(2)}) async-start(f32[4,2,1024,128]{3,2,1,0:T(8,128)} %bitcast.4), calls=%async_computation.2 | async-start | bytes 8388608 | tf_op jit(solution)/shard_map/all_to_all | solution.py:634
  235.4 0.0 copy-done.7
  235.4 0.6 reduce_max.9
  236.0 0.0 collective-permute-start.6
  236.0 1.2 collective-permute-done.6
  238.6 1.4 collective-permute-start.7
  239.9 2.2 collective-permute-done.7
  242.7 1.4 collective-permute-start.8
  244.1 3.1 %collective-permute-done.8 = f32[]{:T(128)} collective-permute-done((f32[]{:T(128)}, f32[]{:T(128)}, u32[]{:S(2)}, u32[]{:S(2)}) %collective-permute-start.8) | collective-permute-done | bytes 36 | tf_op jit(solution)/shard_map/ppermute | solution.py:639
  247.8 33.0 %collective-permute-start.11 = (f32[]{:T(128)}, f32[]{:T(128)}, u32[]{:S(2)}, u32[]{:S(2)}) collective-permute-start(f32[]{:T(128)} %max.20), channel_id=1, source_target_pairs={{0,24},{8,16},{16,8},{24,0},{1,25},{9,17},{17,9},{25,1},{2,26},{10... | collective-permute-start | bytes 20 | tf_op jit(solution)/shard_map/ppermute | solution.py:478
  280.8 3.0 %collective-permute-start.10 = (f32[]{:T(128)}, f32[]{:T(128)}, u32[]{:S(2)}, u32[]{:S(2)}) collective-permute-start(f32[]{:T(128)} %max.20), channel_id=1, source_target_pairs={{0,16},{8,24},{16,0},{24,8},{1,17},{9,25},{17,1},{25,9},{2,18},{10... | collective-permute-start | bytes 20 | tf_op jit(solution)/shard_map/ppermute | solution.py:478
  283.8 2.8 collective-permute-start.9
  286.6 0.7 collective-permute-done.9
  288.0 0.0 collective-permute-done.10
  288.7 0.0 collective-permute-done.11
  289.3 0.0 all-to-all-done.2.near
  289.3 6.5 %encode.1 = (f32[1024,512]{1,0:T(8,128)}, f32[1024,512]{1,0:T(8,128)}) custom-call(f32[1]{0:T(128)} %bitcast.2.peak, f32[4,2,1024,128]{3,2,1,0:T(8,128)} %all-to-all-done.2.near), custom_call_target="tpu_custom_call" | custom-call | tf_op jit(solution)/shard_map/encode/pallas_call | solution.py:650
Async XLA Ops:
  4.5 15.9 %collective-permute-start.3 = (f32[2,4,128,128]{3,2,1,0:T(8,128)}, f32[2,4,128,128]{3,2,1,0:T(8,128)S(1)}, u32[]{:S(2)}, u32[]{:S(2)}) collective-permute-start(f32[2,4,128,128]{3,2,1,0:T(8,128)} %get-tuple-element.19), channel_id=1, source_target_pairs={{0,8},{8,0},{16,24},{24,16},{1,9},{9,1},{17,25},{25,17},{2,10},{10... | collective-permute-start | bytes 1572872 | tf_op jit(solution)/shard_map/ppermute | solution.py:478
  7.5 26.3 %collective-permute-start.4 = (f32[2,4,128,128]{3,2,1,0:T(8,128)}, f32[2,4,128,128]{3,2,1,0:T(8,128)S(1)}, u32[]{:S(2)}, u32[]{:S(2)}) collective-permute-start(f32[2,4,128,128]{3,2,1,0:T(8,128)} %get-tuple-element.20), channel_id=1, source_target_pairs={{0,16},{8,24},{16,0},{24,8},{1,17},{9,25},{17,1},{25,9},{2,18},{10... | collective-permute-start | bytes 1572872 | tf_op jit(solution)/shard_map/ppermute | solution.py:478
  9.0 24.8 %collective-permute-start.5 = (f32[2,4,128,128]{3,2,1,0:T(8,128)}, f32[2,4,128,128]{3,2,1,0:T(8,128)S(1)}, u32[]{:S(2)}, u32[]{:S(2)}) collective-permute-start(f32[2,4,128,128]{3,2,1,0:T(8,128)} %get-tuple-element.21), channel_id=1, source_target_pairs={{0,24},{8,16},{16,8},{24,0},{1,25},{9,17},{17,9},{25,1},{2,26},{10... | collective-permute-start | bytes 1572872 | tf_op jit(solution)/shard_map/ppermute | solution.py:478
  12.8 31.6 %collective-permute-start = (f32[2,4,128,128]{3,2,1,0:T(8,128)}, f32[2,4,128,128]{3,2,1,0:T(8,128)S(1)}, u32[]{:S(2)}, u32[]{:S(2)}) collective-permute-start(f32[2,4,128,128]{3,2,1,0:T(8,128)} %get-tuple-element.15), channel_id=1, source_target_pairs={{0,8},{8,0},{16,24},{24,16},{1,9},{9,1},{17,25},{25,17},{2,10},{10... | collective-permute-start | bytes 1572872 | tf_op jit(solution)/shard_map/ppermute | solution.py:478
  14.7 40.0 %collective-permute-start.1 = (f32[2,4,128,128]{3,2,1,0:T(8,128)}, f32[2,4,128,128]{3,2,1,0:T(8,128)S(1)}, u32[]{:S(2)}, u32[]{:S(2)}) collective-permute-start(f32[2,4,128,128]{3,2,1,0:T(8,128)} %get-tuple-element.16), channel_id=1, source_target_pairs={{0,16},{8,24},{16,0},{24,8},{1,17},{9,25},{17,1},{25,9},{2,18},{10... | collective-permute-start | bytes 1572872 | tf_op jit(solution)/shard_map/ppermute | solution.py:478
  20.4 13.3 %copy-start.4 = (f32[2,4,128,128]{3,2,1,0:T(8,128)}, f32[2,4,128,128]{3,2,1,0:T(8,128)S(1)}, u32[]{:S(2)}) copy-start(f32[2,4,128,128]{3,2,1,0:T(8,128)S(1)} %collective-permute-done.3.refs_1_) | copy-start | bytes 1572868
  20.4 34.3 %collective-permute-start.2 = (f32[2,4,128,128]{3,2,1,0:T(8,128)}, f32[2,4,128,128]{3,2,1,0:T(8,128)S(1)}, u32[]{:S(2)}, u32[]{:S(2)}) collective-permute-start(f32[2,4,128,128]{3,2,1,0:T(8,128)} %get-tuple-element.17), channel_id=1, source_target_pairs={{0,24},{8,16},{16,8},{24,0},{1,25},{9,17},{17,9},{25,1},{2,26},{10... | collective-permute-start | bytes 1572872 | tf_op jit(solution)/shard_map/ppermute | solution.py:478
  33.8 0.8 copy-start.5
  33.8 1.0 copy-start.6
  44.4 10.4 %copy-start.1 = (f32[2,4,128,128]{3,2,1,0:T(8,128)}, f32[2,4,128,128]{3,2,1,0:T(8,128)S(1)}, u32[]{:S(2)}) copy-start(f32[2,4,128,128]{3,2,1,0:T(8,128)S(1)} %collective-permute-done.refs_1_) | copy-start | bytes 1572868
  54.8 0.8 copy-start.2
  54.8 1.0 copy-start.3
  65.4 69.1 %all-to-all-start = ((f32[32,168,128]{2,1,0:T(8,128)}), f32[32,168,128]{2,1,0:T(8,128)S(1)}, u32[]{:S(2)}, u32[]{:S(2)}) async-start(f32[32,168,128]{2,1,0:T(8,128)} %column_forward.3), calls=%async_computation | async-start | bytes 5505024 | tf_op jit(solution)/shard_map/all_to_all | solution.py:580
  134.5 1.6 copy-start
  230.4 5.0 %copy-start.7 = (f32[8,128]{1,0:T(8,128)S(1)}, f32[8,128]{1,0:T(8,128)}, u32[]{:S(2)}) copy-start(f32[8,128]{1,0:T(8,128)} %get-tuple-element.24) | copy-start | bytes 12292
  230.4 58.9 %all-to-all-start.2 = ((f32[4,2,1024,128]{3,2,1,0:T(8,128)}), f32[4,2,1024,128]{3,2,1,0:T(8,128)}, u32[]{:S(2)}, u32[]{:S(2)}) async-start(f32[4,2,1024,128]{3,2,1,0:T(8,128)} %bitcast.4), calls=%async_computation.2 | async-start | bytes 8388608 | tf_op jit(solution)/shard_map/all_to_all | solution.py:634
  236.0 1.2 collective-permute-start.6
  238.6 3.6 %collective-permute-start.7 = (f32[]{:T(128)}, f32[]{:T(128)}, u32[]{:S(2)}, u32[]{:S(2)}) collective-permute-start(f32[]{:T(128)} %max.18), channel_id=1, source_target_pairs={{0,2},{1,3},{2,0},{3,1},{4,6},{5,7},{6,4},{7,5},{8,10},{9,11},{10,... | collective-permute-start | bytes 20 | tf_op jit(solution)/shard_map/ppermute | solution.py:639
  242.7 4.5 %collective-permute-start.8 = (f32[]{:T(128)}, f32[]{:T(128)}, u32[]{:S(2)}, u32[]{:S(2)}) collective-permute-start(f32[]{:T(128)} %max.19), channel_id=1, source_target_pairs={{0,4},{1,5},{2,6},{3,7},{4,0},{5,1},{6,2},{7,3},{8,12},{9,13},{10,... | collective-permute-start | bytes 20 | tf_op jit(solution)/shard_map/ppermute | solution.py:639
  247.8 40.8 %collective-permute-start.11 = (f32[]{:T(128)}, f32[]{:T(128)}, u32[]{:S(2)}, u32[]{:S(2)}) collective-permute-start(f32[]{:T(128)} %max.20), channel_id=1, source_target_pairs={{0,24},{8,16},{16,8},{24,0},{1,25},{9,17},{17,9},{25,1},{2,26},{10... | collective-permute-start | bytes 20 | tf_op jit(solution)/shard_map/ppermute | solution.py:478
  280.8 7.1 %collective-permute-start.10 = (f32[]{:T(128)}, f32[]{:T(128)}, u32[]{:S(2)}, u32[]{:S(2)}) collective-permute-start(f32[]{:T(128)} %max.20), channel_id=1, source_target_pairs={{0,16},{8,24},{16,0},{24,8},{1,17},{9,25},{17,1},{25,9},{2,18},{10... | collective-permute-start | bytes 20 | tf_op jit(solution)/shard_map/ppermute | solution.py:478
  283.8 3.5 %collective-permute-start.9 = (f32[]{:T(128)}, f32[]{:T(128)}, u32[]{:S(2)}, u32[]{:S(2)}) collective-permute-start(f32[]{:T(128)} %max.20), channel_id=1, source_target_pairs={{0,8},{8,0},{16,24},{24,16},{1,9},{9,1},{17,25},{25,17},{2,10},{10... | collective-permute-start | bytes 20 | tf_op jit(solution)/shard_map/ppermute | solution.py:478

commit v6 on v5

--- a/solution.py
+++ b/solution.py
@@ -20,7 +20,8 @@
 HALF = 40
 CHUNKS = 2
 CHUNK = INNER // CHUNKS
-VMEM = 56 * 1024 * 1024
+STEPS = 4
+STEP = INNER // STEPS
 
 
 def optics(padded_side):
@@ -70,8 +71,8 @@
         inverse[:, :, at] = (c, s) if part == 0 else (-s, c)
     forward = forward.reshape(-1, 2, CHUNKS, CHUNK // 8, 8).transpose(2, 0, 3, 1, 4)
     forward = np.concatenate(split16(forward.reshape(CHUNKS, len(rows), 2 * CHUNK)), axis=1)
-    inverse = inverse.reshape(2, CHUNKS, CHUNK, -1).transpose(1, 0, 2, 3)
-    high, low = split16(inverse.reshape(CHUNKS, 2 * CHUNK, len(rows)))
+    inverse = inverse.reshape(2, STEPS, STEP, -1).transpose(1, 0, 2, 3)
+    high, low = split16(inverse.reshape(STEPS, 2 * STEP, len(rows)))
     inverse = np.concatenate([high, high, low], axis=2)
     inverse = np.pad(inverse, ((0, 0), (0, 0), (0, -3 * len(rows) % 16)))
     return forward, inverse
@@ -198,48 +199,60 @@
 
 def column_forward_kernel(count, place, twist, matrix, *refs):
     pieces, refs = refs[:count], refs[count:]
-    before, (out, field, high, low, sems) = refs[:-5], refs[-5:]
-    width = field.shape[-1]
-    per_source = field.shape[2]
+    before, (out, total, high, low, sems) = refs[:-5], refs[-5:]
+    width = pieces[0].shape[-1]
+    per_source = pieces[0].shape[1]
     many = high.shape[-1] // width
+    products = RES // many
     rows_out = out.shape[1]
-    copies = [
-        pltpu.make_async_copy(piece, field.at[place[0] ^ j], sems.at[j])
-        for j, piece in enumerate(pieces)
-    ]
-    copies += [pltpu.make_async_copy(item, out, sems.at[count]) for item in before]
-    for copy in copies:
-        copy.start()
-    for copy in copies[:count]:
-        copy.wait()
-
-    @pl.loop(0, CHUNK // 8)
-    def _(t):
-        q0 = pl.multiple_of(t * 8, 8)
-
-        def get(n):
-            source, block = divmod(n, per_source)
-            rows = pl.ds(q0, 8)
-            return field[source, 0, block, rows, :], field[source, 1, block, rows, :]
-
-        def put(u, value):
-            item = jnp.concatenate(twisted(value, u, 1, column_twist(twist, q0)), axis=0)
-            rows = pl.ds(pl.multiple_of(t * 16, 16), 16)
-            at = (u // many, rows, pl.ds((u % many) * width, width))
-            high[at], low[at] = high_low(item)
-
-        forward_slabs(get, put)
-
-    for copy in copies[count:]:
-        copy.wait()
-
-    @pl.loop(0, RES // many)
+
+    def copy_in(p):
+        part = pl.ds(p * many, many)
+        return pltpu.make_async_copy(before[0].at[part], total.at[part], sems.at[p])
+
+    def copy_out(p):
+        part = pl.ds(p * many, many)
+        return pltpu.make_async_copy(total.at[part], out.at[part], sems.at[products + p])
+
+    if before:
+        for p in range(products):
+            copy_in(p).start()
+
+    for here in range(count):
+
+        @pl.when(place[0] == here)
+        def _():
+            @pl.loop(0, CHUNK // 8)
+            def _(t):
+                q0 = pl.multiple_of(t * 8, 8)
+
+                def get(n):
+                    source, block = divmod(n, per_source)
+                    piece = pieces[source ^ here]
+                    rows = pl.ds(q0, 8)
+                    return piece[0, block, rows, :], piece[1, block, rows, :]
+
+                def put(u, value):
+                    item = jnp.concatenate(twisted(value, u, 1, column_twist(twist, q0)), axis=0)
+                    rows = pl.ds(pl.multiple_of(t * 16, 16), 16)
+                    at = (u // many, rows, pl.ds((u % many) * width, width))
+                    high[at], low[at] = high_low(item)
+
+                forward_slabs(get, put)
+
+    @pl.loop(0, products)
     def _(p):
         done = three_left(matrix, rows_out, high[p], low[p])
+        if before:
+            copy_in(p).wait()
         for part in range(many):
             item = done[:, part * width : (part + 1) * width]
             at = p * many + part
-            out[at] = out[at] + item if before else item
+            total[at] = total[at] + item if before else item
+        copy_out(p).start()
+
+    for p in range(products):
+        copy_out(p).wait()
 
 
 def interleave(tiles, products, butterflies, product):
@@ -255,13 +268,17 @@
                 butterflies(t * (tiles // steps) + part)
 
 
-def column_inverse_kernel(lines, twist, matrix, out, top, deep, back):
+def column_inverse_kernel(source, twist, matrix, out, top, lines, deep, back, sems):
     width = lines.shape[-1]
     rows_in = lines.shape[1]
     per_dest = out.shape[2]
     many = deep.shape[-1] // width
     now = pl.program_id(0)
 
+    def copy_in(p):
+        part = pl.ds(p * many, many)
+        return pltpu.make_async_copy(source.at[part], lines.at[part], sems.at[p])
+
     def product(p):
         done = dot16(matrix[0], deep[p])
         slot = now % 2
@@ -269,6 +286,7 @@
             back[slot, p * many + part] = done[:, part * width : (part + 1) * width]
 
     def prepare(p):
+        copy_in(p).wait()
         blocks = [lines[p * many + part] for part in range(many)]
         joined = jnp.concatenate(blocks, axis=1) if many > 1 else blocks[0]
         high = joined.astype(jnp.bfloat16).astype(jnp.float32)
@@ -285,7 +303,7 @@
 
         def get(u):
             re = back[slot, u, pl.ds(q0, 8), :]
-            im = back[slot, u, pl.ds(CHUNK + q0, 8), :]
+            im = back[slot, u, pl.ds(STEP + q0, 8), :]
             return twisted((re, im), u, -1, column_twist(twist, q0))
 
         def put(n, value):
@@ -301,23 +319,25 @@
 
     @pl.when(now == 0)
     def _():
+        for p in range(RES // many):
+            copy_in(p).start()
         top[...] = jnp.zeros_like(top)
         pl.loop(0, RES // many)(prepare)
 
-    for step in range(1, CHUNKS + 1):
+    for step in range(1, STEPS + 1):
 
         @pl.when(now == step)
         def _():
             interleave(
-                CHUNK // 8, RES // many, butterflies, product if step < CHUNKS else None
+                STEP // 8, RES // many, butterflies, product if step < STEPS else None
             )
 
 
 def line_kernel(
-    order, tail, lines, gain_re, gain_im, twist, fwd_high, fwd_low, inv_high, inv_low, out, *scratch
+    order, own, tail, lines, gain_re, gain_im, twist, fwd_high, fwd_low, inv_high, inv_low, out, *scratch
 ):
     half = RES * 8
-    at_tail = pl.program_id(0) == pl.num_programs(0) - 1
+    at_end = pl.program_id(0) == pl.num_programs(0) - 1
 
     def line_twist(side):
         def read(k):
@@ -379,22 +399,31 @@
 
     if tail:
 
-        @pl.when(at_tail)
+        @pl.when(at_end)
         def _():
             for block in range(N // 128):
                 lines[block, 8:12, :] = lines[block, 4:8, :]
 
     groups = len(scratch) // 2
-    for group in range(groups):
-        forward(group, scratch[group])
-    for group in range(groups):
-        middle(group, scratch[group], scratch[groups + group])
-    for group in range(groups):
-        inverse(group, scratch[groups + group])
+
+    def run(count):
+        for group in range(count):
+            forward(group, scratch[group])
+        for group in range(count):
+            middle(group, scratch[group], scratch[groups + group])
+        for group in range(count):
+            inverse(group, scratch[groups + group])
+
+    rest = own % groups
+    if rest:
+        pl.when(jnp.logical_not(at_end))(lambda: run(groups))
+        pl.when(at_end)(lambda: run(rest))
+    else:
+        run(groups)
 
     if tail:
 
-        @pl.when(at_tail)
+        @pl.when(at_end)
         def _():
             for block in range(N // 128):
                 out[block, 4:8, :] = out[block, 8:12, :]
@@ -441,11 +470,12 @@
     return root * (1.5 - 0.5 * (value * root) * root)
 
 
-def encode(near_real, near_imag, peak, even_cell):
+def encode(near_real, near_imag, peak_sq, even_cell):
     square = near_real * near_real + near_imag * near_imag
     root = inverse_root(jnp.maximum(square, 1.2e-38))
-    amp_level = (square * root) * (0.8 / peak)
-    unit = jnp.minimum(root, 20.0 / peak)
+    top = inverse_root(peak_sq)
+    amp_level = (square * root) * (0.8 * top)
+    unit = jnp.minimum(root, 20.0 * top)
     rest = 1.0 - amp_level * amp_level
     lift_part = rest * inverse_root(rest)
     level = unit * amp_level
@@ -453,23 +483,40 @@
     return (near_real * level + near_imag * lift, near_imag * level - near_real * lift)
 
 
-def encode_kernel(peak, near, slm_real, slm_imag):
-    rows, width = near.shape[2:]
-    cell = lax.broadcasted_iota(jnp.int32, (rows, width), 0)
-    cell = cell + lax.broadcasted_iota(jnp.int32, (rows, width), 1)
+def encode_kernel(count, *refs):
+    tops, (near, slm_real, slm_imag) = refs[:count], refs[count:]
+    height, width = slm_real.shape[0], near.shape[-1]
+    peak_sq = tops[0][0]
+    for top in tops[1:]:
+        peak_sq = jnp.maximum(peak_sq, top[0])
+    peak_sq = jnp.full((1, width), peak_sq, jnp.float32)
+    rows = pl.ds(pl.multiple_of(pl.program_id(0) * height, height), height)
+    cell = lax.broadcasted_iota(jnp.int32, (height, width), 0)
+    cell = cell + lax.broadcasted_iota(jnp.int32, (height, width), 1)
     for r in range(near.shape[0]):
         lanes = pl.ds(r * width, width)
         slm_real[:, lanes], slm_imag[:, lanes] = encode(
-            near[r, 0], near[r, 1], peak[0], (cell & 1) == 0
+            near[r, 0, rows, :], near[r, 1, rows, :], peak_sq, (cell & 1) == 0
         )
 
 
-def pack_kernel(place, field_real, field_imag, *pieces):
+def pack_kernel(chunk, place, field_real, field_imag, *refs):
+    pieces, sems = refs[:-1], refs[-1]
     width = pieces[0].shape[-1]
-    for j, piece in enumerate(pieces):
+    rows = pl.ds(chunk * CHUNK, CHUNK)
+    copies = []
+    for j in list(range(1, len(pieces))) + [0]:
         lanes = pl.ds(pl.multiple_of((place[0] ^ j) * width, width), width)
-        piece[0, 0] = field_real[:, lanes]
-        piece[1, 0] = field_imag[:, lanes]
+        for part, field in enumerate((field_real, field_imag)):
+            copies.append(
+                pltpu.make_async_copy(
+                    field.at[:, rows, lanes], pieces[j].at[part], sems.at[2 * j + part]
+                )
+            )
+    for copy in copies:
+        copy.start()
+    for copy in copies:
+        copy.wait()
 
 
 def exchange(pieces, axis):
@@ -479,8 +526,8 @@
     ]
 
 
-def params():
-    return pltpu.CompilerParams(vmem_limit_bytes=VMEM)
+def params(mebibytes):
+    return pltpu.CompilerParams(vmem_limit_bytes=mebibytes << 20)
 
 
 def cost(megabytes):
@@ -523,12 +570,10 @@
         in_specs=[whole(pltpu.SMEM)],
         out_specs=[gain_spec, gain_spec],
         out_shape=[gain_shape, gain_shape],
-        compiler_params=params(),
+        compiler_params=params(8),
         name="gain",
     )(place)
 
-    pack_rows = min(height, 256)
-    tall = (row_total, 2, height // INNER, CHUNK, width)
     place_row = lax.axis_index("row").reshape(1).astype(jnp.int32)
     blocks = height // INNER
     piece = (2, blocks, CHUNK, width)
@@ -542,16 +587,19 @@
     for chunk in range(CHUNKS):
         if width == 128:
             pieces = pl.pallas_call(
-                pack_kernel,
-                grid=(blocks,),
-                in_specs=[whole(pltpu.SMEM)]
-                + [pl.BlockSpec((CHUNK, tile_width), lambda i: (i * CHUNKS + chunk, 0))] * 2,
-                out_specs=[pl.BlockSpec((2, 1, CHUNK, width), lambda i: (0, i, 0, 0))] * row_total,
+                partial(pack_kernel, chunk),
+                in_specs=[whole(pltpu.SMEM), anywhere, anywhere],
+                out_specs=[anywhere] * row_total,
                 out_shape=[piece_shape] * row_total,
-                compiler_params=params(),
+                scratch_shapes=[pltpu.SemaphoreType.DMA((2 * row_total,))],
+                compiler_params=params(4),
                 cost_estimate=cost(4),
                 name="pack",
-            )(place_row, field_real, field_imag)
+            )(
+                place_row,
+                field_real.reshape(blocks, INNER, tile_width),
+                field_imag.reshape(blocks, INNER, tile_width),
+            )
         else:
             pieces = [packed[chunk, j] for j in range(row_total)]
         pieces = exchange(pieces, "row")
@@ -560,16 +608,16 @@
         lines = [
             pl.pallas_call(
                 partial(column_forward_kernel, row_total),
-                in_specs=[whole(pltpu.SMEM)] + [whole()] * 2 + [anywhere] * (row_total + len(lines)),
-                out_specs=whole(),
+                in_specs=[whole(pltpu.SMEM)] + [whole()] * (2 + row_total) + [anywhere] * len(lines),
+                out_specs=anywhere,
                 out_shape=jax.ShapeDtypeStruct((RES, total_rows, width), jnp.float32),
                 scratch_shapes=[
-                    pltpu.VMEM((row_total,) + piece, jnp.float32),
+                    pltpu.VMEM((RES, total_rows, width), jnp.float32),
                     slab,
                     slab,
-                    pltpu.SemaphoreType.DMA((row_total + 1,)),
+                    pltpu.SemaphoreType.DMA((2 * RES // many,)),
                 ],
-                compiler_params=params(),
+                compiler_params=params(20),
                 cost_estimate=cost(20),
                 name="column_forward",
             )(place_row, twist_col[rows], fwd_col[chunk], *pieces, *lines)
@@ -589,14 +637,14 @@
     line_grain = pl.BlockSpec((N // 128, 16 * at_once, 128), lambda i: (0, i, 0))
     gain_grain = pl.BlockSpec((at_once, RES * 8, 128), lambda i: (i, 0, 0))
     lines = pl.pallas_call(
-        partial(line_kernel, order, tail),
+        partial(line_kernel, order, own, tail),
         grid=(-(-own // at_once),),
         in_specs=[line_grain, gain_grain, gain_grain] + [whole()] * 5,
         out_specs=line_grain,
         out_shape=jax.ShapeDtypeStruct((N // 128, own_rows, 128), jnp.float32),
         scratch_shapes=[pltpu.VMEM((2 * RES * 8, 2 * INNER), jnp.bfloat16)] * at_once
         + [pltpu.VMEM((RES * 8, 2 * INNER), jnp.float32)] * at_once,
-        compiler_params=params(),
+        compiler_params=params(20),
         name="line",
     )(lines, gain_re, gain_im, twist_line, line_fh, line_fl, line_ih, line_il)
 
@@ -606,27 +654,29 @@
     lines = lax.all_to_all(lines, ("row", "col"), split_axis=0, concat_axis=0, tiled=True)
     lines = lines.reshape(RES, total_rows, width)
 
+    tall = pl.BlockSpec(
+        (row_total, 2, blocks, STEP, width), lambda i: (0, 0, 0, jnp.maximum(i - 1, 0), 0)
+    )
     near, top = pl.pallas_call(
         column_inverse_kernel,
-        grid=(CHUNKS + 1,),
+        grid=(STEPS + 1,),
         in_specs=[
-            whole(),
-            pl.BlockSpec((CHUNK, 128), lambda i: (jnp.maximum(i - 1, 0), 0)),
-            pl.BlockSpec((1,) + inv_col.shape[1:], lambda i: (jnp.minimum(i, CHUNKS - 1), 0, 0)),
+            anywhere,
+            pl.BlockSpec((STEP, 128), lambda i: (jnp.maximum(i - 1, 0), 0)),
+            pl.BlockSpec((1,) + inv_col.shape[1:], lambda i: (jnp.minimum(i, STEPS - 1), 0, 0)),
         ],
-        out_specs=[
-            pl.BlockSpec(tall, lambda i: (0, 0, 0, jnp.maximum(i - 1, 0), 0)),
-            whole(),
-        ],
+        out_specs=[tall, whole()],
         out_shape=[
             jax.ShapeDtypeStruct((row_total, 2, blocks, INNER, width), jnp.float32),
             jax.ShapeDtypeStruct((8, width), jnp.float32),
         ],
         scratch_shapes=[
+            pltpu.VMEM((RES, total_rows, width), jnp.float32),
             pltpu.VMEM((RES // many, inv_col.shape[2], many * width), jnp.bfloat16),
-            pltpu.VMEM((2, RES, 2 * CHUNK, width), jnp.float32),
+            pltpu.VMEM((2, RES, 2 * STEP, width), jnp.float32),
+            pltpu.SemaphoreType.DMA((RES // many,)),
         ],
-        compiler_params=params(),
+        compiler_params=params(24),
         name="column_inverse",
     )(lines, twist_col, inv_col)
 
@@ -638,27 +688,23 @@
         partner = [(i, i ^ shift) for i in range(col_total)]
         peak = jnp.maximum(peak, lax.ppermute(peak, "col", partner))
         shift *= 2
-    for item in exchange([peak] * row_total, "row")[1:]:
-        peak = jnp.maximum(peak, item)
-    peak = jnp.sqrt(peak)
+    tops = exchange([peak] * row_total, "row")
     if width != 128:
         near = near.transpose(1, 2, 0, 3).reshape(2, height, tile_width)
         even_cell = (jnp.arange(height)[:, None] + jnp.arange(tile_width)[None, :]) % 2 == 0
-        return encode(near[0], near[1], peak, even_cell)
-    tile_spec = pl.BlockSpec((pack_rows, tile_width), lambda i: (i, 0))
+        return encode(near[0], near[1], jnp.max(jnp.stack(tops)), even_cell)
+    tile_rows = min(height, 128)
+    tile_spec = pl.BlockSpec((tile_rows, tile_width), lambda i: (i, 0))
     tile_shape = jax.ShapeDtypeStruct((height, tile_width), jnp.float32)
     return pl.pallas_call(
-        encode_kernel,
-        grid=(height // pack_rows,),
-        in_specs=[
-            whole(pltpu.SMEM),
-            pl.BlockSpec((row_total, 2, pack_rows, width), lambda i: (0, 0, i, 0)),
-        ],
+        partial(encode_kernel, row_total),
+        grid=(height // tile_rows,),
+        in_specs=[whole(pltpu.SMEM)] * row_total + [whole()],
         out_specs=[tile_spec, tile_spec],
         out_shape=[tile_shape, tile_shape],
-        compiler_params=params(),
+        compiler_params=params(12),
         name="encode",
-    )(peak.reshape(1), near)
+    )(*[top.reshape(1) for top in tops], near)
 
 
 def solution(mesh):

time: 297 us -> 295 us (level)
  Pallas kernels: 66.8 us -> 52.9 us
  waiting for transfers between devices: 88.9 us -> 97.6 us
  local copies, waits for them, and re-layouts: 3.56 us -> 12.1 us
    unnamed x16 -> x36, local copies, waits for them, and re-layouts: 3.56 us -> 12.1 us
    ppermute x9, waiting for transfers between devices: 25.6 us -> 32.8 us  [exchange(): lax.ppermute(pieces[j], axis, [(i, i ^ j) for i in range(total)])]
    pallas_call x5, Pallas kernels: 40.9 us -> 34.6 us  [the longest x1 13.5 us: body(): pl.pallas_call(column_inverse_kernel, grid=(STEPS + 1,), in_specs=[anywhe...]
    pallas_call x2, Pallas kernels: 19.2 us -> 14.3 us  [body(): pl.pallas_call(partial(column_forward_kernel, row_total), in_specs=[whole...]
  transfers between devices with their start and end apart: 14 -> 14, of which waited for: 8 -> 9; matrix products, arithmetic and copies ran while one was open for 0% -> 0% of each run, Pallas kernels for 7% -> 4%
where the time goes in v6:
time: 295 us
  waiting for transfers between devices  97.6 us (33%)
  blocking collectives  66.1 us (22%)
  starting transfers between devices  62 us (21%)
  Pallas kernels  52.9 us (18%)
  local copies, waits for them, and re-layouts  12.1 us (4%)
  between operations  3.33 us (1%)
    all_to_all x1, blocking collectives, body(): lax.all_to_all(lines, ('row', 'col'), split_axis=0, concat_axis=0, tiled=...  66.1 us
    all_to_all x1, waiting for transfers between devices, body(): lax.all_to_all(lines, ('row', 'col'), split_axis=0, concat_axis=0, tiled=...  57.9 us
    ppermute x9, starting transfers between devices, exchange(): lax.ppermute(pieces[j], axis, [(i, i ^ j) for i in range(total)])  49.5 us
    ppermute x9, waiting for transfers between devices, exchange(): lax.ppermute(pieces[j], axis, [(i, i ^ j) for i in range(total)])  32.8 us
    pallas_call x2, Pallas kernels, body(): pl.pallas_call(partial(column_forward_kernel, row_total), in_specs=[whole...  14.3 us
    pallas_call x1, Pallas kernels, body(): pl.pallas_call(column_inverse_kernel, grid=(STEPS + 1,), in_specs=[anywhe...  13.5 us
    unnamed x36, local copies, waits for them, and re-layouts  12.1 us
    pallas_call x1, Pallas kernels, body(): pl.pallas_call(partial(line_kernel, order, own, tail), grid=(-(-own // at...  11.7 us
  transfers between devices with their start and end apart: 14, of which 9 were waited for; matrix products, arithmetic and copies ran while one was open for 0% of the time, Pallas kernels for 4%

profile of v6, /device:TPU:0, one launch (start us, length us, event | category | flops | bytes accessed | tf_op | source)
XLA Modules:
  0.0 294.7 jit_solution(16752292897483716817)
XLA Ops:
  0.6 0.0 copy-start
  0.6 1.6 copy-done
  2.2 1.6 copy-done.1
  3.8 0.4 pack.3
  4.2 0.0 copy-start.14
  4.2 0.0 copy-start.17
  4.2 3.0 %collective-permute-start.3 = (f32[2,4,128,128]{3,2,1,0:T(8,128)S(1)}, f32[2,4,128,128]{3,2,1,0:T(8,128)S(1)}, u32[]{:S(2)}, u32[]{:S(2)}) collective-permute-start(f32[2,4,128,128]{3,2,1,0:T(8,128)S(1)} %get-tuple-element.19), channel_id=1, source_target_pairs={{0,8},{8,0},{16,24},{24,16},{1,9},{9,1},{17,25},{25,17},{2,10},{10... | collective-permute-start | bytes 1572872 | tf_op jit(solution)/shard_map/ppermute | solution.py:525
  7.2 1.5 collective-permute-start.4
  8.7 0.0 collective-permute-start.5
  8.8 0.4 pack.2
  9.1 0.0 copy-start.13
  9.2 0.0 copy-start.16
  9.2 2.0 collective-permute-start
  11.2 1.5 collective-permute-start.1
  12.7 7.3 %collective-permute-done.3.refs_1_ = f32[2,4,128,128]{3,2,1,0:T(8,128)S(1)} collective-permute-done((f32[2,4,128,128]{3,2,1,0:T(8,128)S(1)}, f32[2,4,128,128]{3,2,1,0:T(8,128)S(1)}, u32[]{:S(2)}, u32[]{:S(2)}) %collective-permute-start.3) | collective-permute-done | bytes 524320 | tf_op jit(solution)/shard_map/ppermute | solution.py:525
  20.0 3.0 %collective-permute-start.2 = (f32[2,4,128,128]{3,2,1,0:T(8,128)S(1)}, f32[2,4,128,128]{3,2,1,0:T(8,128)S(1)}, u32[]{:S(2)}, u32[]{:S(2)}) collective-permute-start(f32[2,4,128,128]{3,2,1,0:T(8,128)S(1)} %get-tuple-element.17), channel_id=1, source_target_pairs={{0,24},{8,16},{16,8},{24,0},{1,25},{9,17},{17,9},{25,1},{2,26},{10... | collective-permute-start | bytes 1572872 | tf_op jit(solution)/shard_map/ppermute | solution.py:525
  23.0 10.3 %collective-permute-done.4.refs_2_ = f32[2,4,128,128]{3,2,1,0:T(8,128)S(1)} collective-permute-done((f32[2,4,128,128]{3,2,1,0:T(8,128)S(1)}, f32[2,4,128,128]{3,2,1,0:T(8,128)S(1)}, u32[]{:S(2)}, u32[]{:S(2)}) %collective-permute-start.4) | collective-permute-done | bytes 524320 | tf_op jit(solution)/shard_map/ppermute | solution.py:525
  33.3 0.0 collective-permute-done.5.refs_3_
  33.3 0.0 copy-done.14
  33.3 0.0 copy-done.17
  33.3 6.7 %column_forward.2.refs_4_ = f32[32,168,128]{2,1,0:T(8,128)S(1)} custom-call(s32[1]{0:T(128)} %bitcast.place, f32[128,128]{1,0:T(8,128)S(1)} %copy-done.17, bf16[336,256]{1,0:T(8,128)(2,1)S(1)} %copy-done.14, f32[2,4,128,128]{3,2,1,0:T(8,128)S(1)} %get-tuple-element.18.refs_0_, f32[2,4,128,128]{3,2,1,0:T(8,128)S(1)} %collective-permute-done.3.refs_1_, ...), custom_call_target="tpu_custom_call" | custom-call | bytes 20971520 | tf_op jit(solution)/shard_map/column_forward/pallas_call | solution.py:609
  40.0 2.5 collective-permute-done.refs_1_
  42.5 11.8 %collective-permute-done.1.refs_2_ = f32[2,4,128,128]{3,2,1,0:T(8,128)S(1)} collective-permute-done((f32[2,4,128,128]{3,2,1,0:T(8,128)S(1)}, f32[2,4,128,128]{3,2,1,0:T(8,128)S(1)}, u32[]{:S(2)}, u32[]{:S(2)}) %collective-permute-start.1) | collective-permute-done | bytes 524320 | tf_op jit(solution)/shard_map/ppermute | solution.py:525
  54.3 0.0 collective-permute-done.2.refs_3_
  54.3 0.0 copy-done.13
  54.3 0.0 copy-done.16
  54.3 7.6 %column_forward.3 = f32[32,168,128]{2,1,0:T(8,128)} custom-call(s32[1]{0:T(128)} %bitcast.place, f32[128,128]{1,0:T(8,128)S(1)} %copy-done.16, bf16[336,256]{1,0:T(8,128)(2,1)S(1)} %copy-done.13, f32[2,4,128,128]{3,2,1,0:T(8,128)S(1)} %get-tuple-element.14.refs_0_, f32[2,4,128,128]{3,2,1,0:T(8,128)S(1)} %collective-permute-done.refs_1_, ...), custom_call_target="tpu_custom_call" | custom-call | bytes 20971520 | tf_op jit(solution)/shard_map/column_forward/pallas_call | solution.py:609
  61.9 0.0 copy-start.8
  62.0 0.0 copy-start.9
  62.0 0.0 copy-start.10
  62.0 4.9 %all-to-all-start = ((f32[32,168,128]{2,1,0:T(8,128)}), f32[32,168,128]{2,1,0:T(8,128)S(1)}, u32[]{:S(2)}, u32[]{:S(2)}) async-start(f32[32,168,128]{2,1,0:T(8,128)} %column_forward.3), calls=%async_computation | async-start | bytes 5505024 | tf_op jit(solution)/shard_map/all_to_all | solution.py:628
  66.9 0.1 pad_add_fusion.place
  67.0 4.0 %gain.1 = (f32[11,256,128]{2,1,0:T(8,128)S(1)}, f32[11,256,128]{2,1,0:T(8,128)S(1)}) custom-call(s32[2]{0:T(128)S(1)} %pad_add_fusion.place), custom_call_target="tpu_custom_call" | custom-call | tf_op jit(solution)/shard_map/gain/pallas_call | solution.py:567
  71.0 0.0 copy-start.3
  71.0 1.1 copy-done.3
  72.1 1.1 copy-done.5
  73.2 57.9 %all-to-all-done.lines = f32[32,168,128]{2,1,0:T(8,128)S(1)} async-done(((f32[32,168,128]{2,1,0:T(8,128)}), f32[32,168,128]{2,1,0:T(8,128)S(1)}, u32[]{:S(2)}, u32[]{:S(2)}) %all-to-all-start) | async-done | bytes 2752544 | tf_op jit(solution)/shard_map/all_to_all | solution.py:628
  131.1 0.0 copy-done.8
  131.1 0.0 copy-done.9
  131.1 1.4 copy-done.4
  132.5 1.4 copy-done.6
  133.9 0.9 copy-done.11
  134.8 0.9 copy-done.12
  135.8 11.7 %line.1 = f32[32,168,128]{2,1,0:T(8,128)S(1)} custom-call(f32[32,168,128]{2,1,0:T(8,128)S(1)} %all-to-all-done.lines, f32[11,256,128]{2,1,0:T(8,128)S(1)} %copy-done.4, f32[11,256,128]{2,1,0:T(8,128)S(1)} %copy-done.6, f32[2,17,8,256]{3,2,1,0:T(8,128)S(1)} %copy-done.8, bf16[512,256]{1,0:T(8,128)(2,1)S(1)} %copy-done.12, bf16[512,256]{1,0:T(8,128)(2,1)S(1)} %copy-done.11, ...), custom_call_target="tpu_custom_call" | custom-call | tf_op jit(solution)/shard_map/line/pallas_call | solution.py:639
  147.4 0.0 copy-start.7
  147.4 0.0 copy-start.15
  147.4 66.1 %all_to_all.15.source = f32[32,168,128]{2,1,0:T(8,128)S(1)} all-to-all(f32[32,168,128]{2,1,0:T(8,128)S(1)} %line.1), channel_id=1, replica_groups=mesh['row'=4,'col'=8] {'row','col'}, dimensions={0} | all-to-all | bytes 5505024 | tf_op jit(solution)/shard_map/all_to_all | solution.py:654
  213.5 0.0 copy-done.15
  213.5 13.5 %column_inverse.1 = (f32[4,2,4,256,128]{4,3,2,1,0:T(8,128)S(1)}, f32[8,128]{1,0:T(8,128)S(1)}) custom-call(f32[32,168,128]{2,1,0:T(8,128)S(1)} %all_to_all.15.source, f32[256,128]{1,0:T(8,128)S(1)} %copy-done.15, bf16[4,128,512]{2,1,0:T(8,128)(2,1)S(1)} %copy-done.7), custom_call_target="tpu_custom_call" | custom-call | tf_op jit(solution)/shard_map/column_inverse/pallas_call | solution.py:660
  227.1 2.0 copy-done.2
  229.1 4.8 %all-to-all-start.2 = ((f32[4,2,1024,128]{3,2,1,0:T(8,128)}), f32[4,2,1024,128]{3,2,1,0:T(8,128)}, u32[]{:S(2)}, u32[]{:S(2)}) async-start(f32[4,2,1024,128]{3,2,1,0:T(8,128)} %bitcast.13), calls=%async_computation.2 | async-start | bytes 8388608 | tf_op jit(solution)/shard_map/all_to_all | solution.py:684
  234.0 0.6 reduce_max.9
  234.6 0.0 collective-permute-start.6
  234.6 1.4 collective-permute-done.6
  237.2 1.4 collective-permute-start.7
  238.6 2.3 collective-permute-done.7
  241.6 1.4 collective-permute-start.8
  243.0 3.2 %collective-permute-done.8 = f32[]{:T(128)} collective-permute-done((f32[]{:T(128)}, f32[]{:T(128)}, u32[]{:S(2)}, u32[]{:S(2)}) %collective-permute-start.8) | collective-permute-done | bytes 36 | tf_op jit(solution)/shard_map/ppermute | solution.py:689
  246.7 32.6 %collective-permute-start.11 = (f32[]{:T(128)}, f32[]{:T(128)}, u32[]{:S(2)}, u32[]{:S(2)}) collective-permute-start(f32[]{:T(128)} %max.11), channel_id=1, source_target_pairs={{0,24},{8,16},{16,8},{24,0},{1,25},{9,17},{17,9},{25,1},{2,26},{10... | collective-permute-start | bytes 20 | tf_op jit(solution)/shard_map/ppermute | solution.py:525
  279.4 3.0 %collective-permute-start.10 = (f32[]{:T(128)}, f32[]{:T(128)}, u32[]{:S(2)}, u32[]{:S(2)}) collective-permute-start(f32[]{:T(128)} %max.11), channel_id=1, source_target_pairs={{0,16},{8,24},{16,0},{24,8},{1,17},{9,25},{17,1},{25,9},{2,18},{10... | collective-permute-start | bytes 20 | tf_op jit(solution)/shard_map/ppermute | solution.py:525
  282.4 2.8 collective-permute-start.9
  285.2 0.8 collective-permute-done.9
  286.0 0.0 all-to-all-done.2.refs_4_
  286.0 8.7 %encode.1 = (f32[1024,512]{1,0:T(8,128)}, f32[1024,512]{1,0:T(8,128)}) custom-call(f32[1]{0:T(128)} %bitcast.4.refs_0_, f32[1]{0:T(128)} %bitcast.5.refs_1_, f32[1]{0:T(128)} %bitcast.6.refs_2_, f32[1]{0:T(128)} %bitcast.7.refs_3_, f32[4,2,1024,128]{3,2,1,0:T(8,128)} %all-to-all-done.2.refs_4_), custom_call_target="tpu_custom_call" | custom-call | tf_op jit(solution)/shard_map/encode/pallas_call | solution.py:699
  (11 shorter events, 0.0 us)
Async XLA Ops:
  0.6 1.6 copy-start
  2.2 1.6 copy-start.1
  4.2 29.1 %copy-start.14 = (bf16[336,256]{1,0:T(8,128)(2,1)S(1)}, bf16[336,256]{1,0:T(8,128)(2,1)}, u32[]{:S(2)}) copy-start(bf16[336,256]{1,0:T(8,128)(2,1)} %constant.63.clone.matrix) | copy-start | bytes 516100
  4.2 29.1 %copy-start.17 = (f32[128,128]{1,0:T(8,128)S(1)}, f32[128,128]{1,0:T(8,128)}, u32[]{:S(2)}) copy-start(f32[128,128]{1,0:T(8,128)} %constant.62.clone.twist) | copy-start | bytes 196612
  4.2 15.8 %collective-permute-start.3 = (f32[2,4,128,128]{3,2,1,0:T(8,128)S(1)}, f32[2,4,128,128]{3,2,1,0:T(8,128)S(1)}, u32[]{:S(2)}, u32[]{:S(2)}) collective-permute-start(f32[2,4,128,128]{3,2,1,0:T(8,128)S(1)} %get-tuple-element.19), channel_id=1, source_target_pairs={{0,8},{8,0},{16,24},{24,16},{1,9},{9,1},{17,25},{25,17},{2,10},{10... | collective-permute-start | bytes 1572872 | tf_op jit(solution)/shard_map/ppermute | solution.py:525
  7.2 26.1 %collective-permute-start.4 = (f32[2,4,128,128]{3,2,1,0:T(8,128)S(1)}, f32[2,4,128,128]{3,2,1,0:T(8,128)S(1)}, u32[]{:S(2)}, u32[]{:S(2)}) collective-permute-start(f32[2,4,128,128]{3,2,1,0:T(8,128)S(1)} %get-tuple-element.20), channel_id=1, source_target_pairs={{0,16},{8,24},{16,0},{24,8},{1,17},{9,25},{17,1},{25,9},{2,18},{10... | collective-permute-start | bytes 1572872 | tf_op jit(solution)/shard_map/ppermute | solution.py:525
  8.7 24.6 %collective-permute-start.5 = (f32[2,4,128,128]{3,2,1,0:T(8,128)S(1)}, f32[2,4,128,128]{3,2,1,0:T(8,128)S(1)}, u32[]{:S(2)}, u32[]{:S(2)}) collective-permute-start(f32[2,4,128,128]{3,2,1,0:T(8,128)S(1)} %get-tuple-element.21), channel_id=1, source_target_pairs={{0,24},{8,16},{16,8},{24,0},{1,25},{9,17},{17,9},{25,1},{2,26},{10... | collective-permute-start | bytes 1572872 | tf_op jit(solution)/shard_map/ppermute | solution.py:525
  9.1 45.2 %copy-start.13 = (bf16[336,256]{1,0:T(8,128)(2,1)S(1)}, bf16[336,256]{1,0:T(8,128)(2,1)}, u32[]{:S(2)}) copy-start(bf16[336,256]{1,0:T(8,128)(2,1)} %constant.65.clone.matrix) | copy-start | bytes 516100
  9.2 45.2 %copy-start.16 = (f32[128,128]{1,0:T(8,128)S(1)}, f32[128,128]{1,0:T(8,128)}, u32[]{:S(2)}) copy-start(f32[128,128]{1,0:T(8,128)} %constant.64.clone.twist) | copy-start | bytes 196612
  9.2 33.3 %collective-permute-start = (f32[2,4,128,128]{3,2,1,0:T(8,128)S(1)}, f32[2,4,128,128]{3,2,1,0:T(8,128)S(1)}, u32[]{:S(2)}, u32[]{:S(2)}) collective-permute-start(f32[2,4,128,128]{3,2,1,0:T(8,128)S(1)} %get-tuple-element.15), channel_id=1, source_target_pairs={{0,8},{8,0},{16,24},{24,16},{1,9},{9,1},{17,25},{25,17},{2,10},{10... | collective-permute-start | bytes 1572872 | tf_op jit(solution)/shard_map/ppermute | solution.py:525
  11.2 43.1 %collective-permute-start.1 = (f32[2,4,128,128]{3,2,1,0:T(8,128)S(1)}, f32[2,4,128,128]{3,2,1,0:T(8,128)S(1)}, u32[]{:S(2)}, u32[]{:S(2)}) collective-permute-start(f32[2,4,128,128]{3,2,1,0:T(8,128)S(1)} %get-tuple-element.16), channel_id=1, source_target_pairs={{0,16},{8,24},{16,0},{24,8},{1,17},{9,25},{17,1},{25,9},{2,18},{10... | collective-permute-start | bytes 1572872 | tf_op jit(solution)/shard_map/ppermute | solution.py:525
  20.0 34.3 %collective-permute-start.2 = (f32[2,4,128,128]{3,2,1,0:T(8,128)S(1)}, f32[2,4,128,128]{3,2,1,0:T(8,128)S(1)}, u32[]{:S(2)}, u32[]{:S(2)}) collective-permute-start(f32[2,4,128,128]{3,2,1,0:T(8,128)S(1)} %get-tuple-element.17), channel_id=1, source_target_pairs={{0,24},{8,16},{16,8},{24,0},{1,25},{9,17},{17,9},{25,1},{2,26},{10... | collective-permute-start | bytes 1572872 | tf_op jit(solution)/shard_map/ppermute | solution.py:525
  61.9 69.2 %copy-start.8 = (f32[2,17,8,256]{3,2,1,0:T(8,128)S(1)}, f32[2,17,8,256]{3,2,1,0:T(8,128)}, u32[]{:S(2)}) copy-start(f32[2,17,8,256]{3,2,1,0:T(8,128)} %constant.66.clone.twist) | copy-start | bytes 835588
  62.0 69.2 %copy-start.9 = (bf16[256,512]{1,0:T(8,128)(2,1)S(1)}, bf16[256,512]{1,0:T(8,128)(2,1)}, u32[]{:S(2)}) copy-start(bf16[256,512]{1,0:T(8,128)(2,1)} %constant.70.clone.inv_low) | copy-start | bytes 786436
  62.0 69.2 %copy-start.10 = (bf16[256,512]{1,0:T(8,128)(2,1)S(1)}, bf16[256,512]{1,0:T(8,128)(2,1)}, u32[]{:S(2)}) copy-start(bf16[256,512]{1,0:T(8,128)(2,1)} %constant.69.clone.inv_high) | copy-start | bytes 786436
  62.0 69.1 %all-to-all-start = ((f32[32,168,128]{2,1,0:T(8,128)}), f32[32,168,128]{2,1,0:T(8,128)S(1)}, u32[]{:S(2)}, u32[]{:S(2)}) async-start(f32[32,168,128]{2,1,0:T(8,128)} %column_forward.3), calls=%async_computation | async-start | bytes 5505024 | tf_op jit(solution)/shard_map/all_to_all | solution.py:628
  71.0 1.1 copy-start.3
  72.1 1.1 copy-start.5
  131.1 1.4 copy-start.4
  132.5 1.4 copy-start.6
  133.8 0.9 copy-start.11
  134.8 0.9 copy-start.12
  147.4 66.1 %copy-start.7 = (bf16[4,128,512]{2,1,0:T(8,128)(2,1)S(1)}, bf16[4,128,512]{2,1,0:T(8,128)(2,1)}, u32[]{:S(2)}) copy-start(bf16[4,128,512]{2,1,0:T(8,128)(2,1)} %constant.72.clone.matrix) | copy-start | bytes 1572868
  147.4 66.1 %copy-start.15 = (f32[256,128]{1,0:T(8,128)S(1)}, f32[256,128]{1,0:T(8,128)}, u32[]{:S(2)}) copy-start(f32[256,128]{1,0:T(8,128)} %constant.71.clone.twist) | copy-start | bytes 393220
  227.1 2.0 copy-start.2
  229.1 56.9 %all-to-all-start.2 = ((f32[4,2,1024,128]{3,2,1,0:T(8,128)}), f32[4,2,1024,128]{3,2,1,0:T(8,128)}, u32[]{:S(2)}, u32[]{:S(2)}) async-start(f32[4,2,1024,128]{3,2,1,0:T(8,128)} %bitcast.13), calls=%async_computation.2 | async-start | bytes 8388608 | tf_op jit(solution)/shard_map/all_to_all | solution.py:684
  234.6 1.4 collective-permute-start.6
  237.2 3.7 %collective-permute-start.7 = (f32[]{:T(128)}, f32[]{:T(128)}, u32[]{:S(2)}, u32[]{:S(2)}) collective-permute-start(f32[]{:T(128)} %max.9), channel_id=1, source_target_pairs={{0,2},{1,3},{2,0},{3,1},{4,6},{5,7},{6,4},{7,5},{8,10},{9,11},{10,... | collective-permute-start | bytes 20 | tf_op jit(solution)/shard_map/ppermute | solution.py:689
  241.6 4.6 %collective-permute-start.8 = (f32[]{:T(128)}, f32[]{:T(128)}, u32[]{:S(2)}, u32[]{:S(2)}) collective-permute-start(f32[]{:T(128)} %max.10), channel_id=1, source_target_pairs={{0,4},{1,5},{2,6},{3,7},{4,0},{5,1},{6,2},{7,3},{8,12},{9,13},{10,... | collective-permute-start | bytes 20 | tf_op jit(solution)/shard_map/ppermute | solution.py:689
  246.7 38.4 %collective-permute-start.11 = (f32[]{:T(128)}, f32[]{:T(128)}, u32[]{:S(2)}, u32[]{:S(2)}) collective-permute-start(f32[]{:T(128)} %max.11), channel_id=1, source_target_pairs={{0,24},{8,16},{16,8},{24,0},{1,25},{9,17},{17,9},{25,1},{2,26},{10... | collective-permute-start | bytes 20 | tf_op jit(solution)/shard_map/ppermute | solution.py:525
  279.4 5.8 %collective-permute-start.10 = (f32[]{:T(128)}, f32[]{:T(128)}, u32[]{:S(2)}, u32[]{:S(2)}) collective-permute-start(f32[]{:T(128)} %max.11), channel_id=1, source_target_pairs={{0,16},{8,24},{16,0},{24,8},{1,17},{9,25},{17,1},{25,9},{2,18},{10... | collective-permute-start | bytes 20 | tf_op jit(solution)/shard_map/ppermute | solution.py:525
  282.4 3.6 %collective-permute-start.9 = (f32[]{:T(128)}, f32[]{:T(128)}, u32[]{:S(2)}, u32[]{:S(2)}) collective-permute-start(f32[]{:T(128)} %max.11), channel_id=1, source_target_pairs={{0,8},{8,0},{16,24},{24,16},{1,9},{9,1},{17,25},{25,17},{2,10},{10... | collective-permute-start | bytes 20 | tf_op jit(solution)/shard_map/ppermute | solution.py:525

commit v7 on v6

--- a/solution.py
+++ b/solution.py
@@ -20,7 +20,7 @@
 HALF = 40
 CHUNKS = 2
 CHUNK = INNER // CHUNKS
-STEPS = 4
+STEPS = 2
 STEP = INNER // STEPS
 
 
@@ -255,19 +255,6 @@
         copy_out(p).wait()
 
 
-def interleave(tiles, products, butterflies, product):
-    steps = min(tiles, products)
-
-    @pl.loop(0, steps)
-    def _(t):
-        if product is not None:
-            for part in range(products // steps):
-                product(t * (products // steps) + part)
-        if butterflies is not None:
-            for part in range(tiles // steps):
-                butterflies(t * (tiles // steps) + part)
-
-
 def column_inverse_kernel(source, twist, matrix, out, top, lines, deep, back, sems):
     width = lines.shape[-1]
     rows_in = lines.shape[1]
@@ -279,9 +266,8 @@
         part = pl.ds(p * many, many)
         return pltpu.make_async_copy(source.at[part], lines.at[part], sems.at[p])
 
-    def product(p):
+    def product(p, slot):
         done = dot16(matrix[0], deep[p])
-        slot = now % 2
         for part in range(many):
             back[slot, p * many + part] = done[:, part * width : (part + 1) * width]
 
@@ -294,11 +280,10 @@
         if deep.shape[1] > 3 * rows_in:
             parts.append(jnp.zeros((deep.shape[1] - 3 * rows_in, many * width), jnp.float32))
         deep[p] = jnp.concatenate(parts, axis=0).astype(jnp.bfloat16)
-        product(p)
-
-    def butterflies(t):
+        product(p, 0)
+
+    def butterflies(t, slot):
         q0 = pl.multiple_of(t * 8, 8)
-        slot = (now + 1) % 2
         largest = []
 
         def get(u):
@@ -328,9 +313,16 @@
 
         @pl.when(now == step)
         def _():
-            interleave(
-                STEP // 8, RES // many, butterflies, product if step < STEPS else None
-            )
+            tiles, products = STEP // 8, RES // many
+            steps = min(tiles, products)
+
+            @pl.loop(0, steps)
+            def _(t):
+                for part in range(tiles // steps):
+                    butterflies(t * (tiles // steps) + part, (step - 1) % 2)
+                if step < STEPS:
+                    for part in range(products // steps):
+                        product(t * (products // steps) + part, step % 2)
 
 
 def line_kernel(
@@ -346,8 +338,8 @@
 
         return read
 
-    def forward(group, stacked):
-        for side in range(2):
+    def forward(group, stacked, sides=(0, 1)):
+        for side in sides:
             waiting = {}
 
             def get(m):
@@ -371,18 +363,20 @@
 
             forward_slabs(get, put)
 
-    def middle(group, stacked, back):
+    def filtered(group, stacked):
         spec = three_right(stacked[...], half, fwd_high[...], fwd_low[...])
         spec_re, spec_im = spec[:, :128], spec[:, 128:]
         g_re, g_im = gain_re[group], gain_im[group]
         mixed = jnp.concatenate(
             [spec_re * g_re - spec_im * g_im, spec_re * g_im + spec_im * g_re], axis=1
         )
-        mixed = jnp.concatenate(high_low(mixed), axis=0)
+        return jnp.concatenate(high_low(mixed), axis=0)
+
+    def unfold(mixed, back):
         back[...] = three_right(mixed, half, inv_high[...], inv_low[...])
 
-    def inverse(group, back):
-        for side in range(2):
+    def inverse(group, back, sides=(0, 1)):
+        for side in sides:
 
             def get(u):
                 rows = pl.ds((u % (RES // 2)) * 16 + (u // (RES // 2)) * 8, 8)
@@ -406,13 +400,22 @@
 
     groups = len(scratch) // 2
 
+    stacked, back = scratch[:groups], scratch[groups:]
+
     def run(count):
+        forward(0, stacked[0])
         for group in range(count):
-            forward(group, scratch[group])
-        for group in range(count):
-            middle(group, scratch[group], scratch[groups + group])
-        for group in range(count):
-            inverse(group, scratch[groups + group])
+            mixed = filtered(group, stacked[group])
+            if group + 1 < count:
+                forward(group + 1, stacked[group + 1], (0,))
+            if group > 0:
+                inverse(group - 1, back[group - 1], (0,))
+            unfold(mixed, back[group])
+            if group + 1 < count:
+                forward(group + 1, stacked[group + 1], (1,))
+            if group > 0:
+                inverse(group - 1, back[group - 1], (1,))
+        inverse(count - 1, back[count - 1])
 
     rest = own % groups
     if rest:
@@ -465,21 +468,15 @@
         gain_im[0, at : at + 8, :] = total * sin_part
 
 
-def inverse_root(value):
-    root = lax.rsqrt(value)
-    return root * (1.5 - 0.5 * (value * root) * root)
-
-
-def encode(near_real, near_imag, peak_sq, even_cell):
+def encode(near_real, near_imag, peak_sq, cell_sign):
     square = near_real * near_real + near_imag * near_imag
-    root = inverse_root(jnp.maximum(square, 1.2e-38))
-    top = inverse_root(peak_sq)
+    root = lax.rsqrt(jnp.maximum(square, 1.2e-38))
+    top = lax.rsqrt(peak_sq)
     amp_level = (square * root) * (0.8 * top)
     unit = jnp.minimum(root, 20.0 * top)
     rest = 1.0 - amp_level * amp_level
-    lift_part = rest * inverse_root(rest)
     level = unit * amp_level
-    lift = jnp.where(even_cell, unit * lift_part, -(unit * lift_part))
+    lift = (rest * lax.rsqrt(rest)) * (unit * cell_sign)
     return (near_real * level + near_imag * lift, near_imag * level - near_real * lift)
 
 
@@ -490,14 +487,12 @@
     for top in tops[1:]:
         peak_sq = jnp.maximum(peak_sq, top[0])
     peak_sq = jnp.full((1, width), peak_sq, jnp.float32)
-    rows = pl.ds(pl.multiple_of(pl.program_id(0) * height, height), height)
     cell = lax.broadcasted_iota(jnp.int32, (height, width), 0)
     cell = cell + lax.broadcasted_iota(jnp.int32, (height, width), 1)
+    cell_sign = (1 - 2 * (cell & 1)).astype(jnp.float32)
     for r in range(near.shape[0]):
         lanes = pl.ds(r * width, width)
-        slm_real[:, lanes], slm_imag[:, lanes] = encode(
-            near[r, 0, rows, :], near[r, 1, rows, :], peak_sq, (cell & 1) == 0
-        )
+        slm_real[:, lanes], slm_imag[:, lanes] = encode(near[r, 0], near[r, 1], peak_sq, cell_sign)
 
 
 def pack_kernel(chunk, place, field_real, field_imag, *refs):
@@ -570,7 +565,7 @@
         in_specs=[whole(pltpu.SMEM)],
         out_specs=[gain_spec, gain_spec],
         out_shape=[gain_shape, gain_shape],
-        compiler_params=params(8),
+        compiler_params=params(56),
         name="gain",
     )(place)
 
@@ -592,7 +587,7 @@
                 out_specs=[anywhere] * row_total,
                 out_shape=[piece_shape] * row_total,
                 scratch_shapes=[pltpu.SemaphoreType.DMA((2 * row_total,))],
-                compiler_params=params(4),
+                compiler_params=params(56),
                 cost_estimate=cost(4),
                 name="pack",
             )(
@@ -644,7 +639,7 @@
         out_shape=jax.ShapeDtypeStruct((N // 128, own_rows, 128), jnp.float32),
         scratch_shapes=[pltpu.VMEM((2 * RES * 8, 2 * INNER), jnp.bfloat16)] * at_once
         + [pltpu.VMEM((RES * 8, 2 * INNER), jnp.float32)] * at_once,
-        compiler_params=params(20),
+        compiler_params=params(52),
         name="line",
     )(lines, gain_re, gain_im, twist_line, line_fh, line_fl, line_ih, line_il)
 
@@ -676,7 +671,7 @@
             pltpu.VMEM((2, RES, 2 * STEP, width), jnp.float32),
             pltpu.SemaphoreType.DMA((RES // many,)),
         ],
-        compiler_params=params(24),
+        compiler_params=params(56),
         name="column_inverse",
     )(lines, twist_col, inv_col)
 
@@ -691,18 +686,20 @@
     tops = exchange([peak] * row_total, "row")
     if width != 128:
         near = near.transpose(1, 2, 0, 3).reshape(2, height, tile_width)
-        even_cell = (jnp.arange(height)[:, None] + jnp.arange(tile_width)[None, :]) % 2 == 0
-        return encode(near[0], near[1], jnp.max(jnp.stack(tops)), even_cell)
+        odd_cell = (jnp.arange(height)[:, None] + jnp.arange(tile_width)[None, :]) % 2
+        cell_sign = (1 - 2 * odd_cell).astype(jnp.float32)
+        return encode(near[0], near[1], jnp.max(jnp.stack(tops)), cell_sign)
     tile_rows = min(height, 128)
     tile_spec = pl.BlockSpec((tile_rows, tile_width), lambda i: (i, 0))
     tile_shape = jax.ShapeDtypeStruct((height, tile_width), jnp.float32)
     return pl.pallas_call(
         partial(encode_kernel, row_total),
         grid=(height // tile_rows,),
-        in_specs=[whole(pltpu.SMEM)] * row_total + [whole()],
+        in_specs=[whole(pltpu.SMEM)] * row_total
+        + [pl.BlockSpec((row_total, 2, tile_rows, width), lambda i: (0, 0, i, 0))],
         out_specs=[tile_spec, tile_spec],
         out_shape=[tile_shape, tile_shape],
-        compiler_params=params(12),
+        compiler_params=params(56),
         name="encode",
     )(*[top.reshape(1) for top in tops], near)
 

time: 295 us -> 396 us (1.34)
  Pallas kernels: 52.9 us -> 184 us
  waiting for transfers between devices: 97.6 us -> 80.2 us
  local copies, waits for them, and re-layouts: 12.1 us -> 0.08 us
    pallas_call x2, Pallas kernels: 0.73 us -> 129 us  [body(): pl.pallas_call(partial(pack_kernel, chunk), in_specs=[whole(pltpu.SMEM),...]
    ppermute x9, waiting for transfers between devices: 32.8 us -> 16.6 us  [exchange(): lax.ppermute(pieces[j], axis, [(i, i ^ j) for i in range(total)])]
    unnamed x36 -> x24, local copies, waits for them, and re-layouts: 12.1 us -> 0.08 us
  transfers between devices with their start and end apart: 14 -> 14, of which waited for: 9 -> 7; matrix products, arithmetic and copies ran while one was open for 0% -> 0% of each run, Pallas kernels for 4% -> 20%
where the time goes in v7:
time: 396 us
  Pallas kernels  184 us (46%)
  waiting for transfers between devices  80.2 us (20%)
  blocking collectives  67.6 us (17%)
  starting transfers between devices  59.4 us (15%)
    pallas_call x2, Pallas kernels, body(): pl.pallas_call(partial(pack_kernel, chunk), in_specs=[whole(pltpu.SMEM),...  129 us
    all_to_all x1, blocking collectives, body(): lax.all_to_all(lines, ('row', 'col'), split_axis=0, concat_axis=0, tiled=...  67.6 us
    all_to_all x1, waiting for transfers between devices, body(): lax.all_to_all(lines, ('row', 'col'), split_axis=0, concat_axis=0, tiled=...  56.9 us
    ppermute x9, starting transfers between devices, exchange(): lax.ppermute(pieces[j], axis, [(i, i ^ j) for i in range(total)])  46.7 us
    ppermute x9, waiting for transfers between devices, exchange(): lax.ppermute(pieces[j], axis, [(i, i ^ j) for i in range(total)])  16.6 us
    pallas_call x2, Pallas kernels, body(): pl.pallas_call(partial(column_forward_kernel, row_total), in_specs=[whole...  14.3 us
    pallas_call x1, Pallas kernels, body(): pl.pallas_call(partial(line_kernel, order, own, tail), grid=(-(-own // at...  13.2 us
    pallas_call x1, Pallas kernels, body(): pl.pallas_call(column_inverse_kernel, grid=(STEPS + 1,), in_specs=[anywhe...  11 us
  transfers between devices with their start and end apart: 14, of which 7 were waited for; matrix products, arithmetic and copies ran while one was open for 0% of the time, Pallas kernels for 20%

profile of v7, /device:TPU:0, one launch (start us, length us, event | category | flops | bytes accessed | tf_op | source)
XLA Modules:
  0.0 395.6 jit_solution(14964240429429130200)
XLA Ops:
  0.6 64.7 %pack.3 = (f32[2,4,128,128]{3,2,1,0:T(8,128)}, f32[2,4,128,128]{3,2,1,0:T(8,128)}, f32[2,4,128,128]{3,2,1,0:T(8,128)}, f32[2,4,128,128]{3,2,1,0:T(8,128)}) custom-call(s32[1]{0:T(128)} %bitcast.place, f32[4,256,512]{2,1,0:T(8,128)} %bitcast.9, f32[4,256,512]{2,1,0:T(8,128)} %bitcast.11), custom_call_target="tpu_custom_call" | custom-call | bytes 4194304 | tf_op jit(solution)/shard_map/pack/pallas_call | solution.py:584
  65.3 0.0 copy-start.1
  65.4 0.0 copy-start.8
  65.4 0.0 copy-start.10
  65.4 3.0 collective-permute-start.3
  68.4 1.5 collective-permute-start.4
  69.9 0.0 collective-permute-start.5
  69.9 64.7 %pack.2 = (f32[2,4,128,128]{3,2,1,0:T(8,128)}, f32[2,4,128,128]{3,2,1,0:T(8,128)}, f32[2,4,128,128]{3,2,1,0:T(8,128)}, f32[2,4,128,128]{3,2,1,0:T(8,128)}) custom-call(s32[1]{0:T(128)} %bitcast.place, f32[4,256,512]{2,1,0:T(8,128)} %bitcast.10, f32[4,256,512]{2,1,0:T(8,128)} %bitcast.12), custom_call_target="tpu_custom_call" | custom-call | bytes 4194304 | tf_op jit(solution)/shard_map/pack/pallas_call | solution.py:584
  134.6 0.0 copy-start
  134.6 0.0 copy-start.7
  134.7 0.0 copy-start.9
  134.7 2.0 collective-permute-start
  136.7 1.5 collective-permute-start.1
  138.2 0.0 collective-permute-done.3.refs_1_
  138.2 0.0 collective-permute-start.2
  138.2 0.0 collective-permute-done.4.refs_2_
  138.2 0.0 collective-permute-done.5.refs_3_
  138.2 0.0 copy-done.1
  138.2 0.0 copy-done.8
  138.3 0.0 copy-done.10
  138.3 6.7 %column_forward.2.refs_4_ = f32[32,168,128]{2,1,0:T(8,128)S(1)} custom-call(s32[1]{0:T(128)} %bitcast.place, f32[128,128]{1,0:T(8,128)S(1)} %copy-done.10, bf16[336,256]{1,0:T(8,128)(2,1)S(1)} %copy-done.8, f32[2,4,128,128]{3,2,1,0:T(8,128)S(1)} %copy-done.1, f32[2,4,128,128]{3,2,1,0:T(8,128)S(1)} %collective-permute-done.3.refs_1_, ...), custom_call_target="tpu_custom_call" | custom-call | bytes 20971520 | tf_op jit(solution)/shard_map/column_forward/pallas_call | solution.py:604
  144.9 4.9 %collective-permute-done.refs_1_ = f32[2,4,128,128]{3,2,1,0:T(8,128)S(1)} collective-permute-done((f32[2,4,128,128]{3,2,1,0:T(8,128)}, f32[2,4,128,128]{3,2,1,0:T(8,128)S(1)}, u32[]{:S(2)}, u32[]{:S(2)}) %collective-permute-start) | collective-permute-done | bytes 524320 | tf_op jit(solution)/shard_map/ppermute | solution.py:520
  149.8 10.9 %collective-permute-done.1.refs_2_ = f32[2,4,128,128]{3,2,1,0:T(8,128)S(1)} collective-permute-done((f32[2,4,128,128]{3,2,1,0:T(8,128)}, f32[2,4,128,128]{3,2,1,0:T(8,128)S(1)}, u32[]{:S(2)}, u32[]{:S(2)}) %collective-permute-start.1) | collective-permute-done | bytes 524320 | tf_op jit(solution)/shard_map/ppermute | solution.py:520
  160.7 0.0 collective-permute-done.2.refs_3_
  160.7 0.0 copy-done
  160.7 0.0 copy-done.7
  160.7 0.0 copy-done.9
  160.7 7.6 %column_forward.3 = f32[32,168,128]{2,1,0:T(8,128)} custom-call(s32[1]{0:T(128)} %bitcast.place, f32[128,128]{1,0:T(8,128)S(1)} %copy-done.9, bf16[336,256]{1,0:T(8,128)(2,1)S(1)} %copy-done.7, f32[2,4,128,128]{3,2,1,0:T(8,128)S(1)} %copy-done, f32[2,4,128,128]{3,2,1,0:T(8,128)S(1)} %collective-permute-done.refs_1_, ...), custom_call_target="tpu_custom_call" | custom-call | bytes 20971520 | tf_op jit(solution)/shard_map/column_forward/pallas_call | solution.py:604
  168.3 0.0 copy-start.2
  168.3 0.0 copy-start.3
  168.3 0.0 copy-start.4
  168.4 0.0 copy-start.5
  168.4 0.0 copy-start.6
  168.4 5.0 %all-to-all-start = ((f32[32,168,128]{2,1,0:T(8,128)}), f32[32,168,128]{2,1,0:T(8,128)}, u32[]{:S(2)}, u32[]{:S(2)}) async-start(f32[32,168,128]{2,1,0:T(8,128)} %column_forward.3), calls=%async_computation | async-start | bytes 5505024 | tf_op jit(solution)/shard_map/all_to_all | solution.py:623
  173.4 0.6 pad_add_fusion.place
  174.0 6.7 %gain.1 = (f32[11,256,128]{2,1,0:T(8,128)}, f32[11,256,128]{2,1,0:T(8,128)}) custom-call(s32[2]{0:T(128)} %pad_add_fusion.place), custom_call_target="tpu_custom_call" | custom-call | tf_op jit(solution)/shard_map/gain/pallas_call | solution.py:562
  180.7 56.9 %all-to-all-done.lines = f32[32,168,128]{2,1,0:T(8,128)} async-done(((f32[32,168,128]{2,1,0:T(8,128)}), f32[32,168,128]{2,1,0:T(8,128)}, u32[]{:S(2)}, u32[]{:S(2)}) %all-to-all-start) | async-done | bytes 2752544 | tf_op jit(solution)/shard_map/all_to_all | solution.py:623
  237.6 0.0 copy-done.2
  237.6 0.0 copy-done.3
  237.6 0.0 copy-done.4
  237.6 0.0 copy-done.5
  237.6 0.0 copy-done.6
  237.6 13.2 %line.1 = f32[32,168,128]{2,1,0:T(8,128)} custom-call(f32[32,168,128]{2,1,0:T(8,128)} %all-to-all-done.lines, f32[11,256,128]{2,1,0:T(8,128)} %get-tuple-element.22.gain_re, f32[11,256,128]{2,1,0:T(8,128)} %get-tuple-element.23.gain_im, f32[2,17,8,256]{3,2,1,0:T(8,128)S(1)} %copy-done.2, bf16[512,256]{1,0:T(8,128)(2,1)S(1)} %copy-done.6, ...), custom_call_target="tpu_custom_call" | custom-call | tf_op jit(solution)/shard_map/line/pallas_call | solution.py:634
  250.8 67.6 %all_to_all.15.source = f32[32,168,128]{2,1,0:T(8,128)} all-to-all(f32[32,168,128]{2,1,0:T(8,128)} %line.1), channel_id=1, replica_groups=mesh['row'=4,'col'=8] {'row','col'}, dimensions={0} | all-to-all | bytes 5505024 | tf_op jit(solution)/shard_map/all_to_all | solution.py:649
  318.4 11.0 %column_inverse.1 = (f32[4,2,4,256,128]{4,3,2,1,0:T(8,128)}, f32[8,128]{1,0:T(8,128)}) custom-call(f32[32,168,128]{2,1,0:T(8,128)} %all_to_all.15.source, f32[256,128]{1,0:T(8,128)} %constant.71.clone.twist, bf16[2,256,512]{2,1,0:T(8,128)(2,1)} %constant.72.clone.matrix), custom_call_target="tpu_custom_call" | custom-call | tf_op jit(solution)/shard_map/column_inverse/pallas_call | solution.py:655
  329.5 0.0 copy-start.11
  329.5 4.9 %all-to-all-start.2 = ((f32[4,2,1024,128]{3,2,1,0:T(8,128)}), f32[4,2,1024,128]{3,2,1,0:T(8,128)}, u32[]{:S(2)}, u32[]{:S(2)}) async-start(f32[4,2,1024,128]{3,2,1,0:T(8,128)} %bitcast.13), calls=%async_computation.2 | async-start | bytes 8388608 | tf_op jit(solution)/shard_map/all_to_all | solution.py:679
  334.4 0.0 copy-done.11
  334.4 0.6 reduce_max.9
  335.0 0.0 collective-permute-start.6
  335.0 1.2 collective-permute-done.6
  337.6 1.4 collective-permute-start.7
  339.0 2.2 collective-permute-done.7
  341.9 1.4 collective-permute-start.8
  343.2 3.2 collective-permute-done.8
  347.0 32.8 %collective-permute-start.11 = (f32[]{:T(128)}, f32[]{:T(128)}, u32[]{:S(2)}, u32[]{:S(2)}) collective-permute-start(f32[]{:T(128)} %max.11), channel_id=1, source_target_pairs={{0,24},{8,16},{16,8},{24,0},{1,25},{9,17},{17,9},{25,1},{2,26},{10... | collective-permute-start | bytes 20 | tf_op jit(solution)/shard_map/ppermute | solution.py:520
  379.8 3.0 collective-permute-start.10
  382.8 2.8 collective-permute-start.9
  385.6 0.0 collective-permute-done.11
  385.6 0.0 collective-permute-done.10
  385.6 0.8 collective-permute-done.9
  386.5 0.0 all-to-all-done.2.refs_4_
  386.5 9.1 %encode.1 = (f32[1024,512]{1,0:T(8,128)}, f32[1024,512]{1,0:T(8,128)}) custom-call(f32[1]{0:T(128)} %bitcast.4.refs_0_, f32[1]{0:T(128)} %bitcast.5.refs_1_, f32[1]{0:T(128)} %bitcast.6.refs_2_, f32[1]{0:T(128)} %bitcast.7.refs_3_, f32[4,2,1024,128]{3,2,1,0:T(8,128)} %all-to-all-done.2.refs_4_), custom_call_target="tpu_custom_call" | custom-call | tf_op jit(solution)/shard_map/encode/pallas_call | solution.py:695
Async XLA Ops:
  65.3 72.9 %copy-start.1 = (f32[2,4,128,128]{3,2,1,0:T(8,128)S(1)}, f32[2,4,128,128]{3,2,1,0:T(8,128)}, u32[]{:S(2)}) copy-start(f32[2,4,128,128]{3,2,1,0:T(8,128)} %get-tuple-element.18.refs_0_) | copy-start | bytes 1572868
  65.4 72.9 %copy-start.8 = (bf16[336,256]{1,0:T(8,128)(2,1)S(1)}, bf16[336,256]{1,0:T(8,128)(2,1)}, u32[]{:S(2)}) copy-start(bf16[336,256]{1,0:T(8,128)(2,1)} %constant.63.clone.matrix) | copy-start | bytes 516100
  65.4 72.9 %copy-start.10 = (f32[128,128]{1,0:T(8,128)S(1)}, f32[128,128]{1,0:T(8,128)}, u32[]{:S(2)}) copy-start(f32[128,128]{1,0:T(8,128)} %constant.62.clone.twist) | copy-start | bytes 196612
  65.4 72.8 %collective-permute-start.3 = (f32[2,4,128,128]{3,2,1,0:T(8,128)}, f32[2,4,128,128]{3,2,1,0:T(8,128)S(1)}, u32[]{:S(2)}, u32[]{:S(2)}) collective-permute-start(f32[2,4,128,128]{3,2,1,0:T(8,128)} %get-tuple-element.19), channel_id=1, source_target_pairs={{0,8},{8,0},{16,24},{24,16},{1,9},{9,1},{17,25},{25,17},{2,10},{10... | collective-permute-start | bytes 1572872 | tf_op jit(solution)/shard_map/ppermute | solution.py:520
  68.4 69.8 %collective-permute-start.4 = (f32[2,4,128,128]{3,2,1,0:T(8,128)}, f32[2,4,128,128]{3,2,1,0:T(8,128)S(1)}, u32[]{:S(2)}, u32[]{:S(2)}) collective-permute-start(f32[2,4,128,128]{3,2,1,0:T(8,128)} %get-tuple-element.20), channel_id=1, source_target_pairs={{0,16},{8,24},{16,0},{24,8},{1,17},{9,25},{17,1},{25,9},{2,18},{10... | collective-permute-start | bytes 1572872 | tf_op jit(solution)/shard_map/ppermute | solution.py:520
  69.9 68.3 %collective-permute-start.5 = (f32[2,4,128,128]{3,2,1,0:T(8,128)}, f32[2,4,128,128]{3,2,1,0:T(8,128)S(1)}, u32[]{:S(2)}, u32[]{:S(2)}) collective-permute-start(f32[2,4,128,128]{3,2,1,0:T(8,128)} %get-tuple-element.21), channel_id=1, source_target_pairs={{0,24},{8,16},{16,8},{24,0},{1,25},{9,17},{17,9},{25,1},{2,26},{10... | collective-permute-start | bytes 1572872 | tf_op jit(solution)/shard_map/ppermute | solution.py:520
  134.6 26.0 %copy-start = (f32[2,4,128,128]{3,2,1,0:T(8,128)S(1)}, f32[2,4,128,128]{3,2,1,0:T(8,128)}, u32[]{:S(2)}) copy-start(f32[2,4,128,128]{3,2,1,0:T(8,128)} %get-tuple-element.14.refs_0_) | copy-start | bytes 1572868
  134.6 26.0 %copy-start.7 = (bf16[336,256]{1,0:T(8,128)(2,1)S(1)}, bf16[336,256]{1,0:T(8,128)(2,1)}, u32[]{:S(2)}) copy-start(bf16[336,256]{1,0:T(8,128)(2,1)} %constant.65.clone.matrix) | copy-start | bytes 516100
  134.7 26.0 %copy-start.9 = (f32[128,128]{1,0:T(8,128)S(1)}, f32[128,128]{1,0:T(8,128)}, u32[]{:S(2)}) copy-start(f32[128,128]{1,0:T(8,128)} %constant.64.clone.twist) | copy-start | bytes 196612
  134.7 15.1 %collective-permute-start = (f32[2,4,128,128]{3,2,1,0:T(8,128)}, f32[2,4,128,128]{3,2,1,0:T(8,128)S(1)}, u32[]{:S(2)}, u32[]{:S(2)}) collective-permute-start(f32[2,4,128,128]{3,2,1,0:T(8,128)} %get-tuple-element.15), channel_id=1, source_target_pairs={{0,8},{8,0},{16,24},{24,16},{1,9},{9,1},{17,25},{25,17},{2,10},{10... | collective-permute-start | bytes 1572872 | tf_op jit(solution)/shard_map/ppermute | solution.py:520
  136.7 24.0 %collective-permute-start.1 = (f32[2,4,128,128]{3,2,1,0:T(8,128)}, f32[2,4,128,128]{3,2,1,0:T(8,128)S(1)}, u32[]{:S(2)}, u32[]{:S(2)}) collective-permute-start(f32[2,4,128,128]{3,2,1,0:T(8,128)} %get-tuple-element.16), channel_id=1, source_target_pairs={{0,16},{8,24},{16,0},{24,8},{1,17},{9,25},{17,1},{25,9},{2,18},{10... | collective-permute-start | bytes 1572872 | tf_op jit(solution)/shard_map/ppermute | solution.py:520
  138.2 22.5 %collective-permute-start.2 = (f32[2,4,128,128]{3,2,1,0:T(8,128)}, f32[2,4,128,128]{3,2,1,0:T(8,128)S(1)}, u32[]{:S(2)}, u32[]{:S(2)}) collective-permute-start(f32[2,4,128,128]{3,2,1,0:T(8,128)} %get-tuple-element.17), channel_id=1, source_target_pairs={{0,24},{8,16},{16,8},{24,0},{1,25},{9,17},{17,9},{25,1},{2,26},{10... | collective-permute-start | bytes 1572872 | tf_op jit(solution)/shard_map/ppermute | solution.py:520
  168.3 69.3 %copy-start.2 = (f32[2,17,8,256]{3,2,1,0:T(8,128)S(1)}, f32[2,17,8,256]{3,2,1,0:T(8,128)}, u32[]{:S(2)}) copy-start(f32[2,17,8,256]{3,2,1,0:T(8,128)} %constant.66.clone.twist) | copy-start | bytes 835588
  168.3 69.3 %copy-start.3 = (bf16[256,512]{1,0:T(8,128)(2,1)S(1)}, bf16[256,512]{1,0:T(8,128)(2,1)}, u32[]{:S(2)}) copy-start(bf16[256,512]{1,0:T(8,128)(2,1)} %constant.70.clone.inv_low) | copy-start | bytes 786436
  168.3 69.3 %copy-start.4 = (bf16[256,512]{1,0:T(8,128)(2,1)S(1)}, bf16[256,512]{1,0:T(8,128)(2,1)}, u32[]{:S(2)}) copy-start(bf16[256,512]{1,0:T(8,128)(2,1)} %constant.69.clone.inv_high) | copy-start | bytes 786436
  168.4 69.3 %copy-start.5 = (bf16[512,256]{1,0:T(8,128)(2,1)S(1)}, bf16[512,256]{1,0:T(8,128)(2,1)}, u32[]{:S(2)}) copy-start(bf16[512,256]{1,0:T(8,128)(2,1)} %constant.68.clone.fwd_low) | copy-start | bytes 786436
  168.4 69.3 %copy-start.6 = (bf16[512,256]{1,0:T(8,128)(2,1)S(1)}, bf16[512,256]{1,0:T(8,128)(2,1)}, u32[]{:S(2)}) copy-start(bf16[512,256]{1,0:T(8,128)(2,1)} %constant.67.clone.fwd_high) | copy-start | bytes 786436
  168.4 69.2 %all-to-all-start = ((f32[32,168,128]{2,1,0:T(8,128)}), f32[32,168,128]{2,1,0:T(8,128)}, u32[]{:S(2)}, u32[]{:S(2)}) async-start(f32[32,168,128]{2,1,0:T(8,128)} %column_forward.3), calls=%async_computation | async-start | bytes 5505024 | tf_op jit(solution)/shard_map/all_to_all | solution.py:623
  329.5 4.9 %copy-start.11 = (f32[8,128]{1,0:T(8,128)S(1)}, f32[8,128]{1,0:T(8,128)}, u32[]{:S(2)}) copy-start(f32[8,128]{1,0:T(8,128)} %get-tuple-element.24) | copy-start | bytes 12292
  329.5 56.9 %all-to-all-start.2 = ((f32[4,2,1024,128]{3,2,1,0:T(8,128)}), f32[4,2,1024,128]{3,2,1,0:T(8,128)}, u32[]{:S(2)}, u32[]{:S(2)}) async-start(f32[4,2,1024,128]{3,2,1,0:T(8,128)} %bitcast.13), calls=%async_computation.2 | async-start | bytes 8388608 | tf_op jit(solution)/shard_map/all_to_all | solution.py:679
  335.0 1.2 collective-permute-start.6
  337.6 3.6 collective-permute-start.7
  341.9 4.6 %collective-permute-start.8 = (f32[]{:T(128)}, f32[]{:T(128)}, u32[]{:S(2)}, u32[]{:S(2)}) collective-permute-start(f32[]{:T(128)} %max.10), channel_id=1, source_target_pairs={{0,4},{1,5},{2,6},{3,7},{4,0},{5,1},{6,2},{7,3},{8,12},{9,13},{10,... | collective-permute-start | bytes 20 | tf_op jit(solution)/shard_map/ppermute | solution.py:684
  347.0 38.6 %collective-permute-start.11 = (f32[]{:T(128)}, f32[]{:T(128)}, u32[]{:S(2)}, u32[]{:S(2)}) collective-permute-start(f32[]{:T(128)} %max.11), channel_id=1, source_target_pairs={{0,24},{8,16},{16,8},{24,0},{1,25},{9,17},{17,9},{25,1},{2,26},{10... | collective-permute-start | bytes 20 | tf_op jit(solution)/shard_map/ppermute | solution.py:520
  379.8 5.8 %collective-permute-start.10 = (f32[]{:T(128)}, f32[]{:T(128)}, u32[]{:S(2)}, u32[]{:S(2)}) collective-permute-start(f32[]{:T(128)} %max.11), channel_id=1, source_target_pairs={{0,16},{8,24},{16,0},{24,8},{1,17},{9,25},{17,1},{25,9},{2,18},{10... | collective-permute-start | bytes 20 | tf_op jit(solution)/shard_map/ppermute | solution.py:520
  382.8 3.6 collective-permute-start.9

commit v8 on v7

--- a/solution.py
+++ b/solution.py
@@ -255,10 +255,11 @@
         copy_out(p).wait()
 
 
-def column_inverse_kernel(source, twist, matrix, out, top, lines, deep, back, sems):
+def column_inverse_kernel(count, place, source, twist, matrix, *refs):
+    pieces, (top, near, lines, deep, back, sems, out_sems) = refs[:count], refs[count:]
     width = lines.shape[-1]
     rows_in = lines.shape[1]
-    per_dest = out.shape[2]
+    per_dest = near.shape[3]
     many = deep.shape[-1] // width
     now = pl.program_id(0)
 
@@ -294,13 +295,26 @@
         def put(n, value):
             dest, block = divmod(n, per_dest)
             rows = pl.ds(q0, 8)
-            out[dest, 0, block, rows, :], out[dest, 1, block, rows, :] = value
+            near[slot, dest, 0, block, rows, :], near[slot, dest, 1, block, rows, :] = value
             largest.append(value[0] * value[0] + value[1] * value[1])
 
         inverse_slabs(get, put)
         while len(largest) > 1:
             largest = [jnp.maximum(a, b) for a, b in zip(largest[0::2], largest[1::2])]
         top[...] = jnp.maximum(top[...], largest[0])
+
+    def copies_out(slot, part):
+        size = STEP // 2
+        here = pl.ds(part * size, size)
+        there = pl.ds(slot * STEP + part * size, size)
+        return [
+            pltpu.make_async_copy(
+                near.at[slot, place[0] ^ j, :, :, here],
+                piece.at[:, :, there],
+                out_sems.at[(slot * 2 + part) * count + j],
+            )
+            for j, piece in enumerate(pieces)
+        ]
 
     @pl.when(now == 0)
     def _():
@@ -313,16 +327,27 @@
 
         @pl.when(now == step)
         def _():
-            tiles, products = STEP // 8, RES // many
+            tiles, products = STEP // 16, RES // many // 2
             steps = min(tiles, products)
 
-            @pl.loop(0, steps)
-            def _(t):
-                for part in range(tiles // steps):
-                    butterflies(t * (tiles // steps) + part, (step - 1) % 2)
-                if step < STEPS:
-                    for part in range(products // steps):
-                        product(t * (products // steps) + part, step % 2)
+            for part in range(2):
+
+                @pl.loop(part * steps, (part + 1) * steps)
+                def _(t):
+                    for item in range(tiles // steps):
+                        butterflies(t * (tiles // steps) + item, step - 1)
+                    if step < STEPS:
+                        for item in range(products // steps):
+                            product(t * (products // steps) + item, step)
+
+                for copy in copies_out(step - 1, part):
+                    copy.start()
+
+            if step == STEPS:
+                for slot in range(STEPS):
+                    for part in range(2):
+                        for copy in copies_out(slot, part):
+                            copy.wait()
 
 
 def line_kernel(
@@ -480,32 +505,46 @@
     return (near_real * level + near_imag * lift, near_imag * level - near_real * lift)
 
 
-def encode_kernel(count, *refs):
-    tops, (near, slm_real, slm_imag) = refs[:count], refs[count:]
-    height, width = slm_real.shape[0], near.shape[-1]
-    peak_sq = tops[0][0]
-    for top in tops[1:]:
-        peak_sq = jnp.maximum(peak_sq, top[0])
-    peak_sq = jnp.full((1, width), peak_sq, jnp.float32)
+def encode_kernel(count, place, top, *refs):
+    pieces, (slm_real, slm_imag, tile_real, tile_imag, sems) = refs[:count], refs[count:]
+    blocks, height, width = pieces[0].shape[1:]
+    peak_sq = jnp.full((1, width), top[0], jnp.float32)
     cell = lax.broadcasted_iota(jnp.int32, (height, width), 0)
     cell = cell + lax.broadcasted_iota(jnp.int32, (height, width), 1)
     cell_sign = (1 - 2 * (cell & 1)).astype(jnp.float32)
-    for r in range(near.shape[0]):
-        lanes = pl.ds(r * width, width)
-        slm_real[:, lanes], slm_imag[:, lanes] = encode(near[r, 0], near[r, 1], peak_sq, cell_sign)
-
-
-def pack_kernel(chunk, place, field_real, field_imag, *refs):
+
+    def copies_out(block):
+        rows = pl.ds(block * height, height)
+        return [
+            pltpu.make_async_copy(tile.at[block], slm.at[rows], sems.at[2 * block + part])
+            for part, (tile, slm) in enumerate(((tile_real, slm_real), (tile_imag, slm_imag)))
+        ]
+
+    @pl.loop(0, blocks)
+    def _(block):
+        for j, piece in enumerate(pieces):
+            lanes = pl.ds(pl.multiple_of((place[0] ^ j) * width, width), width)
+            tile_real[block, :, lanes], tile_imag[block, :, lanes] = encode(
+                piece[0, block], piece[1, block], peak_sq, cell_sign
+            )
+        for copy in copies_out(block):
+            copy.start()
+
+    for block in range(blocks):
+        for copy in copies_out(block):
+            copy.wait()
+
+
+def pack_kernel(place, field_real, field_imag, *refs):
     pieces, sems = refs[:-1], refs[-1]
     width = pieces[0].shape[-1]
-    rows = pl.ds(chunk * CHUNK, CHUNK)
     copies = []
     for j in list(range(1, len(pieces))) + [0]:
         lanes = pl.ds(pl.multiple_of((place[0] ^ j) * width, width), width)
         for part, field in enumerate((field_real, field_imag)):
             copies.append(
                 pltpu.make_async_copy(
-                    field.at[:, rows, lanes], pieces[j].at[part], sems.at[2 * j + part]
+                    field.at[:, :, lanes], pieces[j].at[part], sems.at[2 * j + part]
                 )
             )
     for copy in copies:
@@ -582,8 +621,10 @@
     for chunk in range(CHUNKS):
         if width == 128:
             pieces = pl.pallas_call(
-                partial(pack_kernel, chunk),
-                in_specs=[whole(pltpu.SMEM), anywhere, anywhere],
+                pack_kernel,
+                grid=(1,),
+                in_specs=[whole(pltpu.SMEM)]
+                + [pl.BlockSpec((blocks, CHUNK, tile_width), lambda i: (0, chunk, 0))] * 2,
                 out_specs=[anywhere] * row_total,
                 out_shape=[piece_shape] * row_total,
                 scratch_shapes=[pltpu.SemaphoreType.DMA((2 * row_total,))],
@@ -649,59 +690,56 @@
     lines = lax.all_to_all(lines, ("row", "col"), split_axis=0, concat_axis=0, tiled=True)
     lines = lines.reshape(RES, total_rows, width)
 
-    tall = pl.BlockSpec(
-        (row_total, 2, blocks, STEP, width), lambda i: (0, 0, 0, jnp.maximum(i - 1, 0), 0)
-    )
-    near, top = pl.pallas_call(
-        column_inverse_kernel,
+    piece = (2, blocks, INNER, width)
+    piece_shape = jax.ShapeDtypeStruct(piece, jnp.float32)
+    *near, top = pl.pallas_call(
+        partial(column_inverse_kernel, row_total),
         grid=(STEPS + 1,),
         in_specs=[
+            whole(pltpu.SMEM),
             anywhere,
             pl.BlockSpec((STEP, 128), lambda i: (jnp.maximum(i - 1, 0), 0)),
             pl.BlockSpec((1,) + inv_col.shape[1:], lambda i: (jnp.minimum(i, STEPS - 1), 0, 0)),
         ],
-        out_specs=[tall, whole()],
-        out_shape=[
-            jax.ShapeDtypeStruct((row_total, 2, blocks, INNER, width), jnp.float32),
-            jax.ShapeDtypeStruct((8, width), jnp.float32),
-        ],
+        out_specs=[anywhere] * row_total + [whole()],
+        out_shape=[piece_shape] * row_total + [jax.ShapeDtypeStruct((8, width), jnp.float32)],
         scratch_shapes=[
+            pltpu.VMEM((STEPS, row_total, 2, blocks, STEP, width), jnp.float32),
             pltpu.VMEM((RES, total_rows, width), jnp.float32),
             pltpu.VMEM((RES // many, inv_col.shape[2], many * width), jnp.bfloat16),
-            pltpu.VMEM((2, RES, 2 * STEP, width), jnp.float32),
+            pltpu.VMEM((STEPS, RES, 2 * STEP, width), jnp.float32),
             pltpu.SemaphoreType.DMA((RES // many,)),
+            pltpu.SemaphoreType.DMA((2 * STEPS * row_total,)),
         ],
         compiler_params=params(56),
         name="column_inverse",
-    )(lines, twist_col, inv_col)
-
-    near = near.reshape(row_total, 2, height, width)
-    near = lax.all_to_all(near, "row", split_axis=0, concat_axis=0, tiled=True)
-    peak = jnp.max(top)
-    shift = 1
-    while shift < col_total:
-        partner = [(i, i ^ shift) for i in range(col_total)]
-        peak = jnp.maximum(peak, lax.ppermute(peak, "col", partner))
-        shift *= 2
-    tops = exchange([peak] * row_total, "row")
+    )(place_row, lines, twist_col, inv_col)
+
+    near = exchange(near, "row")
+    peak_sq = jnp.max(top)
+    for axis, total in (("col", col_total), ("row", row_total)):
+        shift = 1
+        while shift < total:
+            partner = [(i, i ^ shift) for i in range(total)]
+            peak_sq = jnp.maximum(peak_sq, lax.ppermute(peak_sq, axis, partner))
+            shift *= 2
     if width != 128:
-        near = near.transpose(1, 2, 0, 3).reshape(2, height, tile_width)
+        near = jnp.take(jnp.stack(near), jnp.arange(row_total) ^ place_row[0], axis=0)
+        near = near.transpose(1, 2, 3, 0, 4).reshape(2, height, tile_width)
         odd_cell = (jnp.arange(height)[:, None] + jnp.arange(tile_width)[None, :]) % 2
         cell_sign = (1 - 2 * odd_cell).astype(jnp.float32)
-        return encode(near[0], near[1], jnp.max(jnp.stack(tops)), cell_sign)
-    tile_rows = min(height, 128)
-    tile_spec = pl.BlockSpec((tile_rows, tile_width), lambda i: (i, 0))
+        return encode(near[0], near[1], peak_sq, cell_sign)
     tile_shape = jax.ShapeDtypeStruct((height, tile_width), jnp.float32)
+    tile = pltpu.VMEM((blocks, INNER, tile_width), jnp.float32)
     return pl.pallas_call(
         partial(encode_kernel, row_total),
-        grid=(height // tile_rows,),
-        in_specs=[whole(pltpu.SMEM)] * row_total
-        + [pl.BlockSpec((row_total, 2, tile_rows, width), lambda i: (0, 0, i, 0))],
-        out_specs=[tile_spec, tile_spec],
+        in_specs=[whole(pltpu.SMEM)] * 2 + [whole()] * row_total,
+        out_specs=[anywhere] * 2,
         out_shape=[tile_shape, tile_shape],
-        compiler_params=params(56),
+        scratch_shapes=[tile, tile, pltpu.SemaphoreType.DMA((2 * blocks,))],
+        compiler_params=params(16),
         name="encode",
-    )(*[top.reshape(1) for top in tops], near)
+    )(place_row, peak_sq.reshape(1), *near)
 
 
 def solution(mesh):

time: 396 us -> 280 us (0.71)
  Pallas kernels: 184 us -> 54.2 us
  waiting for transfers between devices: 80.2 us -> 95.8 us
  starting transfers between devices: 59.4 us -> 54.3 us
    pallas_call x4, Pallas kernels: 150 us -> 20.1 us  [the longest x1 11.4 us: body(): pl.pallas_call(partial(column_inverse_kernel, row_total), grid=(STEPS + 1...]
    ppermute x9, starting transfers between devices: 46.7 us -> 14.6 us  [exchange(): lax.ppermute(pieces[j], axis, [(i, i ^ j) for i in range(total)])]
    ppermute x3 -> x5, starting transfers between devices: 2.74 us -> 34.7 us  [body(): peak_sq = jnp.maximum(peak_sq, lax.ppermute(peak_sq, axis, partner))]
    ppermute x9, waiting for transfers between devices: 16.6 us -> 29.6 us  [exchange(): lax.ppermute(pieces[j], axis, [(i, i ^ j) for i in range(total)])]
    all_to_all x1 -> x0, starting transfers between devices: 4.89 us -> none  [body(): near = lax.all_to_all(near, 'row', split_axis=0, concat_axis=0, tiled=True)]
    ppermute x3 -> x5, waiting for transfers between devices: 6.66 us -> 9.37 us  [body(): peak_sq = jnp.maximum(peak_sq, lax.ppermute(peak_sq, axis, partner))]
  transfers between devices with their start and end apart: 14 -> 15, of which waited for: 7 -> 10; matrix products, arithmetic and copies ran while one was open for 0% -> 1% of each run, Pallas kernels for 20% -> 6%
where the time goes in v8:
time: 280 us
  waiting for transfers between devices  95.8 us (34%)
  blocking collectives  67.6 us (24%)
  starting transfers between devices  54.3 us (19%)
  Pallas kernels  54.2 us (19%)
  between operations  4.43 us (2%)
    all_to_all x1, blocking collectives, body(): lax.all_to_all(lines, ('row', 'col'), split_axis=0, concat_axis=0, tiled=...  67.6 us
    all_to_all x1, waiting for transfers between devices, body(): lax.all_to_all(lines, ('row', 'col'), split_axis=0, concat_axis=0, tiled=...  56.9 us
    ppermute x5, starting transfers between devices, body(): peak_sq = jnp.maximum(peak_sq, lax.ppermute(peak_sq, axis, partner))  34.7 us
    ppermute x9, waiting for transfers between devices, exchange(): lax.ppermute(pieces[j], axis, [(i, i ^ j) for i in range(total)])  29.6 us
    ppermute x9, starting transfers between devices, exchange(): lax.ppermute(pieces[j], axis, [(i, i ^ j) for i in range(total)])  14.6 us
    pallas_call x2, Pallas kernels, body(): pl.pallas_call(partial(column_forward_kernel, row_total), in_specs=[whole...  14.3 us
    pallas_call x1, Pallas kernels, body(): pl.pallas_call(partial(line_kernel, order, own, tail), grid=(-(-own // at...  13.2 us
    pallas_call x1, Pallas kernels, body(): pl.pallas_call(partial(column_inverse_kernel, row_total), grid=(STEPS + 1...  11.4 us
  transfers between devices with their start and end apart: 15, of which 10 were waited for; matrix products, arithmetic and copies ran while one was open for 1% of the time, Pallas kernels for 6%

profile of v8, /device:TPU:0, one launch (start us, length us, event | category | flops | bytes accessed | tf_op | source)
XLA Modules:
  0.0 279.6 jit_solution(5218390147087247142)
XLA Ops:
  0.6 2.9 %pack.3 = (f32[2,4,128,128]{3,2,1,0:T(8,128)}, f32[2,4,128,128]{3,2,1,0:T(8,128)}, f32[2,4,128,128]{3,2,1,0:T(8,128)}, f32[2,4,128,128]{3,2,1,0:T(8,128)}) custom-call(s32[1]{0:T(128)} %bitcast.place, f32[4,256,512]{2,1,0:T(8,128)} %bitcast.5, f32[4,256,512]{2,1,0:T(8,128)} %bitcast.7), custom_call_target="tpu_custom_call" | custom-call | bytes 4194304 | tf_op jit(solution)/shard_map/pack/pallas_call | solution.py:623
  3.6 3.0 %collective-permute-start.3 = (f32[2,4,128,128]{3,2,1,0:T(8,128)}, f32[2,4,128,128]{3,2,1,0:T(8,128)S(1)}, u32[]{:S(2)}, u32[]{:S(2)}) collective-permute-start(f32[2,4,128,128]{3,2,1,0:T(8,128)} %get-tuple-element.22), channel_id=1, source_target_pairs={{0,8},{8,0},{16,24},{24,16},{1,9},{9,1},{17,25},{25,17},{2,10},{10... | collective-permute-start | bytes 1572872 | tf_op jit(solution)/shard_map/ppermute | solution.py:559
  6.6 1.5 collective-permute-start.4
  8.1 0.0 copy-start.2
  8.1 0.0 copy-start.9
  8.1 0.1 collective-permute-start.5
  8.2 3.0 %pack.2 = (f32[2,4,128,128]{3,2,1,0:T(8,128)}, f32[2,4,128,128]{3,2,1,0:T(8,128)}, f32[2,4,128,128]{3,2,1,0:T(8,128)}, f32[2,4,128,128]{3,2,1,0:T(8,128)}) custom-call(s32[1]{0:T(128)} %bitcast.place, f32[4,256,512]{2,1,0:T(8,128)} %bitcast.6, f32[4,256,512]{2,1,0:T(8,128)} %bitcast.8), custom_call_target="tpu_custom_call" | custom-call | bytes 4194304 | tf_op jit(solution)/shard_map/pack/pallas_call | solution.py:623
  11.1 1.9 collective-permute-start
  13.1 1.5 collective-permute-start.1
  14.6 5.0 %collective-permute-done.3.refs_1_ = f32[2,4,128,128]{3,2,1,0:T(8,128)S(1)} collective-permute-done((f32[2,4,128,128]{3,2,1,0:T(8,128)}, f32[2,4,128,128]{3,2,1,0:T(8,128)S(1)}, u32[]{:S(2)}, u32[]{:S(2)}) %collective-permute-start.3) | collective-permute-done | bytes 524320 | tf_op jit(solution)/shard_map/ppermute | solution.py:559
  19.5 3.0 %collective-permute-start.2 = (f32[2,4,128,128]{3,2,1,0:T(8,128)}, f32[2,4,128,128]{3,2,1,0:T(8,128)S(1)}, u32[]{:S(2)}, u32[]{:S(2)}) collective-permute-start(f32[2,4,128,128]{3,2,1,0:T(8,128)} %get-tuple-element.20), channel_id=1, source_target_pairs={{0,24},{8,16},{16,8},{24,0},{1,25},{9,17},{17,9},{25,1},{2,26},{10... | collective-permute-start | bytes 1572872 | tf_op jit(solution)/shard_map/ppermute | solution.py:559
  22.6 10.3 %collective-permute-done.4.refs_2_ = f32[2,4,128,128]{3,2,1,0:T(8,128)S(1)} collective-permute-done((f32[2,4,128,128]{3,2,1,0:T(8,128)}, f32[2,4,128,128]{3,2,1,0:T(8,128)S(1)}, u32[]{:S(2)}, u32[]{:S(2)}) %collective-permute-start.4) | collective-permute-done | bytes 524320 | tf_op jit(solution)/shard_map/ppermute | solution.py:559
  32.9 0.0 collective-permute-done.5.refs_3_
  32.9 0.0 copy-done.2
  32.9 0.0 copy-done.9
  32.9 0.0 copy-done.11
  32.9 0.0 copy-start.1
  32.9 0.0 copy-start.8
  32.9 0.0 copy-start.10
  32.9 6.7 %column_forward.2.refs_4_ = f32[32,168,128]{2,1,0:T(8,128)S(1)} custom-call(s32[1]{0:T(128)} %bitcast.place, f32[128,128]{1,0:T(8,128)S(1)} %copy-done.11, bf16[336,256]{1,0:T(8,128)(2,1)S(1)} %copy-done.9, f32[2,4,128,128]{3,2,1,0:T(8,128)S(1)} %copy-done.2, f32[2,4,128,128]{3,2,1,0:T(8,128)S(1)} %collective-permute-done.3.refs_1_, ...), custom_call_target="tpu_custom_call" | custom-call | bytes 20971520 | tf_op jit(solution)/shard_map/column_forward/pallas_call | solution.py:645
  39.6 2.5 collective-permute-done.refs_1_
  42.1 11.8 %collective-permute-done.1.refs_2_ = f32[2,4,128,128]{3,2,1,0:T(8,128)S(1)} collective-permute-done((f32[2,4,128,128]{3,2,1,0:T(8,128)}, f32[2,4,128,128]{3,2,1,0:T(8,128)S(1)}, u32[]{:S(2)}, u32[]{:S(2)}) %collective-permute-start.1) | collective-permute-done | bytes 524320 | tf_op jit(solution)/shard_map/ppermute | solution.py:559
  53.9 0.0 collective-permute-done.2.refs_3_
  53.9 0.0 copy-done.1
  53.9 0.0 copy-done.8
  53.9 0.0 copy-done.10
  53.9 7.6 %column_forward.3 = f32[32,168,128]{2,1,0:T(8,128)} custom-call(s32[1]{0:T(128)} %bitcast.place, f32[128,128]{1,0:T(8,128)S(1)} %copy-done.10, bf16[336,256]{1,0:T(8,128)(2,1)S(1)} %copy-done.8, f32[2,4,128,128]{3,2,1,0:T(8,128)S(1)} %copy-done.1, f32[2,4,128,128]{3,2,1,0:T(8,128)S(1)} %collective-permute-done.refs_1_, ...), custom_call_target="tpu_custom_call" | custom-call | bytes 20971520 | tf_op jit(solution)/shard_map/column_forward/pallas_call | solution.py:645
  61.5 0.0 copy-start.3
  61.5 0.0 copy-start.4
  61.5 0.0 copy-start.5
  61.6 0.0 copy-start.6
  61.6 0.0 copy-start.7
  61.6 5.0 %all-to-all-start = ((f32[32,168,128]{2,1,0:T(8,128)}), f32[32,168,128]{2,1,0:T(8,128)}, u32[]{:S(2)}, u32[]{:S(2)}) async-start(f32[32,168,128]{2,1,0:T(8,128)} %column_forward.3), calls=%async_computation | async-start | bytes 5505024 | tf_op jit(solution)/shard_map/all_to_all | solution.py:664
  66.6 0.6 pad_add_fusion.place
  67.3 6.7 %gain.1 = (f32[11,256,128]{2,1,0:T(8,128)}, f32[11,256,128]{2,1,0:T(8,128)}) custom-call(s32[2]{0:T(128)} %pad_add_fusion.place), custom_call_target="tpu_custom_call" | custom-call | tf_op jit(solution)/shard_map/gain/pallas_call | solution.py:601
  73.9 56.9 %all-to-all-done.lines = f32[32,168,128]{2,1,0:T(8,128)} async-done(((f32[32,168,128]{2,1,0:T(8,128)}), f32[32,168,128]{2,1,0:T(8,128)}, u32[]{:S(2)}, u32[]{:S(2)}) %all-to-all-start) | async-done | bytes 2752544 | tf_op jit(solution)/shard_map/all_to_all | solution.py:664
  130.8 0.0 copy-done.3
  130.8 0.0 copy-done.4
  130.8 0.0 copy-done.5
  130.8 0.0 copy-done.6
  130.8 0.0 copy-done.7
  130.8 13.2 %line.1 = f32[32,168,128]{2,1,0:T(8,128)} custom-call(f32[32,168,128]{2,1,0:T(8,128)} %all-to-all-done.lines, f32[11,256,128]{2,1,0:T(8,128)} %get-tuple-element.25.gain_re, f32[11,256,128]{2,1,0:T(8,128)} %get-tuple-element.26.gain_im, f32[2,17,8,256]{3,2,1,0:T(8,128)S(1)} %copy-done.3, bf16[512,256]{1,0:T(8,128)(2,1)S(1)} %copy-done.7, ...), custom_call_target="tpu_custom_call" | custom-call | tf_op jit(solution)/shard_map/line/pallas_call | solution.py:675
  144.0 67.6 %all_to_all.10.source = f32[32,168,128]{2,1,0:T(8,128)} all-to-all(f32[32,168,128]{2,1,0:T(8,128)} %line.1), channel_id=1, replica_groups=mesh['row'=4,'col'=8] {'row','col'}, dimensions={0} | all-to-all | bytes 5505024 | tf_op jit(solution)/shard_map/all_to_all | solution.py:690
  211.6 11.4 %column_inverse.1 = (f32[2,4,256,128]{3,2,1,0:T(8,128)}, f32[2,4,256,128]{3,2,1,0:T(8,128)}, f32[2,4,256,128]{3,2,1,0:T(8,128)}, f32[2,4,256,128]{3,2,1,0:T(8,128)}, f32[8,128]{1,0:T(8,128)}) custom-call(s32[1]{0:T(128)} %bitcast.place, f32[32,168,128]{2,1,0:T(8,128)} %all_to_all.10.source, f32[256,128]{1,0:T(8,128)} %constant.71.clone.twist, ...), custom_call_target="tpu_custom_call" | custom-call | tf_op jit(solution)/shard_map/column_inverse/pallas_call | solution.py:695
  223.1 0.1 collective-permute-start.11
  223.1 1.1 collective-permute-start.12
  224.2 2.4 collective-permute-start.13
  226.6 1.4 reduce_max.9
  228.0 0.0 collective-permute-start.6
  228.0 1.3 collective-permute-done.6
  230.5 1.4 collective-permute-start.7
  231.9 2.3 collective-permute-done.7
  234.8 1.4 collective-permute-start.8
  236.2 3.2 %collective-permute-done.8 = f32[]{:T(128)} collective-permute-done((f32[]{:T(128)}, f32[]{:T(128)}, u32[]{:S(2)}, u32[]{:S(2)}) %collective-permute-start.8) | collective-permute-done | bytes 36 | tf_op jit(solution)/shard_map/ppermute | solution.py:724
  240.0 29.4 %collective-permute-start.9 = (f32[]{:T(128)}, f32[]{:T(128)}, u32[]{:S(2)}, u32[]{:S(2)}) collective-permute-start(f32[]{:T(128)} %max.17), channel_id=1, source_target_pairs={{0,8},{8,0},{16,24},{24,16},{1,9},{9,1},{17,25},{25,17},{2,10},{10... | collective-permute-start | bytes 20 | tf_op jit(solution)/shard_map/ppermute | solution.py:724
  269.4 1.3 collective-permute-done.9
  271.3 2.5 collective-permute-start.10
  273.8 1.2 collective-permute-done.10
  275.6 0.0 collective-permute-done.11.refs_1_
  275.6 0.0 collective-permute-done.12.refs_2_
  275.6 0.0 collective-permute-done.13.refs_3_
  275.6 0.0 copy-start
  275.6 1.2 copy-done
  276.8 2.8 encode.1
  (1 shorter events, 0.0 us)
Async XLA Ops:
  3.6 16.0 %collective-permute-start.3 = (f32[2,4,128,128]{3,2,1,0:T(8,128)}, f32[2,4,128,128]{3,2,1,0:T(8,128)S(1)}, u32[]{:S(2)}, u32[]{:S(2)}) collective-permute-start(f32[2,4,128,128]{3,2,1,0:T(8,128)} %get-tuple-element.22), channel_id=1, source_target_pairs={{0,8},{8,0},{16,24},{24,16},{1,9},{9,1},{17,25},{25,17},{2,10},{10... | collective-permute-start | bytes 1572872 | tf_op jit(solution)/shard_map/ppermute | solution.py:559
  6.6 26.3 %collective-permute-start.4 = (f32[2,4,128,128]{3,2,1,0:T(8,128)}, f32[2,4,128,128]{3,2,1,0:T(8,128)S(1)}, u32[]{:S(2)}, u32[]{:S(2)}) collective-permute-start(f32[2,4,128,128]{3,2,1,0:T(8,128)} %get-tuple-element.23), channel_id=1, source_target_pairs={{0,16},{8,24},{16,0},{24,8},{1,17},{9,25},{17,1},{25,9},{2,18},{10... | collective-permute-start | bytes 1572872 | tf_op jit(solution)/shard_map/ppermute | solution.py:559
  8.1 24.8 %copy-start.2 = (f32[2,4,128,128]{3,2,1,0:T(8,128)S(1)}, f32[2,4,128,128]{3,2,1,0:T(8,128)}, u32[]{:S(2)}) copy-start(f32[2,4,128,128]{3,2,1,0:T(8,128)} %get-tuple-element.21.refs_0_) | copy-start | bytes 1572868
  8.1 24.8 %copy-start.9 = (bf16[336,256]{1,0:T(8,128)(2,1)S(1)}, bf16[336,256]{1,0:T(8,128)(2,1)}, u32[]{:S(2)}) copy-start(bf16[336,256]{1,0:T(8,128)(2,1)} %constant.63.clone.matrix) | copy-start | bytes 516100
  8.1 24.8 %copy-start.11 = (f32[128,128]{1,0:T(8,128)S(1)}, f32[128,128]{1,0:T(8,128)}, u32[]{:S(2)}) copy-start(f32[128,128]{1,0:T(8,128)} %constant.62.clone.twist) | copy-start | bytes 196612
  8.1 24.8 %collective-permute-start.5 = (f32[2,4,128,128]{3,2,1,0:T(8,128)}, f32[2,4,128,128]{3,2,1,0:T(8,128)S(1)}, u32[]{:S(2)}, u32[]{:S(2)}) collective-permute-start(f32[2,4,128,128]{3,2,1,0:T(8,128)} %get-tuple-element.24), channel_id=1, source_target_pairs={{0,24},{8,16},{16,8},{24,0},{1,25},{9,17},{17,9},{25,1},{2,26},{10... | collective-permute-start | bytes 1572872 | tf_op jit(solution)/shard_map/ppermute | solution.py:559
  11.1 30.9 %collective-permute-start = (f32[2,4,128,128]{3,2,1,0:T(8,128)}, f32[2,4,128,128]{3,2,1,0:T(8,128)S(1)}, u32[]{:S(2)}, u32[]{:S(2)}) collective-permute-start(f32[2,4,128,128]{3,2,1,0:T(8,128)} %get-tuple-element.18), channel_id=1, source_target_pairs={{0,8},{8,0},{16,24},{24,16},{1,9},{9,1},{17,25},{25,17},{2,10},{10... | collective-permute-start | bytes 1572872 | tf_op jit(solution)/shard_map/ppermute | solution.py:559
  13.1 40.8 %collective-permute-start.1 = (f32[2,4,128,128]{3,2,1,0:T(8,128)}, f32[2,4,128,128]{3,2,1,0:T(8,128)S(1)}, u32[]{:S(2)}, u32[]{:S(2)}) collective-permute-start(f32[2,4,128,128]{3,2,1,0:T(8,128)} %get-tuple-element.19), channel_id=1, source_target_pairs={{0,16},{8,24},{16,0},{24,8},{1,17},{9,25},{17,1},{25,9},{2,18},{10... | collective-permute-start | bytes 1572872 | tf_op jit(solution)/shard_map/ppermute | solution.py:559
  19.5 34.3 %collective-permute-start.2 = (f32[2,4,128,128]{3,2,1,0:T(8,128)}, f32[2,4,128,128]{3,2,1,0:T(8,128)S(1)}, u32[]{:S(2)}, u32[]{:S(2)}) collective-permute-start(f32[2,4,128,128]{3,2,1,0:T(8,128)} %get-tuple-element.20), channel_id=1, source_target_pairs={{0,24},{8,16},{16,8},{24,0},{1,25},{9,17},{17,9},{25,1},{2,26},{10... | collective-permute-start | bytes 1572872 | tf_op jit(solution)/shard_map/ppermute | solution.py:559
  32.9 21.0 %copy-start.1 = (f32[2,4,128,128]{3,2,1,0:T(8,128)S(1)}, f32[2,4,128,128]{3,2,1,0:T(8,128)}, u32[]{:S(2)}) copy-start(f32[2,4,128,128]{3,2,1,0:T(8,128)} %get-tuple-element.17.refs_0_) | copy-start | bytes 1572868
  32.9 21.0 %copy-start.8 = (bf16[336,256]{1,0:T(8,128)(2,1)S(1)}, bf16[336,256]{1,0:T(8,128)(2,1)}, u32[]{:S(2)}) copy-start(bf16[336,256]{1,0:T(8,128)(2,1)} %constant.65.clone.matrix) | copy-start | bytes 516100
  32.9 21.0 %copy-start.10 = (f32[128,128]{1,0:T(8,128)S(1)}, f32[128,128]{1,0:T(8,128)}, u32[]{:S(2)}) copy-start(f32[128,128]{1,0:T(8,128)} %constant.64.clone.twist) | copy-start | bytes 196612
  61.5 69.3 %copy-start.3 = (f32[2,17,8,256]{3,2,1,0:T(8,128)S(1)}, f32[2,17,8,256]{3,2,1,0:T(8,128)}, u32[]{:S(2)}) copy-start(f32[2,17,8,256]{3,2,1,0:T(8,128)} %constant.66.clone.twist) | copy-start | bytes 835588
  61.5 69.3 %copy-start.4 = (bf16[256,512]{1,0:T(8,128)(2,1)S(1)}, bf16[256,512]{1,0:T(8,128)(2,1)}, u32[]{:S(2)}) copy-start(bf16[256,512]{1,0:T(8,128)(2,1)} %constant.70.clone.inv_low) | copy-start | bytes 786436
  61.5 69.3 %copy-start.5 = (bf16[256,512]{1,0:T(8,128)(2,1)S(1)}, bf16[256,512]{1,0:T(8,128)(2,1)}, u32[]{:S(2)}) copy-start(bf16[256,512]{1,0:T(8,128)(2,1)} %constant.69.clone.inv_high) | copy-start | bytes 786436
  61.6 69.3 %copy-start.6 = (bf16[512,256]{1,0:T(8,128)(2,1)S(1)}, bf16[512,256]{1,0:T(8,128)(2,1)}, u32[]{:S(2)}) copy-start(bf16[512,256]{1,0:T(8,128)(2,1)} %constant.68.clone.fwd_low) | copy-start | bytes 786436
  61.6 69.3 %copy-start.7 = (bf16[512,256]{1,0:T(8,128)(2,1)S(1)}, bf16[512,256]{1,0:T(8,128)(2,1)}, u32[]{:S(2)}) copy-start(bf16[512,256]{1,0:T(8,128)(2,1)} %constant.67.clone.fwd_high) | copy-start | bytes 786436
  61.6 69.2 %all-to-all-start = ((f32[32,168,128]{2,1,0:T(8,128)}), f32[32,168,128]{2,1,0:T(8,128)}, u32[]{:S(2)}, u32[]{:S(2)}) async-start(f32[32,168,128]{2,1,0:T(8,128)} %column_forward.3), calls=%async_computation | async-start | bytes 5505024 | tf_op jit(solution)/shard_map/all_to_all | solution.py:664
  223.1 52.5 %collective-permute-start.11 = (f32[2,4,256,128]{3,2,1,0:T(8,128)}, f32[2,4,256,128]{3,2,1,0:T(8,128)S(1)}, u32[]{:S(2)}, u32[]{:S(2)}) collective-permute-start(f32[2,4,256,128]{3,2,1,0:T(8,128)} %get-tuple-element.29), channel_id=1, source_target_pairs={{0,8},{8,0},{16,24},{24,16},{1,9},{9,1},{17,25},{25,17},{2,10},{10... | collective-permute-start | bytes 3145736 | tf_op jit(solution)/shard_map/ppermute | solution.py:559
  223.1 52.4 %collective-permute-start.12 = (f32[2,4,256,128]{3,2,1,0:T(8,128)}, f32[2,4,256,128]{3,2,1,0:T(8,128)S(1)}, u32[]{:S(2)}, u32[]{:S(2)}) collective-permute-start(f32[2,4,256,128]{3,2,1,0:T(8,128)} %get-tuple-element.30), channel_id=1, source_target_pairs={{0,16},{8,24},{16,0},{24,8},{1,17},{9,25},{17,1},{25,9},{2,18},{10... | collective-permute-start | bytes 3145736 | tf_op jit(solution)/shard_map/ppermute | solution.py:559
  224.2 51.4 %collective-permute-start.13 = (f32[2,4,256,128]{3,2,1,0:T(8,128)}, f32[2,4,256,128]{3,2,1,0:T(8,128)S(1)}, u32[]{:S(2)}, u32[]{:S(2)}) collective-permute-start(f32[2,4,256,128]{3,2,1,0:T(8,128)} %get-tuple-element.31), channel_id=1, source_target_pairs={{0,24},{8,16},{16,8},{24,0},{1,25},{9,17},{17,9},{25,1},{2,26},{10... | collective-permute-start | bytes 3145736 | tf_op jit(solution)/shard_map/ppermute | solution.py:559
  228.0 1.3 collective-permute-start.6
  230.5 3.7 %collective-permute-start.7 = (f32[]{:T(128)}, f32[]{:T(128)}, u32[]{:S(2)}, u32[]{:S(2)}) collective-permute-start(f32[]{:T(128)} %max.15), channel_id=1, source_target_pairs={{0,2},{1,3},{2,0},{3,1},{4,6},{5,7},{6,4},{7,5},{8,10},{9,11},{10,... | collective-permute-start | bytes 20 | tf_op jit(solution)/shard_map/ppermute | solution.py:724
  234.8 4.6 %collective-permute-start.8 = (f32[]{:T(128)}, f32[]{:T(128)}, u32[]{:S(2)}, u32[]{:S(2)}) collective-permute-start(f32[]{:T(128)} %max.16), channel_id=1, source_target_pairs={{0,4},{1,5},{2,6},{3,7},{4,0},{5,1},{6,2},{7,3},{8,12},{9,13},{10,... | collective-permute-start | bytes 20 | tf_op jit(solution)/shard_map/ppermute | solution.py:724
  240.0 30.7 %collective-permute-start.9 = (f32[]{:T(128)}, f32[]{:T(128)}, u32[]{:S(2)}, u32[]{:S(2)}) collective-permute-start(f32[]{:T(128)} %max.17), channel_id=1, source_target_pairs={{0,8},{8,0},{16,24},{24,16},{1,9},{9,1},{17,25},{25,17},{2,10},{10... | collective-permute-start | bytes 20 | tf_op jit(solution)/shard_map/ppermute | solution.py:724
  271.3 3.7 %collective-permute-start.10 = (f32[]{:T(128)}, f32[]{:T(128)}, u32[]{:S(2)}, u32[]{:S(2)}) collective-permute-start(f32[]{:T(128)} %max.18), channel_id=1, source_target_pairs={{0,16},{8,24},{16,0},{24,8},{1,17},{9,25},{17,1},{25,9},{2,18},{10... | collective-permute-start | bytes 20 | tf_op jit(solution)/shard_map/ppermute | solution.py:724
  275.6 1.2 copy-start

commit v9 on v8

--- a/solution.py
+++ b/solution.py
@@ -21,7 +21,8 @@
 CHUNKS = 2
 CHUNK = INNER // CHUNKS
 STEPS = 2
-STEP = INNER // STEPS
+STEP = CHUNK // STEPS
+SPARE = 8
 
 
 def optics(padded_side):
@@ -71,8 +72,8 @@
         inverse[:, :, at] = (c, s) if part == 0 else (-s, c)
     forward = forward.reshape(-1, 2, CHUNKS, CHUNK // 8, 8).transpose(2, 0, 3, 1, 4)
     forward = np.concatenate(split16(forward.reshape(CHUNKS, len(rows), 2 * CHUNK)), axis=1)
-    inverse = inverse.reshape(2, STEPS, STEP, -1).transpose(1, 0, 2, 3)
-    high, low = split16(inverse.reshape(STEPS, 2 * STEP, len(rows)))
+    inverse = inverse.reshape(2, CHUNKS * STEPS, STEP, -1).transpose(1, 0, 2, 3)
+    high, low = split16(inverse.reshape(CHUNKS * STEPS, 2 * STEP, len(rows)))
     inverse = np.concatenate([high, high, low], axis=2)
     inverse = np.pad(inverse, ((0, 0), (0, 0), (0, -3 * len(rows) % 16)))
     return forward, inverse
@@ -303,18 +304,17 @@
             largest = [jnp.maximum(a, b) for a, b in zip(largest[0::2], largest[1::2])]
         top[...] = jnp.maximum(top[...], largest[0])
 
-    def copies_out(slot, part):
-        size = STEP // 2
-        here = pl.ds(part * size, size)
-        there = pl.ds(slot * STEP + part * size, size)
-        return [
-            pltpu.make_async_copy(
-                near.at[slot, place[0] ^ j, :, :, here],
-                piece.at[:, :, there],
-                out_sems.at[(slot * 2 + part) * count + j],
-            )
-            for j, piece in enumerate(pieces)
-        ]
+    def copies_out(slot):
+        copies = []
+        for j, piece in enumerate(pieces):
+            for part in range(2):
+                for block in range(per_dest):
+                    at = part * per_dest + block
+                    rows = pl.ds(at * CHUNK + slot * STEP, STEP)
+                    sem = out_sems.at[(slot * count + j) * 2 * per_dest + at]
+                    source_rows = near.at[slot, place[0] ^ j, part, block]
+                    copies.append(pltpu.make_async_copy(source_rows, piece.at[rows], sem))
+        return copies
 
     @pl.when(now == 0)
     def _():
@@ -327,27 +327,23 @@
 
         @pl.when(now == step)
         def _():
-            tiles, products = STEP // 16, RES // many // 2
+            tiles, products = STEP // 8, RES // many
             steps = min(tiles, products)
 
-            for part in range(2):
-
-                @pl.loop(part * steps, (part + 1) * steps)
-                def _(t):
-                    for item in range(tiles // steps):
-                        butterflies(t * (tiles // steps) + item, step - 1)
-                    if step < STEPS:
-                        for item in range(products // steps):
-                            product(t * (products // steps) + item, step)
-
-                for copy in copies_out(step - 1, part):
-                    copy.start()
-
+            @pl.loop(0, steps)
+            def _(t):
+                for item in range(tiles // steps):
+                    butterflies(t * (tiles // steps) + item, step - 1)
+                if step < STEPS:
+                    for item in range(products // steps):
+                        product(t * (products // steps) + item, step)
+
+            for copy in copies_out(step - 1):
+                copy.start()
             if step == STEPS:
                 for slot in range(STEPS):
-                    for part in range(2):
-                        for copy in copies_out(slot, part):
-                            copy.wait()
+                    for copy in copies_out(slot):
+                        copy.wait()
 
 
 def line_kernel(
@@ -505,16 +501,41 @@
     return (near_real * level + near_imag * lift, near_imag * level - near_real * lift)
 
 
-def encode_kernel(count, place, top, *refs):
-    pieces, (slm_real, slm_imag, tile_real, tile_imag, sems) = refs[:count], refs[count:]
-    blocks, height, width = pieces[0].shape[1:]
-    peak_sq = jnp.full((1, width), top[0], jnp.float32)
-    cell = lax.broadcasted_iota(jnp.int32, (height, width), 0)
-    cell = cell + lax.broadcasted_iota(jnp.int32, (height, width), 1)
+def stamp_kernel(peak_sq, *refs):
+    count = (len(refs) - 2) // 2
+    pieces, tile, sems = refs[count : 2 * count], refs[-2], refs[-1]
+    tile[...] = jnp.full(tile.shape, peak_sq[0], jnp.float32)
+    copies = []
+    for j, piece in enumerate(pieces):
+        rows = pl.ds(piece.shape[0] - SPARE, SPARE)
+        copies.append(pltpu.make_async_copy(tile, piece.at[rows], sems.at[j]))
+    for copy in copies:
+        copy.start()
+    for copy in copies:
+        copy.wait()
+
+
+def encode_kernel(count, place, peak_sq, *refs):
+    pieces, (slm_real, slm_imag, *refs) = refs[: CHUNKS * count], refs[CHUNKS * count :]
+    own, (tile_real, tile_imag, own_sems, sems) = refs[:CHUNKS], refs[CHUNKS:]
+    blocks, width = tile_real.shape[0], pieces[0].shape[-1]
+    fetches = [
+        pltpu.make_async_copy(pieces[chunk * count], own[chunk], own_sems.at[chunk])
+        for chunk in range(CHUNKS)
+    ]
+    for fetch in fetches:
+        fetch.start()
+    top = jnp.full((1, width), peak_sq[0], jnp.float32)
+    for piece in pieces[(CHUNKS - 1) * count + 1 :]:
+        top = jnp.maximum(top, piece[pl.ds(piece.shape[0] - SPARE, 1), :])
+    cell = lax.broadcasted_iota(jnp.int32, (CHUNK, width), 0)
+    cell = cell + lax.broadcasted_iota(jnp.int32, (CHUNK, width), 1)
     cell_sign = (1 - 2 * (cell & 1)).astype(jnp.float32)
+    for fetch in fetches:
+        fetch.wait()
 
     def copies_out(block):
-        rows = pl.ds(block * height, height)
+        rows = pl.ds(block * INNER, INNER)
         return [
             pltpu.make_async_copy(tile.at[block], slm.at[rows], sems.at[2 * block + part])
             for part, (tile, slm) in enumerate(((tile_real, slm_real), (tile_imag, slm_imag)))
@@ -522,10 +543,15 @@
 
     @pl.loop(0, blocks)
     def _(block):
-        for j, piece in enumerate(pieces):
+        for at in range(CHUNKS * count):
+            chunk, j = divmod(at, count)
+            piece = pieces[at] if j else own[chunk]
             lanes = pl.ds(pl.multiple_of((place[0] ^ j) * width, width), width)
-            tile_real[block, :, lanes], tile_imag[block, :, lanes] = encode(
-                piece[0, block], piece[1, block], peak_sq, cell_sign
+            rows = pl.ds(chunk * CHUNK, CHUNK)
+            real = pl.ds(pl.multiple_of(block * CHUNK, CHUNK), CHUNK)
+            imag = pl.ds(pl.multiple_of((blocks + block) * CHUNK, CHUNK), CHUNK)
+            tile_real[block, rows, lanes], tile_imag[block, rows, lanes] = encode(
+                piece[real, :], piece[imag, :], top, cell_sign
             )
         for copy in copies_out(block):
             copy.start()
@@ -690,42 +716,67 @@
     lines = lax.all_to_all(lines, ("row", "col"), split_axis=0, concat_axis=0, tiled=True)
     lines = lines.reshape(RES, total_rows, width)
 
-    piece = (2, blocks, INNER, width)
-    piece_shape = jax.ShapeDtypeStruct(piece, jnp.float32)
-    *near, top = pl.pallas_call(
-        partial(column_inverse_kernel, row_total),
-        grid=(STEPS + 1,),
-        in_specs=[
-            whole(pltpu.SMEM),
-            anywhere,
-            pl.BlockSpec((STEP, 128), lambda i: (jnp.maximum(i - 1, 0), 0)),
-            pl.BlockSpec((1,) + inv_col.shape[1:], lambda i: (jnp.minimum(i, STEPS - 1), 0, 0)),
+    near, tops = [], []
+    for chunk in range(CHUNKS):
+        spare = SPARE if chunk == CHUNKS - 1 else 0
+        piece_shape = jax.ShapeDtypeStruct((2 * blocks * CHUNK + spare, width), jnp.float32)
+        steps = slice(chunk * STEPS, (chunk + 1) * STEPS)
+        *pieces, top = pl.pallas_call(
+            partial(column_inverse_kernel, row_total),
+            grid=(STEPS + 1,),
+            in_specs=[
+                whole(pltpu.SMEM),
+                anywhere,
+                pl.BlockSpec((STEP, 128), lambda i: (chunk * STEPS + jnp.maximum(i - 1, 0), 0)),
+                pl.BlockSpec((1,) + inv_col.shape[1:], lambda i: (jnp.minimum(i, STEPS - 1), 0, 0)),
+            ],
+            out_specs=[anywhere] * row_total + [whole()],
+            out_shape=[piece_shape] * row_total + [jax.ShapeDtypeStruct((8, width), jnp.float32)],
+            scratch_shapes=[
+                pltpu.VMEM((STEPS, row_total, 2, blocks, STEP, width), jnp.float32),
+                pltpu.VMEM((RES, total_rows, width), jnp.float32),
+                pltpu.VMEM((RES // many, inv_col.shape[2], many * width), jnp.bfloat16),
+                pltpu.VMEM((STEPS, RES, 2 * STEP, width), jnp.float32),
+                pltpu.SemaphoreType.DMA((RES // many,)),
+                pltpu.SemaphoreType.DMA((STEPS * row_total * 2 * blocks,)),
+            ],
+            compiler_params=params(56),
+            cost_estimate=cost(60),
+            name="column_inverse",
+        )(place_row, lines, twist_col, inv_col[steps])
+        near.append(pieces)
+        tops.append(top)
+    near[0] = exchange(near[0], "row")
+    peak_sq = jnp.max(jnp.maximum(*tops))
+    shift = 1
+    while shift < col_total:
+        partner = [(i, i ^ shift) for i in range(col_total)]
+        peak_sq = jnp.maximum(peak_sq, lax.ppermute(peak_sq, "col", partner))
+        shift *= 2
+    near = lax.optimization_barrier(near)
+    peak_own = peak_sq.reshape(1)
+    others = row_total - 1
+    near[1][1:] = pl.pallas_call(
+        stamp_kernel,
+        in_specs=[whole(pltpu.SMEM)] + [anywhere] * others,
+        out_specs=[anywhere] * others,
+        out_shape=[piece_shape] * others,
+        scratch_shapes=[
+            pltpu.VMEM((SPARE, width), jnp.float32),
+            pltpu.SemaphoreType.DMA((others,)),
         ],
-        out_specs=[anywhere] * row_total + [whole()],
-        out_shape=[piece_shape] * row_total + [jax.ShapeDtypeStruct((8, width), jnp.float32)],
-        scratch_shapes=[
-            pltpu.VMEM((STEPS, row_total, 2, blocks, STEP, width), jnp.float32),
-            pltpu.VMEM((RES, total_rows, width), jnp.float32),
-            pltpu.VMEM((RES // many, inv_col.shape[2], many * width), jnp.bfloat16),
-            pltpu.VMEM((STEPS, RES, 2 * STEP, width), jnp.float32),
-            pltpu.SemaphoreType.DMA((RES // many,)),
-            pltpu.SemaphoreType.DMA((2 * STEPS * row_total,)),
-        ],
+        input_output_aliases={1 + j: j for j in range(others)},
         compiler_params=params(56),
-        name="column_inverse",
-    )(place_row, lines, twist_col, inv_col)
-
-    near = exchange(near, "row")
-    peak_sq = jnp.max(top)
-    for axis, total in (("col", col_total), ("row", row_total)):
-        shift = 1
-        while shift < total:
-            partner = [(i, i ^ shift) for i in range(total)]
-            peak_sq = jnp.maximum(peak_sq, lax.ppermute(peak_sq, axis, partner))
-            shift *= 2
+        name="stamp",
+    )(peak_own, *near[1][1:])
+    near[1] = exchange(near[1], "row")
     if width != 128:
-        near = jnp.take(jnp.stack(near), jnp.arange(row_total) ^ place_row[0], axis=0)
-        near = near.transpose(1, 2, 3, 0, 4).reshape(2, height, tile_width)
+        for piece in near[1][1:]:
+            peak_sq = jnp.maximum(peak_sq, piece[-1, 0])
+        near = jnp.stack([jnp.stack([piece[: 2 * blocks * CHUNK] for piece in pieces]) for pieces in near])
+        near = jnp.take(near, jnp.arange(row_total) ^ place_row[0], axis=1)
+        near = near.reshape(CHUNKS, row_total, 2, blocks, CHUNK, width)
+        near = near.transpose(2, 3, 0, 4, 1, 5).reshape(2, height, tile_width)
         odd_cell = (jnp.arange(height)[:, None] + jnp.arange(tile_width)[None, :]) % 2
         cell_sign = (1 - 2 * odd_cell).astype(jnp.float32)
         return encode(near[0], near[1], peak_sq, cell_sign)
@@ -733,13 +784,14 @@
     tile = pltpu.VMEM((blocks, INNER, tile_width), jnp.float32)
     return pl.pallas_call(
         partial(encode_kernel, row_total),
-        in_specs=[whole(pltpu.SMEM)] * 2 + [whole()] * row_total,
+        in_specs=[whole(pltpu.SMEM)] * 2 + ([anywhere] + [whole()] * others) * CHUNKS,
         out_specs=[anywhere] * 2,
         out_shape=[tile_shape, tile_shape],
-        scratch_shapes=[tile, tile, pltpu.SemaphoreType.DMA((2 * blocks,))],
+        scratch_shapes=[pltpu.VMEM(pieces[0].shape, jnp.float32) for pieces in near]
+        + [tile, tile, pltpu.SemaphoreType.DMA((CHUNKS,)), pltpu.SemaphoreType.DMA((2 * blocks,))],
         compiler_params=params(16),
         name="encode",
-    )(place_row, peak_sq.reshape(1), *near)
+    )(place_row, peak_own, *near[0], *near[1])
 
 
 def solution(mesh):

time: 280 us -> 278 us (level)
  starting transfers between devices: 54.3 us -> 25.9 us
  waiting for transfers between devices: 95.8 us -> 114 us
  Pallas kernels: 54.2 us -> 63 us
    ppermute x5 -> x3, starting transfers between devices: 34.7 us -> 2.74 us  [body(): peak_sq = jnp.maximum(peak_sq, lax.ppermute(peak_sq, 'col', partner))]
    ppermute x9 -> x12, waiting for transfers between devices: 29.6 us -> 50.6 us  [exchange(): lax.ppermute(pieces[j], axis, [(i, i ^ j) for i in range(total)])]
    pallas_call x1 -> x2, Pallas kernels: 11.4 us -> 19.6 us  [body(): pl.pallas_call(partial(column_inverse_kernel, row_total), grid=(STEPS + 1...]
    ppermute x9 -> x12, starting transfers between devices: 14.6 us -> 18.1 us  [exchange(): lax.ppermute(pieces[j], axis, [(i, i ^ j) for i in range(total)])]
    ppermute x5 -> x3, waiting for transfers between devices: 9.37 us -> 6.43 us  [body(): peak_sq = jnp.maximum(peak_sq, lax.ppermute(peak_sq, 'col', partner))]
  transfers between devices with their start and end apart: 15 -> 16, of which waited for: 10 -> 10; matrix products, arithmetic and copies ran while one was open for 1% -> 1% of each run, Pallas kernels for 6% -> 9%
where the time goes in v9:
time: 278 us; the launch traced here: 277 us
  waiting for transfers between devices  114 us (41%)
  blocking collectives  67.6 us (24%)
  Pallas kernels  63 us (23%)
  starting transfers between devices  25.9 us (9%)
  between operations  3.61 us (1%)
    all_to_all x1, blocking collectives, body(): lax.all_to_all(lines, ('row', 'col'), split_axis=0, concat_axis=0, tiled=...  67.6 us
    all_to_all x1, waiting for transfers between devices, body(): lax.all_to_all(lines, ('row', 'col'), split_axis=0, concat_axis=0, tiled=...  56.8 us
    ppermute x12, waiting for transfers between devices, exchange(): lax.ppermute(pieces[j], axis, [(i, i ^ j) for i in range(total)])  50.6 us
    pallas_call x2, Pallas kernels, body(): pl.pallas_call(partial(column_inverse_kernel, row_total), grid=(STEPS + 1...  19.6 us
    ppermute x12, starting transfers between devices, exchange(): lax.ppermute(pieces[j], axis, [(i, i ^ j) for i in range(total)])  18.1 us
    pallas_call x2, Pallas kernels, body(): pl.pallas_call(partial(column_forward_kernel, row_total), in_specs=[whole...  14.3 us
    pallas_call x1, Pallas kernels, body(): pl.pallas_call(partial(line_kernel, order, own, tail), grid=(-(-own // at...  13.2 us
    pallas_call x1, Pallas kernels, body(): pl.pallas_call(gain_kernel, grid=(own,), in_specs=[whole(pltpu.SMEM)], ou...  6.67 us
  transfers between devices with their start and end apart: 16, of which 10 were waited for; matrix products, arithmetic and copies ran while one was open for 1% of the time, Pallas kernels for 9%

profile of v9, /device:TPU:0, one launch (start us, length us, event | category | flops | bytes accessed | tf_op | source)
XLA Modules:
  0.0 277.1 jit_solution(15886264729911049799)
XLA Ops:
  0.6 2.9 %pack.3 = (f32[2,4,128,128]{3,2,1,0:T(8,128)}, f32[2,4,128,128]{3,2,1,0:T(8,128)}, f32[2,4,128,128]{3,2,1,0:T(8,128)}, f32[2,4,128,128]{3,2,1,0:T(8,128)}) custom-call(s32[1]{0:T(128)} %bitcast.place, f32[4,256,512]{2,1,0:T(8,128)} %bitcast.5, f32[4,256,512]{2,1,0:T(8,128)} %bitcast.7), custom_call_target="tpu_custom_call" | custom-call | bytes 4194304 | tf_op jit(solution)/shard_map/pack/pallas_call | solution.py:649
  3.6 3.0 %collective-permute-start.3 = (f32[2,4,128,128]{3,2,1,0:T(8,128)}, f32[2,4,128,128]{3,2,1,0:T(8,128)S(1)}, u32[]{:S(2)}, u32[]{:S(2)}) collective-permute-start(f32[2,4,128,128]{3,2,1,0:T(8,128)} %get-tuple-element.38), channel_id=1, source_target_pairs={{0,8},{8,0},{16,24},{24,16},{1,9},{9,1},{17,25},{25,17},{2,10},{10... | collective-permute-start | bytes 1572872 | tf_op jit(solution)/shard_map/ppermute | solution.py:585
  6.6 1.5 collective-permute-start.4
  8.1 0.1 collective-permute-start.5
  8.2 3.0 %pack.2 = (f32[2,4,128,128]{3,2,1,0:T(8,128)}, f32[2,4,128,128]{3,2,1,0:T(8,128)}, f32[2,4,128,128]{3,2,1,0:T(8,128)}, f32[2,4,128,128]{3,2,1,0:T(8,128)}) custom-call(s32[1]{0:T(128)} %bitcast.place, f32[4,256,512]{2,1,0:T(8,128)} %bitcast.6, f32[4,256,512]{2,1,0:T(8,128)} %bitcast.8), custom_call_target="tpu_custom_call" | custom-call | bytes 4194304 | tf_op jit(solution)/shard_map/pack/pallas_call | solution.py:649
  11.1 1.9 collective-permute-start
  13.1 1.5 collective-permute-start.1
  14.6 5.0 %collective-permute-done.3.refs_1_ = f32[2,4,128,128]{3,2,1,0:T(8,128)S(1)} collective-permute-done((f32[2,4,128,128]{3,2,1,0:T(8,128)}, f32[2,4,128,128]{3,2,1,0:T(8,128)S(1)}, u32[]{:S(2)}, u32[]{:S(2)}) %collective-permute-start.3) | collective-permute-done | bytes 524320 | tf_op jit(solution)/shard_map/ppermute | solution.py:585
  19.5 3.0 %collective-permute-start.2 = (f32[2,4,128,128]{3,2,1,0:T(8,128)}, f32[2,4,128,128]{3,2,1,0:T(8,128)S(1)}, u32[]{:S(2)}, u32[]{:S(2)}) collective-permute-start(f32[2,4,128,128]{3,2,1,0:T(8,128)} %get-tuple-element.36), channel_id=1, source_target_pairs={{0,24},{8,16},{16,8},{24,0},{1,25},{9,17},{17,9},{25,1},{2,26},{10... | collective-permute-start | bytes 1572872 | tf_op jit(solution)/shard_map/ppermute | solution.py:585
  22.5 10.3 %collective-permute-done.4.refs_2_ = f32[2,4,128,128]{3,2,1,0:T(8,128)S(1)} collective-permute-done((f32[2,4,128,128]{3,2,1,0:T(8,128)}, f32[2,4,128,128]{3,2,1,0:T(8,128)S(1)}, u32[]{:S(2)}, u32[]{:S(2)}) %collective-permute-start.4) | collective-permute-done | bytes 524320 | tf_op jit(solution)/shard_map/ppermute | solution.py:585
  32.9 0.0 collective-permute-done.5.refs_3_
  32.9 0.0 copy-done.3
  32.9 0.0 copy-done.10
  32.9 0.0 copy-done.12
  32.9 0.0 copy-start.2
  32.9 0.0 copy-start.9
  32.9 0.0 copy-start.11
  32.9 6.7 %column_forward.2.refs_4_ = f32[32,168,128]{2,1,0:T(8,128)S(1)} custom-call(s32[1]{0:T(128)} %bitcast.place, f32[128,128]{1,0:T(8,128)S(1)} %copy-done.12, bf16[336,256]{1,0:T(8,128)(2,1)S(1)} %copy-done.10, f32[2,4,128,128]{3,2,1,0:T(8,128)S(1)} %copy-done.3, f32[2,4,128,128]{3,2,1,0:T(8,128)S(1)} %collective-permute-done.3.refs_1_, ...), custom_call_target="tpu_custom_call" | custom-call | bytes 20971520 | tf_op jit(solution)/shard_map/column_forward/pallas_call | solution.py:671
  39.6 2.5 collective-permute-done.refs_1_
  42.1 11.8 %collective-permute-done.1.refs_2_ = f32[2,4,128,128]{3,2,1,0:T(8,128)S(1)} collective-permute-done((f32[2,4,128,128]{3,2,1,0:T(8,128)}, f32[2,4,128,128]{3,2,1,0:T(8,128)S(1)}, u32[]{:S(2)}, u32[]{:S(2)}) %collective-permute-start.1) | collective-permute-done | bytes 524320 | tf_op jit(solution)/shard_map/ppermute | solution.py:585
  53.9 0.0 collective-permute-done.2.refs_3_
  53.9 0.0 copy-done.2
  53.9 0.0 copy-done.9
  53.9 0.0 copy-done.11
  53.9 7.6 %column_forward.3 = f32[32,168,128]{2,1,0:T(8,128)} custom-call(s32[1]{0:T(128)} %bitcast.place, f32[128,128]{1,0:T(8,128)S(1)} %copy-done.11, bf16[336,256]{1,0:T(8,128)(2,1)S(1)} %copy-done.9, f32[2,4,128,128]{3,2,1,0:T(8,128)S(1)} %copy-done.2, f32[2,4,128,128]{3,2,1,0:T(8,128)S(1)} %collective-permute-done.refs_1_, ...), custom_call_target="tpu_custom_call" | custom-call | bytes 20971520 | tf_op jit(solution)/shard_map/column_forward/pallas_call | solution.py:671
  61.5 0.0 copy-start.4
  61.5 0.0 copy-start.5
  61.5 0.0 copy-start.6
  61.5 0.0 copy-start.7
  61.6 0.0 copy-start.8
  61.6 5.0 %all-to-all-start = ((f32[32,168,128]{2,1,0:T(8,128)}), f32[32,168,128]{2,1,0:T(8,128)}, u32[]{:S(2)}, u32[]{:S(2)}) async-start(f32[32,168,128]{2,1,0:T(8,128)} %column_forward.3), calls=%async_computation | async-start | bytes 5505024 | tf_op jit(solution)/shard_map/all_to_all | solution.py:690
  66.6 0.7 pad_add_fusion.place
  67.3 6.7 %gain.1 = (f32[11,256,128]{2,1,0:T(8,128)}, f32[11,256,128]{2,1,0:T(8,128)}) custom-call(s32[2]{0:T(128)} %pad_add_fusion.place), custom_call_target="tpu_custom_call" | custom-call | tf_op jit(solution)/shard_map/gain/pallas_call | solution.py:627
  74.0 56.8 %all-to-all-done.lines = f32[32,168,128]{2,1,0:T(8,128)} async-done(((f32[32,168,128]{2,1,0:T(8,128)}), f32[32,168,128]{2,1,0:T(8,128)}, u32[]{:S(2)}, u32[]{:S(2)}) %all-to-all-start) | async-done | bytes 2752544 | tf_op jit(solution)/shard_map/all_to_all | solution.py:690
  130.8 0.0 copy-done.4
  130.8 0.0 copy-done.5
  130.8 0.0 copy-done.6
  130.8 13.2 %line.1 = f32[32,168,128]{2,1,0:T(8,128)} custom-call(f32[32,168,128]{2,1,0:T(8,128)} %all-to-all-done.lines, f32[11,256,128]{2,1,0:T(8,128)} %get-tuple-element.41.gain_re, f32[11,256,128]{2,1,0:T(8,128)} %get-tuple-element.42.gain_im, f32[2,17,8,256]{3,2,1,0:T(8,128)S(1)} %copy-done.4, bf16[512,256]{1,0:T(8,128)(2,1)S(1)} %copy-done.8, ...), custom_call_target="tpu_custom_call" | custom-call | tf_op jit(solution)/shard_map/line/pallas_call | solution.py:701
  144.0 67.6 %all_to_all.10.source = f32[32,168,128]{2,1,0:T(8,128)} all-to-all(f32[32,168,128]{2,1,0:T(8,128)} %line.1), channel_id=1, replica_groups=mesh['row'=4,'col'=8] {'row','col'}, dimensions={0} | all-to-all | bytes 5505024 | tf_op jit(solution)/shard_map/all_to_all | solution.py:716
  211.7 9.9 %column_inverse.2 = (f32[1024,128]{1,0:T(8,128)}, f32[1024,128]{1,0:T(8,128)}, f32[1024,128]{1,0:T(8,128)}, f32[1024,128]{1,0:T(8,128)}, f32[8,128]{1,0:T(8,128)}) custom-call(s32[1]{0:T(128)} %bitcast.place, f32[32,168,128]{2,1,0:T(8,128)} %all_to_all.10.source, f32[256,128]{1,0:T(8,128)} %constant.73.clone.twist, bf16[2,128,512]{2,1,0:T(8,128)(2,1)} %constant.74.clone.matrix), custom_call_target="tpu_custom_call" | custom-call | bytes 62914560 | tf_op jit(solution)/shard_map/column_inverse/pallas_call | solution.py:724
  221.5 0.1 collective-permute-start.9
  221.6 1.1 collective-permute-start.10
  222.7 2.4 collective-permute-start.11
  225.1 9.8 %column_inverse.3 = (f32[1032,128]{1,0:T(8,128)}, f32[1032,128]{1,0:T(8,128)}, f32[1032,128]{1,0:T(8,128)}, f32[1032,128]{1,0:T(8,128)}, f32[8,128]{1,0:T(8,128)}) custom-call(s32[1]{0:T(128)} %bitcast.place, f32[32,168,128]{2,1,0:T(8,128)} %all_to_all.10.source, f32[256,128]{1,0:T(8,128)} %constant.73.clone.twist, bf16[2,128,512]{2,1,0:T(8,128)(2,1)} %constant.75.clone.matrix), custom_call_target="tpu_custom_call" | custom-call | bytes 62914560 | tf_op jit(solution)/shard_map/column_inverse/pallas_call | solution.py:724
  234.9 1.3 maximum_reduce_fusion
  236.2 0.0 collective-permute-start.6
  236.2 1.2 collective-permute-done.6
  238.7 1.4 collective-permute-start.7
  240.1 2.2 collective-permute-done.7
  243.0 1.4 collective-permute-start.8
  244.4 3.1 %collective-permute-done.8 = f32[]{:T(128)} collective-permute-done((f32[]{:T(128)}, f32[]{:T(128)}, u32[]{:S(2)}, u32[]{:S(2)}) %collective-permute-start.8) | collective-permute-done | bytes 36 | tf_op jit(solution)/shard_map/ppermute | solution.py:754
  248.1 0.0 collective-permute-done.9.refs_1_
  248.1 0.0 collective-permute-done.10.refs_2_
  248.2 0.0 collective-permute-done.11.refs_3_
  248.2 0.6 stamp.1
  248.8 0.3 collective-permute-start.12
  249.1 1.1 collective-permute-start.13
  250.2 2.2 collective-permute-start.14
  252.4 11.7 %collective-permute-done.12.refs_5_ = f32[1032,128]{1,0:T(8,128)S(1)} collective-permute-done((f32[1032,128]{1,0:T(8,128)}, f32[1032,128]{1,0:T(8,128)S(1)}, u32[]{:S(2)}, u32[]{:S(2)}) %collective-permute-start.12) | collective-permute-done | bytes 528416 | tf_op jit(solution)/shard_map/ppermute | solution.py:585
  264.0 9.4 %collective-permute-done.13.refs_6_ = f32[1032,128]{1,0:T(8,128)S(1)} collective-permute-done((f32[1032,128]{1,0:T(8,128)}, f32[1032,128]{1,0:T(8,128)S(1)}, u32[]{:S(2)}, u32[]{:S(2)}) %collective-permute-start.13) | collective-permute-done | bytes 528416 | tf_op jit(solution)/shard_map/ppermute | solution.py:585
  273.4 0.0 collective-permute-done.14.refs_7_
  273.4 0.0 copy-done.1
  273.4 1.0 copy-done
  274.4 2.7 encode.1
  (9 shorter events, 0.0 us)
Async XLA Ops:
  3.6 16.0 %collective-permute-start.3 = (f32[2,4,128,128]{3,2,1,0:T(8,128)}, f32[2,4,128,128]{3,2,1,0:T(8,128)S(1)}, u32[]{:S(2)}, u32[]{:S(2)}) collective-permute-start(f32[2,4,128,128]{3,2,1,0:T(8,128)} %get-tuple-element.38), channel_id=1, source_target_pairs={{0,8},{8,0},{16,24},{24,16},{1,9},{9,1},{17,25},{25,17},{2,10},{10... | collective-permute-start | bytes 1572872 | tf_op jit(solution)/shard_map/ppermute | solution.py:585
  6.6 26.3 %collective-permute-start.4 = (f32[2,4,128,128]{3,2,1,0:T(8,128)}, f32[2,4,128,128]{3,2,1,0:T(8,128)S(1)}, u32[]{:S(2)}, u32[]{:S(2)}) collective-permute-start(f32[2,4,128,128]{3,2,1,0:T(8,128)} %get-tuple-element.39), channel_id=1, source_target_pairs={{0,16},{8,24},{16,0},{24,8},{1,17},{9,25},{17,1},{25,9},{2,18},{10... | collective-permute-start | bytes 1572872 | tf_op jit(solution)/shard_map/ppermute | solution.py:585
  8.1 24.8 %copy-start.3 = (f32[2,4,128,128]{3,2,1,0:T(8,128)S(1)}, f32[2,4,128,128]{3,2,1,0:T(8,128)}, u32[]{:S(2)}) copy-start(f32[2,4,128,128]{3,2,1,0:T(8,128)} %get-tuple-element.37.refs_0_) | copy-start | bytes 1572868
  8.1 24.8 %copy-start.10 = (bf16[336,256]{1,0:T(8,128)(2,1)S(1)}, bf16[336,256]{1,0:T(8,128)(2,1)}, u32[]{:S(2)}) copy-start(bf16[336,256]{1,0:T(8,128)(2,1)} %constant.65.clone.matrix) | copy-start | bytes 516100
  8.1 24.8 %copy-start.12 = (f32[128,128]{1,0:T(8,128)S(1)}, f32[128,128]{1,0:T(8,128)}, u32[]{:S(2)}) copy-start(f32[128,128]{1,0:T(8,128)} %constant.64.clone.twist) | copy-start | bytes 196612
  8.1 24.8 %collective-permute-start.5 = (f32[2,4,128,128]{3,2,1,0:T(8,128)}, f32[2,4,128,128]{3,2,1,0:T(8,128)S(1)}, u32[]{:S(2)}, u32[]{:S(2)}) collective-permute-start(f32[2,4,128,128]{3,2,1,0:T(8,128)} %get-tuple-element.40), channel_id=1, source_target_pairs={{0,24},{8,16},{16,8},{24,0},{1,25},{9,17},{17,9},{25,1},{2,26},{10... | collective-permute-start | bytes 1572872 | tf_op jit(solution)/shard_map/ppermute | solution.py:585
  11.1 30.9 %collective-permute-start = (f32[2,4,128,128]{3,2,1,0:T(8,128)}, f32[2,4,128,128]{3,2,1,0:T(8,128)S(1)}, u32[]{:S(2)}, u32[]{:S(2)}) collective-permute-start(f32[2,4,128,128]{3,2,1,0:T(8,128)} %get-tuple-element.34), channel_id=1, source_target_pairs={{0,8},{8,0},{16,24},{24,16},{1,9},{9,1},{17,25},{25,17},{2,10},{10... | collective-permute-start | bytes 1572872 | tf_op jit(solution)/shard_map/ppermute | solution.py:585
  13.1 40.8 %collective-permute-start.1 = (f32[2,4,128,128]{3,2,1,0:T(8,128)}, f32[2,4,128,128]{3,2,1,0:T(8,128)S(1)}, u32[]{:S(2)}, u32[]{:S(2)}) collective-permute-start(f32[2,4,128,128]{3,2,1,0:T(8,128)} %get-tuple-element.35), channel_id=1, source_target_pairs={{0,16},{8,24},{16,0},{24,8},{1,17},{9,25},{17,1},{25,9},{2,18},{10... | collective-permute-start | bytes 1572872 | tf_op jit(solution)/shard_map/ppermute | solution.py:585
  19.5 34.3 %collective-permute-start.2 = (f32[2,4,128,128]{3,2,1,0:T(8,128)}, f32[2,4,128,128]{3,2,1,0:T(8,128)S(1)}, u32[]{:S(2)}, u32[]{:S(2)}) collective-permute-start(f32[2,4,128,128]{3,2,1,0:T(8,128)} %get-tuple-element.36), channel_id=1, source_target_pairs={{0,24},{8,16},{16,8},{24,0},{1,25},{9,17},{17,9},{25,1},{2,26},{10... | collective-permute-start | bytes 1572872 | tf_op jit(solution)/shard_map/ppermute | solution.py:585
  32.9 21.0 %copy-start.2 = (f32[2,4,128,128]{3,2,1,0:T(8,128)S(1)}, f32[2,4,128,128]{3,2,1,0:T(8,128)}, u32[]{:S(2)}) copy-start(f32[2,4,128,128]{3,2,1,0:T(8,128)} %get-tuple-element.33.refs_0_) | copy-start | bytes 1572868
  32.9 21.0 %copy-start.9 = (bf16[336,256]{1,0:T(8,128)(2,1)S(1)}, bf16[336,256]{1,0:T(8,128)(2,1)}, u32[]{:S(2)}) copy-start(bf16[336,256]{1,0:T(8,128)(2,1)} %constant.67.clone.matrix) | copy-start | bytes 516100
  32.9 21.0 %copy-start.11 = (f32[128,128]{1,0:T(8,128)S(1)}, f32[128,128]{1,0:T(8,128)}, u32[]{:S(2)}) copy-start(f32[128,128]{1,0:T(8,128)} %constant.66.clone.twist) | copy-start | bytes 196612
  61.5 69.3 %copy-start.4 = (f32[2,17,8,256]{3,2,1,0:T(8,128)S(1)}, f32[2,17,8,256]{3,2,1,0:T(8,128)}, u32[]{:S(2)}) copy-start(f32[2,17,8,256]{3,2,1,0:T(8,128)} %constant.68.clone.twist) | copy-start | bytes 835588
  61.5 69.3 %copy-start.5 = (bf16[256,512]{1,0:T(8,128)(2,1)S(1)}, bf16[256,512]{1,0:T(8,128)(2,1)}, u32[]{:S(2)}) copy-start(bf16[256,512]{1,0:T(8,128)(2,1)} %constant.72.clone.inv_low) | copy-start | bytes 786436
  61.5 69.3 %copy-start.6 = (bf16[256,512]{1,0:T(8,128)(2,1)S(1)}, bf16[256,512]{1,0:T(8,128)(2,1)}, u32[]{:S(2)}) copy-start(bf16[256,512]{1,0:T(8,128)(2,1)} %constant.71.clone.inv_high) | copy-start | bytes 786436
  61.5 69.3 %copy-start.7 = (bf16[512,256]{1,0:T(8,128)(2,1)S(1)}, bf16[512,256]{1,0:T(8,128)(2,1)}, u32[]{:S(2)}) copy-start(bf16[512,256]{1,0:T(8,128)(2,1)} %constant.70.clone.fwd_low) | copy-start | bytes 786436
  61.6 69.3 %copy-start.8 = (bf16[512,256]{1,0:T(8,128)(2,1)S(1)}, bf16[512,256]{1,0:T(8,128)(2,1)}, u32[]{:S(2)}) copy-start(bf16[512,256]{1,0:T(8,128)(2,1)} %constant.69.clone.fwd_high) | copy-start | bytes 786436
  61.6 69.2 %all-to-all-start = ((f32[32,168,128]{2,1,0:T(8,128)}), f32[32,168,128]{2,1,0:T(8,128)}, u32[]{:S(2)}, u32[]{:S(2)}) async-start(f32[32,168,128]{2,1,0:T(8,128)} %column_forward.3), calls=%async_computation | async-start | bytes 5505024 | tf_op jit(solution)/shard_map/all_to_all | solution.py:690
  221.5 13.3 %copy-start.13 = (f32[8,128]{1,0:T(8,128)S(1)}, f32[8,128]{1,0:T(8,128)}, u32[]{:S(2)}) copy-start(f32[8,128]{1,0:T(8,128)} %get-tuple-element.43) | copy-start | bytes 12292
  221.5 26.6 %collective-permute-start.9 = (f32[1024,128]{1,0:T(8,128)}, f32[1024,128]{1,0:T(8,128)S(1)}, u32[]{:S(2)}, u32[]{:S(2)}) collective-permute-start(f32[1024,128]{1,0:T(8,128)} %get-tuple-element.46), channel_id=1, source_target_pairs={{0,8},{8,0},{16,24},{24,16},{1,9},{9,1},{17,25},{25,17},{2,10},{10... | collective-permute-start | bytes 1572872 | tf_op jit(solution)/shard_map/ppermute | solution.py:585
  221.6 26.5 %collective-permute-start.10 = (f32[1024,128]{1,0:T(8,128)}, f32[1024,128]{1,0:T(8,128)S(1)}, u32[]{:S(2)}, u32[]{:S(2)}) collective-permute-start(f32[1024,128]{1,0:T(8,128)} %get-tuple-element.47), channel_id=1, source_target_pairs={{0,16},{8,24},{16,0},{24,8},{1,17},{9,25},{17,1},{25,9},{2,18},{10... | collective-permute-start | bytes 1572872 | tf_op jit(solution)/shard_map/ppermute | solution.py:585
  222.7 50.7 %copy-start.1 = (f32[1024,128]{1,0:T(8,128)S(1)}, f32[1024,128]{1,0:T(8,128)}, u32[]{:S(2)}) copy-start(f32[1024,128]{1,0:T(8,128)} %get-tuple-element.53.refs_0_) | copy-start | bytes 1572868
  222.7 25.4 %collective-permute-start.11 = (f32[1024,128]{1,0:T(8,128)}, f32[1024,128]{1,0:T(8,128)S(1)}, u32[]{:S(2)}, u32[]{:S(2)}) collective-permute-start(f32[1024,128]{1,0:T(8,128)} %get-tuple-element.48), channel_id=1, source_target_pairs={{0,24},{8,16},{16,8},{24,0},{1,25},{9,17},{17,9},{25,1},{2,26},{10... | collective-permute-start | bytes 1572872 | tf_op jit(solution)/shard_map/ppermute | solution.py:585
  236.2 1.2 collective-permute-start.6
  238.7 3.6 %collective-permute-start.7 = (f32[]{:T(128)}, f32[]{:T(128)}, u32[]{:S(2)}, u32[]{:S(2)}) collective-permute-start(f32[]{:T(128)} %max.13), channel_id=1, source_target_pairs={{0,2},{1,3},{2,0},{3,1},{4,6},{5,7},{6,4},{7,5},{8,10},{9,11},{10,... | collective-permute-start | bytes 20 | tf_op jit(solution)/shard_map/ppermute | solution.py:754
  243.0 4.5 %collective-permute-start.8 = (f32[]{:T(128)}, f32[]{:T(128)}, u32[]{:S(2)}, u32[]{:S(2)}) collective-permute-start(f32[]{:T(128)} %max.14), channel_id=1, source_target_pairs={{0,4},{1,5},{2,6},{3,7},{4,0},{5,1},{6,2},{7,3},{8,12},{9,13},{10,... | collective-permute-start | bytes 20 | tf_op jit(solution)/shard_map/ppermute | solution.py:754
  248.8 15.2 %collective-permute-start.12 = (f32[1032,128]{1,0:T(8,128)}, f32[1032,128]{1,0:T(8,128)S(1)}, u32[]{:S(2)}, u32[]{:S(2)}) collective-permute-start(f32[1032,128]{1,0:T(8,128)} %get-tuple-element.61), channel_id=1, source_target_pairs={{0,8},{8,0},{16,24},{24,16},{1,9},{9,1},{17,25},{25,17},{2,10},{10... | collective-permute-start | bytes 1585160 | tf_op jit(solution)/shard_map/ppermute | solution.py:585
  249.1 24.3 %collective-permute-start.13 = (f32[1032,128]{1,0:T(8,128)}, f32[1032,128]{1,0:T(8,128)S(1)}, u32[]{:S(2)}, u32[]{:S(2)}) collective-permute-start(f32[1032,128]{1,0:T(8,128)} %get-tuple-element.62), channel_id=1, source_target_pairs={{0,16},{8,24},{16,0},{24,8},{1,17},{9,25},{17,1},{25,9},{2,18},{10... | collective-permute-start | bytes 1585160 | tf_op jit(solution)/shard_map/ppermute | solution.py:585
  250.2 23.2 %collective-permute-start.14 = (f32[1032,128]{1,0:T(8,128)}, f32[1032,128]{1,0:T(8,128)S(1)}, u32[]{:S(2)}, u32[]{:S(2)}) collective-permute-start(f32[1032,128]{1,0:T(8,128)} %get-tuple-element.63), channel_id=1, source_target_pairs={{0,24},{8,16},{16,8},{24,0},{1,25},{9,17},{17,9},{25,1},{2,26},{10... | collective-permute-start | bytes 1585160 | tf_op jit(solution)/shard_map/ppermute | solution.py:585
  273.4 1.0 copy-start

commit v10 on v9

--- a/solution.py
+++ b/solution.py
@@ -20,8 +20,6 @@
 HALF = 40
 CHUNKS = 2
 CHUNK = INNER // CHUNKS
-STEPS = 2
-STEP = CHUNK // STEPS
 SPARE = 8
 
 
@@ -72,8 +70,8 @@
         inverse[:, :, at] = (c, s) if part == 0 else (-s, c)
     forward = forward.reshape(-1, 2, CHUNKS, CHUNK // 8, 8).transpose(2, 0, 3, 1, 4)
     forward = np.concatenate(split16(forward.reshape(CHUNKS, len(rows), 2 * CHUNK)), axis=1)
-    inverse = inverse.reshape(2, CHUNKS * STEPS, STEP, -1).transpose(1, 0, 2, 3)
-    high, low = split16(inverse.reshape(CHUNKS * STEPS, 2 * STEP, len(rows)))
+    inverse = inverse.reshape(2, CHUNKS, CHUNK, -1).transpose(1, 0, 2, 3)
+    high, low = split16(inverse.reshape(CHUNKS, 2 * CHUNK, len(rows)))
     inverse = np.concatenate([high, high, low], axis=2)
     inverse = np.pad(inverse, ((0, 0), (0, 0), (0, -3 * len(rows) % 16)))
     return forward, inverse
@@ -260,20 +258,30 @@
     pieces, (top, near, lines, deep, back, sems, out_sems) = refs[:count], refs[count:]
     width = lines.shape[-1]
     rows_in = lines.shape[1]
-    per_dest = near.shape[3]
+    per_dest = near.shape[2]
     many = deep.shape[-1] // width
-    now = pl.program_id(0)
 
     def copy_in(p):
         part = pl.ds(p * many, many)
         return pltpu.make_async_copy(source.at[part], lines.at[part], sems.at[p])
 
-    def product(p, slot):
-        done = dot16(matrix[0], deep[p])
-        for part in range(many):
-            back[slot, p * many + part] = done[:, part * width : (part + 1) * width]
-
-    def prepare(p):
+    def copies_out(part):
+        size = CHUNK // 2
+        copies = []
+        for j, piece in enumerate(pieces):
+            for at in range(2 * per_dest):
+                here = near.at[place[0] ^ j, at // per_dest, at % per_dest, pl.ds(part * size, size)]
+                there = piece.at[pl.ds(at * CHUNK + part * size, size)]
+                sem = out_sems.at[(part * count + j) * 2 * per_dest + at]
+                copies.append(pltpu.make_async_copy(here, there, sem))
+        return copies
+
+    for p in range(RES // many):
+        copy_in(p).start()
+    top[...] = jnp.zeros_like(top)
+
+    @pl.loop(0, RES // many)
+    def _(p):
         copy_in(p).wait()
         blocks = [lines[p * many + part] for part in range(many)]
         joined = jnp.concatenate(blocks, axis=1) if many > 1 else blocks[0]
@@ -282,21 +290,23 @@
         if deep.shape[1] > 3 * rows_in:
             parts.append(jnp.zeros((deep.shape[1] - 3 * rows_in, many * width), jnp.float32))
         deep[p] = jnp.concatenate(parts, axis=0).astype(jnp.bfloat16)
-        product(p, 0)
-
-    def butterflies(t, slot):
+        done = dot16(matrix[...], deep[p])
+        for part in range(many):
+            back[p * many + part] = done[:, part * width : (part + 1) * width]
+
+    def butterflies(t):
         q0 = pl.multiple_of(t * 8, 8)
         largest = []
 
         def get(u):
-            re = back[slot, u, pl.ds(q0, 8), :]
-            im = back[slot, u, pl.ds(STEP + q0, 8), :]
+            re = back[u, pl.ds(q0, 8), :]
+            im = back[u, pl.ds(CHUNK + q0, 8), :]
             return twisted((re, im), u, -1, column_twist(twist, q0))
 
         def put(n, value):
             dest, block = divmod(n, per_dest)
             rows = pl.ds(q0, 8)
-            near[slot, dest, 0, block, rows, :], near[slot, dest, 1, block, rows, :] = value
+            near[dest, 0, block, rows, :], near[dest, 1, block, rows, :] = value
             largest.append(value[0] * value[0] + value[1] * value[1])
 
         inverse_slabs(get, put)
@@ -304,53 +314,22 @@
             largest = [jnp.maximum(a, b) for a, b in zip(largest[0::2], largest[1::2])]
         top[...] = jnp.maximum(top[...], largest[0])
 
-    def copies_out(slot):
-        copies = []
-        for j, piece in enumerate(pieces):
-            for part in range(2):
-                for block in range(per_dest):
-                    at = part * per_dest + block
-                    rows = pl.ds(at * CHUNK + slot * STEP, STEP)
-                    sem = out_sems.at[(slot * count + j) * 2 * per_dest + at]
-                    source_rows = near.at[slot, place[0] ^ j, part, block]
-                    copies.append(pltpu.make_async_copy(source_rows, piece.at[rows], sem))
-        return copies
-
-    @pl.when(now == 0)
-    def _():
-        for p in range(RES // many):
-            copy_in(p).start()
-        top[...] = jnp.zeros_like(top)
-        pl.loop(0, RES // many)(prepare)
-
-    for step in range(1, STEPS + 1):
-
-        @pl.when(now == step)
-        def _():
-            tiles, products = STEP // 8, RES // many
-            steps = min(tiles, products)
-
-            @pl.loop(0, steps)
-            def _(t):
-                for item in range(tiles // steps):
-                    butterflies(t * (tiles // steps) + item, step - 1)
-                if step < STEPS:
-                    for item in range(products // steps):
-                        product(t * (products // steps) + item, step)
-
-            for copy in copies_out(step - 1):
-                copy.start()
-            if step == STEPS:
-                for slot in range(STEPS):
-                    for copy in copies_out(slot):
-                        copy.wait()
+    for part in range(2):
+        tiles = CHUNK // 16
+        pl.loop(part * tiles, (part + 1) * tiles)(butterflies)
+        for copy in copies_out(part):
+            copy.start()
+    for part in range(2):
+        for copy in copies_out(part):
+            copy.wait()
 
 
 def line_kernel(
-    order, own, tail, lines, gain_re, gain_im, twist, fwd_high, fwd_low, inv_high, inv_low, out, *scratch
+    order, own, tail, lines, gain_re, gain_im, twist, fwd_high, fwd_low, inv_high, inv_low, out, stacked, back
 ):
     half = RES * 8
     at_end = pl.program_id(0) == pl.num_programs(0) - 1
+    tail_at = (own - 1) % gain_re.shape[0] * 16
 
     def line_twist(side):
         def read(k):
@@ -359,8 +338,8 @@
 
         return read
 
-    def forward(group, stacked, sides=(0, 1)):
-        for side in sides:
+    def forward(group, count):
+        for side in range(2):
             waiting = {}
 
             def get(m):
@@ -373,8 +352,8 @@
                 v = (u + RES // 2) % RES
                 if v in waiting:
                     first = min(u, v)
-                    rows = pl.ds(first * 16, 16)
-                    rows_low = pl.ds(half + first * 16, 16)
+                    rows = pl.ds(group * half + first * 16, 16)
+                    rows_low = pl.ds((count + group) * half + first * 16, 16)
                     for part in range(2):
                         item = jnp.concatenate(
                             [waiting[first][part], waiting[first + RES // 2][part]], axis=0
@@ -384,23 +363,23 @@
 
             forward_slabs(get, put)
 
-    def filtered(group, stacked):
-        spec = three_right(stacked[...], half, fwd_high[...], fwd_low[...])
+    def middle(count):
+        rows = count * half
+        spec = three_right(stacked[: 2 * rows], rows, fwd_high[...], fwd_low[...])
         spec_re, spec_im = spec[:, :128], spec[:, 128:]
-        g_re, g_im = gain_re[group], gain_im[group]
+        g_re = gain_re[:count].reshape(rows, 128)
+        g_im = gain_im[:count].reshape(rows, 128)
         mixed = jnp.concatenate(
             [spec_re * g_re - spec_im * g_im, spec_re * g_im + spec_im * g_re], axis=1
         )
-        return jnp.concatenate(high_low(mixed), axis=0)
-
-    def unfold(mixed, back):
-        back[...] = three_right(mixed, half, inv_high[...], inv_low[...])
-
-    def inverse(group, back, sides=(0, 1)):
-        for side in sides:
+        mixed = jnp.concatenate(high_low(mixed), axis=0)
+        back[:rows] = three_right(mixed, rows, inv_high[...], inv_low[...])
+
+    def inverse(group):
+        for side in range(2):
 
             def get(u):
-                rows = pl.ds((u % (RES // 2)) * 16 + (u // (RES // 2)) * 8, 8)
+                rows = pl.ds(group * half + (u % (RES // 2)) * 16 + (u // (RES // 2)) * 8, 8)
                 re = back[rows, pl.ds(side * 128, 128)]
                 im = back[rows, pl.ds(INNER + side * 128, 128)]
                 return twisted((re, im), u, -1, line_twist(side))
@@ -412,32 +391,21 @@
 
             inverse_slabs(get, put)
 
+    def run(count):
+        for group in range(count):
+            forward(group, count)
+        middle(count)
+        for group in range(count):
+            inverse(group)
+
     if tail:
 
         @pl.when(at_end)
         def _():
             for block in range(N // 128):
-                lines[block, 8:12, :] = lines[block, 4:8, :]
-
-    groups = len(scratch) // 2
-
-    stacked, back = scratch[:groups], scratch[groups:]
-
-    def run(count):
-        forward(0, stacked[0])
-        for group in range(count):
-            mixed = filtered(group, stacked[group])
-            if group + 1 < count:
-                forward(group + 1, stacked[group + 1], (0,))
-            if group > 0:
-                inverse(group - 1, back[group - 1], (0,))
-            unfold(mixed, back[group])
-            if group + 1 < count:
-                forward(group + 1, stacked[group + 1], (1,))
-            if group > 0:
-                inverse(group - 1, back[group - 1], (1,))
-        inverse(count - 1, back[count - 1])
-
+                lines[block, tail_at + 8 : tail_at + 12, :] = lines[block, tail_at + 4 : tail_at + 8, :]
+
+    groups = gain_re.shape[0]
     rest = own % groups
     if rest:
         pl.when(jnp.logical_not(at_end))(lambda: run(groups))
@@ -450,7 +418,7 @@
         @pl.when(at_end)
         def _():
             for block in range(N // 128):
-                out[block, 4:8, :] = out[block, 8:12, :]
+                out[block, tail_at + 4 : tail_at + 8, :] = out[block, tail_at + 8 : tail_at + 12, :]
 
 
 def gain_kernel(place, gain_re, gain_im):
@@ -665,6 +633,8 @@
         else:
             pieces = [packed[chunk, j] for j in range(row_total)]
         pieces = exchange(pieces, "row")
+        if chunk == 0:
+            pieces, gain_re, gain_im = lax.optimization_barrier((pieces, gain_re, gain_im))
         rows = slice(chunk * CHUNK, (chunk + 1) * CHUNK)
         slab = pltpu.VMEM((RES // many, 2 * CHUNK, many * width), jnp.bfloat16)
         lines = [
@@ -695,7 +665,7 @@
         lines = lines.reshape(row_total, col_total, own_rows, width).transpose(2, 1, 0, 3)
         lines = lines.reshape(own_rows, N // 128, 128).transpose(1, 0, 2)
 
-    at_once = 2
+    at_once = 4 if tail else 1
     line_grain = pl.BlockSpec((N // 128, 16 * at_once, 128), lambda i: (0, i, 0))
     gain_grain = pl.BlockSpec((at_once, RES * 8, 128), lambda i: (i, 0, 0))
     lines = pl.pallas_call(
@@ -704,8 +674,10 @@
         in_specs=[line_grain, gain_grain, gain_grain] + [whole()] * 5,
         out_specs=line_grain,
         out_shape=jax.ShapeDtypeStruct((N // 128, own_rows, 128), jnp.float32),
-        scratch_shapes=[pltpu.VMEM((2 * RES * 8, 2 * INNER), jnp.bfloat16)] * at_once
-        + [pltpu.VMEM((RES * 8, 2 * INNER), jnp.float32)] * at_once,
+        scratch_shapes=[
+            pltpu.VMEM((at_once * 2 * RES * 8, 2 * INNER), jnp.bfloat16),
+            pltpu.VMEM((at_once * RES * 8, 2 * INNER), jnp.float32),
+        ],
         compiler_params=params(52),
         name="line",
     )(lines, gain_re, gain_im, twist_line, line_fh, line_fl, line_ih, line_il)
@@ -720,30 +692,24 @@
     for chunk in range(CHUNKS):
         spare = SPARE if chunk == CHUNKS - 1 else 0
         piece_shape = jax.ShapeDtypeStruct((2 * blocks * CHUNK + spare, width), jnp.float32)
-        steps = slice(chunk * STEPS, (chunk + 1) * STEPS)
+        rows = slice(chunk * CHUNK, (chunk + 1) * CHUNK)
         *pieces, top = pl.pallas_call(
             partial(column_inverse_kernel, row_total),
-            grid=(STEPS + 1,),
-            in_specs=[
-                whole(pltpu.SMEM),
-                anywhere,
-                pl.BlockSpec((STEP, 128), lambda i: (chunk * STEPS + jnp.maximum(i - 1, 0), 0)),
-                pl.BlockSpec((1,) + inv_col.shape[1:], lambda i: (jnp.minimum(i, STEPS - 1), 0, 0)),
-            ],
+            in_specs=[whole(pltpu.SMEM), anywhere, whole(), whole()],
             out_specs=[anywhere] * row_total + [whole()],
             out_shape=[piece_shape] * row_total + [jax.ShapeDtypeStruct((8, width), jnp.float32)],
             scratch_shapes=[
-                pltpu.VMEM((STEPS, row_total, 2, blocks, STEP, width), jnp.float32),
+                pltpu.VMEM((row_total, 2, blocks, CHUNK, width), jnp.float32),
                 pltpu.VMEM((RES, total_rows, width), jnp.float32),
                 pltpu.VMEM((RES // many, inv_col.shape[2], many * width), jnp.bfloat16),
-                pltpu.VMEM((STEPS, RES, 2 * STEP, width), jnp.float32),
+                pltpu.VMEM((RES, 2 * CHUNK, width), jnp.float32),
                 pltpu.SemaphoreType.DMA((RES // many,)),
-                pltpu.SemaphoreType.DMA((STEPS * row_total * 2 * blocks,)),
+                pltpu.SemaphoreType.DMA((2 * row_total * 2 * blocks,)),
             ],
             compiler_params=params(56),
             cost_estimate=cost(60),
             name="column_inverse",
-        )(place_row, lines, twist_col, inv_col[steps])
+        )(place_row, lines, twist_col[rows], inv_col[chunk])
         near.append(pieces)
         tops.append(top)
     near[0] = exchange(near[0], "row")
@@ -784,7 +750,7 @@
     tile = pltpu.VMEM((blocks, INNER, tile_width), jnp.float32)
     return pl.pallas_call(
         partial(encode_kernel, row_total),
-        in_specs=[whole(pltpu.SMEM)] * 2 + ([anywhere] + [whole()] * others) * CHUNKS,
+        in_specs=[whole(pltpu.SMEM)] * 2 + ([whole(pltpu.HBM)] + [whole()] * others) * CHUNKS,
         out_specs=[anywhere] * 2,
         out_shape=[tile_shape, tile_shape],
         scratch_shapes=[pltpu.VMEM(pieces[0].shape, jnp.float32) for pieces in near]

time: 278 us -> 279 us (level)
  blocking collectives: 67.6 us -> 137 us
  waiting for transfers between devices: 114 us -> 48.8 us
  starting transfers between devices: 25.9 us -> 20.9 us
  Pallas kernels: 63 us -> 65.8 us
    all_to_all x1 -> x2, blocking collectives: 67.6 us -> 137 us  [body(): lax.all_to_all(lines, ('row', 'col'), split_axis=0, concat_axis=0, tiled=...]
    all_to_all x1 -> x0, waiting for transfers between devices: 56.8 us -> none  [body(): lax.all_to_all(lines, ('row', 'col'), split_axis=0, concat_axis=0, tiled=...]
    ppermute x12, waiting for transfers between devices: 50.6 us -> 42.2 us  [exchange(): lax.ppermute(pieces[j], axis, [(i, i ^ j) for i in range(total)])]
    all_to_all x1 -> x0, starting transfers between devices: 5.04 us -> none  [body(): lax.all_to_all(lines, ('row', 'col'), split_axis=0, concat_axis=0, tiled=...]
  transfers between devices with their start and end apart: 16 -> 15, of which waited for: 10 -> 9; matrix products, arithmetic and copies ran while one was open for 1% -> 1% of each run, Pallas kernels for 9% -> 10%
where the time goes in v10:
time: 279 us
  blocking collectives  137 us (49%)
  Pallas kernels  65.8 us (24%)
  waiting for transfers between devices  48.8 us (17%)
  starting transfers between devices  20.9 us (7%)
  between operations  3.58 us (1%)
    all_to_all x2, blocking collectives, body(): lax.all_to_all(lines, ('row', 'col'), split_axis=0, concat_axis=0, tiled=...  137 us
    ppermute x12, waiting for transfers between devices, exchange(): lax.ppermute(pieces[j], axis, [(i, i ^ j) for i in range(total)])  42.2 us
    pallas_call x2, Pallas kernels, body(): pl.pallas_call(partial(column_inverse_kernel, row_total), in_specs=[whole...  19.6 us
    ppermute x12, starting transfers between devices, exchange(): lax.ppermute(pieces[j], axis, [(i, i ^ j) for i in range(total)])  18.1 us
    pallas_call x2, Pallas kernels, body(): pl.pallas_call(partial(column_forward_kernel, row_total), in_specs=[whole...  15.7 us
    pallas_call x1, Pallas kernels, body(): pl.pallas_call(partial(line_kernel, order, own, tail), grid=(-(-own // at...  14.6 us
    pallas_call x1, Pallas kernels, body(): pl.pallas_call(gain_kernel, grid=(own,), in_specs=[whole(pltpu.SMEM)], ou...  6.67 us
    ppermute x3, waiting for transfers between devices, body(): peak_sq = jnp.maximum(peak_sq, lax.ppermute(peak_sq, 'col', partner))  6.58 us
  transfers between devices with their start and end apart: 15, of which 9 were waited for; matrix products, arithmetic and copies ran while one was open for 1% of the time, Pallas kernels for 10%

profile of v10, /device:TPU:0, one launch (start us, length us, event | category | flops | bytes accessed | tf_op | source)
XLA Modules:
  0.0 278.6 jit_solution(16934557053302349196)
XLA Ops:
  0.6 2.9 %pack.3 = (f32[2,4,128,128]{3,2,1,0:T(8,128)}, f32[2,4,128,128]{3,2,1,0:T(8,128)}, f32[2,4,128,128]{3,2,1,0:T(8,128)}, f32[2,4,128,128]{3,2,1,0:T(8,128)}) custom-call(s32[1]{0:T(128)} %bitcast.place, f32[4,256,512]{2,1,0:T(8,128)} %bitcast.5, f32[4,256,512]{2,1,0:T(8,128)} %bitcast.7), custom_call_target="tpu_custom_call" | custom-call | bytes 4194304 | tf_op jit(solution)/shard_map/pack/pallas_call | solution.py:617
  3.6 3.0 %collective-permute-start.3 = (f32[2,4,128,128]{3,2,1,0:T(8,128)}, f32[2,4,128,128]{3,2,1,0:T(8,128)S(1)}, u32[]{:S(2)}, u32[]{:S(2)}) collective-permute-start(f32[2,4,128,128]{3,2,1,0:T(8,128)} %get-tuple-element.44), channel_id=1, source_target_pairs={{0,8},{8,0},{16,24},{24,16},{1,9},{9,1},{17,25},{25,17},{2,10},{10... | collective-permute-start | bytes 1572872 | tf_op jit(solution)/shard_map/ppermute | solution.py:553
  6.6 1.5 collective-permute-start.4
  8.1 0.1 collective-permute-start.5
  8.2 3.0 %pack.2 = (f32[2,4,128,128]{3,2,1,0:T(8,128)}, f32[2,4,128,128]{3,2,1,0:T(8,128)}, f32[2,4,128,128]{3,2,1,0:T(8,128)}, f32[2,4,128,128]{3,2,1,0:T(8,128)}) custom-call(s32[1]{0:T(128)} %bitcast.place, f32[4,256,512]{2,1,0:T(8,128)} %bitcast.6, f32[4,256,512]{2,1,0:T(8,128)} %bitcast.8), custom_call_target="tpu_custom_call" | custom-call | bytes 4194304 | tf_op jit(solution)/shard_map/pack/pallas_call | solution.py:617
  11.2 1.9 collective-permute-start
  13.1 1.5 collective-permute-start.1
  14.6 4.9 %collective-permute-done.3.refs_1_ = f32[2,4,128,128]{3,2,1,0:T(8,128)S(1)} collective-permute-done((f32[2,4,128,128]{3,2,1,0:T(8,128)}, f32[2,4,128,128]{3,2,1,0:T(8,128)S(1)}, u32[]{:S(2)}, u32[]{:S(2)}) %collective-permute-start.3) | collective-permute-done | bytes 524320 | tf_op jit(solution)/shard_map/ppermute | solution.py:553
  19.6 3.0 %collective-permute-start.2 = (f32[2,4,128,128]{3,2,1,0:T(8,128)}, f32[2,4,128,128]{3,2,1,0:T(8,128)S(1)}, u32[]{:S(2)}, u32[]{:S(2)}) collective-permute-start(f32[2,4,128,128]{3,2,1,0:T(8,128)} %get-tuple-element.42), channel_id=1, source_target_pairs={{0,24},{8,16},{16,8},{24,0},{1,25},{9,17},{17,9},{25,1},{2,26},{10... | collective-permute-start | bytes 1572872 | tf_op jit(solution)/shard_map/ppermute | solution.py:553
  22.6 0.7 pad_add_fusion.place
  23.2 6.7 %gain.1 = (f32[11,256,128]{2,1,0:T(8,128)}, f32[11,256,128]{2,1,0:T(8,128)}) custom-call(s32[2]{0:T(128)} %pad_add_fusion.place), custom_call_target="tpu_custom_call" | custom-call | tf_op jit(solution)/shard_map/gain/pallas_call | solution.py:595
  29.9 3.0 %collective-permute-done.4.refs_2_ = f32[2,4,128,128]{3,2,1,0:T(8,128)S(1)} collective-permute-done((f32[2,4,128,128]{3,2,1,0:T(8,128)}, f32[2,4,128,128]{3,2,1,0:T(8,128)S(1)}, u32[]{:S(2)}, u32[]{:S(2)}) %collective-permute-start.4) | collective-permute-done | bytes 524320 | tf_op jit(solution)/shard_map/ppermute | solution.py:553
  32.9 0.0 collective-permute-done.5.refs_3_
  32.9 0.0 copy-done.3
  32.9 0.0 copy-done.6
  32.9 0.0 copy-done.12
  32.9 0.0 copy-start.2
  32.9 0.0 copy-start.5
  32.9 0.0 copy-start.11
  32.9 7.8 %column_forward.2.refs_4_ = f32[32,168,128]{2,1,0:T(8,128)S(1)} custom-call(s32[1]{0:T(128)} %bitcast.place, f32[128,128]{1,0:T(8,128)S(1)} %copy-done.6, bf16[336,256]{1,0:T(8,128)(2,1)S(1)} %copy-done.12, f32[2,4,128,128]{3,2,1,0:T(8,128)S(1)} %copy-done.3, f32[2,4,128,128]{3,2,1,0:T(8,128)S(1)} %collective-permute-done.3.refs_1_, ...), custom_call_target="tpu_custom_call" | custom-call | bytes 20971520 | tf_op jit(solution)/shard_map/column_forward/pallas_call | solution.py:641
  40.7 1.3 collective-permute-done.refs_1_
  42.1 11.8 %collective-permute-done.1.refs_2_ = f32[2,4,128,128]{3,2,1,0:T(8,128)S(1)} collective-permute-done((f32[2,4,128,128]{3,2,1,0:T(8,128)}, f32[2,4,128,128]{3,2,1,0:T(8,128)S(1)}, u32[]{:S(2)}, u32[]{:S(2)}) %collective-permute-start.1) | collective-permute-done | bytes 524320 | tf_op jit(solution)/shard_map/ppermute | solution.py:553
  53.9 0.0 collective-permute-done.2.refs_3_
  53.9 0.0 copy-done.2
  53.9 0.0 copy-done.5
  53.9 0.0 copy-done.11
  53.9 7.9 %column_forward.3 = f32[32,168,128]{2,1,0:T(8,128)S(1)} custom-call(s32[1]{0:T(128)} %bitcast.place, f32[128,128]{1,0:T(8,128)S(1)} %copy-done.5, bf16[336,256]{1,0:T(8,128)(2,1)S(1)} %copy-done.11, f32[2,4,128,128]{3,2,1,0:T(8,128)S(1)} %copy-done.2, f32[2,4,128,128]{3,2,1,0:T(8,128)S(1)} %collective-permute-done.refs_1_, ...), custom_call_target="tpu_custom_call" | custom-call | bytes 20971520 | tf_op jit(solution)/shard_map/column_forward/pallas_call | solution.py:641
  61.8 0.0 copy-start.4
  61.8 0.0 copy-start.7
  61.8 0.0 copy-start.8
  61.9 0.0 copy-start.9
  61.9 0.0 copy-start.10
  61.9 68.9 %all_to_all.10.lines = f32[32,168,128]{2,1,0:T(8,128)} all-to-all(f32[32,168,128]{2,1,0:T(8,128)S(1)} %column_forward.3), channel_id=1, replica_groups=mesh['row'=4,'col'=8] {'row','col'}, dimensions={0} | all-to-all | bytes 5505024 | tf_op jit(solution)/shard_map/all_to_all | solution.py:660
  130.8 0.0 copy-done.4
  130.8 0.0 copy-done.7
  130.8 0.0 copy-done.8
  130.8 0.0 copy-done.9
  130.8 14.6 %line.1 = f32[32,168,128]{2,1,0:T(8,128)} custom-call(f32[32,168,128]{2,1,0:T(8,128)} %all_to_all.10.lines, f32[11,256,128]{2,1,0:T(8,128)} %get-tuple-element.53.gain_re, f32[11,256,128]{2,1,0:T(8,128)} %get-tuple-element.54.gain_im, f32[2,17,8,256]{3,2,1,0:T(8,128)S(1)} %copy-done.4, bf16[512,256]{1,0:T(8,128)(2,1)S(1)} %copy-done.10, ...), custom_call_target="tpu_custom_call" | custom-call | tf_op jit(solution)/shard_map/line/pallas_call | solution.py:671
  145.5 67.6 %all_to_all.11.source = f32[32,168,128]{2,1,0:T(8,128)} all-to-all(f32[32,168,128]{2,1,0:T(8,128)} %line.1), channel_id=1, replica_groups=mesh['row'=4,'col'=8] {'row','col'}, dimensions={0} | all-to-all | bytes 5505024 | tf_op jit(solution)/shard_map/all_to_all | solution.py:688
  213.1 9.8 %column_inverse.2 = (f32[1024,128]{1,0:T(8,128)}, f32[1024,128]{1,0:T(8,128)}, f32[1024,128]{1,0:T(8,128)}, f32[1024,128]{1,0:T(8,128)}, f32[8,128]{1,0:T(8,128)}) custom-call(s32[1]{0:T(128)} %bitcast.place, f32[32,168,128]{2,1,0:T(8,128)} %all_to_all.11.source, f32[128,128]{1,0:T(8,128)} %constant.62.clone.twist, bf16[256,512]{1,0:T(8,128)(2,1)} %constant.71.clone.matrix), custom_call_target="tpu_custom_call" | custom-call | bytes 62914560 | tf_op jit(solution)/shard_map/column_inverse/pallas_call | solution.py:696
  222.9 0.0 copy-start.13
  222.9 0.1 collective-permute-start.9
  223.0 1.1 collective-permute-start.10
  224.1 2.4 collective-permute-start.11
  226.5 9.7 %column_inverse.3 = (f32[1032,128]{1,0:T(8,128)}, f32[1032,128]{1,0:T(8,128)}, f32[1032,128]{1,0:T(8,128)}, f32[1032,128]{1,0:T(8,128)}, f32[8,128]{1,0:T(8,128)}) custom-call(s32[1]{0:T(128)} %bitcast.place, f32[32,168,128]{2,1,0:T(8,128)} %all_to_all.11.source, f32[128,128]{1,0:T(8,128)} %constant.64.clone.twist, bf16[256,512]{1,0:T(8,128)(2,1)} %constant.72.clone.matrix), custom_call_target="tpu_custom_call" | custom-call | bytes 62914560 | tf_op jit(solution)/shard_map/column_inverse/pallas_call | solution.py:696
  236.2 1.3 maximum_reduce_fusion
  237.6 0.0 collective-permute-start.6
  237.6 1.3 collective-permute-done.6
  240.1 1.4 collective-permute-start.7
  241.5 2.2 collective-permute-done.7
  244.3 1.4 collective-permute-start.8
  245.7 3.1 %collective-permute-done.8 = f32[]{:T(128)} collective-permute-done((f32[]{:T(128)}, f32[]{:T(128)}, u32[]{:S(2)}, u32[]{:S(2)}) %collective-permute-start.8) | collective-permute-done | bytes 36 | tf_op jit(solution)/shard_map/ppermute | solution.py:720
  249.4 0.0 collective-permute-done.9.refs_1_
  249.4 0.0 collective-permute-done.10.refs_2_
  249.5 0.0 collective-permute-done.11.refs_3_
  249.5 0.6 stamp.1
  250.1 0.4 collective-permute-start.12
  250.5 1.1 collective-permute-start.13
  251.6 2.1 collective-permute-start.14
  253.7 11.7 %collective-permute-done.12.refs_5_ = f32[1032,128]{1,0:T(8,128)S(1)} collective-permute-done((f32[1032,128]{1,0:T(8,128)}, f32[1032,128]{1,0:T(8,128)S(1)}, u32[]{:S(2)}, u32[]{:S(2)}) %collective-permute-start.12) | collective-permute-done | bytes 528416 | tf_op jit(solution)/shard_map/ppermute | solution.py:553
  265.3 9.4 %collective-permute-done.13.refs_6_ = f32[1032,128]{1,0:T(8,128)S(1)} collective-permute-done((f32[1032,128]{1,0:T(8,128)}, f32[1032,128]{1,0:T(8,128)S(1)}, u32[]{:S(2)}, u32[]{:S(2)}) %collective-permute-start.13) | collective-permute-done | bytes 528416 | tf_op jit(solution)/shard_map/ppermute | solution.py:553
  274.8 0.0 collective-permute-done.14.refs_7_
  274.8 1.0 copy-done
  275.8 2.7 encode.1
  (8 shorter events, 0.0 us)
Async XLA Ops:
  3.6 16.0 %collective-permute-start.3 = (f32[2,4,128,128]{3,2,1,0:T(8,128)}, f32[2,4,128,128]{3,2,1,0:T(8,128)S(1)}, u32[]{:S(2)}, u32[]{:S(2)}) collective-permute-start(f32[2,4,128,128]{3,2,1,0:T(8,128)} %get-tuple-element.44), channel_id=1, source_target_pairs={{0,8},{8,0},{16,24},{24,16},{1,9},{9,1},{17,25},{25,17},{2,10},{10... | collective-permute-start | bytes 1572872 | tf_op jit(solution)/shard_map/ppermute | solution.py:553
  6.6 26.3 %collective-permute-start.4 = (f32[2,4,128,128]{3,2,1,0:T(8,128)}, f32[2,4,128,128]{3,2,1,0:T(8,128)S(1)}, u32[]{:S(2)}, u32[]{:S(2)}) collective-permute-start(f32[2,4,128,128]{3,2,1,0:T(8,128)} %get-tuple-element.45), channel_id=1, source_target_pairs={{0,16},{8,24},{16,0},{24,8},{1,17},{9,25},{17,1},{25,9},{2,18},{10... | collective-permute-start | bytes 1572872 | tf_op jit(solution)/shard_map/ppermute | solution.py:553
  8.1 24.8 %copy-start.3 = (f32[2,4,128,128]{3,2,1,0:T(8,128)S(1)}, f32[2,4,128,128]{3,2,1,0:T(8,128)}, u32[]{:S(2)}) copy-start(f32[2,4,128,128]{3,2,1,0:T(8,128)} %get-tuple-element.49.refs_0_) | copy-start | bytes 1572868
  8.1 24.8 %copy-start.6 = (f32[128,128]{1,0:T(8,128)S(1)}, f32[128,128]{1,0:T(8,128)}, u32[]{:S(2)}) copy-start(f32[128,128]{1,0:T(8,128)} %constant.62.clone.twist) | copy-start | bytes 196612
  8.1 24.8 %copy-start.12 = (bf16[336,256]{1,0:T(8,128)(2,1)S(1)}, bf16[336,256]{1,0:T(8,128)(2,1)}, u32[]{:S(2)}) copy-start(bf16[336,256]{1,0:T(8,128)(2,1)} %constant.63.clone.matrix) | copy-start | bytes 516100
  8.1 24.8 %collective-permute-start.5 = (f32[2,4,128,128]{3,2,1,0:T(8,128)}, f32[2,4,128,128]{3,2,1,0:T(8,128)}, u32[]{:S(2)}, u32[]{:S(2)}) collective-permute-start(f32[2,4,128,128]{3,2,1,0:T(8,128)} %get-tuple-element.46), channel_id=1, source_target_pairs={{0,24},{8,16},{16,8},{24,0},{1,25},{9,17},{17,9},{25,1},{2,26},{10... | collective-permute-start | bytes 1572872 | tf_op jit(solution)/shard_map/ppermute | solution.py:553
  11.2 30.9 %collective-permute-start = (f32[2,4,128,128]{3,2,1,0:T(8,128)}, f32[2,4,128,128]{3,2,1,0:T(8,128)S(1)}, u32[]{:S(2)}, u32[]{:S(2)}) collective-permute-start(f32[2,4,128,128]{3,2,1,0:T(8,128)} %get-tuple-element.40), channel_id=1, source_target_pairs={{0,8},{8,0},{16,24},{24,16},{1,9},{9,1},{17,25},{25,17},{2,10},{10... | collective-permute-start | bytes 1572872 | tf_op jit(solution)/shard_map/ppermute | solution.py:553
  13.1 40.8 %collective-permute-start.1 = (f32[2,4,128,128]{3,2,1,0:T(8,128)}, f32[2,4,128,128]{3,2,1,0:T(8,128)S(1)}, u32[]{:S(2)}, u32[]{:S(2)}) collective-permute-start(f32[2,4,128,128]{3,2,1,0:T(8,128)} %get-tuple-element.41), channel_id=1, source_target_pairs={{0,16},{8,24},{16,0},{24,8},{1,17},{9,25},{17,1},{25,9},{2,18},{10... | collective-permute-start | bytes 1572872 | tf_op jit(solution)/shard_map/ppermute | solution.py:553
  19.6 34.3 %collective-permute-start.2 = (f32[2,4,128,128]{3,2,1,0:T(8,128)}, f32[2,4,128,128]{3,2,1,0:T(8,128)S(1)}, u32[]{:S(2)}, u32[]{:S(2)}) collective-permute-start(f32[2,4,128,128]{3,2,1,0:T(8,128)} %get-tuple-element.42), channel_id=1, source_target_pairs={{0,24},{8,16},{16,8},{24,0},{1,25},{9,17},{17,9},{25,1},{2,26},{10... | collective-permute-start | bytes 1572872 | tf_op jit(solution)/shard_map/ppermute | solution.py:553
  32.9 21.0 %copy-start.2 = (f32[2,4,128,128]{3,2,1,0:T(8,128)S(1)}, f32[2,4,128,128]{3,2,1,0:T(8,128)}, u32[]{:S(2)}) copy-start(f32[2,4,128,128]{3,2,1,0:T(8,128)} %get-tuple-element.39.refs_0_) | copy-start | bytes 1572868
  32.9 21.0 %copy-start.5 = (f32[128,128]{1,0:T(8,128)S(1)}, f32[128,128]{1,0:T(8,128)}, u32[]{:S(2)}) copy-start(f32[128,128]{1,0:T(8,128)} %constant.64.clone.twist) | copy-start | bytes 196612
  32.9 21.0 %copy-start.11 = (bf16[336,256]{1,0:T(8,128)(2,1)S(1)}, bf16[336,256]{1,0:T(8,128)(2,1)}, u32[]{:S(2)}) copy-start(bf16[336,256]{1,0:T(8,128)(2,1)} %constant.65.clone.matrix) | copy-start | bytes 516100
  61.8 69.0 %copy-start.4 = (f32[2,17,8,256]{3,2,1,0:T(8,128)S(1)}, f32[2,17,8,256]{3,2,1,0:T(8,128)}, u32[]{:S(2)}) copy-start(f32[2,17,8,256]{3,2,1,0:T(8,128)} %constant.66.clone.twist) | copy-start | bytes 835588
  61.8 69.0 %copy-start.7 = (bf16[256,512]{1,0:T(8,128)(2,1)S(1)}, bf16[256,512]{1,0:T(8,128)(2,1)}, u32[]{:S(2)}) copy-start(bf16[256,512]{1,0:T(8,128)(2,1)} %constant.70.clone.inv_low) | copy-start | bytes 786436
  61.8 69.0 %copy-start.8 = (bf16[256,512]{1,0:T(8,128)(2,1)S(1)}, bf16[256,512]{1,0:T(8,128)(2,1)}, u32[]{:S(2)}) copy-start(bf16[256,512]{1,0:T(8,128)(2,1)} %constant.69.clone.inv_high) | copy-start | bytes 786436
  61.9 69.0 %copy-start.9 = (bf16[512,256]{1,0:T(8,128)(2,1)S(1)}, bf16[512,256]{1,0:T(8,128)(2,1)}, u32[]{:S(2)}) copy-start(bf16[512,256]{1,0:T(8,128)(2,1)} %constant.68.clone.fwd_low) | copy-start | bytes 786436
  61.9 69.0 %copy-start.10 = (bf16[512,256]{1,0:T(8,128)(2,1)S(1)}, bf16[512,256]{1,0:T(8,128)(2,1)}, u32[]{:S(2)}) copy-start(bf16[512,256]{1,0:T(8,128)(2,1)} %constant.67.clone.fwd_high) | copy-start | bytes 786436
  222.9 13.3 %copy-start.13 = (f32[8,128]{1,0:T(8,128)S(1)}, f32[8,128]{1,0:T(8,128)}, u32[]{:S(2)}) copy-start(f32[8,128]{1,0:T(8,128)} %get-tuple-element.55) | copy-start | bytes 12292
  222.9 26.5 %collective-permute-start.9 = (f32[1024,128]{1,0:T(8,128)}, f32[1024,128]{1,0:T(8,128)S(1)}, u32[]{:S(2)}, u32[]{:S(2)}) collective-permute-start(f32[1024,128]{1,0:T(8,128)} %get-tuple-element.58), channel_id=1, source_target_pairs={{0,8},{8,0},{16,24},{24,16},{1,9},{9,1},{17,25},{25,17},{2,10},{10... | collective-permute-start | bytes 1572872 | tf_op jit(solution)/shard_map/ppermute | solution.py:553
  223.0 26.4 %collective-permute-start.10 = (f32[1024,128]{1,0:T(8,128)}, f32[1024,128]{1,0:T(8,128)S(1)}, u32[]{:S(2)}, u32[]{:S(2)}) collective-permute-start(f32[1024,128]{1,0:T(8,128)} %get-tuple-element.59), channel_id=1, source_target_pairs={{0,16},{8,24},{16,0},{24,8},{1,17},{9,25},{17,1},{25,9},{2,18},{10... | collective-permute-start | bytes 1572872 | tf_op jit(solution)/shard_map/ppermute | solution.py:553
  224.1 50.7 %copy-start.1 = (f32[1024,128]{1,0:T(8,128)S(1)}, f32[1024,128]{1,0:T(8,128)}, u32[]{:S(2)}) copy-start(f32[1024,128]{1,0:T(8,128)} %get-tuple-element.65.refs_0_) | copy-start | bytes 1572868
  224.1 25.4 %collective-permute-start.11 = (f32[1024,128]{1,0:T(8,128)}, f32[1024,128]{1,0:T(8,128)S(1)}, u32[]{:S(2)}, u32[]{:S(2)}) collective-permute-start(f32[1024,128]{1,0:T(8,128)} %get-tuple-element.60), channel_id=1, source_target_pairs={{0,24},{8,16},{16,8},{24,0},{1,25},{9,17},{17,9},{25,1},{2,26},{10... | collective-permute-start | bytes 1572872 | tf_op jit(solution)/shard_map/ppermute | solution.py:553
  237.6 1.3 collective-permute-start.6
  240.1 3.6 %collective-permute-start.7 = (f32[]{:T(128)}, f32[]{:T(128)}, u32[]{:S(2)}, u32[]{:S(2)}) collective-permute-start(f32[]{:T(128)} %max.13), channel_id=1, source_target_pairs={{0,2},{1,3},{2,0},{3,1},{4,6},{5,7},{6,4},{7,5},{8,10},{9,11},{10,... | collective-permute-start | bytes 20 | tf_op jit(solution)/shard_map/ppermute | solution.py:720
  244.3 4.5 %collective-permute-start.8 = (f32[]{:T(128)}, f32[]{:T(128)}, u32[]{:S(2)}, u32[]{:S(2)}) collective-permute-start(f32[]{:T(128)} %max.14), channel_id=1, source_target_pairs={{0,4},{1,5},{2,6},{3,7},{4,0},{5,1},{6,2},{7,3},{8,12},{9,13},{10,... | collective-permute-start | bytes 20 | tf_op jit(solution)/shard_map/ppermute | solution.py:720
  250.1 15.2 %collective-permute-start.12 = (f32[1032,128]{1,0:T(8,128)}, f32[1032,128]{1,0:T(8,128)S(1)}, u32[]{:S(2)}, u32[]{:S(2)}) collective-permute-start(f32[1032,128]{1,0:T(8,128)} %get-tuple-element.73), channel_id=1, source_target_pairs={{0,8},{8,0},{16,24},{24,16},{1,9},{9,1},{17,25},{25,17},{2,10},{10... | collective-permute-start | bytes 1585160 | tf_op jit(solution)/shard_map/ppermute | solution.py:553
  250.5 24.3 %collective-permute-start.13 = (f32[1032,128]{1,0:T(8,128)}, f32[1032,128]{1,0:T(8,128)S(1)}, u32[]{:S(2)}, u32[]{:S(2)}) collective-permute-start(f32[1032,128]{1,0:T(8,128)} %get-tuple-element.74), channel_id=1, source_target_pairs={{0,16},{8,24},{16,0},{24,8},{1,17},{9,25},{17,1},{25,9},{2,18},{10... | collective-permute-start | bytes 1585160 | tf_op jit(solution)/shard_map/ppermute | solution.py:553
  251.6 23.2 %collective-permute-start.14 = (f32[1032,128]{1,0:T(8,128)}, f32[1032,128]{1,0:T(8,128)S(1)}, u32[]{:S(2)}, u32[]{:S(2)}) collective-permute-start(f32[1032,128]{1,0:T(8,128)} %get-tuple-element.75), channel_id=1, source_target_pairs={{0,24},{8,16},{16,8},{24,0},{1,25},{9,17},{17,9},{25,1},{2,26},{10... | collective-permute-start | bytes 1585160 | tf_op jit(solution)/shard_map/ppermute | solution.py:553
  274.8 1.0 copy-start

commit v11 on v10

--- a/solution.py
+++ b/solution.py
@@ -189,9 +189,13 @@
 
 
 def column_twist(twist, q0):
+    seen = {}
+
     def read(k):
-        rows = pl.ds(q0, 8)
-        return twist[rows, k : k + 1], twist[rows, 64 + k : 65 + k]
+        if k not in seen:
+            rows = pl.ds(q0, 8)
+            seen[k] = twist[rows, k : k + 1], twist[rows, 64 + k : 65 + k]
+        return seen[k]
 
     return read
 
@@ -224,6 +228,7 @@
             @pl.loop(0, CHUNK // 8)
             def _(t):
                 q0 = pl.multiple_of(t * 8, 8)
+                read = column_twist(twist, q0)
 
                 def get(n):
                     source, block = divmod(n, per_source)
@@ -232,7 +237,7 @@
                     return piece[0, block, rows, :], piece[1, block, rows, :]
 
                 def put(u, value):
-                    item = jnp.concatenate(twisted(value, u, 1, column_twist(twist, q0)), axis=0)
+                    item = jnp.concatenate(twisted(value, u, 1, read), axis=0)
                     rows = pl.ds(pl.multiple_of(t * 16, 16), 16)
                     at = (u // many, rows, pl.ds((u % many) * width, width))
                     high[at], low[at] = high_low(item)
@@ -254,8 +259,8 @@
         copy_out(p).wait()
 
 
-def column_inverse_kernel(count, place, source, twist, matrix, *refs):
-    pieces, (top, near, lines, deep, back, sems, out_sems) = refs[:count], refs[count:]
+def column_inverse_kernel(count, place, before, source, twist, matrix, *refs):
+    pieces, (peak_sq, near, lines, deep, back, top, sems, out_sems) = refs[:count], refs[count:]
     width = lines.shape[-1]
     rows_in = lines.shape[1]
     per_dest = near.shape[2]
@@ -280,8 +285,7 @@
         copy_in(p).start()
     top[...] = jnp.zeros_like(top)
 
-    @pl.loop(0, RES // many)
-    def _(p):
+    def prepare(p):
         copy_in(p).wait()
         blocks = [lines[p * many + part] for part in range(many)]
         joined = jnp.concatenate(blocks, axis=1) if many > 1 else blocks[0]
@@ -290,18 +294,30 @@
         if deep.shape[1] > 3 * rows_in:
             parts.append(jnp.zeros((deep.shape[1] - 3 * rows_in, many * width), jnp.float32))
         deep[p] = jnp.concatenate(parts, axis=0).astype(jnp.bfloat16)
+
+    def product(p):
         done = dot16(matrix[...], deep[p])
         for part in range(many):
             back[p * many + part] = done[:, part * width : (part + 1) * width]
 
+    prepare(0)
+
+    @pl.loop(1, RES // many)
+    def _(p):
+        product(p - 1)
+        prepare(p)
+
+    product(RES // many - 1)
+
     def butterflies(t):
         q0 = pl.multiple_of(t * 8, 8)
+        read = column_twist(twist, q0)
         largest = []
 
         def get(u):
             re = back[u, pl.ds(q0, 8), :]
             im = back[u, pl.ds(CHUNK + q0, 8), :]
-            return twisted((re, im), u, -1, column_twist(twist, q0))
+            return twisted((re, im), u, -1, read)
 
         def put(n, value):
             dest, block = divmod(n, per_dest)
@@ -319,17 +335,17 @@
         pl.loop(part * tiles, (part + 1) * tiles)(butterflies)
         for copy in copies_out(part):
             copy.start()
+    peak_sq[0] = jnp.maximum(before[0], jnp.max(top[...]))
     for part in range(2):
         for copy in copies_out(part):
             copy.wait()
 
 
 def line_kernel(
-    order, own, tail, lines, gain_re, gain_im, twist, fwd_high, fwd_low, inv_high, inv_low, out, stacked, back
+    order, own, tail, lines, gain_re, gain_im, twist, fwd_high, fwd_low, inv_high, inv_low, out, *scratch
 ):
     half = RES * 8
     at_end = pl.program_id(0) == pl.num_programs(0) - 1
-    tail_at = (own - 1) % gain_re.shape[0] * 16
 
     def line_twist(side):
         def read(k):
@@ -338,8 +354,8 @@
 
         return read
 
-    def forward(group, count):
-        for side in range(2):
+    def forward(group, stacked, sides=(0, 1)):
+        for side in sides:
             waiting = {}
 
             def get(m):
@@ -352,8 +368,8 @@
                 v = (u + RES // 2) % RES
                 if v in waiting:
                     first = min(u, v)
-                    rows = pl.ds(group * half + first * 16, 16)
-                    rows_low = pl.ds((count + group) * half + first * 16, 16)
+                    rows = pl.ds(first * 16, 16)
+                    rows_low = pl.ds(half + first * 16, 16)
                     for part in range(2):
                         item = jnp.concatenate(
                             [waiting[first][part], waiting[first + RES // 2][part]], axis=0
@@ -363,23 +379,23 @@
 
             forward_slabs(get, put)
 
-    def middle(count):
-        rows = count * half
-        spec = three_right(stacked[: 2 * rows], rows, fwd_high[...], fwd_low[...])
+    def filtered(group, stacked):
+        spec = three_right(stacked[...], half, fwd_high[...], fwd_low[...])
         spec_re, spec_im = spec[:, :128], spec[:, 128:]
-        g_re = gain_re[:count].reshape(rows, 128)
-        g_im = gain_im[:count].reshape(rows, 128)
+        g_re, g_im = gain_re[group], gain_im[group]
         mixed = jnp.concatenate(
             [spec_re * g_re - spec_im * g_im, spec_re * g_im + spec_im * g_re], axis=1
         )
-        mixed = jnp.concatenate(high_low(mixed), axis=0)
-        back[:rows] = three_right(mixed, rows, inv_high[...], inv_low[...])
-
-    def inverse(group):
-        for side in range(2):
+        return jnp.concatenate(high_low(mixed), axis=0)
+
+    def unfold(mixed, back):
+        back[...] = three_right(mixed, half, inv_high[...], inv_low[...])
+
+    def inverse(group, back, sides=(0, 1)):
+        for side in sides:
 
             def get(u):
-                rows = pl.ds(group * half + (u % (RES // 2)) * 16 + (u // (RES // 2)) * 8, 8)
+                rows = pl.ds((u % (RES // 2)) * 16 + (u // (RES // 2)) * 8, 8)
                 re = back[rows, pl.ds(side * 128, 128)]
                 im = back[rows, pl.ds(INNER + side * 128, 128)]
                 return twisted((re, im), u, -1, line_twist(side))
@@ -391,21 +407,32 @@
 
             inverse_slabs(get, put)
 
-    def run(count):
-        for group in range(count):
-            forward(group, count)
-        middle(count)
-        for group in range(count):
-            inverse(group)
-
     if tail:
 
         @pl.when(at_end)
         def _():
             for block in range(N // 128):
-                lines[block, tail_at + 8 : tail_at + 12, :] = lines[block, tail_at + 4 : tail_at + 8, :]
-
-    groups = gain_re.shape[0]
+                lines[block, 8:12, :] = lines[block, 4:8, :]
+
+    groups = len(scratch) // 2
+
+    stacked, back = scratch[:groups], scratch[groups:]
+
+    def run(count):
+        forward(0, stacked[0])
+        for group in range(count):
+            mixed = filtered(group, stacked[group])
+            if group + 1 < count:
+                forward(group + 1, stacked[group + 1], (0,))
+            if group > 0:
+                inverse(group - 1, back[group - 1], (0,))
+            unfold(mixed, back[group])
+            if group + 1 < count:
+                forward(group + 1, stacked[group + 1], (1,))
+            if group > 0:
+                inverse(group - 1, back[group - 1], (1,))
+        inverse(count - 1, back[count - 1])
+
     rest = own % groups
     if rest:
         pl.when(jnp.logical_not(at_end))(lambda: run(groups))
@@ -418,7 +445,7 @@
         @pl.when(at_end)
         def _():
             for block in range(N // 128):
-                out[block, tail_at + 4 : tail_at + 8, :] = out[block, tail_at + 8 : tail_at + 12, :]
+                out[block, 4:8, :] = out[block, 8:12, :]
 
 
 def gain_kernel(place, gain_re, gain_im):
@@ -469,10 +496,10 @@
     return (near_real * level + near_imag * lift, near_imag * level - near_real * lift)
 
 
-def stamp_kernel(peak_sq, *refs):
+def stamp_kernel(peak_one, peak_two, *refs):
     count = (len(refs) - 2) // 2
     pieces, tile, sems = refs[count : 2 * count], refs[-2], refs[-1]
-    tile[...] = jnp.full(tile.shape, peak_sq[0], jnp.float32)
+    tile[...] = jnp.full(tile.shape, jnp.maximum(peak_one[0], peak_two[0]), jnp.float32)
     copies = []
     for j, piece in enumerate(pieces):
         rows = pl.ds(piece.shape[0] - SPARE, SPARE)
@@ -483,7 +510,7 @@
         copy.wait()
 
 
-def encode_kernel(count, place, peak_sq, *refs):
+def encode_kernel(count, place, peak_one, peak_two, *refs):
     pieces, (slm_real, slm_imag, *refs) = refs[: CHUNKS * count], refs[CHUNKS * count :]
     own, (tile_real, tile_imag, own_sems, sems) = refs[:CHUNKS], refs[CHUNKS:]
     blocks, width = tile_real.shape[0], pieces[0].shape[-1]
@@ -493,7 +520,7 @@
     ]
     for fetch in fetches:
         fetch.start()
-    top = jnp.full((1, width), peak_sq[0], jnp.float32)
+    top = jnp.full((1, width), jnp.maximum(peak_one[0], peak_two[0]), jnp.float32)
     for piece in pieces[(CHUNKS - 1) * count + 1 :]:
         top = jnp.maximum(top, piece[pl.ds(piece.shape[0] - SPARE, 1), :])
     cell = lax.broadcasted_iota(jnp.int32, (CHUNK, width), 0)
@@ -633,8 +660,6 @@
         else:
             pieces = [packed[chunk, j] for j in range(row_total)]
         pieces = exchange(pieces, "row")
-        if chunk == 0:
-            pieces, gain_re, gain_im = lax.optimization_barrier((pieces, gain_re, gain_im))
         rows = slice(chunk * CHUNK, (chunk + 1) * CHUNK)
         slab = pltpu.VMEM((RES // many, 2 * CHUNK, many * width), jnp.bfloat16)
         lines = [
@@ -665,7 +690,7 @@
         lines = lines.reshape(row_total, col_total, own_rows, width).transpose(2, 1, 0, 3)
         lines = lines.reshape(own_rows, N // 128, 128).transpose(1, 0, 2)
 
-    at_once = 4 if tail else 1
+    at_once = 2
     line_grain = pl.BlockSpec((N // 128, 16 * at_once, 128), lambda i: (0, i, 0))
     gain_grain = pl.BlockSpec((at_once, RES * 8, 128), lambda i: (i, 0, 0))
     lines = pl.pallas_call(
@@ -674,10 +699,8 @@
         in_specs=[line_grain, gain_grain, gain_grain] + [whole()] * 5,
         out_specs=line_grain,
         out_shape=jax.ShapeDtypeStruct((N // 128, own_rows, 128), jnp.float32),
-        scratch_shapes=[
-            pltpu.VMEM((at_once * 2 * RES * 8, 2 * INNER), jnp.bfloat16),
-            pltpu.VMEM((at_once * RES * 8, 2 * INNER), jnp.float32),
-        ],
+        scratch_shapes=[pltpu.VMEM((2 * RES * 8, 2 * INNER), jnp.bfloat16)] * at_once
+        + [pltpu.VMEM((RES * 8, 2 * INNER), jnp.float32)] * at_once,
         compiler_params=params(52),
         name="line",
     )(lines, gain_re, gain_im, twist_line, line_fh, line_fl, line_ih, line_il)
@@ -688,55 +711,56 @@
     lines = lax.all_to_all(lines, ("row", "col"), split_axis=0, concat_axis=0, tiled=True)
     lines = lines.reshape(RES, total_rows, width)
 
-    near, tops = [], []
+    near, peak_sq = [], jnp.zeros((1,), jnp.float32)
     for chunk in range(CHUNKS):
         spare = SPARE if chunk == CHUNKS - 1 else 0
         piece_shape = jax.ShapeDtypeStruct((2 * blocks * CHUNK + spare, width), jnp.float32)
         rows = slice(chunk * CHUNK, (chunk + 1) * CHUNK)
-        *pieces, top = pl.pallas_call(
+        *pieces, peak_sq = pl.pallas_call(
             partial(column_inverse_kernel, row_total),
-            in_specs=[whole(pltpu.SMEM), anywhere, whole(), whole()],
-            out_specs=[anywhere] * row_total + [whole()],
-            out_shape=[piece_shape] * row_total + [jax.ShapeDtypeStruct((8, width), jnp.float32)],
+            in_specs=[whole(pltpu.SMEM), whole(pltpu.SMEM), anywhere, whole(), whole()],
+            out_specs=[anywhere] * row_total + [whole(pltpu.SMEM)],
+            out_shape=[piece_shape] * row_total + [jax.ShapeDtypeStruct((1,), jnp.float32)],
             scratch_shapes=[
                 pltpu.VMEM((row_total, 2, blocks, CHUNK, width), jnp.float32),
                 pltpu.VMEM((RES, total_rows, width), jnp.float32),
                 pltpu.VMEM((RES // many, inv_col.shape[2], many * width), jnp.bfloat16),
                 pltpu.VMEM((RES, 2 * CHUNK, width), jnp.float32),
+                pltpu.VMEM((8, width), jnp.float32),
                 pltpu.SemaphoreType.DMA((RES // many,)),
                 pltpu.SemaphoreType.DMA((2 * row_total * 2 * blocks,)),
             ],
             compiler_params=params(56),
             cost_estimate=cost(60),
             name="column_inverse",
-        )(place_row, lines, twist_col[rows], inv_col[chunk])
+        )(place_row, peak_sq, lines, twist_col[rows], inv_col[chunk])
         near.append(pieces)
-        tops.append(top)
     near[0] = exchange(near[0], "row")
-    peak_sq = jnp.max(jnp.maximum(*tops))
     shift = 1
     while shift < col_total:
         partner = [(i, i ^ shift) for i in range(col_total)]
-        peak_sq = jnp.maximum(peak_sq, lax.ppermute(peak_sq, "col", partner))
+        peaks = [peak_sq, lax.ppermute(peak_sq, "col", partner)]
         shift *= 2
+        if shift < col_total:
+            peak_sq = jnp.maximum(*peaks)
     near = lax.optimization_barrier(near)
-    peak_own = peak_sq.reshape(1)
     others = row_total - 1
     near[1][1:] = pl.pallas_call(
         stamp_kernel,
-        in_specs=[whole(pltpu.SMEM)] + [anywhere] * others,
+        in_specs=[whole(pltpu.SMEM)] * 2 + [anywhere] * others,
         out_specs=[anywhere] * others,
         out_shape=[piece_shape] * others,
         scratch_shapes=[
             pltpu.VMEM((SPARE, width), jnp.float32),
             pltpu.SemaphoreType.DMA((others,)),
         ],
-        input_output_aliases={1 + j: j for j in range(others)},
+        input_output_aliases={2 + j: j for j in range(others)},
         compiler_params=params(56),
         name="stamp",
-    )(peak_own, *near[1][1:])
+    )(*peaks, *near[1][1:])
     near[1] = exchange(near[1], "row")
     if width != 128:
+        peak_sq = jnp.maximum(*peaks)[0]
         for piece in near[1][1:]:
             peak_sq = jnp.maximum(peak_sq, piece[-1, 0])
         near = jnp.stack([jnp.stack([piece[: 2 * blocks * CHUNK] for piece in pieces]) for pieces in near])
@@ -750,14 +774,14 @@
     tile = pltpu.VMEM((blocks, INNER, tile_width), jnp.float32)
     return pl.pallas_call(
         partial(encode_kernel, row_total),
-        in_specs=[whole(pltpu.SMEM)] * 2 + ([whole(pltpu.HBM)] + [whole()] * others) * CHUNKS,
+        in_specs=[whole(pltpu.SMEM)] * 3 + ([anywhere] + [whole()] * others) * CHUNKS,
         out_specs=[anywhere] * 2,
         out_shape=[tile_shape, tile_shape],
         scratch_shapes=[pltpu.VMEM(pieces[0].shape, jnp.float32) for pieces in near]
         + [tile, tile, pltpu.SemaphoreType.DMA((CHUNKS,)), pltpu.SemaphoreType.DMA((2 * blocks,))],
         compiler_params=params(16),
         name="encode",
-    )(place_row, peak_own, *near[0], *near[1])
+    )(place_row, *peaks, *near[0], *near[1])
 
 
 def solution(mesh):

time: 279 us -> 278 us (level)
  blocking collectives: 137 us -> 67.6 us
  waiting for transfers between devices: 48.8 us -> 116 us
  starting transfers between devices: 20.9 us -> 26 us
    all_to_all x2 -> x1, blocking collectives: 137 us -> 67.6 us  [body(): lax.all_to_all(lines, ('row', 'col'), split_axis=0, concat_axis=0, tiled=...]
    all_to_all x0 -> x1, waiting for transfers between devices: none -> 56.9 us  [body(): lax.all_to_all(lines, ('row', 'col'), split_axis=0, concat_axis=0, tiled=...]
    ppermute x12, waiting for transfers between devices: 42.2 us -> 55.4 us  [exchange(): lax.ppermute(pieces[j], axis, [(i, i ^ j) for i in range(total)])]
    all_to_all x0 -> x1, starting transfers between devices: none -> 5.04 us  [body(): lax.all_to_all(lines, ('row', 'col'), split_axis=0, concat_axis=0, tiled=...]
    pallas_call x2, Pallas kernels: 15.7 us -> 12.8 us  [body(): pl.pallas_call(partial(column_forward_kernel, row_total), in_specs=[whole...]
    ppermute x3, waiting for transfers between devices: 6.58 us -> 3.79 us  [body(): peaks = [peak_sq, lax.ppermute(peak_sq, 'col', partner)]]
  transfers between devices with their start and end apart: 15 -> 16, of which waited for: 9 -> 10; matrix products, arithmetic and copies ran while one was open for 1% -> 0% of each run, Pallas kernels for 10% -> 9%
where the time goes in v11:
time: 278 us
  waiting for transfers between devices  116 us (42%)
  blocking collectives  67.6 us (24%)
  Pallas kernels  63.7 us (23%)
  starting transfers between devices  26 us (9%)
    all_to_all x1, blocking collectives, body(): lax.all_to_all(lines, ('row', 'col'), split_axis=0, concat_axis=0, tiled=...  67.6 us
    all_to_all x1, waiting for transfers between devices, body(): lax.all_to_all(lines, ('row', 'col'), split_axis=0, concat_axis=0, tiled=...  56.9 us
    ppermute x12, waiting for transfers between devices, exchange(): lax.ppermute(pieces[j], axis, [(i, i ^ j) for i in range(total)])  55.4 us
    pallas_call x2, Pallas kernels, body(): pl.pallas_call(partial(column_inverse_kernel, row_total), in_specs=[whole...  20.7 us
    ppermute x12, starting transfers between devices, exchange(): lax.ppermute(pieces[j], axis, [(i, i ^ j) for i in range(total)])  18.1 us
    pallas_call x1, Pallas kernels, body(): pl.pallas_call(partial(line_kernel, order, own, tail), grid=(-(-own // at...  13.2 us
    pallas_call x2, Pallas kernels, body(): pl.pallas_call(partial(column_forward_kernel, row_total), in_specs=[whole...  12.8 us
    pallas_call x1, Pallas kernels, body(): pl.pallas_call(gain_kernel, grid=(own,), in_specs=[whole(pltpu.SMEM)], ou...  6.67 us
  transfers between devices with their start and end apart: 16, of which 10 were waited for; matrix products, arithmetic and copies ran while one was open for 0% of the time, Pallas kernels for 9%

profile of v11, /device:TPU:0, one launch (start us, length us, event | category | flops | bytes accessed | tf_op | source)
XLA Modules:
  0.0 277.7 jit_solution(12030306413569074513)
XLA Ops:
  0.6 2.9 %pack.3 = (f32[2,4,128,128]{3,2,1,0:T(8,128)}, f32[2,4,128,128]{3,2,1,0:T(8,128)}, f32[2,4,128,128]{3,2,1,0:T(8,128)}, f32[2,4,128,128]{3,2,1,0:T(8,128)}) custom-call(s32[1]{0:T(128)} %bitcast.place, f32[4,256,512]{2,1,0:T(8,128)} %bitcast.4, f32[4,256,512]{2,1,0:T(8,128)} %bitcast.6), custom_call_target="tpu_custom_call" | custom-call | bytes 4194304 | tf_op jit(solution)/shard_map/pack/pallas_call | solution.py:644
  3.6 3.0 %collective-permute-start.3 = (f32[2,4,128,128]{3,2,1,0:T(8,128)}, f32[2,4,128,128]{3,2,1,0:T(8,128)S(1)}, u32[]{:S(2)}, u32[]{:S(2)}) collective-permute-start(f32[2,4,128,128]{3,2,1,0:T(8,128)} %get-tuple-element.38), channel_id=1, source_target_pairs={{0,8},{8,0},{16,24},{24,16},{1,9},{9,1},{17,25},{25,17},{2,10},{10... | collective-permute-start | bytes 1572872 | tf_op jit(solution)/shard_map/ppermute | solution.py:580
  6.6 1.5 collective-permute-start.4
  8.1 0.1 collective-permute-start.5
  8.1 3.0 %pack.2 = (f32[2,4,128,128]{3,2,1,0:T(8,128)}, f32[2,4,128,128]{3,2,1,0:T(8,128)}, f32[2,4,128,128]{3,2,1,0:T(8,128)}, f32[2,4,128,128]{3,2,1,0:T(8,128)}) custom-call(s32[1]{0:T(128)} %bitcast.place, f32[4,256,512]{2,1,0:T(8,128)} %bitcast.5, f32[4,256,512]{2,1,0:T(8,128)} %bitcast.7), custom_call_target="tpu_custom_call" | custom-call | bytes 4194304 | tf_op jit(solution)/shard_map/pack/pallas_call | solution.py:644
  11.1 1.9 collective-permute-start
  13.1 1.5 collective-permute-start.1
  14.6 5.0 %collective-permute-done.3.refs_1_ = f32[2,4,128,128]{3,2,1,0:T(8,128)S(1)} collective-permute-done((f32[2,4,128,128]{3,2,1,0:T(8,128)}, f32[2,4,128,128]{3,2,1,0:T(8,128)S(1)}, u32[]{:S(2)}, u32[]{:S(2)}) %collective-permute-start.3) | collective-permute-done | bytes 524320 | tf_op jit(solution)/shard_map/ppermute | solution.py:580
  19.5 3.0 %collective-permute-start.2 = (f32[2,4,128,128]{3,2,1,0:T(8,128)}, f32[2,4,128,128]{3,2,1,0:T(8,128)S(1)}, u32[]{:S(2)}, u32[]{:S(2)}) collective-permute-start(f32[2,4,128,128]{3,2,1,0:T(8,128)} %get-tuple-element.36), channel_id=1, source_target_pairs={{0,24},{8,16},{16,8},{24,0},{1,25},{9,17},{17,9},{25,1},{2,26},{10... | collective-permute-start | bytes 1572872 | tf_op jit(solution)/shard_map/ppermute | solution.py:580
  22.5 10.3 %collective-permute-done.4.refs_2_ = f32[2,4,128,128]{3,2,1,0:T(8,128)S(1)} collective-permute-done((f32[2,4,128,128]{3,2,1,0:T(8,128)}, f32[2,4,128,128]{3,2,1,0:T(8,128)S(1)}, u32[]{:S(2)}, u32[]{:S(2)}) %collective-permute-start.4) | collective-permute-done | bytes 524320 | tf_op jit(solution)/shard_map/ppermute | solution.py:580
  32.9 0.0 collective-permute-done.5.refs_3_
  32.9 0.0 copy-done.3
  32.9 0.0 copy-done.6
  32.9 0.0 copy-done.12
  32.9 0.0 copy-start.2
  32.9 0.0 copy-start.5
  32.9 0.0 copy-start.11
  32.9 5.9 %column_forward.2.refs_4_ = f32[32,168,128]{2,1,0:T(8,128)S(1)} custom-call(s32[1]{0:T(128)} %bitcast.place, f32[128,128]{1,0:T(8,128)S(1)} %copy-done.6, bf16[336,256]{1,0:T(8,128)(2,1)S(1)} %copy-done.12, f32[2,4,128,128]{3,2,1,0:T(8,128)S(1)} %copy-done.3, f32[2,4,128,128]{3,2,1,0:T(8,128)S(1)} %collective-permute-done.3.refs_1_, ...), custom_call_target="tpu_custom_call" | custom-call | bytes 20971520 | tf_op jit(solution)/shard_map/column_forward/pallas_call | solution.py:666
  38.8 3.2 %collective-permute-done.refs_1_ = f32[2,4,128,128]{3,2,1,0:T(8,128)S(1)} collective-permute-done((f32[2,4,128,128]{3,2,1,0:T(8,128)}, f32[2,4,128,128]{3,2,1,0:T(8,128)S(1)}, u32[]{:S(2)}, u32[]{:S(2)}) %collective-permute-start) | collective-permute-done | bytes 524320 | tf_op jit(solution)/shard_map/ppermute | solution.py:580
  42.0 11.8 %collective-permute-done.1.refs_2_ = f32[2,4,128,128]{3,2,1,0:T(8,128)S(1)} collective-permute-done((f32[2,4,128,128]{3,2,1,0:T(8,128)}, f32[2,4,128,128]{3,2,1,0:T(8,128)S(1)}, u32[]{:S(2)}, u32[]{:S(2)}) %collective-permute-start.1) | collective-permute-done | bytes 524320 | tf_op jit(solution)/shard_map/ppermute | solution.py:580
  53.9 0.0 collective-permute-done.2.refs_3_
  53.9 0.0 copy-done.2
  53.9 0.0 copy-done.5
  53.9 0.0 copy-done.11
  53.9 6.9 %column_forward.3 = f32[32,168,128]{2,1,0:T(8,128)} custom-call(s32[1]{0:T(128)} %bitcast.place, f32[128,128]{1,0:T(8,128)S(1)} %copy-done.5, bf16[336,256]{1,0:T(8,128)(2,1)S(1)} %copy-done.11, f32[2,4,128,128]{3,2,1,0:T(8,128)S(1)} %copy-done.2, f32[2,4,128,128]{3,2,1,0:T(8,128)S(1)} %collective-permute-done.refs_1_, ...), custom_call_target="tpu_custom_call" | custom-call | bytes 20971520 | tf_op jit(solution)/shard_map/column_forward/pallas_call | solution.py:666
  60.8 0.0 copy-start.4
  60.8 0.0 copy-start.7
  60.8 0.0 copy-start.8
  60.8 0.0 copy-start.9
  60.8 0.0 copy-start.10
  60.8 5.0 %all-to-all-start = ((f32[32,168,128]{2,1,0:T(8,128)}), f32[32,168,128]{2,1,0:T(8,128)}, u32[]{:S(2)}, u32[]{:S(2)}) async-start(f32[32,168,128]{2,1,0:T(8,128)} %column_forward.3), calls=%async_computation | async-start | bytes 5505024 | tf_op jit(solution)/shard_map/all_to_all | solution.py:685
  65.9 0.6 pad_add_fusion.place
  66.5 6.7 %gain.1 = (f32[11,256,128]{2,1,0:T(8,128)}, f32[11,256,128]{2,1,0:T(8,128)}) custom-call(s32[2]{0:T(128)} %pad_add_fusion.place), custom_call_target="tpu_custom_call" | custom-call | tf_op jit(solution)/shard_map/gain/pallas_call | solution.py:622
  73.2 56.9 %all-to-all-done.lines = f32[32,168,128]{2,1,0:T(8,128)} async-done(((f32[32,168,128]{2,1,0:T(8,128)}), f32[32,168,128]{2,1,0:T(8,128)}, u32[]{:S(2)}, u32[]{:S(2)}) %all-to-all-start) | async-done | bytes 2752544 | tf_op jit(solution)/shard_map/all_to_all | solution.py:685
  130.0 0.0 copy-done.4
  130.1 0.0 copy-done.7
  130.1 0.0 copy-done.8
  130.1 0.0 copy-done.9
  130.1 0.0 copy-done.10
  130.1 13.2 %line.1 = f32[32,168,128]{2,1,0:T(8,128)} custom-call(f32[32,168,128]{2,1,0:T(8,128)} %all-to-all-done.lines, f32[11,256,128]{2,1,0:T(8,128)} %get-tuple-element.41.gain_re, f32[11,256,128]{2,1,0:T(8,128)} %get-tuple-element.42.gain_im, f32[2,17,8,256]{3,2,1,0:T(8,128)S(1)} %copy-done.4, bf16[512,256]{1,0:T(8,128)(2,1)S(1)} %copy-done.10, ...), custom_call_target="tpu_custom_call" | custom-call | tf_op jit(solution)/shard_map/line/pallas_call | solution.py:696
  143.2 67.6 %all_to_all.10.source = f32[32,168,128]{2,1,0:T(8,128)} all-to-all(f32[32,168,128]{2,1,0:T(8,128)} %line.1), channel_id=1, replica_groups=mesh['row'=4,'col'=8] {'row','col'}, dimensions={0} | all-to-all | bytes 5505024 | tf_op jit(solution)/shard_map/all_to_all | solution.py:711
  210.9 10.1 %column_inverse.2 = (f32[1024,128]{1,0:T(8,128)}, f32[1024,128]{1,0:T(8,128)}, f32[1024,128]{1,0:T(8,128)}, f32[1024,128]{1,0:T(8,128)}, f32[1]{0:T(128)}) custom-call(s32[1]{0:T(128)} %bitcast.place, f32[1]{0:T(128)} %constant.56.clone.1.before, f32[32,168,128]{2,1,0:T(8,128)} %all_to_all.10.source, f32[128,128]{1,0:T(8,128)} %constant.62.clone.twist, ...), custom_call_target="tpu_custom_call" | custom-call | bytes 62914560 | tf_op jit(solution)/shard_map/column_inverse/pallas_call | solution.py:719
  221.0 0.1 collective-permute-start.9
  221.0 1.1 collective-permute-start.10
  222.1 2.4 collective-permute-start.11
  224.5 10.7 %column_inverse.3 = (f32[1032,128]{1,0:T(8,128)}, f32[1032,128]{1,0:T(8,128)}, f32[1032,128]{1,0:T(8,128)}, f32[1032,128]{1,0:T(8,128)}, f32[1]{0:T(128)}) custom-call(s32[1]{0:T(128)} %bitcast.place, f32[1]{0:T(128)} %get-tuple-element.43.before, f32[32,168,128]{2,1,0:T(8,128)} %all_to_all.10.source, f32[128,128]{1,0:T(8,128)} %constant.64.clone.twist, ...), custom_call_target="tpu_custom_call" | custom-call | bytes 62914560 | tf_op jit(solution)/shard_map/column_inverse/pallas_call | solution.py:719
  235.2 0.1 collective-permute-start.6
  235.3 1.4 collective-permute-done.6
  237.9 1.4 collective-permute-start.7
  239.3 2.3 collective-permute-done.7
  242.2 1.4 collective-permute-start.8
  243.5 0.0 collective-permute-done.9.refs_1_
  243.6 3.3 %collective-permute-done.10.refs_2_ = f32[1024,128]{1,0:T(8,128)S(1)} collective-permute-done((f32[1024,128]{1,0:T(8,128)}, f32[1024,128]{1,0:T(8,128)S(1)}, u32[]{:S(2)}, u32[]{:S(2)}) %collective-permute-start.10) | collective-permute-done | bytes 524320 | tf_op jit(solution)/shard_map/ppermute | solution.py:580
  246.9 0.0 collective-permute-done.11.refs_3_
  246.9 1.2 stamp.1
  248.1 1.0 collective-permute-start.12
  249.1 1.1 collective-permute-start.13
  250.2 1.5 collective-permute-start.14
  251.6 11.7 %collective-permute-done.12.refs_5_ = f32[1032,128]{1,0:T(8,128)S(1)} collective-permute-done((f32[1032,128]{1,0:T(8,128)}, f32[1032,128]{1,0:T(8,128)S(1)}, u32[]{:S(2)}, u32[]{:S(2)}) %collective-permute-start.12) | collective-permute-done | bytes 528416 | tf_op jit(solution)/shard_map/ppermute | solution.py:580
  263.3 10.1 %collective-permute-done.13.refs_6_ = f32[1032,128]{1,0:T(8,128)S(1)} collective-permute-done((f32[1032,128]{1,0:T(8,128)}, f32[1032,128]{1,0:T(8,128)S(1)}, u32[]{:S(2)}, u32[]{:S(2)}) %collective-permute-start.13) | collective-permute-done | bytes 528416 | tf_op jit(solution)/shard_map/ppermute | solution.py:580
  273.4 0.0 collective-permute-done.14.refs_7_
  273.4 0.0 copy-done.1
  273.4 1.0 copy-done
  274.4 3.2 %encode.1 = (f32[1024,512]{1,0:T(8,128)}, f32[1024,512]{1,0:T(8,128)}) custom-call(s32[1]{0:T(128)} %bitcast.place, f32[1]{0:T(128)} %max.7.peak_one, f32[1]{0:T(128)} %collective-permute-done.8.peak_two, f32[1024,128]{1,0:T(8,128)S(1)} %copy-done.1, f32[1024,128]{1,0:T(8,128)S(1)} %collective-permute-done.9.refs_1_, ...), custom_call_target="tpu_custom_call" | custom-call | tf_op jit(solution)/shard_map/encode/pallas_call | solution.py:775
  (6 shorter events, 0.0 us)
Async XLA Ops:
  3.6 16.0 %collective-permute-start.3 = (f32[2,4,128,128]{3,2,1,0:T(8,128)}, f32[2,4,128,128]{3,2,1,0:T(8,128)S(1)}, u32[]{:S(2)}, u32[]{:S(2)}) collective-permute-start(f32[2,4,128,128]{3,2,1,0:T(8,128)} %get-tuple-element.38), channel_id=1, source_target_pairs={{0,8},{8,0},{16,24},{24,16},{1,9},{9,1},{17,25},{25,17},{2,10},{10... | collective-permute-start | bytes 1572872 | tf_op jit(solution)/shard_map/ppermute | solution.py:580
  6.6 26.3 %collective-permute-start.4 = (f32[2,4,128,128]{3,2,1,0:T(8,128)}, f32[2,4,128,128]{3,2,1,0:T(8,128)S(1)}, u32[]{:S(2)}, u32[]{:S(2)}) collective-permute-start(f32[2,4,128,128]{3,2,1,0:T(8,128)} %get-tuple-element.39), channel_id=1, source_target_pairs={{0,16},{8,24},{16,0},{24,8},{1,17},{9,25},{17,1},{25,9},{2,18},{10... | collective-permute-start | bytes 1572872 | tf_op jit(solution)/shard_map/ppermute | solution.py:580
  8.1 24.8 %copy-start.3 = (f32[2,4,128,128]{3,2,1,0:T(8,128)S(1)}, f32[2,4,128,128]{3,2,1,0:T(8,128)}, u32[]{:S(2)}) copy-start(f32[2,4,128,128]{3,2,1,0:T(8,128)} %get-tuple-element.37.refs_0_) | copy-start | bytes 1572868
  8.1 24.8 %copy-start.6 = (f32[128,128]{1,0:T(8,128)S(1)}, f32[128,128]{1,0:T(8,128)}, u32[]{:S(2)}) copy-start(f32[128,128]{1,0:T(8,128)} %constant.62.clone.twist) | copy-start | bytes 196612
  8.1 24.8 %copy-start.12 = (bf16[336,256]{1,0:T(8,128)(2,1)S(1)}, bf16[336,256]{1,0:T(8,128)(2,1)}, u32[]{:S(2)}) copy-start(bf16[336,256]{1,0:T(8,128)(2,1)} %constant.63.clone.matrix) | copy-start | bytes 516100
  8.1 24.8 %collective-permute-start.5 = (f32[2,4,128,128]{3,2,1,0:T(8,128)}, f32[2,4,128,128]{3,2,1,0:T(8,128)S(1)}, u32[]{:S(2)}, u32[]{:S(2)}) collective-permute-start(f32[2,4,128,128]{3,2,1,0:T(8,128)} %get-tuple-element.40), channel_id=1, source_target_pairs={{0,24},{8,16},{16,8},{24,0},{1,25},{9,17},{17,9},{25,1},{2,26},{10... | collective-permute-start | bytes 1572872 | tf_op jit(solution)/shard_map/ppermute | solution.py:580
  11.1 30.9 %collective-permute-start = (f32[2,4,128,128]{3,2,1,0:T(8,128)}, f32[2,4,128,128]{3,2,1,0:T(8,128)S(1)}, u32[]{:S(2)}, u32[]{:S(2)}) collective-permute-start(f32[2,4,128,128]{3,2,1,0:T(8,128)} %get-tuple-element.34), channel_id=1, source_target_pairs={{0,8},{8,0},{16,24},{24,16},{1,9},{9,1},{17,25},{25,17},{2,10},{10... | collective-permute-start | bytes 1572872 | tf_op jit(solution)/shard_map/ppermute | solution.py:580
  13.1 40.8 %collective-permute-start.1 = (f32[2,4,128,128]{3,2,1,0:T(8,128)}, f32[2,4,128,128]{3,2,1,0:T(8,128)S(1)}, u32[]{:S(2)}, u32[]{:S(2)}) collective-permute-start(f32[2,4,128,128]{3,2,1,0:T(8,128)} %get-tuple-element.35), channel_id=1, source_target_pairs={{0,16},{8,24},{16,0},{24,8},{1,17},{9,25},{17,1},{25,9},{2,18},{10... | collective-permute-start | bytes 1572872 | tf_op jit(solution)/shard_map/ppermute | solution.py:580
  19.5 34.3 %collective-permute-start.2 = (f32[2,4,128,128]{3,2,1,0:T(8,128)}, f32[2,4,128,128]{3,2,1,0:T(8,128)S(1)}, u32[]{:S(2)}, u32[]{:S(2)}) collective-permute-start(f32[2,4,128,128]{3,2,1,0:T(8,128)} %get-tuple-element.36), channel_id=1, source_target_pairs={{0,24},{8,16},{16,8},{24,0},{1,25},{9,17},{17,9},{25,1},{2,26},{10... | collective-permute-start | bytes 1572872 | tf_op jit(solution)/shard_map/ppermute | solution.py:580
  32.9 21.0 %copy-start.2 = (f32[2,4,128,128]{3,2,1,0:T(8,128)S(1)}, f32[2,4,128,128]{3,2,1,0:T(8,128)}, u32[]{:S(2)}) copy-start(f32[2,4,128,128]{3,2,1,0:T(8,128)} %get-tuple-element.33.refs_0_) | copy-start | bytes 1572868
  32.9 21.0 %copy-start.5 = (f32[128,128]{1,0:T(8,128)S(1)}, f32[128,128]{1,0:T(8,128)}, u32[]{:S(2)}) copy-start(f32[128,128]{1,0:T(8,128)} %constant.64.clone.twist) | copy-start | bytes 196612
  32.9 21.0 %copy-start.11 = (bf16[336,256]{1,0:T(8,128)(2,1)S(1)}, bf16[336,256]{1,0:T(8,128)(2,1)}, u32[]{:S(2)}) copy-start(bf16[336,256]{1,0:T(8,128)(2,1)} %constant.65.clone.matrix) | copy-start | bytes 516100
  60.8 69.3 %copy-start.4 = (f32[2,17,8,256]{3,2,1,0:T(8,128)S(1)}, f32[2,17,8,256]{3,2,1,0:T(8,128)}, u32[]{:S(2)}) copy-start(f32[2,17,8,256]{3,2,1,0:T(8,128)} %constant.66.clone.twist) | copy-start | bytes 835588
  60.8 69.3 %copy-start.7 = (bf16[256,512]{1,0:T(8,128)(2,1)S(1)}, bf16[256,512]{1,0:T(8,128)(2,1)}, u32[]{:S(2)}) copy-start(bf16[256,512]{1,0:T(8,128)(2,1)} %constant.70.clone.inv_low) | copy-start | bytes 786436
  60.8 69.3 %copy-start.8 = (bf16[256,512]{1,0:T(8,128)(2,1)S(1)}, bf16[256,512]{1,0:T(8,128)(2,1)}, u32[]{:S(2)}) copy-start(bf16[256,512]{1,0:T(8,128)(2,1)} %constant.69.clone.inv_high) | copy-start | bytes 786436
  60.8 69.3 %copy-start.9 = (bf16[512,256]{1,0:T(8,128)(2,1)S(1)}, bf16[512,256]{1,0:T(8,128)(2,1)}, u32[]{:S(2)}) copy-start(bf16[512,256]{1,0:T(8,128)(2,1)} %constant.68.clone.fwd_low) | copy-start | bytes 786436
  60.8 69.3 %copy-start.10 = (bf16[512,256]{1,0:T(8,128)(2,1)S(1)}, bf16[512,256]{1,0:T(8,128)(2,1)}, u32[]{:S(2)}) copy-start(bf16[512,256]{1,0:T(8,128)(2,1)} %constant.67.clone.fwd_high) | copy-start | bytes 786436
  60.8 69.2 %all-to-all-start = ((f32[32,168,128]{2,1,0:T(8,128)}), f32[32,168,128]{2,1,0:T(8,128)}, u32[]{:S(2)}, u32[]{:S(2)}) async-start(f32[32,168,128]{2,1,0:T(8,128)} %column_forward.3), calls=%async_computation | async-start | bytes 5505024 | tf_op jit(solution)/shard_map/all_to_all | solution.py:685
  221.0 22.6 %collective-permute-start.9 = (f32[1024,128]{1,0:T(8,128)}, f32[1024,128]{1,0:T(8,128)S(1)}, u32[]{:S(2)}, u32[]{:S(2)}) collective-permute-start(f32[1024,128]{1,0:T(8,128)} %get-tuple-element.46), channel_id=1, source_target_pairs={{0,8},{8,0},{16,24},{24,16},{1,9},{9,1},{17,25},{25,17},{2,10},{10... | collective-permute-start | bytes 1572872 | tf_op jit(solution)/shard_map/ppermute | solution.py:580
  221.0 25.8 %collective-permute-start.10 = (f32[1024,128]{1,0:T(8,128)}, f32[1024,128]{1,0:T(8,128)S(1)}, u32[]{:S(2)}, u32[]{:S(2)}) collective-permute-start(f32[1024,128]{1,0:T(8,128)} %get-tuple-element.47), channel_id=1, source_target_pairs={{0,16},{8,24},{16,0},{24,8},{1,17},{9,25},{17,1},{25,9},{2,18},{10... | collective-permute-start | bytes 1572872 | tf_op jit(solution)/shard_map/ppermute | solution.py:580
  222.1 24.7 %collective-permute-start.11 = (f32[1024,128]{1,0:T(8,128)}, f32[1024,128]{1,0:T(8,128)S(1)}, u32[]{:S(2)}, u32[]{:S(2)}) collective-permute-start(f32[1024,128]{1,0:T(8,128)} %get-tuple-element.48), channel_id=1, source_target_pairs={{0,24},{8,16},{16,8},{24,0},{1,25},{9,17},{17,9},{25,1},{2,26},{10... | collective-permute-start | bytes 1572872 | tf_op jit(solution)/shard_map/ppermute | solution.py:580
  224.5 48.8 %copy-start.1 = (f32[1024,128]{1,0:T(8,128)S(1)}, f32[1024,128]{1,0:T(8,128)}, u32[]{:S(2)}) copy-start(f32[1024,128]{1,0:T(8,128)} %get-tuple-element.53.refs_0_) | copy-start | bytes 1572868
  235.2 1.5 collective-permute-start.6
  237.9 3.7 %collective-permute-start.7 = (f32[1]{0:T(128)}, f32[1]{0:T(128)}, u32[]{:S(2)}, u32[]{:S(2)}) collective-permute-start(f32[1]{0:T(128)} %max.6), channel_id=1, source_target_pairs={{0,2},{1,3},{2,0},{3,1},{4,6},{5,7},{6,4},{7,5},{8,10},{9,11},{10,... | collective-permute-start | bytes 20 | tf_op jit(solution)/shard_map/ppermute | solution.py:742
  242.2 4.7 %collective-permute-start.8 = (f32[1]{0:T(128)}, f32[1]{0:T(128)}, u32[]{:S(2)}, u32[]{:S(2)}) collective-permute-start(f32[1]{0:T(128)} %max.7.peak_one), channel_id=1, source_target_pairs={{0,4},{1,5},{2,6},{3,7},{4,0},{5,1},{6,2},{7,3},{8,12},{9,13},{10,... | collective-permute-start | bytes 20 | tf_op jit(solution)/shard_map/ppermute | solution.py:742
  248.1 15.2 %collective-permute-start.12 = (f32[1032,128]{1,0:T(8,128)}, f32[1032,128]{1,0:T(8,128)S(1)}, u32[]{:S(2)}, u32[]{:S(2)}) collective-permute-start(f32[1032,128]{1,0:T(8,128)} %get-tuple-element.61), channel_id=1, source_target_pairs={{0,8},{8,0},{16,24},{24,16},{1,9},{9,1},{17,25},{25,17},{2,10},{10... | collective-permute-start | bytes 1585160 | tf_op jit(solution)/shard_map/ppermute | solution.py:580
  249.1 24.3 %collective-permute-start.13 = (f32[1032,128]{1,0:T(8,128)}, f32[1032,128]{1,0:T(8,128)S(1)}, u32[]{:S(2)}, u32[]{:S(2)}) collective-permute-start(f32[1032,128]{1,0:T(8,128)} %get-tuple-element.62), channel_id=1, source_target_pairs={{0,16},{8,24},{16,0},{24,8},{1,17},{9,25},{17,1},{25,9},{2,18},{10... | collective-permute-start | bytes 1585160 | tf_op jit(solution)/shard_map/ppermute | solution.py:580
  250.2 23.2 %collective-permute-start.14 = (f32[1032,128]{1,0:T(8,128)}, f32[1032,128]{1,0:T(8,128)S(1)}, u32[]{:S(2)}, u32[]{:S(2)}) collective-permute-start(f32[1032,128]{1,0:T(8,128)} %get-tuple-element.63), channel_id=1, source_target_pairs={{0,24},{8,16},{16,8},{24,0},{1,25},{9,17},{17,9},{25,1},{2,26},{10... | collective-permute-start | bytes 1585160 | tf_op jit(solution)/shard_map/ppermute | solution.py:580
  273.4 1.0 copy-start

commit v12 on v11

--- a/solution.py
+++ b/solution.py
@@ -259,31 +259,29 @@
         copy_out(p).wait()
 
 
-def column_inverse_kernel(count, place, before, source, twist, matrix, *refs):
-    pieces, (peak_sq, near, lines, deep, back, top, sems, out_sems) = refs[:count], refs[count:]
+def column_inverse_kernel(count, place, source, twist, matrix, *refs):
+    pieces, (peak_sq, near, lines, deep, back, top, sems, out_sems) = refs[:-8], refs[-8:]
     width = lines.shape[-1]
     rows_in = lines.shape[1]
-    per_dest = near.shape[2]
+    per_dest = near.shape[3]
     many = deep.shape[-1] // width
+    products = RES // many
 
     def copy_in(p):
         part = pl.ds(p * many, many)
         return pltpu.make_async_copy(source.at[part], lines.at[part], sems.at[p])
 
-    def copies_out(part):
+    def copies_out(chunk, part):
         size = CHUNK // 2
         copies = []
-        for j, piece in enumerate(pieces):
+        for j in range(count):
             for at in range(2 * per_dest):
-                here = near.at[place[0] ^ j, at // per_dest, at % per_dest, pl.ds(part * size, size)]
-                there = piece.at[pl.ds(at * CHUNK + part * size, size)]
-                sem = out_sems.at[(part * count + j) * 2 * per_dest + at]
+                rows = pl.ds(part * size, size)
+                here = near.at[chunk, place[0] ^ j, at // per_dest, at % per_dest, rows]
+                there = pieces[chunk * count + j].at[pl.ds(at * CHUNK + part * size, size)]
+                sem = out_sems.at[((chunk * 2 + part) * count + j) * 2 * per_dest + at]
                 copies.append(pltpu.make_async_copy(here, there, sem))
         return copies
-
-    for p in range(RES // many):
-        copy_in(p).start()
-    top[...] = jnp.zeros_like(top)
 
     def prepare(p):
         copy_in(p).wait()
@@ -295,34 +293,25 @@
             parts.append(jnp.zeros((deep.shape[1] - 3 * rows_in, many * width), jnp.float32))
         deep[p] = jnp.concatenate(parts, axis=0).astype(jnp.bfloat16)
 
-    def product(p):
-        done = dot16(matrix[...], deep[p])
+    def product(p, chunk):
+        done = dot16(matrix[chunk], deep[p])
         for part in range(many):
-            back[p * many + part] = done[:, part * width : (part + 1) * width]
-
-    prepare(0)
-
-    @pl.loop(1, RES // many)
-    def _(p):
-        product(p - 1)
-        prepare(p)
-
-    product(RES // many - 1)
-
-    def butterflies(t):
+            back[chunk, p * many + part] = done[:, part * width : (part + 1) * width]
+
+    def butterflies(t, chunk):
         q0 = pl.multiple_of(t * 8, 8)
-        read = column_twist(twist, q0)
         largest = []
+        read = column_twist(twist, pl.multiple_of(chunk * CHUNK + q0, 8))
 
         def get(u):
-            re = back[u, pl.ds(q0, 8), :]
-            im = back[u, pl.ds(CHUNK + q0, 8), :]
+            re = back[chunk, u, pl.ds(q0, 8), :]
+            im = back[chunk, u, pl.ds(CHUNK + q0, 8), :]
             return twisted((re, im), u, -1, read)
 
         def put(n, value):
             dest, block = divmod(n, per_dest)
             rows = pl.ds(q0, 8)
-            near[dest, 0, block, rows, :], near[dest, 1, block, rows, :] = value
+            near[chunk, dest, 0, block, rows, :], near[chunk, dest, 1, block, rows, :] = value
             largest.append(value[0] * value[0] + value[1] * value[1])
 
         inverse_slabs(get, put)
@@ -330,15 +319,35 @@
             largest = [jnp.maximum(a, b) for a, b in zip(largest[0::2], largest[1::2])]
         top[...] = jnp.maximum(top[...], largest[0])
 
-    for part in range(2):
-        tiles = CHUNK // 16
-        pl.loop(part * tiles, (part + 1) * tiles)(butterflies)
-        for copy in copies_out(part):
-            copy.start()
-    peak_sq[0] = jnp.maximum(before[0], jnp.max(top[...]))
-    for part in range(2):
-        for copy in copies_out(part):
-            copy.wait()
+    for p in range(products):
+        copy_in(p).start()
+    top[...] = jnp.zeros_like(top)
+
+    @pl.loop(0, products)
+    def _(p):
+        prepare(p)
+        product(p, 0)
+
+    tiles = CHUNK // 16
+    steps = min(tiles, products // 2)
+    for chunk in range(CHUNKS):
+        for part in range(2):
+
+            @pl.loop(part * steps, (part + 1) * steps)
+            def _(t):
+                for item in range(tiles // steps):
+                    butterflies(t * (tiles // steps) + item, chunk)
+                if chunk + 1 < CHUNKS:
+                    for item in range(products // 2 // steps):
+                        product(t * (products // 2 // steps) + item, chunk + 1)
+
+            for copy in copies_out(chunk, part):
+                copy.start()
+    peak_sq[0] = jnp.max(top[...])
+    for chunk in range(CHUNKS):
+        for part in range(2):
+            for copy in copies_out(chunk, part):
+                copy.wait()
 
 
 def line_kernel(
@@ -711,30 +720,30 @@
     lines = lax.all_to_all(lines, ("row", "col"), split_axis=0, concat_axis=0, tiled=True)
     lines = lines.reshape(RES, total_rows, width)
 
-    near, peak_sq = [], jnp.zeros((1,), jnp.float32)
-    for chunk in range(CHUNKS):
-        spare = SPARE if chunk == CHUNKS - 1 else 0
-        piece_shape = jax.ShapeDtypeStruct((2 * blocks * CHUNK + spare, width), jnp.float32)
-        rows = slice(chunk * CHUNK, (chunk + 1) * CHUNK)
-        *pieces, peak_sq = pl.pallas_call(
-            partial(column_inverse_kernel, row_total),
-            in_specs=[whole(pltpu.SMEM), whole(pltpu.SMEM), anywhere, whole(), whole()],
-            out_specs=[anywhere] * row_total + [whole(pltpu.SMEM)],
-            out_shape=[piece_shape] * row_total + [jax.ShapeDtypeStruct((1,), jnp.float32)],
-            scratch_shapes=[
-                pltpu.VMEM((row_total, 2, blocks, CHUNK, width), jnp.float32),
-                pltpu.VMEM((RES, total_rows, width), jnp.float32),
-                pltpu.VMEM((RES // many, inv_col.shape[2], many * width), jnp.bfloat16),
-                pltpu.VMEM((RES, 2 * CHUNK, width), jnp.float32),
-                pltpu.VMEM((8, width), jnp.float32),
-                pltpu.SemaphoreType.DMA((RES // many,)),
-                pltpu.SemaphoreType.DMA((2 * row_total * 2 * blocks,)),
-            ],
-            compiler_params=params(56),
-            cost_estimate=cost(60),
-            name="column_inverse",
-        )(place_row, peak_sq, lines, twist_col[rows], inv_col[chunk])
-        near.append(pieces)
+    piece_shapes = [
+        jax.ShapeDtypeStruct((2 * blocks * CHUNK + spare, width), jnp.float32)
+        for spare in (0,) * (CHUNKS - 1) + (SPARE,)
+    ]
+    *near, peak_sq = pl.pallas_call(
+        partial(column_inverse_kernel, row_total),
+        in_specs=[whole(pltpu.SMEM), anywhere, whole(), whole()],
+        out_specs=[anywhere] * (CHUNKS * row_total) + [whole(pltpu.SMEM)],
+        out_shape=[shape for shape in piece_shapes for _ in range(row_total)]
+        + [jax.ShapeDtypeStruct((1,), jnp.float32)],
+        scratch_shapes=[
+            pltpu.VMEM((CHUNKS, row_total, 2, blocks, CHUNK, width), jnp.float32),
+            pltpu.VMEM((RES, total_rows, width), jnp.float32),
+            pltpu.VMEM((RES // many, inv_col.shape[2], many * width), jnp.bfloat16),
+            pltpu.VMEM((CHUNKS, RES, 2 * CHUNK, width), jnp.float32),
+            pltpu.VMEM((8, width), jnp.float32),
+            pltpu.SemaphoreType.DMA((RES // many,)),
+            pltpu.SemaphoreType.DMA((2 * CHUNKS * row_total * 2 * blocks,)),
+        ],
+        compiler_params=params(56),
+        name="column_inverse",
+    )(place_row, lines, twist_col, inv_col)
+    near = [near[:row_total], near[row_total:]]
+    piece_shape = piece_shapes[-1]
     near[0] = exchange(near[0], "row")
     shift = 1
     while shift < col_total:
@@ -743,7 +752,6 @@
         shift *= 2
         if shift < col_total:
             peak_sq = jnp.maximum(*peaks)
-    near = lax.optimization_barrier(near)
     others = row_total - 1
     near[1][1:] = pl.pallas_call(
         stamp_kernel,
@@ -758,6 +766,7 @@
         compiler_params=params(56),
         name="stamp",
     )(*peaks, *near[1][1:])
+    near[0][1:], near[1][-1] = lax.optimization_barrier((near[0][1:], near[1][-1]))
     near[1] = exchange(near[1], "row")
     if width != 128:
         peak_sq = jnp.maximum(*peaks)[0]

time: 278 us -> 278 us (level)
  Pallas kernels: 63.7 us -> 55.5 us
  waiting for transfers between devices: 116 us -> 124 us
    pallas_call x2 -> x1, Pallas kernels: 20.7 us -> 12.4 us  [body(): pl.pallas_call(partial(column_inverse_kernel, row_total), in_specs=[whole...]
    ppermute x12, waiting for transfers between devices: 55.4 us -> 60.6 us  [exchange(): lax.ppermute(pieces[j], axis, [(i, i ^ j) for i in range(total)])]
  transfers between devices with their start and end apart: 16 -> 16, of which waited for: 10 -> 12; matrix products, arithmetic and copies ran while one was open for 0% -> 0% of each run, Pallas kernels for 9% -> 6%
where the time goes in v12:
time: 278 us; the launch traced here: 277 us
  waiting for transfers between devices  124 us (45%)
  blocking collectives  67.6 us (24%)
  Pallas kernels  55.5 us (20%)
  starting transfers between devices  24.8 us (9%)
    all_to_all x1, blocking collectives, body(): lax.all_to_all(lines, ('row', 'col'), split_axis=0, concat_axis=0, tiled=...  67.6 us
    ppermute x12, waiting for transfers between devices, exchange(): lax.ppermute(pieces[j], axis, [(i, i ^ j) for i in range(total)])  60.6 us
    all_to_all x1, waiting for transfers between devices, body(): lax.all_to_all(lines, ('row', 'col'), split_axis=0, concat_axis=0, tiled=...  56.8 us
    ppermute x12, starting transfers between devices, exchange(): lax.ppermute(pieces[j], axis, [(i, i ^ j) for i in range(total)])  17 us
    pallas_call x1, Pallas kernels, body(): pl.pallas_call(partial(line_kernel, order, own, tail), grid=(-(-own // at...  13.2 us
    pallas_call x2, Pallas kernels, body(): pl.pallas_call(partial(column_forward_kernel, row_total), in_specs=[whole...  12.7 us
    pallas_call x1, Pallas kernels, body(): pl.pallas_call(partial(column_inverse_kernel, row_total), in_specs=[whole...  12.4 us
    pallas_call x1, Pallas kernels, body(): pl.pallas_call(gain_kernel, grid=(own,), in_specs=[whole(pltpu.SMEM)], ou...  6.67 us
  transfers between devices with their start and end apart: 16, of which 12 were waited for; matrix products, arithmetic and copies ran while one was open for 0% of the time, Pallas kernels for 6%

profile of v12, /device:TPU:0, one launch (start us, length us, event | category | flops | bytes accessed | tf_op | source)
XLA Modules:
  0.0 277.3 jit_solution(16933134980490299094)
XLA Ops:
  0.6 2.9 %pack.3 = (f32[2,4,128,128]{3,2,1,0:T(8,128)}, f32[2,4,128,128]{3,2,1,0:T(8,128)}, f32[2,4,128,128]{3,2,1,0:T(8,128)}, f32[2,4,128,128]{3,2,1,0:T(8,128)}) custom-call(s32[1]{0:T(128)} %bitcast.place, f32[4,256,512]{2,1,0:T(8,128)} %bitcast.4, f32[4,256,512]{2,1,0:T(8,128)} %bitcast.6), custom_call_target="tpu_custom_call" | custom-call | bytes 4194304 | tf_op jit(solution)/shard_map/pack/pallas_call | solution.py:653
  3.6 3.0 %collective-permute-start.3 = (f32[2,4,128,128]{3,2,1,0:T(8,128)}, f32[2,4,128,128]{3,2,1,0:T(8,128)S(1)}, u32[]{:S(2)}, u32[]{:S(2)}) collective-permute-start(f32[2,4,128,128]{3,2,1,0:T(8,128)} %get-tuple-element.33), channel_id=1, source_target_pairs={{0,8},{8,0},{16,24},{24,16},{1,9},{9,1},{17,25},{25,17},{2,10},{10... | collective-permute-start | bytes 1572872 | tf_op jit(solution)/shard_map/ppermute | solution.py:589
  6.6 1.5 collective-permute-start.4
  8.1 0.1 collective-permute-start.5
  8.2 3.0 %pack.2 = (f32[2,4,128,128]{3,2,1,0:T(8,128)}, f32[2,4,128,128]{3,2,1,0:T(8,128)}, f32[2,4,128,128]{3,2,1,0:T(8,128)}, f32[2,4,128,128]{3,2,1,0:T(8,128)}) custom-call(s32[1]{0:T(128)} %bitcast.place, f32[4,256,512]{2,1,0:T(8,128)} %bitcast.5, f32[4,256,512]{2,1,0:T(8,128)} %bitcast.7), custom_call_target="tpu_custom_call" | custom-call | bytes 4194304 | tf_op jit(solution)/shard_map/pack/pallas_call | solution.py:653
  11.1 1.9 collective-permute-start
  13.1 1.5 collective-permute-start.1
  14.6 5.0 %collective-permute-done.3.refs_1_ = f32[2,4,128,128]{3,2,1,0:T(8,128)S(1)} collective-permute-done((f32[2,4,128,128]{3,2,1,0:T(8,128)}, f32[2,4,128,128]{3,2,1,0:T(8,128)S(1)}, u32[]{:S(2)}, u32[]{:S(2)}) %collective-permute-start.3) | collective-permute-done | bytes 524320 | tf_op jit(solution)/shard_map/ppermute | solution.py:589
  19.5 3.0 %collective-permute-start.2 = (f32[2,4,128,128]{3,2,1,0:T(8,128)}, f32[2,4,128,128]{3,2,1,0:T(8,128)S(1)}, u32[]{:S(2)}, u32[]{:S(2)}) collective-permute-start(f32[2,4,128,128]{3,2,1,0:T(8,128)} %get-tuple-element.31), channel_id=1, source_target_pairs={{0,24},{8,16},{16,8},{24,0},{1,25},{9,17},{17,9},{25,1},{2,26},{10... | collective-permute-start | bytes 1572872 | tf_op jit(solution)/shard_map/ppermute | solution.py:589
  22.5 10.3 %collective-permute-done.4.refs_2_ = f32[2,4,128,128]{3,2,1,0:T(8,128)S(1)} collective-permute-done((f32[2,4,128,128]{3,2,1,0:T(8,128)}, f32[2,4,128,128]{3,2,1,0:T(8,128)S(1)}, u32[]{:S(2)}, u32[]{:S(2)}) %collective-permute-start.4) | collective-permute-done | bytes 524320 | tf_op jit(solution)/shard_map/ppermute | solution.py:589
  32.9 0.0 collective-permute-done.5.refs_3_
  32.9 0.0 copy-done.3
  32.9 0.0 copy-done.10
  32.9 0.0 copy-done.12
  32.9 0.0 copy-start.2
  32.9 0.0 copy-start.9
  32.9 0.0 copy-start.11
  32.9 5.9 %column_forward.2.refs_4_ = f32[32,168,128]{2,1,0:T(8,128)S(1)} custom-call(s32[1]{0:T(128)} %bitcast.place, f32[128,128]{1,0:T(8,128)S(1)} %copy-done.12, bf16[336,256]{1,0:T(8,128)(2,1)S(1)} %copy-done.10, f32[2,4,128,128]{3,2,1,0:T(8,128)S(1)} %copy-done.3, f32[2,4,128,128]{3,2,1,0:T(8,128)S(1)} %collective-permute-done.3.refs_1_, ...), custom_call_target="tpu_custom_call" | custom-call | bytes 20971520 | tf_op jit(solution)/shard_map/column_forward/pallas_call | solution.py:675
  38.8 3.2 %collective-permute-done.refs_1_ = f32[2,4,128,128]{3,2,1,0:T(8,128)S(1)} collective-permute-done((f32[2,4,128,128]{3,2,1,0:T(8,128)}, f32[2,4,128,128]{3,2,1,0:T(8,128)S(1)}, u32[]{:S(2)}, u32[]{:S(2)}) %collective-permute-start) | collective-permute-done | bytes 524320 | tf_op jit(solution)/shard_map/ppermute | solution.py:589
  42.1 11.8 %collective-permute-done.1.refs_2_ = f32[2,4,128,128]{3,2,1,0:T(8,128)S(1)} collective-permute-done((f32[2,4,128,128]{3,2,1,0:T(8,128)}, f32[2,4,128,128]{3,2,1,0:T(8,128)S(1)}, u32[]{:S(2)}, u32[]{:S(2)}) %collective-permute-start.1) | collective-permute-done | bytes 524320 | tf_op jit(solution)/shard_map/ppermute | solution.py:589
  53.9 0.0 collective-permute-done.2.refs_3_
  53.9 0.0 copy-done.2
  53.9 0.0 copy-done.9
  53.9 0.0 copy-done.11
  53.9 6.8 %column_forward.3 = f32[32,168,128]{2,1,0:T(8,128)} custom-call(s32[1]{0:T(128)} %bitcast.place, f32[128,128]{1,0:T(8,128)S(1)} %copy-done.11, bf16[336,256]{1,0:T(8,128)(2,1)S(1)} %copy-done.9, f32[2,4,128,128]{3,2,1,0:T(8,128)S(1)} %copy-done.2, f32[2,4,128,128]{3,2,1,0:T(8,128)S(1)} %collective-permute-done.refs_1_, ...), custom_call_target="tpu_custom_call" | custom-call | bytes 20971520 | tf_op jit(solution)/shard_map/column_forward/pallas_call | solution.py:675
  60.7 0.0 copy-start.4
  60.8 0.0 copy-start.5
  60.8 0.0 copy-start.6
  60.8 0.0 copy-start.7
  60.8 0.0 copy-start.8
  60.8 5.0 %all-to-all-start = ((f32[32,168,128]{2,1,0:T(8,128)}), f32[32,168,128]{2,1,0:T(8,128)}, u32[]{:S(2)}, u32[]{:S(2)}) async-start(f32[32,168,128]{2,1,0:T(8,128)} %column_forward.3), calls=%async_computation | async-start | bytes 5505024 | tf_op jit(solution)/shard_map/all_to_all | solution.py:694
  65.9 0.7 pad_add_fusion.place
  66.5 6.7 %gain.1 = (f32[11,256,128]{2,1,0:T(8,128)}, f32[11,256,128]{2,1,0:T(8,128)}) custom-call(s32[2]{0:T(128)} %pad_add_fusion.place), custom_call_target="tpu_custom_call" | custom-call | tf_op jit(solution)/shard_map/gain/pallas_call | solution.py:631
  73.2 56.8 %all-to-all-done.lines = f32[32,168,128]{2,1,0:T(8,128)} async-done(((f32[32,168,128]{2,1,0:T(8,128)}), f32[32,168,128]{2,1,0:T(8,128)}, u32[]{:S(2)}, u32[]{:S(2)}) %all-to-all-start) | async-done | bytes 2752544 | tf_op jit(solution)/shard_map/all_to_all | solution.py:694
  130.0 0.0 copy-done.4
  130.0 0.0 copy-done.5
  130.0 0.0 copy-done.6
  130.1 0.0 copy-done.7
  130.1 0.0 copy-done.8
  130.1 13.2 %line.1 = f32[32,168,128]{2,1,0:T(8,128)} custom-call(f32[32,168,128]{2,1,0:T(8,128)} %all-to-all-done.lines, f32[11,256,128]{2,1,0:T(8,128)} %get-tuple-element.36.gain_re, f32[11,256,128]{2,1,0:T(8,128)} %get-tuple-element.37.gain_im, f32[2,17,8,256]{3,2,1,0:T(8,128)S(1)} %copy-done.4, bf16[512,256]{1,0:T(8,128)(2,1)S(1)} %copy-done.8, ...), custom_call_target="tpu_custom_call" | custom-call | tf_op jit(solution)/shard_map/line/pallas_call | solution.py:705
  143.3 67.6 %all_to_all.10.source = f32[32,168,128]{2,1,0:T(8,128)} all-to-all(f32[32,168,128]{2,1,0:T(8,128)} %line.1), channel_id=1, replica_groups=mesh['row'=4,'col'=8] {'row','col'}, dimensions={0} | all-to-all | bytes 5505024 | tf_op jit(solution)/shard_map/all_to_all | solution.py:720
  210.9 12.4 %column_inverse.1 = (f32[1024,128]{1,0:T(8,128)}, f32[1024,128]{1,0:T(8,128)}, f32[1024,128]{1,0:T(8,128)}, f32[1024,128]{1,0:T(8,128)}, f32[1032,128]{1,0:T(8,1...) custom-call(s32[1]{0:T(128)} %bitcast.place, ...), custom_call_target="tpu_custom_call" | custom-call | tf_op jit(solution)/shard_map/column_inverse/pallas_call | solution.py:727
  223.3 0.1 collective-permute-start.9
  223.4 1.1 collective-permute-start.10
  224.5 2.4 collective-permute-start.11
  226.9 0.0 collective-permute-start.6
  226.9 1.2 collective-permute-done.6
  229.3 1.4 collective-permute-start.7
  230.7 2.2 collective-permute-done.7
  233.5 1.4 collective-permute-start.8
  234.9 3.1 %collective-permute-done.8.peak_two = f32[1]{0:T(128)} collective-permute-done((f32[1]{0:T(128)}, f32[1]{0:T(128)}, u32[]{:S(2)}, u32[]{:S(2)}) %collective-permute-start.8) | collective-permute-done | bytes 36 | tf_op jit(solution)/shard_map/ppermute | solution.py:751
  238.0 1.2 stamp.1
  239.2 0.1 collective-permute-start.12
  239.3 1.0 collective-permute-start.13
  240.4 0.0 collective-permute-done.9.refs_1_
  240.4 8.7 %collective-permute-done.10.refs_2_ = f32[1024,128]{1,0:T(8,128)S(1)} collective-permute-done((f32[1024,128]{1,0:T(8,128)}, f32[1024,128]{1,0:T(8,128)S(1)}, u32[]{:S(2)}, u32[]{:S(2)}) %collective-permute-start.10) | collective-permute-done | bytes 524320 | tf_op jit(solution)/shard_map/ppermute | solution.py:589
  249.1 0.5 collective-permute-done.11.refs_3_
  249.6 1.2 collective-permute-start.14
  250.8 10.2 %collective-permute-done.12.refs_5_ = f32[1032,128]{1,0:T(8,128)S(1)} collective-permute-done((f32[1032,128]{1,0:T(8,128)}, f32[1032,128]{1,0:T(8,128)S(1)}, u32[]{:S(2)}, u32[]{:S(2)}) %collective-permute-start.12) | collective-permute-done | bytes 528416 | tf_op jit(solution)/shard_map/ppermute | solution.py:589
  261.0 10.9 %collective-permute-done.13.refs_6_ = f32[1032,128]{1,0:T(8,128)S(1)} collective-permute-done((f32[1032,128]{1,0:T(8,128)}, f32[1032,128]{1,0:T(8,128)S(1)}, u32[]{:S(2)}, u32[]{:S(2)}) %collective-permute-start.13) | collective-permute-done | bytes 528416 | tf_op jit(solution)/shard_map/ppermute | solution.py:589
  271.9 0.0 collective-permute-done.14.refs_7_
  271.9 1.0 copy-done
  272.9 1.0 copy-done.1
  274.0 3.3 %encode.1 = (f32[1024,512]{1,0:T(8,128)}, f32[1024,512]{1,0:T(8,128)}) custom-call(s32[1]{0:T(128)} %bitcast.place, f32[1]{0:T(128)} %max.7.peak_one, f32[1]{0:T(128)} %collective-permute-done.8.peak_two, f32[1024,128]{1,0:T(8,128)S(1)} %copy-done.1, f32[1024,128]{1,0:T(8,128)S(1)} %collective-permute-done.9.refs_1_, ...), custom_call_target="tpu_custom_call" | custom-call | tf_op jit(solution)/shard_map/encode/pallas_call | solution.py:784
  (5 shorter events, 0.0 us)
Async XLA Ops:
  3.6 16.0 %collective-permute-start.3 = (f32[2,4,128,128]{3,2,1,0:T(8,128)}, f32[2,4,128,128]{3,2,1,0:T(8,128)S(1)}, u32[]{:S(2)}, u32[]{:S(2)}) collective-permute-start(f32[2,4,128,128]{3,2,1,0:T(8,128)} %get-tuple-element.33), channel_id=1, source_target_pairs={{0,8},{8,0},{16,24},{24,16},{1,9},{9,1},{17,25},{25,17},{2,10},{10... | collective-permute-start | bytes 1572872 | tf_op jit(solution)/shard_map/ppermute | solution.py:589
  6.6 26.3 %collective-permute-start.4 = (f32[2,4,128,128]{3,2,1,0:T(8,128)}, f32[2,4,128,128]{3,2,1,0:T(8,128)S(1)}, u32[]{:S(2)}, u32[]{:S(2)}) collective-permute-start(f32[2,4,128,128]{3,2,1,0:T(8,128)} %get-tuple-element.34), channel_id=1, source_target_pairs={{0,16},{8,24},{16,0},{24,8},{1,17},{9,25},{17,1},{25,9},{2,18},{10... | collective-permute-start | bytes 1572872 | tf_op jit(solution)/shard_map/ppermute | solution.py:589
  8.1 24.8 %copy-start.3 = (f32[2,4,128,128]{3,2,1,0:T(8,128)S(1)}, f32[2,4,128,128]{3,2,1,0:T(8,128)}, u32[]{:S(2)}) copy-start(f32[2,4,128,128]{3,2,1,0:T(8,128)} %get-tuple-element.32.refs_0_) | copy-start | bytes 1572868
  8.1 24.8 %copy-start.10 = (bf16[336,256]{1,0:T(8,128)(2,1)S(1)}, bf16[336,256]{1,0:T(8,128)(2,1)}, u32[]{:S(2)}) copy-start(bf16[336,256]{1,0:T(8,128)(2,1)} %constant.61.clone.matrix) | copy-start | bytes 516100
  8.1 24.8 %copy-start.12 = (f32[128,128]{1,0:T(8,128)S(1)}, f32[128,128]{1,0:T(8,128)}, u32[]{:S(2)}) copy-start(f32[128,128]{1,0:T(8,128)} %constant.60.clone.twist) | copy-start | bytes 196612
  8.1 24.8 %collective-permute-start.5 = (f32[2,4,128,128]{3,2,1,0:T(8,128)}, f32[2,4,128,128]{3,2,1,0:T(8,128)S(1)}, u32[]{:S(2)}, u32[]{:S(2)}) collective-permute-start(f32[2,4,128,128]{3,2,1,0:T(8,128)} %get-tuple-element.35), channel_id=1, source_target_pairs={{0,24},{8,16},{16,8},{24,0},{1,25},{9,17},{17,9},{25,1},{2,26},{10... | collective-permute-start | bytes 1572872 | tf_op jit(solution)/shard_map/ppermute | solution.py:589
  11.1 30.9 %collective-permute-start = (f32[2,4,128,128]{3,2,1,0:T(8,128)}, f32[2,4,128,128]{3,2,1,0:T(8,128)S(1)}, u32[]{:S(2)}, u32[]{:S(2)}) collective-permute-start(f32[2,4,128,128]{3,2,1,0:T(8,128)} %get-tuple-element.29), channel_id=1, source_target_pairs={{0,8},{8,0},{16,24},{24,16},{1,9},{9,1},{17,25},{25,17},{2,10},{10... | collective-permute-start | bytes 1572872 | tf_op jit(solution)/shard_map/ppermute | solution.py:589
  13.1 40.8 %collective-permute-start.1 = (f32[2,4,128,128]{3,2,1,0:T(8,128)}, f32[2,4,128,128]{3,2,1,0:T(8,128)S(1)}, u32[]{:S(2)}, u32[]{:S(2)}) collective-permute-start(f32[2,4,128,128]{3,2,1,0:T(8,128)} %get-tuple-element.30), channel_id=1, source_target_pairs={{0,16},{8,24},{16,0},{24,8},{1,17},{9,25},{17,1},{25,9},{2,18},{10... | collective-permute-start | bytes 1572872 | tf_op jit(solution)/shard_map/ppermute | solution.py:589
  19.5 34.3 %collective-permute-start.2 = (f32[2,4,128,128]{3,2,1,0:T(8,128)}, f32[2,4,128,128]{3,2,1,0:T(8,128)S(1)}, u32[]{:S(2)}, u32[]{:S(2)}) collective-permute-start(f32[2,4,128,128]{3,2,1,0:T(8,128)} %get-tuple-element.31), channel_id=1, source_target_pairs={{0,24},{8,16},{16,8},{24,0},{1,25},{9,17},{17,9},{25,1},{2,26},{10... | collective-permute-start | bytes 1572872 | tf_op jit(solution)/shard_map/ppermute | solution.py:589
  32.9 21.0 %copy-start.2 = (f32[2,4,128,128]{3,2,1,0:T(8,128)S(1)}, f32[2,4,128,128]{3,2,1,0:T(8,128)}, u32[]{:S(2)}) copy-start(f32[2,4,128,128]{3,2,1,0:T(8,128)} %get-tuple-element.28.refs_0_) | copy-start | bytes 1572868
  32.9 21.0 %copy-start.9 = (bf16[336,256]{1,0:T(8,128)(2,1)S(1)}, bf16[336,256]{1,0:T(8,128)(2,1)}, u32[]{:S(2)}) copy-start(bf16[336,256]{1,0:T(8,128)(2,1)} %constant.63.clone.matrix) | copy-start | bytes 516100
  32.9 21.0 %copy-start.11 = (f32[128,128]{1,0:T(8,128)S(1)}, f32[128,128]{1,0:T(8,128)}, u32[]{:S(2)}) copy-start(f32[128,128]{1,0:T(8,128)} %constant.62.clone.twist) | copy-start | bytes 196612
  60.7 69.3 %copy-start.4 = (f32[2,17,8,256]{3,2,1,0:T(8,128)S(1)}, f32[2,17,8,256]{3,2,1,0:T(8,128)}, u32[]{:S(2)}) copy-start(f32[2,17,8,256]{3,2,1,0:T(8,128)} %constant.64.clone.twist) | copy-start | bytes 835588
  60.8 69.3 %copy-start.5 = (bf16[256,512]{1,0:T(8,128)(2,1)S(1)}, bf16[256,512]{1,0:T(8,128)(2,1)}, u32[]{:S(2)}) copy-start(bf16[256,512]{1,0:T(8,128)(2,1)} %constant.68.clone.inv_low) | copy-start | bytes 786436
  60.8 69.3 %copy-start.6 = (bf16[256,512]{1,0:T(8,128)(2,1)S(1)}, bf16[256,512]{1,0:T(8,128)(2,1)}, u32[]{:S(2)}) copy-start(bf16[256,512]{1,0:T(8,128)(2,1)} %constant.67.clone.inv_high) | copy-start | bytes 786436
  60.8 69.3 %copy-start.7 = (bf16[512,256]{1,0:T(8,128)(2,1)S(1)}, bf16[512,256]{1,0:T(8,128)(2,1)}, u32[]{:S(2)}) copy-start(bf16[512,256]{1,0:T(8,128)(2,1)} %constant.66.clone.fwd_low) | copy-start | bytes 786436
  60.8 69.3 %copy-start.8 = (bf16[512,256]{1,0:T(8,128)(2,1)S(1)}, bf16[512,256]{1,0:T(8,128)(2,1)}, u32[]{:S(2)}) copy-start(bf16[512,256]{1,0:T(8,128)(2,1)} %constant.65.clone.fwd_high) | copy-start | bytes 786436
  60.8 69.2 %all-to-all-start = ((f32[32,168,128]{2,1,0:T(8,128)}), f32[32,168,128]{2,1,0:T(8,128)}, u32[]{:S(2)}, u32[]{:S(2)}) async-start(f32[32,168,128]{2,1,0:T(8,128)} %column_forward.3), calls=%async_computation | async-start | bytes 5505024 | tf_op jit(solution)/shard_map/all_to_all | solution.py:694
  223.3 17.1 %collective-permute-start.9 = (f32[1024,128]{1,0:T(8,128)}, f32[1024,128]{1,0:T(8,128)S(1)}, u32[]{:S(2)}, u32[]{:S(2)}) collective-permute-start(f32[1024,128]{1,0:T(8,128)} %get-tuple-element.40), channel_id=1, source_target_pairs={{0,8},{8,0},{16,24},{24,16},{1,9},{9,1},{17,25},{25,17},{2,10},{10... | collective-permute-start | bytes 1572872 | tf_op jit(solution)/shard_map/ppermute | solution.py:589
  223.4 25.7 %collective-permute-start.10 = (f32[1024,128]{1,0:T(8,128)}, f32[1024,128]{1,0:T(8,128)S(1)}, u32[]{:S(2)}, u32[]{:S(2)}) collective-permute-start(f32[1024,128]{1,0:T(8,128)} %get-tuple-element.41), channel_id=1, source_target_pairs={{0,16},{8,24},{16,0},{24,8},{1,17},{9,25},{17,1},{25,9},{2,18},{10... | collective-permute-start | bytes 1572872 | tf_op jit(solution)/shard_map/ppermute | solution.py:589
  224.5 25.1 %collective-permute-start.11 = (f32[1024,128]{1,0:T(8,128)}, f32[1024,128]{1,0:T(8,128)S(1)}, u32[]{:S(2)}, u32[]{:S(2)}) collective-permute-start(f32[1024,128]{1,0:T(8,128)} %get-tuple-element.42), channel_id=1, source_target_pairs={{0,24},{8,16},{16,8},{24,0},{1,25},{9,17},{17,9},{25,1},{2,26},{10... | collective-permute-start | bytes 1572872 | tf_op jit(solution)/shard_map/ppermute | solution.py:589
  226.9 1.2 collective-permute-start.6
  229.3 3.6 %collective-permute-start.7 = (f32[1]{0:T(128)}, f32[1]{0:T(128)}, u32[]{:S(2)}, u32[]{:S(2)}) collective-permute-start(f32[1]{0:T(128)} %max.6), channel_id=1, source_target_pairs={{0,2},{1,3},{2,0},{3,1},{4,6},{5,7},{6,4},{7,5},{8,10},{9,11},{10,... | collective-permute-start | bytes 20 | tf_op jit(solution)/shard_map/ppermute | solution.py:751
  233.5 4.5 %collective-permute-start.8 = (f32[1]{0:T(128)}, f32[1]{0:T(128)}, u32[]{:S(2)}, u32[]{:S(2)}) collective-permute-start(f32[1]{0:T(128)} %max.7.peak_one), channel_id=1, source_target_pairs={{0,4},{1,5},{2,6},{3,7},{4,0},{5,1},{6,2},{7,3},{8,12},{9,13},{10,... | collective-permute-start | bytes 20 | tf_op jit(solution)/shard_map/ppermute | solution.py:751
  239.2 21.8 %collective-permute-start.12 = (f32[1032,128]{1,0:T(8,128)}, f32[1032,128]{1,0:T(8,128)S(1)}, u32[]{:S(2)}, u32[]{:S(2)}) collective-permute-start(f32[1032,128]{1,0:T(8,128)} %get-tuple-element.51), channel_id=1, source_target_pairs={{0,8},{8,0},{16,24},{24,16},{1,9},{9,1},{17,25},{25,17},{2,10},{10... | collective-permute-start | bytes 1585160 | tf_op jit(solution)/shard_map/ppermute | solution.py:589
  239.3 32.5 %collective-permute-start.13 = (f32[1032,128]{1,0:T(8,128)}, f32[1032,128]{1,0:T(8,128)S(1)}, u32[]{:S(2)}, u32[]{:S(2)}) collective-permute-start(f32[1032,128]{1,0:T(8,128)} %get-tuple-element.52), channel_id=1, source_target_pairs={{0,16},{8,24},{16,0},{24,8},{1,17},{9,25},{17,1},{25,9},{2,18},{10... | collective-permute-start | bytes 1585160 | tf_op jit(solution)/shard_map/ppermute | solution.py:589
  249.6 22.3 %collective-permute-start.14 = (f32[1032,128]{1,0:T(8,128)}, f32[1032,128]{1,0:T(8,128)S(1)}, u32[]{:S(2)}, u32[]{:S(2)}) collective-permute-start(f32[1032,128]{1,0:T(8,128)} %get-tuple-element.53), channel_id=1, source_target_pairs={{0,24},{8,16},{16,8},{24,0},{1,25},{9,17},{17,9},{25,1},{2,26},{10... | collective-permute-start | bytes 1585160 | tf_op jit(solution)/shard_map/ppermute | solution.py:589
  271.9 1.0 copy-start
  272.9 1.0 copy-start.1

commit v13 on v12

--- a/solution.py
+++ b/solution.py
@@ -351,7 +351,7 @@
 
 
 def line_kernel(
-    order, own, tail, lines, gain_re, gain_im, twist, fwd_high, fwd_low, inv_high, inv_low, out, *scratch
+    order, own, tail, lines, gain, twist, fwd_high, fwd_low, inv_high, inv_low, out, *scratch
 ):
     half = RES * 8
     at_end = pl.program_id(0) == pl.num_programs(0) - 1
@@ -391,7 +391,7 @@
     def filtered(group, stacked):
         spec = three_right(stacked[...], half, fwd_high[...], fwd_low[...])
         spec_re, spec_im = spec[:, :128], spec[:, 128:]
-        g_re, g_im = gain_re[group], gain_im[group]
+        g_re, g_im = gain[0, group], gain[1, group]
         mixed = jnp.concatenate(
             [spec_re * g_re - spec_im * g_im, spec_re * g_im + spec_im * g_re], axis=1
         )
@@ -457,7 +457,7 @@
                 out[block, 4:8, :] = out[block, 8:12, :]
 
 
-def gain_kernel(place, gain_re, gain_im):
+def gain_kernel(place, gain):
     k0 = place[0]
     group = place[1] + pl.program_id(0)
     down = lax.broadcasted_iota(jnp.int32, (8, 128), 0)
@@ -489,8 +489,8 @@
         cos_part = jnp.where((which == 1) | (which == 2), -cos_part, cos_part)
         sin_part = jnp.where(which >= 2, -sin_part, sin_part)
         at = (u % (RES // 2)) * 16 + (u // (RES // 2)) * 8
-        gain_re[0, at : at + 8, :] = total * cos_part
-        gain_im[0, at : at + 8, :] = total * sin_part
+        gain[0, 0, at : at + 8, :] = total * cos_part
+        gain[1, 0, at : at + 8, :] = total * sin_part
 
 
 def encode(near_real, near_imag, peak_sq, cell_sign):
@@ -505,14 +505,17 @@
     return (near_real * level + near_imag * lift, near_imag * level - near_real * lift)
 
 
-def stamp_kernel(peak_one, peak_two, *refs):
-    count = (len(refs) - 2) // 2
-    pieces, tile, sems = refs[count : 2 * count], refs[-2], refs[-1]
+def stamp_kernel(others, peak_one, peak_two, *refs):
+    refs = refs[others:]
+    stay, pieces, refs = refs[:CHUNKS], refs[CHUNKS : CHUNKS + others], refs[CHUNKS + others :]
+    fetched, (tile, sems) = refs[:CHUNKS], refs[CHUNKS:]
     tile[...] = jnp.full(tile.shape, jnp.maximum(peak_one[0], peak_two[0]), jnp.float32)
     copies = []
     for j, piece in enumerate(pieces):
         rows = pl.ds(piece.shape[0] - SPARE, SPARE)
         copies.append(pltpu.make_async_copy(tile, piece.at[rows], sems.at[j]))
+    for chunk in range(CHUNKS):
+        copies.append(pltpu.make_async_copy(stay[chunk], fetched[chunk], sems.at[others + chunk]))
     for copy in copies:
         copy.start()
     for copy in copies:
@@ -520,23 +523,15 @@
 
 
 def encode_kernel(count, place, peak_one, peak_two, *refs):
-    pieces, (slm_real, slm_imag, *refs) = refs[: CHUNKS * count], refs[CHUNKS * count :]
-    own, (tile_real, tile_imag, own_sems, sems) = refs[:CHUNKS], refs[CHUNKS:]
+    pieces, refs = refs[: CHUNKS * count], refs[CHUNKS * count :]
+    slm_real, slm_imag, tile_real, tile_imag, sems = refs
     blocks, width = tile_real.shape[0], pieces[0].shape[-1]
-    fetches = [
-        pltpu.make_async_copy(pieces[chunk * count], own[chunk], own_sems.at[chunk])
-        for chunk in range(CHUNKS)
-    ]
-    for fetch in fetches:
-        fetch.start()
     top = jnp.full((1, width), jnp.maximum(peak_one[0], peak_two[0]), jnp.float32)
     for piece in pieces[(CHUNKS - 1) * count + 1 :]:
         top = jnp.maximum(top, piece[pl.ds(piece.shape[0] - SPARE, 1), :])
     cell = lax.broadcasted_iota(jnp.int32, (CHUNK, width), 0)
     cell = cell + lax.broadcasted_iota(jnp.int32, (CHUNK, width), 1)
     cell_sign = (1 - 2 * (cell & 1)).astype(jnp.float32)
-    for fetch in fetches:
-        fetch.wait()
 
     def copies_out(block):
         rows = pl.ds(block * INNER, INNER)
@@ -549,7 +544,7 @@
     def _(block):
         for at in range(CHUNKS * count):
             chunk, j = divmod(at, count)
-            piece = pieces[at] if j else own[chunk]
+            piece = pieces[at]
             lanes = pl.ds(pl.multiple_of((place[0] ^ j) * width, width), width)
             rows = pl.ds(chunk * CHUNK, CHUNK)
             real = pl.ds(pl.multiple_of(block * CHUNK, CHUNK), CHUNK)
@@ -626,14 +621,12 @@
     u = device // parts
     k0 = jnp.where(u >= RES // 2, u - RES, u)
     place = jnp.stack([k0, (device % parts) * own]).astype(jnp.int32)
-    gain_shape = jax.ShapeDtypeStruct((own, RES * 8, 128), jnp.float32)
-    gain_spec = pl.BlockSpec((1, RES * 8, 128), lambda g: (g, 0, 0))
-    gain_re, gain_im = pl.pallas_call(
+    gain = pl.pallas_call(
         gain_kernel,
         grid=(own,),
         in_specs=[whole(pltpu.SMEM)],
-        out_specs=[gain_spec, gain_spec],
-        out_shape=[gain_shape, gain_shape],
+        out_specs=pl.BlockSpec((2, 1, RES * 8, 128), lambda g: (0, g, 0, 0)),
+        out_shape=jax.ShapeDtypeStruct((2, own, RES * 8, 128), jnp.float32),
         compiler_params=params(56),
         name="gain",
     )(place)
@@ -701,18 +694,18 @@
 
     at_once = 2
     line_grain = pl.BlockSpec((N // 128, 16 * at_once, 128), lambda i: (0, i, 0))
-    gain_grain = pl.BlockSpec((at_once, RES * 8, 128), lambda i: (i, 0, 0))
+    gain_grain = pl.BlockSpec((2, at_once, RES * 8, 128), lambda i: (0, i, 0, 0))
     lines = pl.pallas_call(
         partial(line_kernel, order, own, tail),
         grid=(-(-own // at_once),),
-        in_specs=[line_grain, gain_grain, gain_grain] + [whole()] * 5,
+        in_specs=[line_grain, gain_grain] + [whole()] * 5,
         out_specs=line_grain,
         out_shape=jax.ShapeDtypeStruct((N // 128, own_rows, 128), jnp.float32),
         scratch_shapes=[pltpu.VMEM((2 * RES * 8, 2 * INNER), jnp.bfloat16)] * at_once
         + [pltpu.VMEM((RES * 8, 2 * INNER), jnp.float32)] * at_once,
-        compiler_params=params(52),
+        compiler_params=params(48),
         name="line",
-    )(lines, gain_re, gain_im, twist_line, line_fh, line_fl, line_ih, line_il)
+    )(lines, gain, twist_line, line_fh, line_fl, line_ih, line_il)
 
     if width != 128:
         lines = lines.transpose(1, 0, 2).reshape(own_rows, col_total, row_total, width)
@@ -753,19 +746,21 @@
         if shift < col_total:
             peak_sq = jnp.maximum(*peaks)
     others = row_total - 1
-    near[1][1:] = pl.pallas_call(
-        stamp_kernel,
-        in_specs=[whole(pltpu.SMEM)] * 2 + [anywhere] * others,
-        out_specs=[anywhere] * others,
-        out_shape=[piece_shape] * others,
+    stamped = pl.pallas_call(
+        partial(stamp_kernel, others),
+        in_specs=[whole(pltpu.SMEM)] * 2 + [anywhere] * (others + CHUNKS),
+        out_specs=[anywhere] * others + [whole()] * CHUNKS,
+        out_shape=[piece_shape] * others + piece_shapes,
         scratch_shapes=[
             pltpu.VMEM((SPARE, width), jnp.float32),
-            pltpu.SemaphoreType.DMA((others,)),
+            pltpu.SemaphoreType.DMA((others + CHUNKS,)),
         ],
         input_output_aliases={2 + j: j for j in range(others)},
-        compiler_params=params(56),
+        compiler_params=params(16),
         name="stamp",
-    )(*peaks, *near[1][1:])
+    )(*peaks, *near[1][1:], near[0][0], near[1][0])
+    near[1][1:] = stamped[:others]
+    near[0][0], near[1][0] = stamped[others:]
     near[0][1:], near[1][-1] = lax.optimization_barrier((near[0][1:], near[1][-1]))
     near[1] = exchange(near[1], "row")
     if width != 128:
@@ -783,11 +778,10 @@
     tile = pltpu.VMEM((blocks, INNER, tile_width), jnp.float32)
     return pl.pallas_call(
         partial(encode_kernel, row_total),
-        in_specs=[whole(pltpu.SMEM)] * 3 + ([anywhere] + [whole()] * others) * CHUNKS,
+        in_specs=[whole(pltpu.SMEM)] * 3 + [whole()] * (CHUNKS * row_total),
         out_specs=[anywhere] * 2,
         out_shape=[tile_shape, tile_shape],
-        scratch_shapes=[pltpu.VMEM(pieces[0].shape, jnp.float32) for pieces in near]
-        + [tile, tile, pltpu.SemaphoreType.DMA((CHUNKS,)), pltpu.SemaphoreType.DMA((2 * blocks,))],
+        scratch_shapes=[tile, tile, pltpu.SemaphoreType.DMA((2 * blocks,))],
         compiler_params=params(16),
         name="encode",
     )(place_row, *peaks, *near[0], *near[1])

time: 278 us -> 274 us (0.986)
  waiting for transfers between devices: 124 us -> 119 us
  local copies, waits for them, and re-layouts: 2.15 us -> 5.28 us
    ppermute x12, waiting for transfers between devices: 60.6 us -> 55.6 us  [exchange(): lax.ppermute(pieces[j], axis, [(i, i ^ j) for i in range(total)])]
    unnamed x26 -> x32, local copies, waits for them, and re-layouts: 2.15 us -> 5.28 us
where the time goes in v13:
time: 274 us; the launch traced here: 273 us
  waiting for transfers between devices  119 us (43%)
  blocking collectives  66.5 us (24%)
  Pallas kernels  54.3 us (20%)
  starting transfers between devices  24.9 us (9%)
  local copies, waits for them, and re-layouts  5.28 us (2%)
    all_to_all x1, blocking collectives, body(): lax.all_to_all(lines, ('row', 'col'), split_axis=0, concat_axis=0, tiled=...  66.5 us
    all_to_all x1, waiting for transfers between devices, body(): lax.all_to_all(lines, ('row', 'col'), split_axis=0, concat_axis=0, tiled=...  56.8 us
    ppermute x12, waiting for transfers between devices, exchange(): lax.ppermute(pieces[j], axis, [(i, i ^ j) for i in range(total)])  55.6 us
    ppermute x12, starting transfers between devices, exchange(): lax.ppermute(pieces[j], axis, [(i, i ^ j) for i in range(total)])  17.1 us
    pallas_call x2, Pallas kernels, body(): pl.pallas_call(partial(column_forward_kernel, row_total), in_specs=[whole...  12.8 us
    pallas_call x1, Pallas kernels, body(): pl.pallas_call(partial(line_kernel, order, own, tail), grid=(-(-own // at...  12.7 us
    pallas_call x1, Pallas kernels, body(): pl.pallas_call(partial(column_inverse_kernel, row_total), in_specs=[whole...  12.4 us
    ppermute x3, waiting for transfers between devices, body(): peaks = [peak_sq, lax.ppermute(peak_sq, 'col', partner)]  6.89 us
  transfers between devices with their start and end apart: 16, of which 12 were waited for; matrix products, arithmetic and copies ran while one was open for 0% of the time, Pallas kernels for 6%

profile of v13, /device:TPU:0, one launch (start us, length us, event | category | flops | bytes accessed | tf_op | source)
XLA Modules:
  0.0 273.5 jit_solution(15816100845690308743)
XLA Ops:
  0.6 2.9 %pack.3 = (f32[2,4,128,128]{3,2,1,0:T(8,128)}, f32[2,4,128,128]{3,2,1,0:T(8,128)}, f32[2,4,128,128]{3,2,1,0:T(8,128)}, f32[2,4,128,128]{3,2,1,0:T(8,128)}) custom-call(s32[1]{0:T(128)} %bitcast.place, f32[4,256,512]{2,1,0:T(8,128)} %bitcast.4, f32[4,256,512]{2,1,0:T(8,128)} %bitcast.6), custom_call_target="tpu_custom_call" | custom-call | bytes 4194304 | tf_op jit(solution)/shard_map/pack/pallas_call | solution.py:646
  3.6 0.0 copy-start.6
  3.6 0.0 copy-start.13
  3.6 0.0 copy-start.15
  3.6 3.0 %collective-permute-start.3 = (f32[2,4,128,128]{3,2,1,0:T(8,128)}, f32[2,4,128,128]{3,2,1,0:T(8,128)S(1)}, u32[]{:S(2)}, u32[]{:S(2)}) collective-permute-start(f32[2,4,128,128]{3,2,1,0:T(8,128)} %get-tuple-element.33), channel_id=1, source_target_pairs={{0,8},{8,0},{16,24},{24,16},{1,9},{9,1},{17,25},{25,17},{2,10},{10... | collective-permute-start | bytes 1572872 | tf_op jit(solution)/shard_map/ppermute | solution.py:584
  6.6 1.5 collective-permute-start.4
  8.1 0.0 collective-permute-start.5
  8.2 2.9 %pack.2 = (f32[2,4,128,128]{3,2,1,0:T(8,128)}, f32[2,4,128,128]{3,2,1,0:T(8,128)}, f32[2,4,128,128]{3,2,1,0:T(8,128)}, f32[2,4,128,128]{3,2,1,0:T(8,128)}) custom-call(s32[1]{0:T(128)} %bitcast.place, f32[4,256,512]{2,1,0:T(8,128)} %bitcast.5, f32[4,256,512]{2,1,0:T(8,128)} %bitcast.7), custom_call_target="tpu_custom_call" | custom-call | bytes 4194304 | tf_op jit(solution)/shard_map/pack/pallas_call | solution.py:646
  11.1 0.0 copy-start.5
  11.1 0.0 copy-start.12
  11.1 0.0 copy-start.14
  11.1 2.0 collective-permute-start
  13.1 1.5 collective-permute-start.1
  14.6 4.9 %collective-permute-done.3.refs_1_ = f32[2,4,128,128]{3,2,1,0:T(8,128)S(1)} collective-permute-done((f32[2,4,128,128]{3,2,1,0:T(8,128)}, f32[2,4,128,128]{3,2,1,0:T(8,128)S(1)}, u32[]{:S(2)}, u32[]{:S(2)}) %collective-permute-start.3) | collective-permute-done | bytes 524320 | tf_op jit(solution)/shard_map/ppermute | solution.py:584
  19.6 3.0 %collective-permute-start.2 = (f32[2,4,128,128]{3,2,1,0:T(8,128)}, f32[2,4,128,128]{3,2,1,0:T(8,128)S(1)}, u32[]{:S(2)}, u32[]{:S(2)}) collective-permute-start(f32[2,4,128,128]{3,2,1,0:T(8,128)} %get-tuple-element.31), channel_id=1, source_target_pairs={{0,24},{8,16},{16,8},{24,0},{1,25},{9,17},{17,9},{25,1},{2,26},{10... | collective-permute-start | bytes 1572872 | tf_op jit(solution)/shard_map/ppermute | solution.py:584
  22.6 10.3 %collective-permute-done.4.refs_2_ = f32[2,4,128,128]{3,2,1,0:T(8,128)S(1)} collective-permute-done((f32[2,4,128,128]{3,2,1,0:T(8,128)}, f32[2,4,128,128]{3,2,1,0:T(8,128)S(1)}, u32[]{:S(2)}, u32[]{:S(2)}) %collective-permute-start.4) | collective-permute-done | bytes 524320 | tf_op jit(solution)/shard_map/ppermute | solution.py:584
  32.9 0.0 collective-permute-done.5.refs_3_
  32.9 0.0 copy-done.6
  32.9 0.0 copy-done.13
  32.9 5.9 %column_forward.2.refs_4_ = f32[32,168,128]{2,1,0:T(8,128)S(1)} custom-call(s32[1]{0:T(128)} %bitcast.place, f32[128,128]{1,0:T(8,128)S(1)} %copy-done.15, bf16[336,256]{1,0:T(8,128)(2,1)S(1)} %copy-done.13, f32[2,4,128,128]{3,2,1,0:T(8,128)S(1)} %copy-done.6, f32[2,4,128,128]{3,2,1,0:T(8,128)S(1)} %collective-permute-done.3.refs_1_, ...), custom_call_target="tpu_custom_call" | custom-call | bytes 20971520 | tf_op jit(solution)/shard_map/column_forward/pallas_call | solution.py:668
  38.8 3.3 %collective-permute-done.refs_1_ = f32[2,4,128,128]{3,2,1,0:T(8,128)S(1)} collective-permute-done((f32[2,4,128,128]{3,2,1,0:T(8,128)}, f32[2,4,128,128]{3,2,1,0:T(8,128)S(1)}, u32[]{:S(2)}, u32[]{:S(2)}) %collective-permute-start) | collective-permute-done | bytes 524320 | tf_op jit(solution)/shard_map/ppermute | solution.py:584
  42.1 11.8 %collective-permute-done.1.refs_2_ = f32[2,4,128,128]{3,2,1,0:T(8,128)S(1)} collective-permute-done((f32[2,4,128,128]{3,2,1,0:T(8,128)}, f32[2,4,128,128]{3,2,1,0:T(8,128)S(1)}, u32[]{:S(2)}, u32[]{:S(2)}) %collective-permute-start.1) | collective-permute-done | bytes 524320 | tf_op jit(solution)/shard_map/ppermute | solution.py:584
  53.9 0.0 collective-permute-done.2.refs_3_
  53.9 0.0 copy-done.12
  53.9 0.0 copy-done.14
  53.9 6.9 %column_forward.3 = f32[32,168,128]{2,1,0:T(8,128)} custom-call(s32[1]{0:T(128)} %bitcast.place, f32[128,128]{1,0:T(8,128)S(1)} %copy-done.14, bf16[336,256]{1,0:T(8,128)(2,1)S(1)} %copy-done.12, f32[2,4,128,128]{3,2,1,0:T(8,128)S(1)} %copy-done.5, f32[2,4,128,128]{3,2,1,0:T(8,128)S(1)} %collective-permute-done.refs_1_, ...), custom_call_target="tpu_custom_call" | custom-call | bytes 20971520 | tf_op jit(solution)/shard_map/column_forward/pallas_call | solution.py:668
  60.8 5.0 %all-to-all-start = ((f32[32,168,128]{2,1,0:T(8,128)}), f32[32,168,128]{2,1,0:T(8,128)}, u32[]{:S(2)}, u32[]{:S(2)}) async-start(f32[32,168,128]{2,1,0:T(8,128)} %column_forward.3), calls=%async_computation | async-start | bytes 5505024 | tf_op jit(solution)/shard_map/all_to_all | solution.py:687
  65.8 0.0 copy-start.7
  65.9 0.0 copy-start.8
  65.9 0.0 copy-start.9
  65.9 0.0 copy-start.10
  65.9 0.0 copy-start.11
  65.9 0.6 pad_add_fusion.place
  66.5 6.7 %gain.1 = f32[2,11,256,128]{3,2,1,0:T(8,128)} custom-call(s32[2]{0:T(128)} %pad_add_fusion.place), custom_call_target="tpu_custom_call" | custom-call | tf_op jit(solution)/shard_map/gain/pallas_call | solution.py:624
  73.2 56.8 %all-to-all-done.lines = f32[32,168,128]{2,1,0:T(8,128)} async-done(((f32[32,168,128]{2,1,0:T(8,128)}), f32[32,168,128]{2,1,0:T(8,128)}, u32[]{:S(2)}, u32[]{:S(2)}) %all-to-all-start) | async-done | bytes 2752544 | tf_op jit(solution)/shard_map/all_to_all | solution.py:687
  130.0 0.0 copy-done.8
  130.1 12.7 %line.1 = f32[32,168,128]{2,1,0:T(8,128)S(1)} custom-call(f32[32,168,128]{2,1,0:T(8,128)} %all-to-all-done.lines, f32[2,11,256,128]{3,2,1,0:T(8,128)} %gain.1, f32[2,17,8,256]{3,2,1,0:T(8,128)S(1)} %copy-done.7, bf16[512,256]{1,0:T(8,128)(2,1)S(1)} %copy-done.11, bf16[512,256]{1,0:T(8,128)(2,1)S(1)} %copy-done.10, bf16[256,512]{1,0:T(8,128)(2,1)S(1)} %copy-done.9, ...), custom_call_target="tpu_custom_call" | custom-call | tf_op jit(solution)/shard_map/line/pallas_call | solution.py:698
  142.8 66.5 %all_to_all.10.source = f32[32,168,128]{2,1,0:T(8,128)} all-to-all(f32[32,168,128]{2,1,0:T(8,128)S(1)} %line.1), channel_id=1, replica_groups=mesh['row'=4,'col'=8] {'row','col'}, dimensions={0} | all-to-all | bytes 5505024 | tf_op jit(solution)/shard_map/all_to_all | solution.py:713
  209.3 12.4 %column_inverse.1 = (f32[1024,128]{1,0:T(8,128)}, f32[1024,128]{1,0:T(8,128)}, f32[1024,128]{1,0:T(8,128)}, f32[1024,128]{1,0:T(8,128)}, f32[1032,128]{1,0:T(8,1...) custom-call(s32[1]{0:T(128)} %bitcast.place, ...), custom_call_target="tpu_custom_call" | custom-call | tf_op jit(solution)/shard_map/column_inverse/pallas_call | solution.py:720
  221.8 0.1 collective-permute-start.9
  221.8 1.1 collective-permute-start.10
  222.9 2.4 collective-permute-start.11
  225.3 0.0 collective-permute-start.6
  225.3 1.3 collective-permute-done.6
  227.8 1.4 collective-permute-start.7
  229.2 2.3 collective-permute-done.7
  232.1 1.4 collective-permute-start.8
  233.4 3.2 %collective-permute-done.8.peak_two = f32[1]{0:T(128)} collective-permute-done((f32[1]{0:T(128)}, f32[1]{0:T(128)}, u32[]{:S(2)}, u32[]{:S(2)}) %collective-permute-start.8) | collective-permute-done | bytes 36 | tf_op jit(solution)/shard_map/ppermute | solution.py:744
  236.7 1.0 copy-done
  237.7 1.0 copy-done.1
  238.8 1.0 copy-done.2
  239.8 1.0 copy-done.3
  240.9 1.0 copy-done.4
  241.9 0.7 stamp.1
  242.6 0.1 collective-permute-start.12
  242.8 1.1 collective-permute-start.13
  243.8 0.0 collective-permute-done.9.refs_1_
  243.8 3.8 %collective-permute-done.10.refs_2_ = f32[1024,128]{1,0:T(8,128)S(1)} collective-permute-done((f32[1024,128]{1,0:T(8,128)}, f32[1024,128]{1,0:T(8,128)S(1)}, u32[]{:S(2)}, u32[]{:S(2)}) %collective-permute-start.10) | collective-permute-done | bytes 524320 | tf_op jit(solution)/shard_map/ppermute | solution.py:584
  247.6 0.5 collective-permute-done.11.refs_3_
  248.0 1.3 collective-permute-start.14
  249.3 10.2 %collective-permute-done.12.refs_5_ = f32[1032,128]{1,0:T(8,128)S(1)} collective-permute-done((f32[1032,128]{1,0:T(8,128)S(1)}, f32[1032,128]{1,0:T(8,128)S(1)}, u32[]{:S(2)}, u32[]{:S(2)}) %collective-permute-start.12) | collective-permute-done | bytes 528416 | tf_op jit(solution)/shard_map/ppermute | solution.py:584
  259.4 10.9 %collective-permute-done.13.refs_6_ = f32[1032,128]{1,0:T(8,128)S(1)} collective-permute-done((f32[1032,128]{1,0:T(8,128)S(1)}, f32[1032,128]{1,0:T(8,128)S(1)}, u32[]{:S(2)}, u32[]{:S(2)}) %collective-permute-start.13) | collective-permute-done | bytes 528416 | tf_op jit(solution)/shard_map/ppermute | solution.py:584
  270.3 0.0 collective-permute-done.14.refs_7_
  270.3 3.2 %encode.1 = (f32[1024,512]{1,0:T(8,128)}, f32[1024,512]{1,0:T(8,128)}) custom-call(s32[1]{0:T(128)} %bitcast.place, f32[1]{0:T(128)} %max.7.peak_one, f32[1]{0:T(128)} %collective-permute-done.8.peak_two, f32[1024,128]{1,0:T(8,128)S(1)} %get-tuple-element.42.refs_0_, f32[1024,128]{1,0:T(8,128)S(1)} %collective-permute-done.9.refs_1_, ...), custom_call_target="tpu_custom_call" | custom-call | tf_op jit(solution)/shard_map/encode/pallas_call | solution.py:779
  (11 shorter events, 0.0 us)
Async XLA Ops:
  3.6 29.3 %copy-start.6 = (f32[2,4,128,128]{3,2,1,0:T(8,128)S(1)}, f32[2,4,128,128]{3,2,1,0:T(8,128)}, u32[]{:S(2)}) copy-start(f32[2,4,128,128]{3,2,1,0:T(8,128)} %get-tuple-element.32.refs_0_) | copy-start | bytes 1572868
  3.6 29.3 %copy-start.13 = (bf16[336,256]{1,0:T(8,128)(2,1)S(1)}, bf16[336,256]{1,0:T(8,128)(2,1)}, u32[]{:S(2)}) copy-start(bf16[336,256]{1,0:T(8,128)(2,1)} %constant.61.clone.matrix) | copy-start | bytes 516100
  3.6 29.3 %copy-start.15 = (f32[128,128]{1,0:T(8,128)S(1)}, f32[128,128]{1,0:T(8,128)}, u32[]{:S(2)}) copy-start(f32[128,128]{1,0:T(8,128)} %constant.60.clone.twist) | copy-start | bytes 196612
  3.6 16.0 %collective-permute-start.3 = (f32[2,4,128,128]{3,2,1,0:T(8,128)}, f32[2,4,128,128]{3,2,1,0:T(8,128)S(1)}, u32[]{:S(2)}, u32[]{:S(2)}) collective-permute-start(f32[2,4,128,128]{3,2,1,0:T(8,128)} %get-tuple-element.33), channel_id=1, source_target_pairs={{0,8},{8,0},{16,24},{24,16},{1,9},{9,1},{17,25},{25,17},{2,10},{10... | collective-permute-start | bytes 1572872 | tf_op jit(solution)/shard_map/ppermute | solution.py:584
  6.6 26.3 %collective-permute-start.4 = (f32[2,4,128,128]{3,2,1,0:T(8,128)}, f32[2,4,128,128]{3,2,1,0:T(8,128)S(1)}, u32[]{:S(2)}, u32[]{:S(2)}) collective-permute-start(f32[2,4,128,128]{3,2,1,0:T(8,128)} %get-tuple-element.34), channel_id=1, source_target_pairs={{0,16},{8,24},{16,0},{24,8},{1,17},{9,25},{17,1},{25,9},{2,18},{10... | collective-permute-start | bytes 1572872 | tf_op jit(solution)/shard_map/ppermute | solution.py:584
  8.1 24.8 %collective-permute-start.5 = (f32[2,4,128,128]{3,2,1,0:T(8,128)}, f32[2,4,128,128]{3,2,1,0:T(8,128)S(1)}, u32[]{:S(2)}, u32[]{:S(2)}) collective-permute-start(f32[2,4,128,128]{3,2,1,0:T(8,128)} %get-tuple-element.35), channel_id=1, source_target_pairs={{0,24},{8,16},{16,8},{24,0},{1,25},{9,17},{17,9},{25,1},{2,26},{10... | collective-permute-start | bytes 1572872 | tf_op jit(solution)/shard_map/ppermute | solution.py:584
  11.1 42.8 %copy-start.5 = (f32[2,4,128,128]{3,2,1,0:T(8,128)S(1)}, f32[2,4,128,128]{3,2,1,0:T(8,128)}, u32[]{:S(2)}) copy-start(f32[2,4,128,128]{3,2,1,0:T(8,128)} %get-tuple-element.28.refs_0_) | copy-start | bytes 1572868
  11.1 42.8 %copy-start.12 = (bf16[336,256]{1,0:T(8,128)(2,1)S(1)}, bf16[336,256]{1,0:T(8,128)(2,1)}, u32[]{:S(2)}) copy-start(bf16[336,256]{1,0:T(8,128)(2,1)} %constant.63.clone.matrix) | copy-start | bytes 516100
  11.1 42.8 %copy-start.14 = (f32[128,128]{1,0:T(8,128)S(1)}, f32[128,128]{1,0:T(8,128)}, u32[]{:S(2)}) copy-start(f32[128,128]{1,0:T(8,128)} %constant.62.clone.twist) | copy-start | bytes 196612
  11.1 31.0 %collective-permute-start = (f32[2,4,128,128]{3,2,1,0:T(8,128)}, f32[2,4,128,128]{3,2,1,0:T(8,128)S(1)}, u32[]{:S(2)}, u32[]{:S(2)}) collective-permute-start(f32[2,4,128,128]{3,2,1,0:T(8,128)} %get-tuple-element.29), channel_id=1, source_target_pairs={{0,8},{8,0},{16,24},{24,16},{1,9},{9,1},{17,25},{25,17},{2,10},{10... | collective-permute-start | bytes 1572872 | tf_op jit(solution)/shard_map/ppermute | solution.py:584
  13.1 40.8 %collective-permute-start.1 = (f32[2,4,128,128]{3,2,1,0:T(8,128)}, f32[2,4,128,128]{3,2,1,0:T(8,128)S(1)}, u32[]{:S(2)}, u32[]{:S(2)}) collective-permute-start(f32[2,4,128,128]{3,2,1,0:T(8,128)} %get-tuple-element.30), channel_id=1, source_target_pairs={{0,16},{8,24},{16,0},{24,8},{1,17},{9,25},{17,1},{25,9},{2,18},{10... | collective-permute-start | bytes 1572872 | tf_op jit(solution)/shard_map/ppermute | solution.py:584
  19.6 34.3 %collective-permute-start.2 = (f32[2,4,128,128]{3,2,1,0:T(8,128)}, f32[2,4,128,128]{3,2,1,0:T(8,128)S(1)}, u32[]{:S(2)}, u32[]{:S(2)}) collective-permute-start(f32[2,4,128,128]{3,2,1,0:T(8,128)} %get-tuple-element.31), channel_id=1, source_target_pairs={{0,24},{8,16},{16,8},{24,0},{1,25},{9,17},{17,9},{25,1},{2,26},{10... | collective-permute-start | bytes 1572872 | tf_op jit(solution)/shard_map/ppermute | solution.py:584
  60.8 69.2 %all-to-all-start = ((f32[32,168,128]{2,1,0:T(8,128)}), f32[32,168,128]{2,1,0:T(8,128)}, u32[]{:S(2)}, u32[]{:S(2)}) async-start(f32[32,168,128]{2,1,0:T(8,128)} %column_forward.3), calls=%async_computation | async-start | bytes 5505024 | tf_op jit(solution)/shard_map/all_to_all | solution.py:687
  65.8 64.2 %copy-start.7 = (f32[2,17,8,256]{3,2,1,0:T(8,128)S(1)}, f32[2,17,8,256]{3,2,1,0:T(8,128)}, u32[]{:S(2)}) copy-start(f32[2,17,8,256]{3,2,1,0:T(8,128)} %constant.64.clone.twist) | copy-start | bytes 835588
  65.9 64.2 %copy-start.8 = (bf16[256,512]{1,0:T(8,128)(2,1)S(1)}, bf16[256,512]{1,0:T(8,128)(2,1)}, u32[]{:S(2)}) copy-start(bf16[256,512]{1,0:T(8,128)(2,1)} %constant.68.clone.inv_low) | copy-start | bytes 786436
  65.9 64.2 %copy-start.9 = (bf16[256,512]{1,0:T(8,128)(2,1)S(1)}, bf16[256,512]{1,0:T(8,128)(2,1)}, u32[]{:S(2)}) copy-start(bf16[256,512]{1,0:T(8,128)(2,1)} %constant.67.clone.inv_high) | copy-start | bytes 786436
  65.9 64.2 %copy-start.10 = (bf16[512,256]{1,0:T(8,128)(2,1)S(1)}, bf16[512,256]{1,0:T(8,128)(2,1)}, u32[]{:S(2)}) copy-start(bf16[512,256]{1,0:T(8,128)(2,1)} %constant.66.clone.fwd_low) | copy-start | bytes 786436
  65.9 64.2 %copy-start.11 = (bf16[512,256]{1,0:T(8,128)(2,1)S(1)}, bf16[512,256]{1,0:T(8,128)(2,1)}, u32[]{:S(2)}) copy-start(bf16[512,256]{1,0:T(8,128)(2,1)} %constant.65.clone.fwd_high) | copy-start | bytes 786436
  221.8 22.1 %collective-permute-start.9 = (f32[1024,128]{1,0:T(8,128)}, f32[1024,128]{1,0:T(8,128)S(1)}, u32[]{:S(2)}, u32[]{:S(2)}) collective-permute-start(f32[1024,128]{1,0:T(8,128)} %get-tuple-element.43), channel_id=1, source_target_pairs={{0,8},{8,0},{16,24},{24,16},{1,9},{9,1},{17,25},{25,17},{2,10},{10... | collective-permute-start | bytes 1572872 | tf_op jit(solution)/shard_map/ppermute | solution.py:584
  221.8 25.7 %collective-permute-start.10 = (f32[1024,128]{1,0:T(8,128)}, f32[1024,128]{1,0:T(8,128)S(1)}, u32[]{:S(2)}, u32[]{:S(2)}) collective-permute-start(f32[1024,128]{1,0:T(8,128)} %get-tuple-element.44), channel_id=1, source_target_pairs={{0,16},{8,24},{16,0},{24,8},{1,17},{9,25},{17,1},{25,9},{2,18},{10... | collective-permute-start | bytes 1572872 | tf_op jit(solution)/shard_map/ppermute | solution.py:584
  222.9 25.1 %collective-permute-start.11 = (f32[1024,128]{1,0:T(8,128)}, f32[1024,128]{1,0:T(8,128)S(1)}, u32[]{:S(2)}, u32[]{:S(2)}) collective-permute-start(f32[1024,128]{1,0:T(8,128)} %get-tuple-element.45), channel_id=1, source_target_pairs={{0,24},{8,16},{16,8},{24,0},{1,25},{9,17},{17,9},{25,1},{2,26},{10... | collective-permute-start | bytes 1572872 | tf_op jit(solution)/shard_map/ppermute | solution.py:584
  225.3 1.3 collective-permute-start.6
  227.8 3.7 %collective-permute-start.7 = (f32[1]{0:T(128)}, f32[1]{0:T(128)}, u32[]{:S(2)}, u32[]{:S(2)}) collective-permute-start(f32[1]{0:T(128)} %max.6), channel_id=1, source_target_pairs={{0,2},{1,3},{2,0},{3,1},{4,6},{5,7},{6,4},{7,5},{8,10},{9,11},{10,... | collective-permute-start | bytes 20 | tf_op jit(solution)/shard_map/ppermute | solution.py:744
  232.1 4.6 %collective-permute-start.8 = (f32[1]{0:T(128)}, f32[1]{0:T(128)}, u32[]{:S(2)}, u32[]{:S(2)}) collective-permute-start(f32[1]{0:T(128)} %max.7.peak_one), channel_id=1, source_target_pairs={{0,4},{1,5},{2,6},{3,7},{4,0},{5,1},{6,2},{7,3},{8,12},{9,13},{10,... | collective-permute-start | bytes 20 | tf_op jit(solution)/shard_map/ppermute | solution.py:744
  236.7 1.0 copy-start
  237.7 1.0 copy-start.1
  238.8 1.0 copy-start.2
  239.8 1.0 copy-start.3
  240.9 1.0 copy-start.4
  242.6 16.8 %collective-permute-start.12 = (f32[1032,128]{1,0:T(8,128)S(1)}, f32[1032,128]{1,0:T(8,128)S(1)}, u32[]{:S(2)}, u32[]{:S(2)}) collective-permute-start(f32[1032,128]{1,0:T(8,128)S(1)} %get-tuple-element.51), channel_id=1, source_target_pairs={{0,8},{8,0},{16,24},{24,16},{1,9},{9,1},{17,25},{25,17},{2,10},{10... | collective-permute-start | bytes 1585160 | tf_op jit(solution)/shard_map/ppermute | solution.py:584
  242.8 27.6 %collective-permute-start.13 = (f32[1032,128]{1,0:T(8,128)S(1)}, f32[1032,128]{1,0:T(8,128)S(1)}, u32[]{:S(2)}, u32[]{:S(2)}) collective-permute-start(f32[1032,128]{1,0:T(8,128)S(1)} %get-tuple-element.52), channel_id=1, source_target_pairs={{0,16},{8,24},{16,0},{24,8},{1,17},{9,25},{17,1},{25,9},{2,18},{10... | collective-permute-start | bytes 1585160 | tf_op jit(solution)/shard_map/ppermute | solution.py:584
  248.0 22.3 %collective-permute-start.14 = (f32[1032,128]{1,0:T(8,128)S(1)}, f32[1032,128]{1,0:T(8,128)S(1)}, u32[]{:S(2)}, u32[]{:S(2)}) collective-permute-start(f32[1032,128]{1,0:T(8,128)S(1)} %get-tuple-element.53), channel_id=1, source_target_pairs={{0,24},{8,16},{16,8},{24,0},{1,25},{9,17},{17,9},{25,1},{2,26},{10... | collective-permute-start | bytes 1585160 | tf_op jit(solution)/shard_map/ppermute | solution.py:584

commit v14 on v13

--- a/solution.py
+++ b/solution.py
@@ -20,6 +20,7 @@
 HALF = 40
 CHUNKS = 2
 CHUNK = INNER // CHUNKS
+FRONT = ((0, 64), (128, 128), (64, 64))
 SPARE = 8
 
 
@@ -68,13 +69,16 @@
         c, s = np.cos(angle), np.sin(angle)
         forward[at] = (c, s) if part == 0 else (-s, c)
         inverse[:, :, at] = (c, s) if part == 0 else (-s, c)
-    forward = forward.reshape(-1, 2, CHUNKS, CHUNK // 8, 8).transpose(2, 0, 3, 1, 4)
-    forward = np.concatenate(split16(forward.reshape(CHUNKS, len(rows), 2 * CHUNK)), axis=1)
+    tables = []
+    for start, size in FRONT:
+        part = forward[:, :, start : start + size].reshape(-1, 2, size // 8, 8)
+        part = part.transpose(0, 2, 1, 3).reshape(-1, 2 * size)
+        tables.append(np.concatenate(split16(part), axis=0))
     inverse = inverse.reshape(2, CHUNKS, CHUNK, -1).transpose(1, 0, 2, 3)
     high, low = split16(inverse.reshape(CHUNKS, 2 * CHUNK, len(rows)))
     inverse = np.concatenate([high, high, low], axis=2)
     inverse = np.pad(inverse, ((0, 0), (0, 0), (0, -3 * len(rows) % 16)))
-    return forward, inverse
+    return tables, inverse
 
 
 def line_tables():
@@ -204,7 +208,7 @@
     pieces, refs = refs[:count], refs[count:]
     before, (out, total, high, low, sems) = refs[:-5], refs[-5:]
     width = pieces[0].shape[-1]
-    per_source = pieces[0].shape[1]
+    per_source, size = pieces[0].shape[1:3]
     many = high.shape[-1] // width
     products = RES // many
     rows_out = out.shape[1]
@@ -225,7 +229,7 @@
 
         @pl.when(place[0] == here)
         def _():
-            @pl.loop(0, CHUNK // 8)
+            @pl.loop(0, size // 8)
             def _(t):
                 q0 = pl.multiple_of(t * 8, 8)
                 read = column_twist(twist, q0)
@@ -272,15 +276,16 @@
         return pltpu.make_async_copy(source.at[part], lines.at[part], sems.at[p])
 
     def copies_out(chunk, part):
-        size = CHUNK // 2
+        parts = 1 if chunk + 1 < CHUNKS else 2
+        if part >= parts:
+            return []
+        rows = pl.ds(part * CHUNK // parts, CHUNK // parts)
         copies = []
         for j in range(count):
-            for at in range(2 * per_dest):
-                rows = pl.ds(part * size, size)
-                here = near.at[chunk, place[0] ^ j, at // per_dest, at % per_dest, rows]
-                there = pieces[chunk * count + j].at[pl.ds(at * CHUNK + part * size, size)]
-                sem = out_sems.at[((chunk * 2 + part) * count + j) * 2 * per_dest + at]
-                copies.append(pltpu.make_async_copy(here, there, sem))
+            piece = pieces[chunk * count + j].at[pl.ds(0, 2 * per_dest * CHUNK)]
+            there = piece.reshape(2, per_dest, CHUNK, width).at[:, :, rows]
+            here = near.at[chunk, place[0] ^ j, :, :, rows]
+            copies.append(pltpu.make_async_copy(here, there, out_sems.at[(chunk * 2 + part) * count + j]))
         return copies
 
     def prepare(p):
@@ -341,7 +346,7 @@
                     for item in range(products // 2 // steps):
                         product(t * (products // 2 // steps) + item, chunk + 1)
 
-            for copy in copies_out(chunk, part):
+            for copy in copies_out(chunk, part if chunk + 1 == CHUNKS else 1 - part):
                 copy.start()
     peak_sq[0] = jnp.max(top[...])
     for chunk in range(CHUNKS):
@@ -633,21 +638,20 @@
 
     place_row = lax.axis_index("row").reshape(1).astype(jnp.int32)
     blocks = height // INNER
-    piece = (2, blocks, CHUNK, width)
-    piece_shape = jax.ShapeDtypeStruct(piece, jnp.float32)
     anywhere = whole(pl.ANY)
     if width != 128:
-        packed = jnp.stack([field_real, field_imag])
-        packed = packed.reshape(2, blocks, CHUNKS, CHUNK, row_total, width).transpose(2, 4, 0, 1, 3, 5)
-        packed = jnp.take(packed, jnp.arange(row_total) ^ place_row[0], axis=1)
+        packed = jnp.stack([field_real, field_imag]).reshape(2, blocks, INNER, row_total, width)
+        packed = jnp.take(packed, jnp.arange(row_total) ^ place_row[0], axis=3)
     lines = []
-    for chunk in range(CHUNKS):
+    for chunk, (start, size) in enumerate(FRONT):
+        piece_shape = jax.ShapeDtypeStruct((2, blocks, size, width), jnp.float32)
+        at = start // size
         if width == 128:
             pieces = pl.pallas_call(
                 pack_kernel,
                 grid=(1,),
                 in_specs=[whole(pltpu.SMEM)]
-                + [pl.BlockSpec((blocks, CHUNK, tile_width), lambda i: (0, chunk, 0))] * 2,
+                + [pl.BlockSpec((blocks, size, tile_width), lambda i: (0, at, 0))] * 2,
                 out_specs=[anywhere] * row_total,
                 out_shape=[piece_shape] * row_total,
                 scratch_shapes=[pltpu.SemaphoreType.DMA((2 * row_total,))],
@@ -660,10 +664,10 @@
                 field_imag.reshape(blocks, INNER, tile_width),
             )
         else:
-            pieces = [packed[chunk, j] for j in range(row_total)]
+            pieces = [packed[:, :, start : start + size, j] for j in range(row_total)]
         pieces = exchange(pieces, "row")
-        rows = slice(chunk * CHUNK, (chunk + 1) * CHUNK)
-        slab = pltpu.VMEM((RES // many, 2 * CHUNK, many * width), jnp.bfloat16)
+        rows = slice(start, start + size)
+        slab = pltpu.VMEM((RES // many, 2 * size, many * width), jnp.bfloat16)
         lines = [
             pl.pallas_call(
                 partial(column_forward_kernel, row_total),
@@ -730,7 +734,7 @@
             pltpu.VMEM((CHUNKS, RES, 2 * CHUNK, width), jnp.float32),
             pltpu.VMEM((8, width), jnp.float32),
             pltpu.SemaphoreType.DMA((RES // many,)),
-            pltpu.SemaphoreType.DMA((2 * CHUNKS * row_total * 2 * blocks,)),
+            pltpu.SemaphoreType.DMA((2 * CHUNKS * row_total,)),
         ],
         compiler_params=params(56),
         name="column_inverse",

time: 274 us -> 279 us (1.018)
  waiting for transfers between devices: 119 us -> 112 us
  starting transfers between devices: 24.9 us -> 30.7 us
  Pallas kernels: 54.3 us -> 59.6 us
    ppermute x12 -> x15, waiting for transfers between devices: 55.6 us -> 49 us  [exchange(): lax.ppermute(pieces[j], axis, [(i, i ^ j) for i in range(total)])]
    pallas_call x2 -> x3, Pallas kernels: 12.8 us -> 17.3 us  [body(): pl.pallas_call(partial(column_forward_kernel, row_total), in_specs=[whole...]
    ppermute x12 -> x15, starting transfers between devices: 17.1 us -> 20.9 us  [exchange(): lax.ppermute(pieces[j], axis, [(i, i ^ j) for i in range(total)])]
    pallas_call x2 -> x3, Pallas kernels: 5.84 us -> 7.42 us  [body(): pl.pallas_call(pack_kernel, grid=(1,), in_specs=[whole(pltpu.SMEM)] + [pl...]
  transfers between devices with their start and end apart: 16 -> 19, of which waited for: 12 -> 10; matrix products, arithmetic and copies ran while one was open for 0% -> 0% of each run, Pallas kernels for 6% -> 9%
where the time goes in v14:
time: 279 us; the launch traced here: 278 us
  waiting for transfers between devices  112 us (40%)
  blocking collectives  66.5 us (24%)
  Pallas kernels  59.6 us (21%)
  starting transfers between devices  30.7 us (11%)
  local copies, waits for them, and re-layouts  5.31 us (2%)
  between operations  2.98 us (1%)
    all_to_all x1, blocking collectives, body(): lax.all_to_all(lines, ('row', 'col'), split_axis=0, concat_axis=0, tiled=...  66.5 us
    all_to_all x1, waiting for transfers between devices, body(): lax.all_to_all(lines, ('row', 'col'), split_axis=0, concat_axis=0, tiled=...  56.8 us
    ppermute x15, waiting for transfers between devices, exchange(): lax.ppermute(pieces[j], axis, [(i, i ^ j) for i in range(total)])  49 us
    ppermute x15, starting transfers between devices, exchange(): lax.ppermute(pieces[j], axis, [(i, i ^ j) for i in range(total)])  20.9 us
    pallas_call x3, Pallas kernels, body(): pl.pallas_call(partial(column_forward_kernel, row_total), in_specs=[whole...  17.3 us
    pallas_call x1, Pallas kernels, body(): pl.pallas_call(partial(line_kernel, order, own, tail), grid=(-(-own // at...  12.7 us
    pallas_call x1, Pallas kernels, body(): pl.pallas_call(partial(column_inverse_kernel, row_total), in_specs=[whole...  11.4 us
    pallas_call x3, Pallas kernels, body(): pl.pallas_call(pack_kernel, grid=(1,), in_specs=[whole(pltpu.SMEM)] + [pl...  7.42 us
  transfers between devices with their start and end apart: 19, of which 10 were waited for; matrix products, arithmetic and copies ran while one was open for 0% of the time, Pallas kernels for 9%

profile of v14, /device:TPU:0, one launch (start us, length us, event | category | flops | bytes accessed | tf_op | source)
XLA Modules:
  0.0 278.0 jit_solution(10671299045920227945)
XLA Ops:
  0.6 2.3 pack.5
  2.9 3.0 %collective-permute-start.6 = (f32[2,4,64,128]{3,2,1,0:T(8,128)}, f32[2,4,64,128]{3,2,1,0:T(8,128)S(1)}, u32[]{:S(2)}, u32[]{:S(2)}) collective-permute-start(f32[2,4,64,128]{3,2,1,0:T(8,128)} %get-tuple-element.41), channel_id=1, source_target_pairs={{0,8},{8,0},{16,24},{24,16},{1,9},{9,1},{17,25},{25,17},{2,10},{10... | collective-permute-start | bytes 786440 | tf_op jit(solution)/shard_map/ppermute | solution.py:589
  5.9 2.9 %pack.4 = (f32[2,4,128,128]{3,2,1,0:T(8,128)}, f32[2,4,128,128]{3,2,1,0:T(8,128)}, f32[2,4,128,128]{3,2,1,0:T(8,128)}, f32[2,4,128,128]{3,2,1,0:T(8,128)}) custom-call(s32[1]{0:T(128)} %bitcast.place, f32[4,256,512]{2,1,0:T(8,128)} %bitcast.5, f32[4,256,512]{2,1,0:T(8,128)} %bitcast.8), custom_call_target="tpu_custom_call" | custom-call | bytes 4194304 | tf_op jit(solution)/shard_map/pack/pallas_call | solution.py:650
  8.9 0.0 copy-start.15
  8.9 0.0 copy-start.18
  8.9 0.1 collective-permute-start.3
  9.0 2.0 collective-permute-start.7
  11.0 0.1 collective-permute-start.4
  11.1 2.9 %collective-permute-start.5 = (f32[2,4,128,128]{3,2,1,0:T(8,128)}, f32[2,4,128,128]{3,2,1,0:T(8,128)S(1)}, u32[]{:S(2)}, u32[]{:S(2)}) collective-permute-start(f32[2,4,128,128]{3,2,1,0:T(8,128)} %get-tuple-element.39), channel_id=1, source_target_pairs={{0,24},{8,16},{16,8},{24,0},{1,25},{9,17},{17,9},{25,1},{2,26},{10... | collective-permute-start | bytes 1572872 | tf_op jit(solution)/shard_map/ppermute | solution.py:589
  14.0 0.0 collective-permute-done.6.refs_1_
  14.0 2.3 collective-permute-start.8
  16.3 2.3 pack.3
  18.5 0.0 copy-start.4
  18.6 0.0 copy-start.13
  18.6 0.0 copy-start.16
  18.6 1.6 collective-permute-start
  20.2 22.7 %collective-permute-done.8.refs_3_ = f32[2,4,64,128]{3,2,1,0:T(8,128)S(1)} collective-permute-done((f32[2,4,64,128]{3,2,1,0:T(8,128)S(1)}, f32[2,4,64,128]{3,2,1,0:T(8,128)S(1)}, u32[]{:S(2)}, u32[]{:S(2)}) %collective-permute-start.8) | collective-permute-done | bytes 262176 | tf_op jit(solution)/shard_map/ppermute | solution.py:589
  42.9 0.0 collective-permute-start.1
  42.9 0.0 collective-permute-done.3.refs_1_
  42.9 3.0 %collective-permute-start.2 = (f32[2,4,64,128]{3,2,1,0:T(8,128)}, f32[2,4,64,128]{3,2,1,0:T(8,128)S(1)}, u32[]{:S(2)}, u32[]{:S(2)}) collective-permute-start(f32[2,4,64,128]{3,2,1,0:T(8,128)} %get-tuple-element.35), channel_id=1, source_target_pairs={{0,24},{8,16},{16,8},{24,0},{1,25},{9,17},{17,9},{25,1},{2,26},{10... | collective-permute-start | bytes 786440 | tf_op jit(solution)/shard_map/ppermute | solution.py:589
  45.9 4.6 %column_forward.3.refs_4_ = f32[32,168,128]{2,1,0:T(8,128)S(1)} custom-call(s32[1]{0:T(128)} %bitcast.place, f32[64,128]{1,0:T(8,128)S(1)} %copy-done.18, bf16[336,128]{1,0:T(8,128)(2,1)S(1)} %copy-done.15, f32[2,4,64,128]{3,2,1,0:T(8,128)S(1)} %copy-done.11, f32[2,4,64,128]{3,2,1,0:T(8,128)S(1)} %collective-permute-done.6.refs_1_, ...), custom_call_target="tpu_custom_call" | custom-call | bytes 20971520 | tf_op jit(solution)/shard_map/column_forward/pallas_call | solution.py:672
  50.5 1.0 collective-permute-done.4.refs_2_
  51.4 0.0 collective-permute-done.5.refs_3_
  51.5 0.0 copy-start.14
  51.5 0.0 copy-start.17
  51.5 7.1 %column_forward.4.refs_4_ = f32[32,168,128]{2,1,0:T(8,128)S(1)} custom-call(s32[1]{0:T(128)} %bitcast.place, f32[128,128]{1,0:T(8,128)S(1)} %copy-done.16, bf16[336,256]{1,0:T(8,128)(2,1)S(1)} %copy-done.13, f32[2,4,128,128]{3,2,1,0:T(8,128)S(1)} %copy-done.4, f32[2,4,128,128]{3,2,1,0:T(8,128)S(1)} %collective-permute-done.3.refs_1_, ...), custom_call_target="tpu_custom_call" | custom-call | bytes 20971520 | tf_op jit(solution)/shard_map/column_forward/pallas_call | solution.py:672
  58.6 0.0 collective-permute-done.1.refs_2_
  58.6 0.0 collective-permute-done.2.refs_3_
  58.7 5.6 %column_forward.5 = f32[32,168,128]{2,1,0:T(8,128)} custom-call(s32[1]{0:T(128)} %bitcast.place, f32[64,128]{1,0:T(8,128)S(1)} %copy-done.17, bf16[336,128]{1,0:T(8,128)(2,1)S(1)} %copy-done.14, f32[2,4,64,128]{3,2,1,0:T(8,128)S(1)} %copy-done.12, f32[2,4,64,128]{3,2,1,0:T(8,128)S(1)} %collective-permute-done.refs_1_, ...), custom_call_target="tpu_custom_call" | custom-call | bytes 20971520 | tf_op jit(solution)/shard_map/column_forward/pallas_call | solution.py:672
  64.2 7.0 %all-to-all-start = ((f32[32,168,128]{2,1,0:T(8,128)}), f32[32,168,128]{2,1,0:T(8,128)}, u32[]{:S(2)}, u32[]{:S(2)}) async-start(f32[32,168,128]{2,1,0:T(8,128)} %column_forward.5), calls=%async_computation | async-start | bytes 5505024 | tf_op jit(solution)/shard_map/all_to_all | solution.py:691
  71.2 0.0 copy-start.6
  71.3 0.0 copy-start.7
  71.3 0.0 copy-start.8
  71.3 0.0 copy-start.9
  71.3 0.0 copy-start.10
  71.3 0.6 pad_add_fusion.place
  71.9 6.7 %gain.1 = f32[2,11,256,128]{3,2,1,0:T(8,128)} custom-call(s32[2]{0:T(128)} %pad_add_fusion.place), custom_call_target="tpu_custom_call" | custom-call | tf_op jit(solution)/shard_map/gain/pallas_call | solution.py:629
  78.6 56.8 %all-to-all-done.lines = f32[32,168,128]{2,1,0:T(8,128)} async-done(((f32[32,168,128]{2,1,0:T(8,128)}), f32[32,168,128]{2,1,0:T(8,128)}, u32[]{:S(2)}, u32[]{:S(2)}) %all-to-all-start) | async-done | bytes 2752544 | tf_op jit(solution)/shard_map/all_to_all | solution.py:691
  135.5 12.7 %line.1 = f32[32,168,128]{2,1,0:T(8,128)S(1)} custom-call(f32[32,168,128]{2,1,0:T(8,128)} %all-to-all-done.lines, f32[2,11,256,128]{3,2,1,0:T(8,128)} %gain.1, f32[2,17,8,256]{3,2,1,0:T(8,128)S(1)} %copy-done.6, bf16[512,256]{1,0:T(8,128)(2,1)S(1)} %copy-done.7, bf16[512,256]{1,0:T(8,128)(2,1)S(1)} %copy-done.8, bf16[256,512]{1,0:T(8,128)(2,1)S(1)} %copy-done.9, ...), custom_call_target="tpu_custom_call" | custom-call | tf_op jit(solution)/shard_map/line/pallas_call | solution.py:702
  148.2 66.5 %all_to_all.10.source = f32[32,168,128]{2,1,0:T(8,128)} all-to-all(f32[32,168,128]{2,1,0:T(8,128)S(1)} %line.1), channel_id=1, replica_groups=mesh['row'=4,'col'=8] {'row','col'}, dimensions={0} | all-to-all | bytes 5505024 | tf_op jit(solution)/shard_map/all_to_all | solution.py:717
  214.7 11.4 %column_inverse.1 = (f32[1024,128]{1,0:T(8,128)}, f32[1024,128]{1,0:T(8,128)}, f32[1024,128]{1,0:T(8,128)}, f32[1024,128]{1,0:T(8,128)}, f32[1032,128]{1,0:T(8,1...) custom-call(s32[1]{0:T(128)} %bitcast.place, ...), custom_call_target="tpu_custom_call" | custom-call | tf_op jit(solution)/shard_map/column_inverse/pallas_call | solution.py:724
  226.1 0.1 collective-permute-start.12
  226.2 1.1 collective-permute-start.13
  227.3 2.4 collective-permute-start.14
  229.7 0.0 collective-permute-start.9
  229.7 1.2 collective-permute-done.9
  232.1 1.4 collective-permute-start.10
  233.5 2.2 collective-permute-done.10
  236.4 1.4 collective-permute-start.11
  237.8 3.1 %collective-permute-done.11.peak_two = f32[1]{0:T(128)} collective-permute-done((f32[1]{0:T(128)}, f32[1]{0:T(128)}, u32[]{:S(2)}, u32[]{:S(2)}) %collective-permute-start.11) | collective-permute-done | bytes 36 | tf_op jit(solution)/shard_map/ppermute | solution.py:748
  240.9 1.0 copy-done
  241.9 1.0 copy-done.1
  242.9 1.0 copy-done.2
  244.0 1.0 copy-done.3
  245.0 1.0 copy-done.5
  246.1 0.8 stamp.1
  246.9 0.1 collective-permute-start.15
  247.1 1.0 collective-permute-start.16
  248.1 3.8 %collective-permute-done.13.refs_2_ = f32[1024,128]{1,0:T(8,128)S(1)} collective-permute-done((f32[1024,128]{1,0:T(8,128)}, f32[1024,128]{1,0:T(8,128)S(1)}, u32[]{:S(2)}, u32[]{:S(2)}) %collective-permute-start.13) | collective-permute-done | bytes 524320 | tf_op jit(solution)/shard_map/ppermute | solution.py:589
  251.9 0.5 collective-permute-done.14.refs_3_
  252.4 1.2 collective-permute-start.17
  253.6 10.2 %collective-permute-done.15.refs_5_ = f32[1032,128]{1,0:T(8,128)S(1)} collective-permute-done((f32[1032,128]{1,0:T(8,128)S(1)}, f32[1032,128]{1,0:T(8,128)S(1)}, u32[]{:S(2)}, u32[]{:S(2)}) %collective-permute-start.15) | collective-permute-done | bytes 528416 | tf_op jit(solution)/shard_map/ppermute | solution.py:589
  263.8 10.9 %collective-permute-done.16.refs_6_ = f32[1032,128]{1,0:T(8,128)S(1)} collective-permute-done((f32[1032,128]{1,0:T(8,128)S(1)}, f32[1032,128]{1,0:T(8,128)S(1)}, u32[]{:S(2)}, u32[]{:S(2)}) %collective-permute-start.16) | collective-permute-done | bytes 528416 | tf_op jit(solution)/shard_map/ppermute | solution.py:589
  274.7 3.3 %encode.1 = (f32[1024,512]{1,0:T(8,128)}, f32[1024,512]{1,0:T(8,128)}) custom-call(s32[1]{0:T(128)} %bitcast.place, f32[1]{0:T(128)} %max.7.peak_one, f32[1]{0:T(128)} %collective-permute-done.11.peak_two, f32[1024,128]{1,0:T(8,128)S(1)} %get-tuple-element.50.refs_0_, f32[1024,128]{1,0:T(8,128)S(1)} %collective-permute-done.12.refs_1_, ...), custom_call_target="tpu_custom_call" | custom-call | tf_op jit(solution)/shard_map/encode/pallas_call | solution.py:783
  (29 shorter events, 0.1 us)
Async XLA Ops:
  2.9 6.1 %copy-start.20 = (f32[2,4,64,128]{3,2,1,0:T(8,128)S(1)}, f32[2,4,64,128]{3,2,1,0:T(8,128)}, u32[]{:S(2)}) copy-start(f32[2,4,64,128]{3,2,1,0:T(8,128)} %get-tuple-element.42) | copy-start | bytes 786436
  2.9 11.1 %copy-start.19 = (f32[2,4,64,128]{3,2,1,0:T(8,128)S(1)}, f32[2,4,64,128]{3,2,1,0:T(8,128)}, u32[]{:S(2)}) copy-start(f32[2,4,64,128]{3,2,1,0:T(8,128)} %get-tuple-element.43) | copy-start | bytes 786436
  2.9 11.0 %collective-permute-start.6 = (f32[2,4,64,128]{3,2,1,0:T(8,128)}, f32[2,4,64,128]{3,2,1,0:T(8,128)S(1)}, u32[]{:S(2)}, u32[]{:S(2)}) collective-permute-start(f32[2,4,64,128]{3,2,1,0:T(8,128)} %get-tuple-element.41), channel_id=1, source_target_pairs={{0,8},{8,0},{16,24},{24,16},{1,9},{9,1},{17,25},{25,17},{2,10},{10... | collective-permute-start | bytes 786440 | tf_op jit(solution)/shard_map/ppermute | solution.py:589
  8.8 37.0 %copy-start.11 = (f32[2,4,64,128]{3,2,1,0:T(8,128)S(1)}, f32[2,4,64,128]{3,2,1,0:T(8,128)}, u32[]{:S(2)}) copy-start(f32[2,4,64,128]{3,2,1,0:T(8,128)} %get-tuple-element.40.refs_0_) | copy-start | bytes 786436
  8.9 37.0 %copy-start.15 = (bf16[336,128]{1,0:T(8,128)(2,1)S(1)}, bf16[336,128]{1,0:T(8,128)(2,1)}, u32[]{:S(2)}) copy-start(bf16[336,128]{1,0:T(8,128)(2,1)} %constant.65.clone.matrix) | copy-start | bytes 258052
  8.9 37.0 %copy-start.18 = (f32[64,128]{1,0:T(8,128)S(1)}, f32[64,128]{1,0:T(8,128)}, u32[]{:S(2)}) copy-start(f32[64,128]{1,0:T(8,128)} %constant.64.clone.twist) | copy-start | bytes 98308
  8.9 34.1 %collective-permute-start.3 = (f32[2,4,128,128]{3,2,1,0:T(8,128)}, f32[2,4,128,128]{3,2,1,0:T(8,128)S(1)}, u32[]{:S(2)}, u32[]{:S(2)}) collective-permute-start(f32[2,4,128,128]{3,2,1,0:T(8,128)} %get-tuple-element.37), channel_id=1, source_target_pairs={{0,8},{8,0},{16,24},{24,16},{1,9},{9,1},{17,25},{25,17},{2,10},{10... | collective-permute-start | bytes 1572872 | tf_op jit(solution)/shard_map/ppermute | solution.py:589
  9.0 9.6 %collective-permute-start.7 = (f32[2,4,64,128]{3,2,1,0:T(8,128)S(1)}, f32[2,4,64,128]{3,2,1,0:T(8,128)S(1)}, u32[]{:S(2)}, u32[]{:S(2)}) collective-permute-start(f32[2,4,64,128]{3,2,1,0:T(8,128)S(1)} %copy-done.20), channel_id=1, source_target_pairs={{0,16},{8,24},{16,0},{24,8},{1,17},{9,25},{17,1},{25,9},{2,18},{10... | collective-permute-start | bytes 786440 | tf_op jit(solution)/shard_map/ppermute | solution.py:589
  11.0 40.4 %collective-permute-start.4 = (f32[2,4,128,128]{3,2,1,0:T(8,128)}, f32[2,4,128,128]{3,2,1,0:T(8,128)S(1)}, u32[]{:S(2)}, u32[]{:S(2)}) collective-permute-start(f32[2,4,128,128]{3,2,1,0:T(8,128)} %get-tuple-element.38), channel_id=1, source_target_pairs={{0,16},{8,24},{16,0},{24,8},{1,17},{9,25},{17,1},{25,9},{2,18},{10... | collective-permute-start | bytes 1572872 | tf_op jit(solution)/shard_map/ppermute | solution.py:589
  11.1 40.4 %collective-permute-start.5 = (f32[2,4,128,128]{3,2,1,0:T(8,128)}, f32[2,4,128,128]{3,2,1,0:T(8,128)S(1)}, u32[]{:S(2)}, u32[]{:S(2)}) collective-permute-start(f32[2,4,128,128]{3,2,1,0:T(8,128)} %get-tuple-element.39), channel_id=1, source_target_pairs={{0,24},{8,16},{16,8},{24,0},{1,25},{9,17},{17,9},{25,1},{2,26},{10... | collective-permute-start | bytes 1572872 | tf_op jit(solution)/shard_map/ppermute | solution.py:589
  14.0 29.0 %collective-permute-start.8 = (f32[2,4,64,128]{3,2,1,0:T(8,128)S(1)}, f32[2,4,64,128]{3,2,1,0:T(8,128)S(1)}, u32[]{:S(2)}, u32[]{:S(2)}) collective-permute-start(f32[2,4,64,128]{3,2,1,0:T(8,128)S(1)} %copy-done.19), channel_id=1, source_target_pairs={{0,24},{8,16},{16,8},{24,0},{1,25},{9,17},{17,9},{25,1},{2,26},{10... | collective-permute-start | bytes 786440 | tf_op jit(solution)/shard_map/ppermute | solution.py:589
  18.5 32.9 %copy-start.4 = (f32[2,4,128,128]{3,2,1,0:T(8,128)S(1)}, f32[2,4,128,128]{3,2,1,0:T(8,128)}, u32[]{:S(2)}) copy-start(f32[2,4,128,128]{3,2,1,0:T(8,128)} %get-tuple-element.36.refs_0_) | copy-start | bytes 1572868
  18.6 32.9 %copy-start.13 = (bf16[336,256]{1,0:T(8,128)(2,1)S(1)}, bf16[336,256]{1,0:T(8,128)(2,1)}, u32[]{:S(2)}) copy-start(bf16[336,256]{1,0:T(8,128)(2,1)} %constant.67.clone.matrix) | copy-start | bytes 516100
  18.6 32.9 %copy-start.16 = (f32[128,128]{1,0:T(8,128)S(1)}, f32[128,128]{1,0:T(8,128)}, u32[]{:S(2)}) copy-start(f32[128,128]{1,0:T(8,128)} %constant.66.clone.twist) | copy-start | bytes 196612
  18.6 40.0 %collective-permute-start = (f32[2,4,64,128]{3,2,1,0:T(8,128)}, f32[2,4,64,128]{3,2,1,0:T(8,128)S(1)}, u32[]{:S(2)}, u32[]{:S(2)}) collective-permute-start(f32[2,4,64,128]{3,2,1,0:T(8,128)} %get-tuple-element.33), channel_id=1, source_target_pairs={{0,8},{8,0},{16,24},{24,16},{1,9},{9,1},{17,25},{25,17},{2,10},{10... | collective-permute-start | bytes 786440 | tf_op jit(solution)/shard_map/ppermute | solution.py:589
  42.9 15.7 %collective-permute-start.1 = (f32[2,4,64,128]{3,2,1,0:T(8,128)}, f32[2,4,64,128]{3,2,1,0:T(8,128)S(1)}, u32[]{:S(2)}, u32[]{:S(2)}) collective-permute-start(f32[2,4,64,128]{3,2,1,0:T(8,128)} %get-tuple-element.34), channel_id=1, source_target_pairs={{0,16},{8,24},{16,0},{24,8},{1,17},{9,25},{17,1},{25,9},{2,18},{10... | collective-permute-start | bytes 786440 | tf_op jit(solution)/shard_map/ppermute | solution.py:589
  42.9 15.7 %collective-permute-start.2 = (f32[2,4,64,128]{3,2,1,0:T(8,128)}, f32[2,4,64,128]{3,2,1,0:T(8,128)S(1)}, u32[]{:S(2)}, u32[]{:S(2)}) collective-permute-start(f32[2,4,64,128]{3,2,1,0:T(8,128)} %get-tuple-element.35), channel_id=1, source_target_pairs={{0,24},{8,16},{16,8},{24,0},{1,25},{9,17},{17,9},{25,1},{2,26},{10... | collective-permute-start | bytes 786440 | tf_op jit(solution)/shard_map/ppermute | solution.py:589
  51.5 7.2 %copy-start.12 = (f32[2,4,64,128]{3,2,1,0:T(8,128)S(1)}, f32[2,4,64,128]{3,2,1,0:T(8,128)}, u32[]{:S(2)}) copy-start(f32[2,4,64,128]{3,2,1,0:T(8,128)} %get-tuple-element.32.refs_0_) | copy-start | bytes 786436
  51.5 7.2 %copy-start.14 = (bf16[336,128]{1,0:T(8,128)(2,1)S(1)}, bf16[336,128]{1,0:T(8,128)(2,1)}, u32[]{:S(2)}) copy-start(bf16[336,128]{1,0:T(8,128)(2,1)} %constant.69.clone.matrix) | copy-start | bytes 258052
  51.5 7.2 %copy-start.17 = (f32[64,128]{1,0:T(8,128)S(1)}, f32[64,128]{1,0:T(8,128)}, u32[]{:S(2)}) copy-start(f32[64,128]{1,0:T(8,128)} %constant.68.clone.twist) | copy-start | bytes 98308
  64.2 71.2 %all-to-all-start = ((f32[32,168,128]{2,1,0:T(8,128)}), f32[32,168,128]{2,1,0:T(8,128)}, u32[]{:S(2)}, u32[]{:S(2)}) async-start(f32[32,168,128]{2,1,0:T(8,128)} %column_forward.5), calls=%async_computation | async-start | bytes 5505024 | tf_op jit(solution)/shard_map/all_to_all | solution.py:691
  71.2 64.2 %copy-start.6 = (f32[2,17,8,256]{3,2,1,0:T(8,128)S(1)}, f32[2,17,8,256]{3,2,1,0:T(8,128)}, u32[]{:S(2)}) copy-start(f32[2,17,8,256]{3,2,1,0:T(8,128)} %constant.70.clone.twist) | copy-start | bytes 835588
  71.3 64.2 %copy-start.7 = (bf16[512,256]{1,0:T(8,128)(2,1)S(1)}, bf16[512,256]{1,0:T(8,128)(2,1)}, u32[]{:S(2)}) copy-start(bf16[512,256]{1,0:T(8,128)(2,1)} %constant.71.clone.fwd_high) | copy-start | bytes 786436
  71.3 64.2 %copy-start.8 = (bf16[512,256]{1,0:T(8,128)(2,1)S(1)}, bf16[512,256]{1,0:T(8,128)(2,1)}, u32[]{:S(2)}) copy-start(bf16[512,256]{1,0:T(8,128)(2,1)} %constant.72.clone.fwd_low) | copy-start | bytes 786436
  71.3 64.2 %copy-start.9 = (bf16[256,512]{1,0:T(8,128)(2,1)S(1)}, bf16[256,512]{1,0:T(8,128)(2,1)}, u32[]{:S(2)}) copy-start(bf16[256,512]{1,0:T(8,128)(2,1)} %constant.73.clone.inv_high) | copy-start | bytes 786436
  71.3 64.2 %copy-start.10 = (bf16[256,512]{1,0:T(8,128)(2,1)S(1)}, bf16[256,512]{1,0:T(8,128)(2,1)}, u32[]{:S(2)}) copy-start(bf16[256,512]{1,0:T(8,128)(2,1)} %constant.74.clone.inv_low) | copy-start | bytes 786436
  226.1 22.0 %collective-permute-start.12 = (f32[1024,128]{1,0:T(8,128)}, f32[1024,128]{1,0:T(8,128)S(1)}, u32[]{:S(2)}, u32[]{:S(2)}) collective-permute-start(f32[1024,128]{1,0:T(8,128)} %get-tuple-element.51), channel_id=1, source_target_pairs={{0,8},{8,0},{16,24},{24,16},{1,9},{9,1},{17,25},{25,17},{2,10},{10... | collective-permute-start | bytes 1572872 | tf_op jit(solution)/shard_map/ppermute | solution.py:589
  226.2 25.7 %collective-permute-start.13 = (f32[1024,128]{1,0:T(8,128)}, f32[1024,128]{1,0:T(8,128)S(1)}, u32[]{:S(2)}, u32[]{:S(2)}) collective-permute-start(f32[1024,128]{1,0:T(8,128)} %get-tuple-element.52), channel_id=1, source_target_pairs={{0,16},{8,24},{16,0},{24,8},{1,17},{9,25},{17,1},{25,9},{2,18},{10... | collective-permute-start | bytes 1572872 | tf_op jit(solution)/shard_map/ppermute | solution.py:589
  227.3 25.1 %collective-permute-start.14 = (f32[1024,128]{1,0:T(8,128)}, f32[1024,128]{1,0:T(8,128)S(1)}, u32[]{:S(2)}, u32[]{:S(2)}) collective-permute-start(f32[1024,128]{1,0:T(8,128)} %get-tuple-element.53), channel_id=1, source_target_pairs={{0,24},{8,16},{16,8},{24,0},{1,25},{9,17},{17,9},{25,1},{2,26},{10... | collective-permute-start | bytes 1572872 | tf_op jit(solution)/shard_map/ppermute | solution.py:589
  229.7 1.2 collective-permute-start.9
  232.1 3.6 %collective-permute-start.10 = (f32[1]{0:T(128)}, f32[1]{0:T(128)}, u32[]{:S(2)}, u32[]{:S(2)}) collective-permute-start(f32[1]{0:T(128)} %max.6), channel_id=1, source_target_pairs={{0,2},{1,3},{2,0},{3,1},{4,6},{5,7},{6,4},{7,5},{8,10},{9,11},{10,... | collective-permute-start | bytes 20 | tf_op jit(solution)/shard_map/ppermute | solution.py:748
  236.4 4.5 %collective-permute-start.11 = (f32[1]{0:T(128)}, f32[1]{0:T(128)}, u32[]{:S(2)}, u32[]{:S(2)}) collective-permute-start(f32[1]{0:T(128)} %max.7.peak_one), channel_id=1, source_target_pairs={{0,4},{1,5},{2,6},{3,7},{4,0},{5,1},{6,2},{7,3},{8,12},{9,13},{10,... | collective-permute-start | bytes 20 | tf_op jit(solution)/shard_map/ppermute | solution.py:748
  240.8 1.0 copy-start
  241.9 1.0 copy-start.1
  242.9 1.0 copy-start.2
  244.0 1.0 copy-start.3
  245.0 1.0 copy-start.5
  246.9 16.9 %collective-permute-start.15 = (f32[1032,128]{1,0:T(8,128)S(1)}, f32[1032,128]{1,0:T(8,128)S(1)}, u32[]{:S(2)}, u32[]{:S(2)}) collective-permute-start(f32[1032,128]{1,0:T(8,128)S(1)} %get-tuple-element.59), channel_id=1, source_target_pairs={{0,8},{8,0},{16,24},{24,16},{1,9},{9,1},{17,25},{25,17},{2,10},{10... | collective-permute-start | bytes 1585160 | tf_op jit(solution)/shard_map/ppermute | solution.py:589
  247.1 27.6 %collective-permute-start.16 = (f32[1032,128]{1,0:T(8,128)S(1)}, f32[1032,128]{1,0:T(8,128)S(1)}, u32[]{:S(2)}, u32[]{:S(2)}) collective-permute-start(f32[1032,128]{1,0:T(8,128)S(1)} %get-tuple-element.60), channel_id=1, source_target_pairs={{0,16},{8,24},{16,0},{24,8},{1,17},{9,25},{17,1},{25,9},{2,18},{10... | collective-permute-start | bytes 1585160 | tf_op jit(solution)/shard_map/ppermute | solution.py:589
  252.4 22.3 %collective-permute-start.17 = (f32[1032,128]{1,0:T(8,128)S(1)}, f32[1032,128]{1,0:T(8,128)S(1)}, u32[]{:S(2)}, u32[]{:S(2)}) collective-permute-start(f32[1032,128]{1,0:T(8,128)S(1)} %get-tuple-element.61), channel_id=1, source_target_pairs={{0,24},{8,16},{16,8},{24,0},{1,25},{9,17},{17,9},{25,1},{2,26},{10... | collective-permute-start | bytes 1585160 | tf_op jit(solution)/shard_map/ppermute | solution.py:589

commit v15 on v14

--- a/solution.py
+++ b/solution.py
@@ -20,7 +20,7 @@
 HALF = 40
 CHUNKS = 2
 CHUNK = INNER // CHUNKS
-FRONT = ((0, 64), (128, 128), (64, 64))
+FRONT = ((0, 128), (128, 128))
 SPARE = 8
 
 
@@ -765,7 +765,7 @@
     )(*peaks, *near[1][1:], near[0][0], near[1][0])
     near[1][1:] = stamped[:others]
     near[0][0], near[1][0] = stamped[others:]
-    near[0][1:], near[1][-1] = lax.optimization_barrier((near[0][1:], near[1][-1]))
+    near[0][1:], near[1][1] = lax.optimization_barrier((near[0][1:], near[1][1]))
     near[1] = exchange(near[1], "row")
     if width != 128:
         peak_sq = jnp.maximum(*peaks)[0]

time: 279 us -> 273 us (0.978)
  waiting for transfers between devices: 112 us -> 119 us
  Pallas kernels: 59.6 us -> 53.2 us
  starting transfers between devices: 30.7 us -> 25.5 us
    ppermute x15 -> x12, waiting for transfers between devices: 49 us -> 55 us  [exchange(): lax.ppermute(pieces[j], axis, [(i, i ^ j) for i in range(total)])]
    pallas_call x3 -> x2, Pallas kernels: 17.3 us -> 12.8 us  [body(): pl.pallas_call(partial(column_forward_kernel, row_total), in_specs=[whole...]
    ppermute x15 -> x12, starting transfers between devices: 20.9 us -> 17.7 us  [exchange(): lax.ppermute(pieces[j], axis, [(i, i ^ j) for i in range(total)])]
    pallas_call x3 -> x2, Pallas kernels: 7.42 us -> 5.84 us  [body(): pl.pallas_call(pack_kernel, grid=(1,), in_specs=[whole(pltpu.SMEM)] + [pl...]
  transfers between devices with their start and end apart: 19 -> 16, of which waited for: 10 -> 10; matrix products, arithmetic and copies ran while one was open for 0% -> 0% of each run, Pallas kernels for 9% -> 6%
where the time goes in v15:
time: 273 us; the launch traced here: 272 us
  waiting for transfers between devices  119 us (44%)
  blocking collectives  66.5 us (24%)
  Pallas kernels  53.2 us (19%)
  starting transfers between devices  25.5 us (9%)
  local copies, waits for them, and re-layouts  5.28 us (2%)
    all_to_all x1, blocking collectives, body(): lax.all_to_all(lines, ('row', 'col'), split_axis=0, concat_axis=0, tiled=...  66.5 us
    all_to_all x1, waiting for transfers between devices, body(): lax.all_to_all(lines, ('row', 'col'), split_axis=0, concat_axis=0, tiled=...  56.8 us
    ppermute x12, waiting for transfers between devices, exchange(): lax.ppermute(pieces[j], axis, [(i, i ^ j) for i in range(total)])  55 us
    ppermute x12, starting transfers between devices, exchange(): lax.ppermute(pieces[j], axis, [(i, i ^ j) for i in range(total)])  17.7 us
    pallas_call x2, Pallas kernels, body(): pl.pallas_call(partial(column_forward_kernel, row_total), in_specs=[whole...  12.8 us
    pallas_call x1, Pallas kernels, body(): pl.pallas_call(partial(line_kernel, order, own, tail), grid=(-(-own // at...  12.7 us
    pallas_call x1, Pallas kernels, body(): pl.pallas_call(partial(column_inverse_kernel, row_total), in_specs=[whole...  11.3 us
    ppermute x3, waiting for transfers between devices, body(): peaks = [peak_sq, lax.ppermute(peak_sq, 'col', partner)]  6.89 us
  transfers between devices with their start and end apart: 16, of which 10 were waited for; matrix products, arithmetic and copies ran while one was open for 0% of the time, Pallas kernels for 6%

profile of v15, /device:TPU:0, one launch (start us, length us, event | category | flops | bytes accessed | tf_op | source)
XLA Modules:
  0.0 272.4 jit_solution(18294841179725564291)
XLA Ops:
  0.6 2.9 %pack.3 = (f32[2,4,128,128]{3,2,1,0:T(8,128)}, f32[2,4,128,128]{3,2,1,0:T(8,128)}, f32[2,4,128,128]{3,2,1,0:T(8,128)}, f32[2,4,128,128]{3,2,1,0:T(8,128)}) custom-call(s32[1]{0:T(128)} %bitcast.place, f32[4,256,512]{2,1,0:T(8,128)} %bitcast.4, f32[4,256,512]{2,1,0:T(8,128)} %bitcast.6), custom_call_target="tpu_custom_call" | custom-call | bytes 4194304 | tf_op jit(solution)/shard_map/pack/pallas_call | solution.py:650
  3.6 0.0 copy-start.6
  3.6 0.0 copy-start.13
  3.6 0.0 copy-start.15
  3.6 3.0 %collective-permute-start.3 = (f32[2,4,128,128]{3,2,1,0:T(8,128)}, f32[2,4,128,128]{3,2,1,0:T(8,128)S(1)}, u32[]{:S(2)}, u32[]{:S(2)}) collective-permute-start(f32[2,4,128,128]{3,2,1,0:T(8,128)} %get-tuple-element.33), channel_id=1, source_target_pairs={{0,8},{8,0},{16,24},{24,16},{1,9},{9,1},{17,25},{25,17},{2,10},{10... | collective-permute-start | bytes 1572872 | tf_op jit(solution)/shard_map/ppermute | solution.py:589
  6.6 1.5 collective-permute-start.4
  8.1 0.0 collective-permute-start.5
  8.2 2.9 %pack.2 = (f32[2,4,128,128]{3,2,1,0:T(8,128)}, f32[2,4,128,128]{3,2,1,0:T(8,128)}, f32[2,4,128,128]{3,2,1,0:T(8,128)}, f32[2,4,128,128]{3,2,1,0:T(8,128)}) custom-call(s32[1]{0:T(128)} %bitcast.place, f32[4,256,512]{2,1,0:T(8,128)} %bitcast.5, f32[4,256,512]{2,1,0:T(8,128)} %bitcast.7), custom_call_target="tpu_custom_call" | custom-call | bytes 4194304 | tf_op jit(solution)/shard_map/pack/pallas_call | solution.py:650
  11.1 0.0 copy-start.5
  11.1 0.0 copy-start.12
  11.1 0.0 copy-start.14
  11.1 2.0 collective-permute-start
  13.1 1.5 collective-permute-start.1
  14.6 4.9 %collective-permute-done.3.refs_1_ = f32[2,4,128,128]{3,2,1,0:T(8,128)S(1)} collective-permute-done((f32[2,4,128,128]{3,2,1,0:T(8,128)}, f32[2,4,128,128]{3,2,1,0:T(8,128)S(1)}, u32[]{:S(2)}, u32[]{:S(2)}) %collective-permute-start.3) | collective-permute-done | bytes 524320 | tf_op jit(solution)/shard_map/ppermute | solution.py:589
  19.6 3.0 %collective-permute-start.2 = (f32[2,4,128,128]{3,2,1,0:T(8,128)}, f32[2,4,128,128]{3,2,1,0:T(8,128)S(1)}, u32[]{:S(2)}, u32[]{:S(2)}) collective-permute-start(f32[2,4,128,128]{3,2,1,0:T(8,128)} %get-tuple-element.31), channel_id=1, source_target_pairs={{0,24},{8,16},{16,8},{24,0},{1,25},{9,17},{17,9},{25,1},{2,26},{10... | collective-permute-start | bytes 1572872 | tf_op jit(solution)/shard_map/ppermute | solution.py:589
  22.6 10.3 %collective-permute-done.4.refs_2_ = f32[2,4,128,128]{3,2,1,0:T(8,128)S(1)} collective-permute-done((f32[2,4,128,128]{3,2,1,0:T(8,128)}, f32[2,4,128,128]{3,2,1,0:T(8,128)S(1)}, u32[]{:S(2)}, u32[]{:S(2)}) %collective-permute-start.4) | collective-permute-done | bytes 524320 | tf_op jit(solution)/shard_map/ppermute | solution.py:589
  32.9 0.0 collective-permute-done.5.refs_3_
  32.9 0.0 copy-done.6
  32.9 0.0 copy-done.13
  32.9 0.0 copy-done.15
  32.9 5.9 %column_forward.2.refs_4_ = f32[32,168,128]{2,1,0:T(8,128)S(1)} custom-call(s32[1]{0:T(128)} %bitcast.place, f32[128,128]{1,0:T(8,128)S(1)} %copy-done.15, bf16[336,256]{1,0:T(8,128)(2,1)S(1)} %copy-done.13, f32[2,4,128,128]{3,2,1,0:T(8,128)S(1)} %copy-done.6, f32[2,4,128,128]{3,2,1,0:T(8,128)S(1)} %collective-permute-done.3.refs_1_, ...), custom_call_target="tpu_custom_call" | custom-call | bytes 20971520 | tf_op jit(solution)/shard_map/column_forward/pallas_call | solution.py:672
  38.8 3.3 %collective-permute-done.refs_1_ = f32[2,4,128,128]{3,2,1,0:T(8,128)S(1)} collective-permute-done((f32[2,4,128,128]{3,2,1,0:T(8,128)}, f32[2,4,128,128]{3,2,1,0:T(8,128)S(1)}, u32[]{:S(2)}, u32[]{:S(2)}) %collective-permute-start) | collective-permute-done | bytes 524320 | tf_op jit(solution)/shard_map/ppermute | solution.py:589
  42.1 11.8 %collective-permute-done.1.refs_2_ = f32[2,4,128,128]{3,2,1,0:T(8,128)S(1)} collective-permute-done((f32[2,4,128,128]{3,2,1,0:T(8,128)}, f32[2,4,128,128]{3,2,1,0:T(8,128)S(1)}, u32[]{:S(2)}, u32[]{:S(2)}) %collective-permute-start.1) | collective-permute-done | bytes 524320 | tf_op jit(solution)/shard_map/ppermute | solution.py:589
  53.9 0.0 collective-permute-done.2.refs_3_
  53.9 6.9 %column_forward.3 = f32[32,168,128]{2,1,0:T(8,128)} custom-call(s32[1]{0:T(128)} %bitcast.place, f32[128,128]{1,0:T(8,128)S(1)} %copy-done.14, bf16[336,256]{1,0:T(8,128)(2,1)S(1)} %copy-done.12, f32[2,4,128,128]{3,2,1,0:T(8,128)S(1)} %copy-done.5, f32[2,4,128,128]{3,2,1,0:T(8,128)S(1)} %collective-permute-done.refs_1_, ...), custom_call_target="tpu_custom_call" | custom-call | bytes 20971520 | tf_op jit(solution)/shard_map/column_forward/pallas_call | solution.py:672
  60.8 5.0 %all-to-all-start = ((f32[32,168,128]{2,1,0:T(8,128)}), f32[32,168,128]{2,1,0:T(8,128)}, u32[]{:S(2)}, u32[]{:S(2)}) async-start(f32[32,168,128]{2,1,0:T(8,128)} %column_forward.3), calls=%async_computation | async-start | bytes 5505024 | tf_op jit(solution)/shard_map/all_to_all | solution.py:691
  65.8 0.0 copy-start.7
  65.9 0.0 copy-start.8
  65.9 0.0 copy-start.9
  65.9 0.0 copy-start.10
  65.9 0.0 copy-start.11
  65.9 0.6 pad_add_fusion.place
  66.5 6.7 %gain.1 = f32[2,11,256,128]{3,2,1,0:T(8,128)} custom-call(s32[2]{0:T(128)} %pad_add_fusion.place), custom_call_target="tpu_custom_call" | custom-call | tf_op jit(solution)/shard_map/gain/pallas_call | solution.py:629
  73.2 56.8 %all-to-all-done.lines = f32[32,168,128]{2,1,0:T(8,128)} async-done(((f32[32,168,128]{2,1,0:T(8,128)}), f32[32,168,128]{2,1,0:T(8,128)}, u32[]{:S(2)}, u32[]{:S(2)}) %all-to-all-start) | async-done | bytes 2752544 | tf_op jit(solution)/shard_map/all_to_all | solution.py:691
  130.0 0.0 copy-done.7
  130.0 0.0 copy-done.9
  130.1 12.7 %line.1 = f32[32,168,128]{2,1,0:T(8,128)S(1)} custom-call(f32[32,168,128]{2,1,0:T(8,128)} %all-to-all-done.lines, f32[2,11,256,128]{3,2,1,0:T(8,128)} %gain.1, f32[2,17,8,256]{3,2,1,0:T(8,128)S(1)} %copy-done.7, bf16[512,256]{1,0:T(8,128)(2,1)S(1)} %copy-done.11, bf16[512,256]{1,0:T(8,128)(2,1)S(1)} %copy-done.10, bf16[256,512]{1,0:T(8,128)(2,1)S(1)} %copy-done.9, ...), custom_call_target="tpu_custom_call" | custom-call | tf_op jit(solution)/shard_map/line/pallas_call | solution.py:702
  142.8 66.5 %all_to_all.10.source = f32[32,168,128]{2,1,0:T(8,128)} all-to-all(f32[32,168,128]{2,1,0:T(8,128)S(1)} %line.1), channel_id=1, replica_groups=mesh['row'=4,'col'=8] {'row','col'}, dimensions={0} | all-to-all | bytes 5505024 | tf_op jit(solution)/shard_map/all_to_all | solution.py:717
  209.3 11.3 %column_inverse.1 = (f32[1024,128]{1,0:T(8,128)}, f32[1024,128]{1,0:T(8,128)}, f32[1024,128]{1,0:T(8,128)}, f32[1024,128]{1,0:T(8,128)}, f32[1032,128]{1,0:T(8,1...) custom-call(s32[1]{0:T(128)} %bitcast.place, ...), custom_call_target="tpu_custom_call" | custom-call | tf_op jit(solution)/shard_map/column_inverse/pallas_call | solution.py:724
  220.7 0.1 collective-permute-start.9
  220.8 1.1 collective-permute-start.10
  221.9 2.4 collective-permute-start.11
  224.2 0.0 collective-permute-start.6
  224.2 1.3 collective-permute-done.6
  226.7 1.4 collective-permute-start.7
  228.1 2.3 collective-permute-done.7
  231.0 1.4 collective-permute-start.8
  232.4 3.2 %collective-permute-done.8.peak_two = f32[1]{0:T(128)} collective-permute-done((f32[1]{0:T(128)}, f32[1]{0:T(128)}, u32[]{:S(2)}, u32[]{:S(2)}) %collective-permute-start.8) | collective-permute-done | bytes 36 | tf_op jit(solution)/shard_map/ppermute | solution.py:748
  235.6 1.0 copy-done
  236.7 1.0 copy-done.1
  237.7 1.0 copy-done.2
  238.7 1.0 copy-done.3
  239.8 1.0 copy-done.4
  240.8 0.7 stamp.1
  241.5 0.6 collective-permute-start.13
  242.2 1.0 collective-permute-start.14
  243.2 0.0 collective-permute-done.9.refs_1_
  243.2 14.7 %collective-permute-done.10.refs_2_ = f32[1024,128]{1,0:T(8,128)S(1)} collective-permute-done((f32[1024,128]{1,0:T(8,128)}, f32[1024,128]{1,0:T(8,128)S(1)}, u32[]{:S(2)}, u32[]{:S(2)}) %collective-permute-start.10) | collective-permute-done | bytes 524320 | tf_op jit(solution)/shard_map/ppermute | solution.py:589
  257.9 0.0 collective-permute-done.11.refs_3_
  257.9 1.5 collective-permute-start.12
  259.3 9.9 %collective-permute-done.13.refs_6_ = f32[1032,128]{1,0:T(8,128)S(1)} collective-permute-done((f32[1032,128]{1,0:T(8,128)S(1)}, f32[1032,128]{1,0:T(8,128)S(1)}, u32[]{:S(2)}, u32[]{:S(2)}) %collective-permute-start.13) | collective-permute-done | bytes 528416 | tf_op jit(solution)/shard_map/ppermute | solution.py:589
  269.3 0.0 collective-permute-done.14.refs_7_
  269.3 0.0 collective-permute-done.12.refs_5_
  269.3 3.2 %encode.1 = (f32[1024,512]{1,0:T(8,128)}, f32[1024,512]{1,0:T(8,128)}) custom-call(s32[1]{0:T(128)} %bitcast.place, f32[1]{0:T(128)} %max.7.peak_one, f32[1]{0:T(128)} %collective-permute-done.8.peak_two, f32[1024,128]{1,0:T(8,128)S(1)} %get-tuple-element.42.refs_0_, f32[1024,128]{1,0:T(8,128)S(1)} %collective-permute-done.9.refs_1_, ...), custom_call_target="tpu_custom_call" | custom-call | tf_op jit(solution)/shard_map/encode/pallas_call | solution.py:783
  (11 shorter events, 0.0 us)
Async XLA Ops:
  3.6 29.3 %copy-start.6 = (f32[2,4,128,128]{3,2,1,0:T(8,128)S(1)}, f32[2,4,128,128]{3,2,1,0:T(8,128)}, u32[]{:S(2)}) copy-start(f32[2,4,128,128]{3,2,1,0:T(8,128)} %get-tuple-element.32.refs_0_) | copy-start | bytes 1572868
  3.6 29.3 %copy-start.13 = (bf16[336,256]{1,0:T(8,128)(2,1)S(1)}, bf16[336,256]{1,0:T(8,128)(2,1)}, u32[]{:S(2)}) copy-start(bf16[336,256]{1,0:T(8,128)(2,1)} %constant.61.clone.matrix) | copy-start | bytes 516100
  3.6 29.3 %copy-start.15 = (f32[128,128]{1,0:T(8,128)S(1)}, f32[128,128]{1,0:T(8,128)}, u32[]{:S(2)}) copy-start(f32[128,128]{1,0:T(8,128)} %constant.60.clone.twist) | copy-start | bytes 196612
  3.6 16.0 %collective-permute-start.3 = (f32[2,4,128,128]{3,2,1,0:T(8,128)}, f32[2,4,128,128]{3,2,1,0:T(8,128)S(1)}, u32[]{:S(2)}, u32[]{:S(2)}) collective-permute-start(f32[2,4,128,128]{3,2,1,0:T(8,128)} %get-tuple-element.33), channel_id=1, source_target_pairs={{0,8},{8,0},{16,24},{24,16},{1,9},{9,1},{17,25},{25,17},{2,10},{10... | collective-permute-start | bytes 1572872 | tf_op jit(solution)/shard_map/ppermute | solution.py:589
  6.6 26.3 %collective-permute-start.4 = (f32[2,4,128,128]{3,2,1,0:T(8,128)}, f32[2,4,128,128]{3,2,1,0:T(8,128)S(1)}, u32[]{:S(2)}, u32[]{:S(2)}) collective-permute-start(f32[2,4,128,128]{3,2,1,0:T(8,128)} %get-tuple-element.34), channel_id=1, source_target_pairs={{0,16},{8,24},{16,0},{24,8},{1,17},{9,25},{17,1},{25,9},{2,18},{10... | collective-permute-start | bytes 1572872 | tf_op jit(solution)/shard_map/ppermute | solution.py:589
  8.1 24.8 %collective-permute-start.5 = (f32[2,4,128,128]{3,2,1,0:T(8,128)}, f32[2,4,128,128]{3,2,1,0:T(8,128)S(1)}, u32[]{:S(2)}, u32[]{:S(2)}) collective-permute-start(f32[2,4,128,128]{3,2,1,0:T(8,128)} %get-tuple-element.35), channel_id=1, source_target_pairs={{0,24},{8,16},{16,8},{24,0},{1,25},{9,17},{17,9},{25,1},{2,26},{10... | collective-permute-start | bytes 1572872 | tf_op jit(solution)/shard_map/ppermute | solution.py:589
  11.1 42.8 %copy-start.5 = (f32[2,4,128,128]{3,2,1,0:T(8,128)S(1)}, f32[2,4,128,128]{3,2,1,0:T(8,128)}, u32[]{:S(2)}) copy-start(f32[2,4,128,128]{3,2,1,0:T(8,128)} %get-tuple-element.28.refs_0_) | copy-start | bytes 1572868
  11.1 42.8 %copy-start.12 = (bf16[336,256]{1,0:T(8,128)(2,1)S(1)}, bf16[336,256]{1,0:T(8,128)(2,1)}, u32[]{:S(2)}) copy-start(bf16[336,256]{1,0:T(8,128)(2,1)} %constant.63.clone.matrix) | copy-start | bytes 516100
  11.1 42.8 %copy-start.14 = (f32[128,128]{1,0:T(8,128)S(1)}, f32[128,128]{1,0:T(8,128)}, u32[]{:S(2)}) copy-start(f32[128,128]{1,0:T(8,128)} %constant.62.clone.twist) | copy-start | bytes 196612
  11.1 31.0 %collective-permute-start = (f32[2,4,128,128]{3,2,1,0:T(8,128)}, f32[2,4,128,128]{3,2,1,0:T(8,128)S(1)}, u32[]{:S(2)}, u32[]{:S(2)}) collective-permute-start(f32[2,4,128,128]{3,2,1,0:T(8,128)} %get-tuple-element.29), channel_id=1, source_target_pairs={{0,8},{8,0},{16,24},{24,16},{1,9},{9,1},{17,25},{25,17},{2,10},{10... | collective-permute-start | bytes 1572872 | tf_op jit(solution)/shard_map/ppermute | solution.py:589
  13.1 40.8 %collective-permute-start.1 = (f32[2,4,128,128]{3,2,1,0:T(8,128)}, f32[2,4,128,128]{3,2,1,0:T(8,128)S(1)}, u32[]{:S(2)}, u32[]{:S(2)}) collective-permute-start(f32[2,4,128,128]{3,2,1,0:T(8,128)} %get-tuple-element.30), channel_id=1, source_target_pairs={{0,16},{8,24},{16,0},{24,8},{1,17},{9,25},{17,1},{25,9},{2,18},{10... | collective-permute-start | bytes 1572872 | tf_op jit(solution)/shard_map/ppermute | solution.py:589
  19.6 34.3 %collective-permute-start.2 = (f32[2,4,128,128]{3,2,1,0:T(8,128)}, f32[2,4,128,128]{3,2,1,0:T(8,128)S(1)}, u32[]{:S(2)}, u32[]{:S(2)}) collective-permute-start(f32[2,4,128,128]{3,2,1,0:T(8,128)} %get-tuple-element.31), channel_id=1, source_target_pairs={{0,24},{8,16},{16,8},{24,0},{1,25},{9,17},{17,9},{25,1},{2,26},{10... | collective-permute-start | bytes 1572872 | tf_op jit(solution)/shard_map/ppermute | solution.py:589
  60.8 69.2 %all-to-all-start = ((f32[32,168,128]{2,1,0:T(8,128)}), f32[32,168,128]{2,1,0:T(8,128)}, u32[]{:S(2)}, u32[]{:S(2)}) async-start(f32[32,168,128]{2,1,0:T(8,128)} %column_forward.3), calls=%async_computation | async-start | bytes 5505024 | tf_op jit(solution)/shard_map/all_to_all | solution.py:691
  65.8 64.2 %copy-start.7 = (f32[2,17,8,256]{3,2,1,0:T(8,128)S(1)}, f32[2,17,8,256]{3,2,1,0:T(8,128)}, u32[]{:S(2)}) copy-start(f32[2,17,8,256]{3,2,1,0:T(8,128)} %constant.64.clone.twist) | copy-start | bytes 835588
  65.9 64.2 %copy-start.8 = (bf16[256,512]{1,0:T(8,128)(2,1)S(1)}, bf16[256,512]{1,0:T(8,128)(2,1)}, u32[]{:S(2)}) copy-start(bf16[256,512]{1,0:T(8,128)(2,1)} %constant.68.clone.inv_low) | copy-start | bytes 786436
  65.9 64.2 %copy-start.9 = (bf16[256,512]{1,0:T(8,128)(2,1)S(1)}, bf16[256,512]{1,0:T(8,128)(2,1)}, u32[]{:S(2)}) copy-start(bf16[256,512]{1,0:T(8,128)(2,1)} %constant.67.clone.inv_high) | copy-start | bytes 786436
  65.9 64.2 %copy-start.10 = (bf16[512,256]{1,0:T(8,128)(2,1)S(1)}, bf16[512,256]{1,0:T(8,128)(2,1)}, u32[]{:S(2)}) copy-start(bf16[512,256]{1,0:T(8,128)(2,1)} %constant.66.clone.fwd_low) | copy-start | bytes 786436
  65.9 64.2 %copy-start.11 = (bf16[512,256]{1,0:T(8,128)(2,1)S(1)}, bf16[512,256]{1,0:T(8,128)(2,1)}, u32[]{:S(2)}) copy-start(bf16[512,256]{1,0:T(8,128)(2,1)} %constant.65.clone.fwd_high) | copy-start | bytes 786436
  220.7 22.5 %collective-permute-start.9 = (f32[1024,128]{1,0:T(8,128)}, f32[1024,128]{1,0:T(8,128)S(1)}, u32[]{:S(2)}, u32[]{:S(2)}) collective-permute-start(f32[1024,128]{1,0:T(8,128)} %get-tuple-element.43), channel_id=1, source_target_pairs={{0,8},{8,0},{16,24},{24,16},{1,9},{9,1},{17,25},{25,17},{2,10},{10... | collective-permute-start | bytes 1572872 | tf_op jit(solution)/shard_map/ppermute | solution.py:589
  220.8 37.1 %collective-permute-start.10 = (f32[1024,128]{1,0:T(8,128)}, f32[1024,128]{1,0:T(8,128)S(1)}, u32[]{:S(2)}, u32[]{:S(2)}) collective-permute-start(f32[1024,128]{1,0:T(8,128)} %get-tuple-element.44), channel_id=1, source_target_pairs={{0,16},{8,24},{16,0},{24,8},{1,17},{9,25},{17,1},{25,9},{2,18},{10... | collective-permute-start | bytes 1572872 | tf_op jit(solution)/shard_map/ppermute | solution.py:589
  221.9 36.0 %collective-permute-start.11 = (f32[1024,128]{1,0:T(8,128)}, f32[1024,128]{1,0:T(8,128)S(1)}, u32[]{:S(2)}, u32[]{:S(2)}) collective-permute-start(f32[1024,128]{1,0:T(8,128)} %get-tuple-element.45), channel_id=1, source_target_pairs={{0,24},{8,16},{16,8},{24,0},{1,25},{9,17},{17,9},{25,1},{2,26},{10... | collective-permute-start | bytes 1572872 | tf_op jit(solution)/shard_map/ppermute | solution.py:589
  224.2 1.3 collective-permute-start.6
  226.7 3.7 %collective-permute-start.7 = (f32[1]{0:T(128)}, f32[1]{0:T(128)}, u32[]{:S(2)}, u32[]{:S(2)}) collective-permute-start(f32[1]{0:T(128)} %max.6), channel_id=1, source_target_pairs={{0,2},{1,3},{2,0},{3,1},{4,6},{5,7},{6,4},{7,5},{8,10},{9,11},{10,... | collective-permute-start | bytes 20 | tf_op jit(solution)/shard_map/ppermute | solution.py:748
  231.0 4.6 %collective-permute-start.8 = (f32[1]{0:T(128)}, f32[1]{0:T(128)}, u32[]{:S(2)}, u32[]{:S(2)}) collective-permute-start(f32[1]{0:T(128)} %max.7.peak_one), channel_id=1, source_target_pairs={{0,4},{1,5},{2,6},{3,7},{4,0},{5,1},{6,2},{7,3},{8,12},{9,13},{10,... | collective-permute-start | bytes 20 | tf_op jit(solution)/shard_map/ppermute | solution.py:748
  235.6 1.0 copy-start
  236.7 1.0 copy-start.1
  237.7 1.0 copy-start.2
  238.7 1.0 copy-start.3
  239.8 1.0 copy-start.4
  241.5 27.7 %collective-permute-start.13 = (f32[1032,128]{1,0:T(8,128)S(1)}, f32[1032,128]{1,0:T(8,128)S(1)}, u32[]{:S(2)}, u32[]{:S(2)}) collective-permute-start(f32[1032,128]{1,0:T(8,128)S(1)} %get-tuple-element.52), channel_id=1, source_target_pairs={{0,16},{8,24},{16,0},{24,8},{1,17},{9,25},{17,1},{25,9},{2,18},{10... | collective-permute-start | bytes 1585160 | tf_op jit(solution)/shard_map/ppermute | solution.py:589
  242.2 27.1 %collective-permute-start.14 = (f32[1032,128]{1,0:T(8,128)S(1)}, f32[1032,128]{1,0:T(8,128)S(1)}, u32[]{:S(2)}, u32[]{:S(2)}) collective-permute-start(f32[1032,128]{1,0:T(8,128)S(1)} %get-tuple-element.53), channel_id=1, source_target_pairs={{0,24},{8,16},{16,8},{24,0},{1,25},{9,17},{17,9},{25,1},{2,26},{10... | collective-permute-start | bytes 1585160 | tf_op jit(solution)/shard_map/ppermute | solution.py:589
  257.9 11.4 %collective-permute-start.12 = (f32[1032,128]{1,0:T(8,128)S(1)}, f32[1032,128]{1,0:T(8,128)S(1)}, u32[]{:S(2)}, u32[]{:S(2)}) collective-permute-start(f32[1032,128]{1,0:T(8,128)S(1)} %get-tuple-element.51), channel_id=1, source_target_pairs={{0,8},{8,0},{16,24},{24,16},{1,9},{9,1},{17,25},{25,17},{2,10},{10... | collective-permute-start | bytes 1585160 | tf_op jit(solution)/shard_map/ppermute | solution.py:589

commit v16 on v15

--- a/solution.py
+++ b/solution.py
@@ -632,7 +632,7 @@
         in_specs=[whole(pltpu.SMEM)],
         out_specs=pl.BlockSpec((2, 1, RES * 8, 128), lambda g: (0, g, 0, 0)),
         out_shape=jax.ShapeDtypeStruct((2, own, RES * 8, 128), jnp.float32),
-        compiler_params=params(56),
+        compiler_params=params(50),
         name="gain",
     )(place)
 
@@ -666,6 +666,8 @@
         else:
             pieces = [packed[:, :, start : start + size, j] for j in range(row_total)]
         pieces = exchange(pieces, "row")
+        if chunk == 0:
+            pieces, gain = lax.optimization_barrier((pieces, gain))
         rows = slice(start, start + size)
         slab = pltpu.VMEM((RES // many, 2 * size, many * width), jnp.bfloat16)
         lines = [
@@ -707,7 +709,7 @@
         out_shape=jax.ShapeDtypeStruct((N // 128, own_rows, 128), jnp.float32),
         scratch_shapes=[pltpu.VMEM((2 * RES * 8, 2 * INNER), jnp.bfloat16)] * at_once
         + [pltpu.VMEM((RES * 8, 2 * INNER), jnp.float32)] * at_once,
-        compiler_params=params(48),
+        compiler_params=params(44),
         name="line",
     )(lines, gain, twist_line, line_fh, line_fl, line_ih, line_il)
 

time: 273 us -> 272 us (level)
  blocking collectives: 66.5 us -> 135 us
  waiting for transfers between devices: 119 us -> 56.3 us
  starting transfers between devices: 25.5 us -> 20.5 us
    all_to_all x1 -> x2, blocking collectives: 66.5 us -> 135 us  [body(): lax.all_to_all(lines, ('row', 'col'), split_axis=0, concat_axis=0, tiled=...]
    all_to_all x1 -> x0, waiting for transfers between devices: 56.8 us -> none  [body(): lax.all_to_all(lines, ('row', 'col'), split_axis=0, concat_axis=0, tiled=...]
    ppermute x12, waiting for transfers between devices: 55 us -> 49.8 us  [exchange(): lax.ppermute(pieces[j], axis, [(i, i ^ j) for i in range(total)])]
    all_to_all x1 -> x0, starting transfers between devices: 5.04 us -> none  [body(): lax.all_to_all(lines, ('row', 'col'), split_axis=0, concat_axis=0, tiled=...]
  transfers between devices with their start and end apart: 16 -> 15, of which waited for: 10 -> 9; matrix products, arithmetic and copies ran while one was open for 0% -> 0% of each run, Pallas kernels for 6% -> 5%
where the time goes in v16:
time: 272 us
  blocking collectives  135 us (50%)
  waiting for transfers between devices  56.3 us (21%)
  Pallas kernels  51.3 us (19%)
  starting transfers between devices  20.5 us (8%)
  local copies, waits for them, and re-layouts  5.28 us (2%)
  between operations  2.75 us (1%)
    all_to_all x2, blocking collectives, body(): lax.all_to_all(lines, ('row', 'col'), split_axis=0, concat_axis=0, tiled=...  135 us
    ppermute x12, waiting for transfers between devices, exchange(): lax.ppermute(pieces[j], axis, [(i, i ^ j) for i in range(total)])  49.8 us
    ppermute x12, starting transfers between devices, exchange(): lax.ppermute(pieces[j], axis, [(i, i ^ j) for i in range(total)])  17.8 us
    pallas_call x2, Pallas kernels, body(): pl.pallas_call(partial(column_forward_kernel, row_total), in_specs=[whole...  14 us
    pallas_call x1, Pallas kernels, body(): pl.pallas_call(partial(line_kernel, order, own, tail), grid=(-(-own // at...  12 us
    pallas_call x1, Pallas kernels, body(): pl.pallas_call(partial(column_inverse_kernel, row_total), in_specs=[whole...  11.4 us
    ppermute x3, waiting for transfers between devices, body(): peaks = [peak_sq, lax.ppermute(peak_sq, 'col', partner)]  6.43 us
    pallas_call x2, Pallas kernels, body(): pl.pallas_call(pack_kernel, grid=(1,), in_specs=[whole(pltpu.SMEM)] + [pl...  5.91 us
  transfers between devices with their start and end apart: 15, of which 9 were waited for; matrix products, arithmetic and copies ran while one was open for 0% of the time, Pallas kernels for 5%

profile of v16, /device:TPU:0, one launch (start us, length us, event | category | flops | bytes accessed | tf_op | source)
XLA Modules:
  0.0 271.6 jit_solution(1505161321191053197)
XLA Ops:
  0.6 2.9 %pack.3 = (f32[2,4,128,128]{3,2,1,0:T(8,128)}, f32[2,4,128,128]{3,2,1,0:T(8,128)}, f32[2,4,128,128]{3,2,1,0:T(8,128)}, f32[2,4,128,128]{3,2,1,0:T(8,128)}) custom-call(s32[1]{0:T(128)} %bitcast.place, f32[4,256,512]{2,1,0:T(8,128)} %bitcast.4, f32[4,256,512]{2,1,0:T(8,128)} %bitcast.6), custom_call_target="tpu_custom_call" | custom-call | bytes 4194304 | tf_op jit(solution)/shard_map/pack/pallas_call | solution.py:650
  3.6 3.0 %collective-permute-start.3 = (f32[2,4,128,128]{3,2,1,0:T(8,128)}, f32[2,4,128,128]{3,2,1,0:T(8,128)S(1)}, u32[]{:S(2)}, u32[]{:S(2)}) collective-permute-start(f32[2,4,128,128]{3,2,1,0:T(8,128)} %get-tuple-element.38), channel_id=1, source_target_pairs={{0,8},{8,0},{16,24},{24,16},{1,9},{9,1},{17,25},{25,17},{2,10},{10... | collective-permute-start | bytes 1572872 | tf_op jit(solution)/shard_map/ppermute | solution.py:589
  6.6 1.5 collective-permute-start.4
  8.1 0.1 collective-permute-start.5
  8.2 3.0 %pack.2 = (f32[2,4,128,128]{3,2,1,0:T(8,128)}, f32[2,4,128,128]{3,2,1,0:T(8,128)}, f32[2,4,128,128]{3,2,1,0:T(8,128)}, f32[2,4,128,128]{3,2,1,0:T(8,128)}) custom-call(s32[1]{0:T(128)} %bitcast.place, f32[4,256,512]{2,1,0:T(8,128)} %bitcast.5, f32[4,256,512]{2,1,0:T(8,128)} %bitcast.7), custom_call_target="tpu_custom_call" | custom-call | bytes 4194304 | tf_op jit(solution)/shard_map/pack/pallas_call | solution.py:650
  11.1 1.9 collective-permute-start
  13.1 1.5 collective-permute-start.1
  14.6 5.0 %collective-permute-done.3.refs_1_ = f32[2,4,128,128]{3,2,1,0:T(8,128)S(1)} collective-permute-done((f32[2,4,128,128]{3,2,1,0:T(8,128)}, f32[2,4,128,128]{3,2,1,0:T(8,128)S(1)}, u32[]{:S(2)}, u32[]{:S(2)}) %collective-permute-start.3) | collective-permute-done | bytes 524320 | tf_op jit(solution)/shard_map/ppermute | solution.py:589
  19.5 3.0 %collective-permute-start.2 = (f32[2,4,128,128]{3,2,1,0:T(8,128)}, f32[2,4,128,128]{3,2,1,0:T(8,128)S(1)}, u32[]{:S(2)}, u32[]{:S(2)}) collective-permute-start(f32[2,4,128,128]{3,2,1,0:T(8,128)} %get-tuple-element.36), channel_id=1, source_target_pairs={{0,24},{8,16},{16,8},{24,0},{1,25},{9,17},{17,9},{25,1},{2,26},{10... | collective-permute-start | bytes 1572872 | tf_op jit(solution)/shard_map/ppermute | solution.py:589
  22.6 0.1 pad_add_fusion.place
  22.6 4.1 %gain.1 = f32[2,11,256,128]{3,2,1,0:T(8,128)S(1)} custom-call(s32[2]{0:T(128)S(1)} %pad_add_fusion.place), custom_call_target="tpu_custom_call" | custom-call | tf_op jit(solution)/shard_map/gain/pallas_call | solution.py:629
  26.7 0.0 copy-start.4
  26.7 0.0 copy-start.12
  26.8 0.0 copy-start.14
  26.8 6.1 %collective-permute-done.4.refs_2_ = f32[2,4,128,128]{3,2,1,0:T(8,128)S(1)} collective-permute-done((f32[2,4,128,128]{3,2,1,0:T(8,128)}, f32[2,4,128,128]{3,2,1,0:T(8,128)S(1)}, u32[]{:S(2)}, u32[]{:S(2)}) %collective-permute-start.4) | collective-permute-done | bytes 524320 | tf_op jit(solution)/shard_map/ppermute | solution.py:589
  32.9 0.0 collective-permute-done.5.refs_3_
  32.9 0.0 copy-done.6
  32.9 0.0 copy-done.13
  32.9 0.0 copy-done.15
  32.9 6.9 %column_forward.2.refs_4_ = f32[32,168,128]{2,1,0:T(8,128)S(1)} custom-call(s32[1]{0:T(128)} %bitcast.place, f32[128,128]{1,0:T(8,128)S(1)} %copy-done.15, bf16[336,256]{1,0:T(8,128)(2,1)S(1)} %copy-done.13, f32[2,4,128,128]{3,2,1,0:T(8,128)S(1)} %copy-done.6, f32[2,4,128,128]{3,2,1,0:T(8,128)S(1)} %collective-permute-done.3.refs_1_, ...), custom_call_target="tpu_custom_call" | custom-call | bytes 20971520 | tf_op jit(solution)/shard_map/column_forward/pallas_call | solution.py:674
  39.8 2.2 collective-permute-done.refs_1_
  42.1 11.8 %collective-permute-done.1.refs_2_ = f32[2,4,128,128]{3,2,1,0:T(8,128)S(1)} collective-permute-done((f32[2,4,128,128]{3,2,1,0:T(8,128)}, f32[2,4,128,128]{3,2,1,0:T(8,128)S(1)}, u32[]{:S(2)}, u32[]{:S(2)}) %collective-permute-start.1) | collective-permute-done | bytes 524320 | tf_op jit(solution)/shard_map/ppermute | solution.py:589
  53.9 0.0 collective-permute-done.2.refs_3_
  53.9 0.0 copy-done.4
  53.9 0.0 copy-done.12
  53.9 0.0 copy-done.14
  53.9 7.1 %column_forward.3 = f32[32,168,128]{2,1,0:T(8,128)S(1)} custom-call(s32[1]{0:T(128)} %bitcast.place, f32[128,128]{1,0:T(8,128)S(1)} %copy-done.14, bf16[336,256]{1,0:T(8,128)(2,1)S(1)} %copy-done.12, f32[2,4,128,128]{3,2,1,0:T(8,128)S(1)} %copy-done.4, f32[2,4,128,128]{3,2,1,0:T(8,128)S(1)} %collective-permute-done.refs_1_, ...), custom_call_target="tpu_custom_call" | custom-call | bytes 20971520 | tf_op jit(solution)/shard_map/column_forward/pallas_call | solution.py:674
  61.0 0.0 copy-start.7
  61.1 0.0 copy-start.8
  61.1 0.0 copy-start.9
  61.1 0.0 copy-start.10
  61.1 0.0 copy-start.11
  61.1 68.8 %all_to_all.10.lines = f32[32,168,128]{2,1,0:T(8,128)S(1)} all-to-all(f32[32,168,128]{2,1,0:T(8,128)S(1)} %column_forward.3), channel_id=1, replica_groups=mesh['row'=4,'col'=8] {'row','col'}, dimensions={0} | all-to-all | bytes 5505024 | tf_op jit(solution)/shard_map/all_to_all | solution.py:693
  129.9 0.0 copy-done.9
  129.9 0.0 copy-done.10
  130.0 0.0 copy-done.11
  130.0 12.0 %line.1 = f32[32,168,128]{2,1,0:T(8,128)S(1)} custom-call(f32[32,168,128]{2,1,0:T(8,128)S(1)} %all_to_all.10.lines, f32[2,11,256,128]{3,2,1,0:T(8,128)S(1)} %gain.1, f32[2,17,8,256]{3,2,1,0:T(8,128)S(1)} %copy-done.7, bf16[512,256]{1,0:T(8,128)(2,1)S(1)} %copy-done.11, bf16[512,256]{1,0:T(8,128)(2,1)S(1)} %copy-done.10, bf16[256,512]{1,0:T(8,128)(2,1)S(1)} %copy-done.9, ...), custom_call_target="tpu_custom_call" | custom-call | tf_op jit(solution)/shard_map/line/pallas_call | solution.py:704
  141.9 66.5 %all_to_all.11.source = f32[32,168,128]{2,1,0:T(8,128)} all-to-all(f32[32,168,128]{2,1,0:T(8,128)S(1)} %line.1), channel_id=1, replica_groups=mesh['row'=4,'col'=8] {'row','col'}, dimensions={0} | all-to-all | bytes 5505024 | tf_op jit(solution)/shard_map/all_to_all | solution.py:719
  208.5 11.4 %column_inverse.1 = (f32[1024,128]{1,0:T(8,128)}, f32[1024,128]{1,0:T(8,128)}, f32[1024,128]{1,0:T(8,128)}, f32[1024,128]{1,0:T(8,128)}, f32[1032,128]{1,0:T(8,1...) custom-call(s32[1]{0:T(128)} %bitcast.place, ...), custom_call_target="tpu_custom_call" | custom-call | tf_op jit(solution)/shard_map/column_inverse/pallas_call | solution.py:726
  219.8 0.1 collective-permute-start.9
  219.9 1.1 collective-permute-start.10
  221.0 2.4 collective-permute-start.11
  223.4 0.0 collective-permute-start.6
  223.4 1.2 collective-permute-done.6
  225.9 1.4 collective-permute-start.7
  227.2 2.2 collective-permute-done.7
  230.0 1.4 collective-permute-start.8
  231.4 3.1 %collective-permute-done.8.peak_two = f32[1]{0:T(128)} collective-permute-done((f32[1]{0:T(128)}, f32[1]{0:T(128)}, u32[]{:S(2)}, u32[]{:S(2)}) %collective-permute-start.8) | collective-permute-done | bytes 36 | tf_op jit(solution)/shard_map/ppermute | solution.py:750
  234.5 1.0 copy-done
  235.5 1.0 copy-done.1
  236.6 1.0 copy-done.2
  237.6 1.0 copy-done.3
  238.7 1.0 copy-done.5
  239.7 0.8 stamp.1
  240.5 0.6 collective-permute-start.13
  241.0 1.1 collective-permute-start.14
  242.1 0.0 collective-permute-done.9.refs_1_
  242.1 14.8 %collective-permute-done.10.refs_2_ = f32[1024,128]{1,0:T(8,128)S(1)} collective-permute-done((f32[1024,128]{1,0:T(8,128)}, f32[1024,128]{1,0:T(8,128)S(1)}, u32[]{:S(2)}, u32[]{:S(2)}) %collective-permute-start.10) | collective-permute-done | bytes 524320 | tf_op jit(solution)/shard_map/ppermute | solution.py:589
  256.9 0.0 collective-permute-done.11.refs_3_
  256.9 1.6 collective-permute-start.12
  258.5 9.9 %collective-permute-done.13.refs_6_ = f32[1032,128]{1,0:T(8,128)S(1)} collective-permute-done((f32[1032,128]{1,0:T(8,128)S(1)}, f32[1032,128]{1,0:T(8,128)S(1)}, u32[]{:S(2)}, u32[]{:S(2)}) %collective-permute-start.13) | collective-permute-done | bytes 528416 | tf_op jit(solution)/shard_map/ppermute | solution.py:589
  268.4 0.0 collective-permute-done.14.refs_7_
  268.4 0.0 collective-permute-done.12.refs_5_
  268.4 3.2 %encode.1 = (f32[1024,512]{1,0:T(8,128)}, f32[1024,512]{1,0:T(8,128)}) custom-call(s32[1]{0:T(128)} %bitcast.place, f32[1]{0:T(128)} %max.7.peak_one, f32[1]{0:T(128)} %collective-permute-done.8.peak_two, f32[1024,128]{1,0:T(8,128)S(1)} %get-tuple-element.52.refs_0_, f32[1024,128]{1,0:T(8,128)S(1)} %collective-permute-done.9.refs_1_, ...), custom_call_target="tpu_custom_call" | custom-call | tf_op jit(solution)/shard_map/encode/pallas_call | solution.py:785
  (10 shorter events, 0.0 us)
Async XLA Ops:
  3.6 16.0 %collective-permute-start.3 = (f32[2,4,128,128]{3,2,1,0:T(8,128)}, f32[2,4,128,128]{3,2,1,0:T(8,128)S(1)}, u32[]{:S(2)}, u32[]{:S(2)}) collective-permute-start(f32[2,4,128,128]{3,2,1,0:T(8,128)} %get-tuple-element.38), channel_id=1, source_target_pairs={{0,8},{8,0},{16,24},{24,16},{1,9},{9,1},{17,25},{25,17},{2,10},{10... | collective-permute-start | bytes 1572872 | tf_op jit(solution)/shard_map/ppermute | solution.py:589
  6.6 26.3 %collective-permute-start.4 = (f32[2,4,128,128]{3,2,1,0:T(8,128)}, f32[2,4,128,128]{3,2,1,0:T(8,128)S(1)}, u32[]{:S(2)}, u32[]{:S(2)}) collective-permute-start(f32[2,4,128,128]{3,2,1,0:T(8,128)} %get-tuple-element.39), channel_id=1, source_target_pairs={{0,16},{8,24},{16,0},{24,8},{1,17},{9,25},{17,1},{25,9},{2,18},{10... | collective-permute-start | bytes 1572872 | tf_op jit(solution)/shard_map/ppermute | solution.py:589
  8.1 24.8 %copy-start.6 = (f32[2,4,128,128]{3,2,1,0:T(8,128)S(1)}, f32[2,4,128,128]{3,2,1,0:T(8,128)}, u32[]{:S(2)}) copy-start(f32[2,4,128,128]{3,2,1,0:T(8,128)} %get-tuple-element.41.refs_0_) | copy-start | bytes 1572868
  8.1 24.8 %copy-start.13 = (bf16[336,256]{1,0:T(8,128)(2,1)S(1)}, bf16[336,256]{1,0:T(8,128)(2,1)}, u32[]{:S(2)}) copy-start(bf16[336,256]{1,0:T(8,128)(2,1)} %constant.61.clone.matrix) | copy-start | bytes 516100
  8.1 24.8 %copy-start.15 = (f32[128,128]{1,0:T(8,128)S(1)}, f32[128,128]{1,0:T(8,128)}, u32[]{:S(2)}) copy-start(f32[128,128]{1,0:T(8,128)} %constant.60.clone.twist) | copy-start | bytes 196612
  8.1 24.8 %collective-permute-start.5 = (f32[2,4,128,128]{3,2,1,0:T(8,128)}, f32[2,4,128,128]{3,2,1,0:T(8,128)}, u32[]{:S(2)}, u32[]{:S(2)}) collective-permute-start(f32[2,4,128,128]{3,2,1,0:T(8,128)} %get-tuple-element.40), channel_id=1, source_target_pairs={{0,24},{8,16},{16,8},{24,0},{1,25},{9,17},{17,9},{25,1},{2,26},{10... | collective-permute-start | bytes 1572872 | tf_op jit(solution)/shard_map/ppermute | solution.py:589
  11.1 30.9 %collective-permute-start = (f32[2,4,128,128]{3,2,1,0:T(8,128)}, f32[2,4,128,128]{3,2,1,0:T(8,128)S(1)}, u32[]{:S(2)}, u32[]{:S(2)}) collective-permute-start(f32[2,4,128,128]{3,2,1,0:T(8,128)} %get-tuple-element.34), channel_id=1, source_target_pairs={{0,8},{8,0},{16,24},{24,16},{1,9},{9,1},{17,25},{25,17},{2,10},{10... | collective-permute-start | bytes 1572872 | tf_op jit(solution)/shard_map/ppermute | solution.py:589
  13.1 40.8 %collective-permute-start.1 = (f32[2,4,128,128]{3,2,1,0:T(8,128)}, f32[2,4,128,128]{3,2,1,0:T(8,128)S(1)}, u32[]{:S(2)}, u32[]{:S(2)}) collective-permute-start(f32[2,4,128,128]{3,2,1,0:T(8,128)} %get-tuple-element.35), channel_id=1, source_target_pairs={{0,16},{8,24},{16,0},{24,8},{1,17},{9,25},{17,1},{25,9},{2,18},{10... | collective-permute-start | bytes 1572872 | tf_op jit(solution)/shard_map/ppermute | solution.py:589
  19.5 34.3 %collective-permute-start.2 = (f32[2,4,128,128]{3,2,1,0:T(8,128)}, f32[2,4,128,128]{3,2,1,0:T(8,128)S(1)}, u32[]{:S(2)}, u32[]{:S(2)}) collective-permute-start(f32[2,4,128,128]{3,2,1,0:T(8,128)} %get-tuple-element.36), channel_id=1, source_target_pairs={{0,24},{8,16},{16,8},{24,0},{1,25},{9,17},{17,9},{25,1},{2,26},{10... | collective-permute-start | bytes 1572872 | tf_op jit(solution)/shard_map/ppermute | solution.py:589
  26.7 27.2 %copy-start.4 = (f32[2,4,128,128]{3,2,1,0:T(8,128)S(1)}, f32[2,4,128,128]{3,2,1,0:T(8,128)}, u32[]{:S(2)}) copy-start(f32[2,4,128,128]{3,2,1,0:T(8,128)} %get-tuple-element.33.refs_0_) | copy-start | bytes 1572868
  26.7 27.1 %copy-start.12 = (bf16[336,256]{1,0:T(8,128)(2,1)S(1)}, bf16[336,256]{1,0:T(8,128)(2,1)}, u32[]{:S(2)}) copy-start(bf16[336,256]{1,0:T(8,128)(2,1)} %constant.63.clone.matrix) | copy-start | bytes 516100
  26.8 27.1 %copy-start.14 = (f32[128,128]{1,0:T(8,128)S(1)}, f32[128,128]{1,0:T(8,128)}, u32[]{:S(2)}) copy-start(f32[128,128]{1,0:T(8,128)} %constant.62.clone.twist) | copy-start | bytes 196612
  61.0 68.9 %copy-start.7 = (f32[2,17,8,256]{3,2,1,0:T(8,128)S(1)}, f32[2,17,8,256]{3,2,1,0:T(8,128)}, u32[]{:S(2)}) copy-start(f32[2,17,8,256]{3,2,1,0:T(8,128)} %constant.64.clone.twist) | copy-start | bytes 835588
  61.1 68.9 %copy-start.8 = (bf16[256,512]{1,0:T(8,128)(2,1)S(1)}, bf16[256,512]{1,0:T(8,128)(2,1)}, u32[]{:S(2)}) copy-start(bf16[256,512]{1,0:T(8,128)(2,1)} %constant.68.clone.inv_low) | copy-start | bytes 786436
  61.1 68.9 %copy-start.9 = (bf16[256,512]{1,0:T(8,128)(2,1)S(1)}, bf16[256,512]{1,0:T(8,128)(2,1)}, u32[]{:S(2)}) copy-start(bf16[256,512]{1,0:T(8,128)(2,1)} %constant.67.clone.inv_high) | copy-start | bytes 786436
  61.1 68.9 %copy-start.10 = (bf16[512,256]{1,0:T(8,128)(2,1)S(1)}, bf16[512,256]{1,0:T(8,128)(2,1)}, u32[]{:S(2)}) copy-start(bf16[512,256]{1,0:T(8,128)(2,1)} %constant.66.clone.fwd_low) | copy-start | bytes 786436
  61.1 68.9 %copy-start.11 = (bf16[512,256]{1,0:T(8,128)(2,1)S(1)}, bf16[512,256]{1,0:T(8,128)(2,1)}, u32[]{:S(2)}) copy-start(bf16[512,256]{1,0:T(8,128)(2,1)} %constant.65.clone.fwd_high) | copy-start | bytes 786436
  219.8 22.2 %collective-permute-start.9 = (f32[1024,128]{1,0:T(8,128)}, f32[1024,128]{1,0:T(8,128)S(1)}, u32[]{:S(2)}, u32[]{:S(2)}) collective-permute-start(f32[1024,128]{1,0:T(8,128)} %get-tuple-element.53), channel_id=1, source_target_pairs={{0,8},{8,0},{16,24},{24,16},{1,9},{9,1},{17,25},{25,17},{2,10},{10... | collective-permute-start | bytes 1572872 | tf_op jit(solution)/shard_map/ppermute | solution.py:589
  219.9 37.0 %collective-permute-start.10 = (f32[1024,128]{1,0:T(8,128)}, f32[1024,128]{1,0:T(8,128)S(1)}, u32[]{:S(2)}, u32[]{:S(2)}) collective-permute-start(f32[1024,128]{1,0:T(8,128)} %get-tuple-element.54), channel_id=1, source_target_pairs={{0,16},{8,24},{16,0},{24,8},{1,17},{9,25},{17,1},{25,9},{2,18},{10... | collective-permute-start | bytes 1572872 | tf_op jit(solution)/shard_map/ppermute | solution.py:589
  221.0 35.9 %collective-permute-start.11 = (f32[1024,128]{1,0:T(8,128)}, f32[1024,128]{1,0:T(8,128)S(1)}, u32[]{:S(2)}, u32[]{:S(2)}) collective-permute-start(f32[1024,128]{1,0:T(8,128)} %get-tuple-element.55), channel_id=1, source_target_pairs={{0,24},{8,16},{16,8},{24,0},{1,25},{9,17},{17,9},{25,1},{2,26},{10... | collective-permute-start | bytes 1572872 | tf_op jit(solution)/shard_map/ppermute | solution.py:589
  223.4 1.2 collective-permute-start.6
  225.9 3.6 %collective-permute-start.7 = (f32[1]{0:T(128)}, f32[1]{0:T(128)}, u32[]{:S(2)}, u32[]{:S(2)}) collective-permute-start(f32[1]{0:T(128)} %max.6), channel_id=1, source_target_pairs={{0,2},{1,3},{2,0},{3,1},{4,6},{5,7},{6,4},{7,5},{8,10},{9,11},{10,... | collective-permute-start | bytes 20 | tf_op jit(solution)/shard_map/ppermute | solution.py:750
  230.0 4.5 %collective-permute-start.8 = (f32[1]{0:T(128)}, f32[1]{0:T(128)}, u32[]{:S(2)}, u32[]{:S(2)}) collective-permute-start(f32[1]{0:T(128)} %max.7.peak_one), channel_id=1, source_target_pairs={{0,4},{1,5},{2,6},{3,7},{4,0},{5,1},{6,2},{7,3},{8,12},{9,13},{10,... | collective-permute-start | bytes 20 | tf_op jit(solution)/shard_map/ppermute | solution.py:750
  234.5 1.0 copy-start
  235.5 1.0 copy-start.1
  236.6 1.0 copy-start.2
  237.6 1.0 copy-start.3
  238.7 1.0 copy-start.5
  240.5 27.9 %collective-permute-start.13 = (f32[1032,128]{1,0:T(8,128)S(1)}, f32[1032,128]{1,0:T(8,128)S(1)}, u32[]{:S(2)}, u32[]{:S(2)}) collective-permute-start(f32[1032,128]{1,0:T(8,128)S(1)} %get-tuple-element.62), channel_id=1, source_target_pairs={{0,16},{8,24},{16,0},{24,8},{1,17},{9,25},{17,1},{25,9},{2,18},{10... | collective-permute-start | bytes 1585160 | tf_op jit(solution)/shard_map/ppermute | solution.py:589
  241.0 27.4 %collective-permute-start.14 = (f32[1032,128]{1,0:T(8,128)S(1)}, f32[1032,128]{1,0:T(8,128)S(1)}, u32[]{:S(2)}, u32[]{:S(2)}) collective-permute-start(f32[1032,128]{1,0:T(8,128)S(1)} %get-tuple-element.63), channel_id=1, source_target_pairs={{0,24},{8,16},{16,8},{24,0},{1,25},{9,17},{17,9},{25,1},{2,26},{10... | collective-permute-start | bytes 1585160 | tf_op jit(solution)/shard_map/ppermute | solution.py:589
  256.9 11.5 %collective-permute-start.12 = (f32[1032,128]{1,0:T(8,128)S(1)}, f32[1032,128]{1,0:T(8,128)S(1)}, u32[]{:S(2)}, u32[]{:S(2)}) collective-permute-start(f32[1032,128]{1,0:T(8,128)S(1)} %get-tuple-element.61), channel_id=1, source_target_pairs={{0,8},{8,0},{16,24},{24,16},{1,9},{9,1},{17,25},{25,17},{2,10},{10... | collective-permute-start | bytes 1585160 | tf_op jit(solution)/shard_map/ppermute | solution.py:589

commit v17 on v16

--- a/solution.py
+++ b/solution.py
@@ -206,24 +206,12 @@
 
 def column_forward_kernel(count, place, twist, matrix, *refs):
     pieces, refs = refs[:count], refs[count:]
-    before, (out, total, high, low, sems) = refs[:-5], refs[-5:]
+    before, (out, high, low) = refs[:-3], refs[-3:]
     width = pieces[0].shape[-1]
     per_source, size = pieces[0].shape[1:3]
     many = high.shape[-1] // width
     products = RES // many
     rows_out = out.shape[1]
-
-    def copy_in(p):
-        part = pl.ds(p * many, many)
-        return pltpu.make_async_copy(before[0].at[part], total.at[part], sems.at[p])
-
-    def copy_out(p):
-        part = pl.ds(p * many, many)
-        return pltpu.make_async_copy(total.at[part], out.at[part], sems.at[products + p])
-
-    if before:
-        for p in range(products):
-            copy_in(p).start()
 
     for here in range(count):
 
@@ -251,16 +239,10 @@
     @pl.loop(0, products)
     def _(p):
         done = three_left(matrix, rows_out, high[p], low[p])
-        if before:
-            copy_in(p).wait()
         for part in range(many):
             item = done[:, part * width : (part + 1) * width]
             at = p * many + part
-            total[at] = total[at] + item if before else item
-        copy_out(p).start()
-
-    for p in range(products):
-        copy_out(p).wait()
+            out[at] = before[0][at] + item if before else item
 
 
 def column_inverse_kernel(count, place, source, twist, matrix, *refs):
@@ -673,15 +655,10 @@
         lines = [
             pl.pallas_call(
                 partial(column_forward_kernel, row_total),
-                in_specs=[whole(pltpu.SMEM)] + [whole()] * (2 + row_total) + [anywhere] * len(lines),
-                out_specs=anywhere,
+                in_specs=[whole(pltpu.SMEM)] + [whole()] * (2 + row_total + len(lines)),
+                out_specs=whole(),
                 out_shape=jax.ShapeDtypeStruct((RES, total_rows, width), jnp.float32),
-                scratch_shapes=[
-                    pltpu.VMEM((RES, total_rows, width), jnp.float32),
-                    slab,
-                    slab,
-                    pltpu.SemaphoreType.DMA((2 * RES // many,)),
-                ],
+                scratch_shapes=[slab, slab],
                 compiler_params=params(20),
                 cost_estimate=cost(20),
                 name="column_forward",
@@ -738,7 +715,7 @@
             pltpu.SemaphoreType.DMA((RES // many,)),
             pltpu.SemaphoreType.DMA((2 * CHUNKS * row_total,)),
         ],
-        compiler_params=params(56),
+        compiler_params=params(36),
         name="column_inverse",
     )(place_row, lines, twist_col, inv_col)
     near = [near[:row_total], near[row_total:]]

time: 272 us -> 267 us (0.982)
  waiting for transfers between devices: 56.3 us -> 62.6 us
  local copies, waits for them, and re-layouts: 5.28 us -> 0.08 us
  Pallas kernels: 51.3 us -> 46.2 us
    ppermute x12, waiting for transfers between devices: 49.8 us -> 55.8 us  [exchange(): lax.ppermute(pieces[j], axis, [(i, i ^ j) for i in range(total)])]
    unnamed x32 -> x26, local copies, waits for them, and re-layouts: 5.28 us -> 0.08 us
    pallas_call x2, Pallas kernels: 14 us -> 10.5 us  [body(): pl.pallas_call(partial(column_forward_kernel, row_total), in_specs=[whole...]
where the time goes in v17:
time: 267 us
  blocking collectives  135 us (51%)
  waiting for transfers between devices  62.6 us (23%)
  Pallas kernels  46.2 us (17%)
  starting transfers between devices  20.4 us (8%)
  between operations  2.76 us (1%)
    all_to_all x2, blocking collectives, body(): lax.all_to_all(lines, ('row', 'col'), split_axis=0, concat_axis=0, tiled=...  135 us
    ppermute x12, waiting for transfers between devices, exchange(): lax.ppermute(pieces[j], axis, [(i, i ^ j) for i in range(total)])  55.8 us
    ppermute x12, starting transfers between devices, exchange(): lax.ppermute(pieces[j], axis, [(i, i ^ j) for i in range(total)])  17.7 us
    pallas_call x1, Pallas kernels, body(): pl.pallas_call(partial(line_kernel, order, own, tail), grid=(-(-own // at...  12 us
    pallas_call x2, Pallas kernels, body(): pl.pallas_call(partial(column_forward_kernel, row_total), in_specs=[whole...  10.5 us
    pallas_call x1, Pallas kernels, body(): pl.pallas_call(partial(column_inverse_kernel, row_total), in_specs=[whole...  9.78 us
    ppermute x3, waiting for transfers between devices, body(): peaks = [peak_sq, lax.ppermute(peak_sq, 'col', partner)]  6.81 us
    pallas_call x2, Pallas kernels, body(): pl.pallas_call(pack_kernel, grid=(1,), in_specs=[whole(pltpu.SMEM)] + [pl...  5.94 us
  transfers between devices with their start and end apart: 15, of which 9 were waited for; matrix products, arithmetic and copies ran while one was open for 0% of the time, Pallas kernels for 5%

profile of v17, /device:TPU:0, one launch (start us, length us, event | category | flops | bytes accessed | tf_op | source)
XLA Modules:
  0.0 267.1 jit_solution(3332994133947596570)
XLA Ops:
  0.6 3.0 %pack.3 = (f32[2,4,128,128]{3,2,1,0:T(8,128)}, f32[2,4,128,128]{3,2,1,0:T(8,128)}, f32[2,4,128,128]{3,2,1,0:T(8,128)}, f32[2,4,128,128]{3,2,1,0:T(8,128)}) custom-call(s32[1]{0:T(128)} %bitcast.place, f32[4,256,512]{2,1,0:T(8,128)} %bitcast.4, f32[4,256,512]{2,1,0:T(8,128)} %bitcast.6), custom_call_target="tpu_custom_call" | custom-call | bytes 4194304 | tf_op jit(solution)/shard_map/pack/pallas_call | solution.py:632
  3.6 3.0 %collective-permute-start.3 = (f32[2,4,128,128]{3,2,1,0:T(8,128)}, f32[2,4,128,128]{3,2,1,0:T(8,128)S(1)}, u32[]{:S(2)}, u32[]{:S(2)}) collective-permute-start(f32[2,4,128,128]{3,2,1,0:T(8,128)} %get-tuple-element.38), channel_id=1, source_target_pairs={{0,8},{8,0},{16,24},{24,16},{1,9},{9,1},{17,25},{25,17},{2,10},{10... | collective-permute-start | bytes 1572872 | tf_op jit(solution)/shard_map/ppermute | solution.py:571
  6.6 1.5 collective-permute-start.4
  8.1 0.1 collective-permute-start.5
  8.2 3.0 %pack.2 = (f32[2,4,128,128]{3,2,1,0:T(8,128)}, f32[2,4,128,128]{3,2,1,0:T(8,128)}, f32[2,4,128,128]{3,2,1,0:T(8,128)}, f32[2,4,128,128]{3,2,1,0:T(8,128)}) custom-call(s32[1]{0:T(128)} %bitcast.place, f32[4,256,512]{2,1,0:T(8,128)} %bitcast.5, f32[4,256,512]{2,1,0:T(8,128)} %bitcast.7), custom_call_target="tpu_custom_call" | custom-call | bytes 4194304 | tf_op jit(solution)/shard_map/pack/pallas_call | solution.py:632
  11.2 1.9 collective-permute-start
  13.1 1.5 collective-permute-start.1
  14.6 5.0 %collective-permute-done.3.refs_1_ = f32[2,4,128,128]{3,2,1,0:T(8,128)S(1)} collective-permute-done((f32[2,4,128,128]{3,2,1,0:T(8,128)}, f32[2,4,128,128]{3,2,1,0:T(8,128)S(1)}, u32[]{:S(2)}, u32[]{:S(2)}) %collective-permute-start.3) | collective-permute-done | bytes 524320 | tf_op jit(solution)/shard_map/ppermute | solution.py:571
  19.6 3.0 %collective-permute-start.2 = (f32[2,4,128,128]{3,2,1,0:T(8,128)}, f32[2,4,128,128]{3,2,1,0:T(8,128)S(1)}, u32[]{:S(2)}, u32[]{:S(2)}) collective-permute-start(f32[2,4,128,128]{3,2,1,0:T(8,128)} %get-tuple-element.36), channel_id=1, source_target_pairs={{0,24},{8,16},{16,8},{24,0},{1,25},{9,17},{17,9},{25,1},{2,26},{10... | collective-permute-start | bytes 1572872 | tf_op jit(solution)/shard_map/ppermute | solution.py:571
  22.6 0.1 pad_add_fusion.place
  22.7 4.1 %gain.1 = f32[2,11,256,128]{3,2,1,0:T(8,128)S(1)} custom-call(s32[2]{0:T(128)S(1)} %pad_add_fusion.place), custom_call_target="tpu_custom_call" | custom-call | tf_op jit(solution)/shard_map/gain/pallas_call | solution.py:611
  26.8 0.0 copy-start
  26.8 0.0 copy-start.8
  26.8 0.0 copy-start.11
  26.8 6.1 %collective-permute-done.4.refs_2_ = f32[2,4,128,128]{3,2,1,0:T(8,128)S(1)} collective-permute-done((f32[2,4,128,128]{3,2,1,0:T(8,128)}, f32[2,4,128,128]{3,2,1,0:T(8,128)S(1)}, u32[]{:S(2)}, u32[]{:S(2)}) %collective-permute-start.4) | collective-permute-done | bytes 524320 | tf_op jit(solution)/shard_map/ppermute | solution.py:571
  32.9 0.0 collective-permute-done.5.refs_3_
  32.9 0.0 copy-done.2
  32.9 0.0 copy-done.9
  32.9 0.0 copy-done.12
  32.9 5.8 %column_forward.2.refs_4_ = f32[32,168,128]{2,1,0:T(8,128)S(1)} custom-call(s32[1]{0:T(128)} %bitcast.place, f32[128,128]{1,0:T(8,128)S(1)} %copy-done.12, bf16[336,256]{1,0:T(8,128)(2,1)S(1)} %copy-done.9, f32[2,4,128,128]{3,2,1,0:T(8,128)S(1)} %copy-done.2, f32[2,4,128,128]{3,2,1,0:T(8,128)S(1)} %collective-permute-done.3.refs_1_, ...), custom_call_target="tpu_custom_call" | custom-call | bytes 20971520 | tf_op jit(solution)/shard_map/column_forward/pallas_call | solution.py:656
  38.7 3.4 %collective-permute-done.refs_1_ = f32[2,4,128,128]{3,2,1,0:T(8,128)S(1)} collective-permute-done((f32[2,4,128,128]{3,2,1,0:T(8,128)}, f32[2,4,128,128]{3,2,1,0:T(8,128)S(1)}, u32[]{:S(2)}, u32[]{:S(2)}) %collective-permute-start) | collective-permute-done | bytes 524320 | tf_op jit(solution)/shard_map/ppermute | solution.py:571
  42.1 11.8 %collective-permute-done.1.refs_2_ = f32[2,4,128,128]{3,2,1,0:T(8,128)S(1)} collective-permute-done((f32[2,4,128,128]{3,2,1,0:T(8,128)}, f32[2,4,128,128]{3,2,1,0:T(8,128)S(1)}, u32[]{:S(2)}, u32[]{:S(2)}) %collective-permute-start.1) | collective-permute-done | bytes 524320 | tf_op jit(solution)/shard_map/ppermute | solution.py:571
  53.9 0.0 collective-permute-done.2.refs_3_
  53.9 0.0 copy-done
  53.9 0.0 copy-done.8
  53.9 0.0 copy-done.11
  53.9 4.8 %column_forward.3 = f32[32,168,128]{2,1,0:T(8,128)S(1)} custom-call(s32[1]{0:T(128)} %bitcast.place, f32[128,128]{1,0:T(8,128)S(1)} %copy-done.11, bf16[336,256]{1,0:T(8,128)(2,1)S(1)} %copy-done.8, f32[2,4,128,128]{3,2,1,0:T(8,128)S(1)} %copy-done, f32[2,4,128,128]{3,2,1,0:T(8,128)S(1)} %collective-permute-done.refs_1_, ...), custom_call_target="tpu_custom_call" | custom-call | bytes 20971520 | tf_op jit(solution)/shard_map/column_forward/pallas_call | solution.py:656
  58.7 0.0 copy-start.3
  58.7 0.0 copy-start.4
  58.8 0.0 copy-start.5
  58.8 0.0 copy-start.6
  58.8 0.0 copy-start.7
  58.8 68.8 %all_to_all.10.lines = f32[32,168,128]{2,1,0:T(8,128)S(1)} all-to-all(f32[32,168,128]{2,1,0:T(8,128)S(1)} %column_forward.3), channel_id=1, replica_groups=mesh['row'=4,'col'=8] {'row','col'}, dimensions={0} | all-to-all | bytes 5505024 | tf_op jit(solution)/shard_map/all_to_all | solution.py:670
  127.6 0.0 copy-done.3
  127.6 0.0 copy-done.4
  127.6 0.0 copy-done.5
  127.6 0.0 copy-done.6
  127.6 0.0 copy-done.7
  127.7 12.0 %line.1 = f32[32,168,128]{2,1,0:T(8,128)S(1)} custom-call(f32[32,168,128]{2,1,0:T(8,128)S(1)} %all_to_all.10.lines, f32[2,11,256,128]{3,2,1,0:T(8,128)S(1)} %gain.1, f32[2,17,8,256]{3,2,1,0:T(8,128)S(1)} %copy-done.3, bf16[512,256]{1,0:T(8,128)(2,1)S(1)} %copy-done.7, bf16[512,256]{1,0:T(8,128)(2,1)S(1)} %copy-done.6, bf16[256,512]{1,0:T(8,128)(2,1)S(1)} %copy-done.5, ...), custom_call_target="tpu_custom_call" | custom-call | tf_op jit(solution)/shard_map/line/pallas_call | solution.py:681
  139.6 0.0 copy-start.1
  139.6 0.0 copy-start.10
  139.7 66.1 %all_to_all.11.source = f32[32,168,128]{2,1,0:T(8,128)S(1)} all-to-all(f32[32,168,128]{2,1,0:T(8,128)S(1)} %line.1), channel_id=1, replica_groups=mesh['row'=4,'col'=8] {'row','col'}, dimensions={0} | all-to-all | bytes 5505024 | tf_op jit(solution)/shard_map/all_to_all | solution.py:696
  205.8 0.0 copy-done.10
  205.8 9.8 %column_inverse.1 = (f32[1024,128]{1,0:T(8,128)S(1)}, f32[1024,128]{1,0:T(8,128)S(1)}, f32[1024,128]{1,0:T(8,128)S(1)}, f32[1024,128]{1,0:T(8,128)S(1)}, f32[103...) custom-call(s32[1]{0:T(128)} %bitcast.place, ...), custom_call_target="tpu_custom_call" | custom-call | tf_op jit(solution)/shard_map/column_inverse/pallas_call | solution.py:703
  215.6 0.1 collective-permute-start.9
  215.7 1.1 collective-permute-start.10
  216.8 2.4 collective-permute-start.11
  219.1 0.0 collective-permute-start.6
  219.1 1.2 collective-permute-done.6
  221.7 1.4 collective-permute-start.7
  223.1 2.3 collective-permute-done.7
  226.0 1.4 collective-permute-start.8
  227.4 3.2 %collective-permute-done.8.peak_two = f32[1]{0:T(128)} collective-permute-done((f32[1]{0:T(128)}, f32[1]{0:T(128)}, u32[]{:S(2)}, u32[]{:S(2)}) %collective-permute-start.8) | collective-permute-done | bytes 36 | tf_op jit(solution)/shard_map/ppermute | solution.py:727
  230.6 0.7 stamp.1
  231.3 0.6 collective-permute-start.13
  231.9 1.0 collective-permute-start.14
  232.9 0.0 collective-permute-done.9.refs_1_
  232.9 19.6 %collective-permute-done.10.refs_2_ = f32[1024,128]{1,0:T(8,128)S(1)} collective-permute-done((f32[1024,128]{1,0:T(8,128)S(1)}, f32[1024,128]{1,0:T(8,128)S(1)}, u32[]{:S(2)}, u32[]{:S(2)}) %collective-permute-start.10) | collective-permute-done | bytes 524320 | tf_op jit(solution)/shard_map/ppermute | solution.py:571
  252.5 0.0 collective-permute-done.11.refs_3_
  252.5 1.5 collective-permute-start.12
  254.0 9.9 %collective-permute-done.13.refs_6_ = f32[1032,128]{1,0:T(8,128)S(1)} collective-permute-done((f32[1032,128]{1,0:T(8,128)S(1)}, f32[1032,128]{1,0:T(8,128)S(1)}, u32[]{:S(2)}, u32[]{:S(2)}) %collective-permute-start.13) | collective-permute-done | bytes 528416 | tf_op jit(solution)/shard_map/ppermute | solution.py:571
  263.9 0.0 collective-permute-done.14.refs_7_
  263.9 0.0 collective-permute-done.12.refs_5_
  263.9 3.2 %encode.1 = (f32[1024,512]{1,0:T(8,128)}, f32[1024,512]{1,0:T(8,128)}) custom-call(s32[1]{0:T(128)} %bitcast.place, f32[1]{0:T(128)} %max.7.peak_one, f32[1]{0:T(128)} %collective-permute-done.8.peak_two, f32[1024,128]{1,0:T(8,128)S(1)} %get-tuple-element.52.refs_0_, f32[1024,128]{1,0:T(8,128)S(1)} %collective-permute-done.9.refs_1_, ...), custom_call_target="tpu_custom_call" | custom-call | tf_op jit(solution)/shard_map/encode/pallas_call | solution.py:762
  (4 shorter events, 0.0 us)
Async XLA Ops:
  3.6 16.0 %collective-permute-start.3 = (f32[2,4,128,128]{3,2,1,0:T(8,128)}, f32[2,4,128,128]{3,2,1,0:T(8,128)S(1)}, u32[]{:S(2)}, u32[]{:S(2)}) collective-permute-start(f32[2,4,128,128]{3,2,1,0:T(8,128)} %get-tuple-element.38), channel_id=1, source_target_pairs={{0,8},{8,0},{16,24},{24,16},{1,9},{9,1},{17,25},{25,17},{2,10},{10... | collective-permute-start | bytes 1572872 | tf_op jit(solution)/shard_map/ppermute | solution.py:571
  6.6 26.3 %collective-permute-start.4 = (f32[2,4,128,128]{3,2,1,0:T(8,128)}, f32[2,4,128,128]{3,2,1,0:T(8,128)S(1)}, u32[]{:S(2)}, u32[]{:S(2)}) collective-permute-start(f32[2,4,128,128]{3,2,1,0:T(8,128)} %get-tuple-element.39), channel_id=1, source_target_pairs={{0,16},{8,24},{16,0},{24,8},{1,17},{9,25},{17,1},{25,9},{2,18},{10... | collective-permute-start | bytes 1572872 | tf_op jit(solution)/shard_map/ppermute | solution.py:571
  8.1 24.8 %copy-start.2 = (f32[2,4,128,128]{3,2,1,0:T(8,128)S(1)}, f32[2,4,128,128]{3,2,1,0:T(8,128)}, u32[]{:S(2)}) copy-start(f32[2,4,128,128]{3,2,1,0:T(8,128)} %get-tuple-element.41.refs_0_) | copy-start | bytes 1572868
  8.1 24.8 %copy-start.9 = (bf16[336,256]{1,0:T(8,128)(2,1)S(1)}, bf16[336,256]{1,0:T(8,128)(2,1)}, u32[]{:S(2)}) copy-start(bf16[336,256]{1,0:T(8,128)(2,1)} %constant.61.clone.matrix) | copy-start | bytes 516100
  8.1 24.8 %copy-start.12 = (f32[128,128]{1,0:T(8,128)S(1)}, f32[128,128]{1,0:T(8,128)}, u32[]{:S(2)}) copy-start(f32[128,128]{1,0:T(8,128)} %constant.60.clone.twist) | copy-start | bytes 196612
  8.1 24.8 %collective-permute-start.5 = (f32[2,4,128,128]{3,2,1,0:T(8,128)}, f32[2,4,128,128]{3,2,1,0:T(8,128)}, u32[]{:S(2)}, u32[]{:S(2)}) collective-permute-start(f32[2,4,128,128]{3,2,1,0:T(8,128)} %get-tuple-element.40), channel_id=1, source_target_pairs={{0,24},{8,16},{16,8},{24,0},{1,25},{9,17},{17,9},{25,1},{2,26},{10... | collective-permute-start | bytes 1572872 | tf_op jit(solution)/shard_map/ppermute | solution.py:571
  11.2 30.9 %collective-permute-start = (f32[2,4,128,128]{3,2,1,0:T(8,128)}, f32[2,4,128,128]{3,2,1,0:T(8,128)S(1)}, u32[]{:S(2)}, u32[]{:S(2)}) collective-permute-start(f32[2,4,128,128]{3,2,1,0:T(8,128)} %get-tuple-element.34), channel_id=1, source_target_pairs={{0,8},{8,0},{16,24},{24,16},{1,9},{9,1},{17,25},{25,17},{2,10},{10... | collective-permute-start | bytes 1572872 | tf_op jit(solution)/shard_map/ppermute | solution.py:571
  13.1 40.8 %collective-permute-start.1 = (f32[2,4,128,128]{3,2,1,0:T(8,128)}, f32[2,4,128,128]{3,2,1,0:T(8,128)S(1)}, u32[]{:S(2)}, u32[]{:S(2)}) collective-permute-start(f32[2,4,128,128]{3,2,1,0:T(8,128)} %get-tuple-element.35), channel_id=1, source_target_pairs={{0,16},{8,24},{16,0},{24,8},{1,17},{9,25},{17,1},{25,9},{2,18},{10... | collective-permute-start | bytes 1572872 | tf_op jit(solution)/shard_map/ppermute | solution.py:571
  19.6 34.3 %collective-permute-start.2 = (f32[2,4,128,128]{3,2,1,0:T(8,128)}, f32[2,4,128,128]{3,2,1,0:T(8,128)S(1)}, u32[]{:S(2)}, u32[]{:S(2)}) collective-permute-start(f32[2,4,128,128]{3,2,1,0:T(8,128)} %get-tuple-element.36), channel_id=1, source_target_pairs={{0,24},{8,16},{16,8},{24,0},{1,25},{9,17},{17,9},{25,1},{2,26},{10... | collective-permute-start | bytes 1572872 | tf_op jit(solution)/shard_map/ppermute | solution.py:571
  26.8 27.2 %copy-start = (f32[2,4,128,128]{3,2,1,0:T(8,128)S(1)}, f32[2,4,128,128]{3,2,1,0:T(8,128)}, u32[]{:S(2)}) copy-start(f32[2,4,128,128]{3,2,1,0:T(8,128)} %get-tuple-element.33.refs_0_) | copy-start | bytes 1572868
  26.8 27.1 %copy-start.8 = (bf16[336,256]{1,0:T(8,128)(2,1)S(1)}, bf16[336,256]{1,0:T(8,128)(2,1)}, u32[]{:S(2)}) copy-start(bf16[336,256]{1,0:T(8,128)(2,1)} %constant.63.clone.matrix) | copy-start | bytes 516100
  26.8 27.1 %copy-start.11 = (f32[128,128]{1,0:T(8,128)S(1)}, f32[128,128]{1,0:T(8,128)}, u32[]{:S(2)}) copy-start(f32[128,128]{1,0:T(8,128)} %constant.62.clone.twist) | copy-start | bytes 196612
  58.7 68.9 %copy-start.3 = (f32[2,17,8,256]{3,2,1,0:T(8,128)S(1)}, f32[2,17,8,256]{3,2,1,0:T(8,128)}, u32[]{:S(2)}) copy-start(f32[2,17,8,256]{3,2,1,0:T(8,128)} %constant.64.clone.twist) | copy-start | bytes 835588
  58.7 68.9 %copy-start.4 = (bf16[256,512]{1,0:T(8,128)(2,1)S(1)}, bf16[256,512]{1,0:T(8,128)(2,1)}, u32[]{:S(2)}) copy-start(bf16[256,512]{1,0:T(8,128)(2,1)} %constant.68.clone.inv_low) | copy-start | bytes 786436
  58.8 68.9 %copy-start.5 = (bf16[256,512]{1,0:T(8,128)(2,1)S(1)}, bf16[256,512]{1,0:T(8,128)(2,1)}, u32[]{:S(2)}) copy-start(bf16[256,512]{1,0:T(8,128)(2,1)} %constant.67.clone.inv_high) | copy-start | bytes 786436
  58.8 68.9 %copy-start.6 = (bf16[512,256]{1,0:T(8,128)(2,1)S(1)}, bf16[512,256]{1,0:T(8,128)(2,1)}, u32[]{:S(2)}) copy-start(bf16[512,256]{1,0:T(8,128)(2,1)} %constant.66.clone.fwd_low) | copy-start | bytes 786436
  58.8 68.9 %copy-start.7 = (bf16[512,256]{1,0:T(8,128)(2,1)S(1)}, bf16[512,256]{1,0:T(8,128)(2,1)}, u32[]{:S(2)}) copy-start(bf16[512,256]{1,0:T(8,128)(2,1)} %constant.65.clone.fwd_high) | copy-start | bytes 786436
  139.6 66.2 %copy-start.1 = (bf16[2,256,512]{2,1,0:T(8,128)(2,1)S(1)}, bf16[2,256,512]{2,1,0:T(8,128)(2,1)}, u32[]{:S(2)}) copy-start(bf16[2,256,512]{2,1,0:T(8,128)(2,1)} %constant.70.clone.matrix) | copy-start | bytes 1572868
  139.6 66.1 %copy-start.10 = (f32[256,128]{1,0:T(8,128)S(1)}, f32[256,128]{1,0:T(8,128)}, u32[]{:S(2)}) copy-start(f32[256,128]{1,0:T(8,128)} %constant.69.clone.twist) | copy-start | bytes 393220
  215.6 17.4 %collective-permute-start.9 = (f32[1024,128]{1,0:T(8,128)S(1)}, f32[1024,128]{1,0:T(8,128)S(1)}, u32[]{:S(2)}, u32[]{:S(2)}) collective-permute-start(f32[1024,128]{1,0:T(8,128)S(1)} %get-tuple-element.53), channel_id=1, source_target_pairs={{0,8},{8,0},{16,24},{24,16},{1,9},{9,1},{17,25},{25,17},{2,10},{10... | collective-permute-start | bytes 1572872 | tf_op jit(solution)/shard_map/ppermute | solution.py:571
  215.7 36.8 %collective-permute-start.10 = (f32[1024,128]{1,0:T(8,128)S(1)}, f32[1024,128]{1,0:T(8,128)S(1)}, u32[]{:S(2)}, u32[]{:S(2)}) collective-permute-start(f32[1024,128]{1,0:T(8,128)S(1)} %get-tuple-element.54), channel_id=1, source_target_pairs={{0,16},{8,24},{16,0},{24,8},{1,17},{9,25},{17,1},{25,9},{2,18},{10... | collective-permute-start | bytes 1572872 | tf_op jit(solution)/shard_map/ppermute | solution.py:571
  216.8 35.7 %collective-permute-start.11 = (f32[1024,128]{1,0:T(8,128)S(1)}, f32[1024,128]{1,0:T(8,128)S(1)}, u32[]{:S(2)}, u32[]{:S(2)}) collective-permute-start(f32[1024,128]{1,0:T(8,128)S(1)} %get-tuple-element.55), channel_id=1, source_target_pairs={{0,24},{8,16},{16,8},{24,0},{1,25},{9,17},{17,9},{25,1},{2,26},{10... | collective-permute-start | bytes 1572872 | tf_op jit(solution)/shard_map/ppermute | solution.py:571
  219.1 1.2 collective-permute-start.6
  221.7 3.7 %collective-permute-start.7 = (f32[1]{0:T(128)}, f32[1]{0:T(128)}, u32[]{:S(2)}, u32[]{:S(2)}) collective-permute-start(f32[1]{0:T(128)} %max.6), channel_id=1, source_target_pairs={{0,2},{1,3},{2,0},{3,1},{4,6},{5,7},{6,4},{7,5},{8,10},{9,11},{10,... | collective-permute-start | bytes 20 | tf_op jit(solution)/shard_map/ppermute | solution.py:727
  226.0 4.6 %collective-permute-start.8 = (f32[1]{0:T(128)}, f32[1]{0:T(128)}, u32[]{:S(2)}, u32[]{:S(2)}) collective-permute-start(f32[1]{0:T(128)} %max.7.peak_one), channel_id=1, source_target_pairs={{0,4},{1,5},{2,6},{3,7},{4,0},{5,1},{6,2},{7,3},{8,12},{9,13},{10,... | collective-permute-start | bytes 20 | tf_op jit(solution)/shard_map/ppermute | solution.py:727
  231.3 32.6 %collective-permute-start.13 = (f32[1032,128]{1,0:T(8,128)S(1)}, f32[1032,128]{1,0:T(8,128)S(1)}, u32[]{:S(2)}, u32[]{:S(2)}) collective-permute-start(f32[1032,128]{1,0:T(8,128)S(1)} %get-tuple-element.62), channel_id=1, source_target_pairs={{0,16},{8,24},{16,0},{24,8},{1,17},{9,25},{17,1},{25,9},{2,18},{10... | collective-permute-start | bytes 1585160 | tf_op jit(solution)/shard_map/ppermute | solution.py:571
  231.9 32.0 %collective-permute-start.14 = (f32[1032,128]{1,0:T(8,128)S(1)}, f32[1032,128]{1,0:T(8,128)S(1)}, u32[]{:S(2)}, u32[]{:S(2)}) collective-permute-start(f32[1032,128]{1,0:T(8,128)S(1)} %get-tuple-element.63), channel_id=1, source_target_pairs={{0,24},{8,16},{16,8},{24,0},{1,25},{9,17},{17,9},{25,1},{2,26},{10... | collective-permute-start | bytes 1585160 | tf_op jit(solution)/shard_map/ppermute | solution.py:571
  252.5 11.4 %collective-permute-start.12 = (f32[1032,128]{1,0:T(8,128)S(1)}, f32[1032,128]{1,0:T(8,128)S(1)}, u32[]{:S(2)}, u32[]{:S(2)}) collective-permute-start(f32[1032,128]{1,0:T(8,128)S(1)} %get-tuple-element.61), channel_id=1, source_target_pairs={{0,8},{8,0},{16,24},{24,16},{1,9},{9,1},{17,25},{25,17},{2,10},{10... | collective-permute-start | bytes 1585160 | tf_op jit(solution)/shard_map/ppermute | solution.py:571

commit v18 on v17

--- a/solution.py
+++ b/solution.py
@@ -21,6 +21,7 @@
 CHUNKS = 2
 CHUNK = INNER // CHUNKS
 FRONT = ((0, 128), (128, 128))
+BACK = (192, 64)
 SPARE = 8
 
 
@@ -258,14 +259,15 @@
         return pltpu.make_async_copy(source.at[part], lines.at[part], sems.at[p])
 
     def copies_out(chunk, part):
-        parts = 1 if chunk + 1 < CHUNKS else 2
-        if part >= parts:
-            return []
-        rows = pl.ds(part * CHUNK // parts, CHUNK // parts)
+        size = CHUNK // 2
+        rows = pl.ds(part * size, size)
+        first = chunk * CHUNK + part * size
+        which = 0 if first < BACK[0] else 1
+        there_rows = pl.ds(first - which * BACK[0], size)
         copies = []
         for j in range(count):
-            piece = pieces[chunk * count + j].at[pl.ds(0, 2 * per_dest * CHUNK)]
-            there = piece.reshape(2, per_dest, CHUNK, width).at[:, :, rows]
+            piece = pieces[which * count + j].at[pl.ds(0, 2 * per_dest * BACK[which])]
+            there = piece.reshape(2, per_dest, BACK[which], width).at[:, :, there_rows]
             here = near.at[chunk, place[0] ^ j, :, :, rows]
             copies.append(pltpu.make_async_copy(here, there, out_sems.at[(chunk * 2 + part) * count + j]))
         return copies
@@ -328,7 +330,7 @@
                     for item in range(products // 2 // steps):
                         product(t * (products // 2 // steps) + item, chunk + 1)
 
-            for copy in copies_out(chunk, part if chunk + 1 == CHUNKS else 1 - part):
+            for copy in copies_out(chunk, part):
                 copy.start()
     peak_sq[0] = jnp.max(top[...])
     for chunk in range(CHUNKS):
@@ -510,14 +512,14 @@
 
 
 def encode_kernel(count, place, peak_one, peak_two, *refs):
-    pieces, refs = refs[: CHUNKS * count], refs[CHUNKS * count :]
+    pieces, refs = refs[: 2 * count], refs[2 * count :]
     slm_real, slm_imag, tile_real, tile_imag, sems = refs
     blocks, width = tile_real.shape[0], pieces[0].shape[-1]
     top = jnp.full((1, width), jnp.maximum(peak_one[0], peak_two[0]), jnp.float32)
-    for piece in pieces[(CHUNKS - 1) * count + 1 :]:
+    for piece in pieces[count + 1 :]:
         top = jnp.maximum(top, piece[pl.ds(piece.shape[0] - SPARE, 1), :])
-    cell = lax.broadcasted_iota(jnp.int32, (CHUNK, width), 0)
-    cell = cell + lax.broadcasted_iota(jnp.int32, (CHUNK, width), 1)
+    cell = lax.broadcasted_iota(jnp.int32, (BACK[0], width), 0)
+    cell = cell + lax.broadcasted_iota(jnp.int32, (BACK[0], width), 1)
     cell_sign = (1 - 2 * (cell & 1)).astype(jnp.float32)
 
     def copies_out(block):
@@ -529,15 +531,15 @@
 
     @pl.loop(0, blocks)
     def _(block):
-        for at in range(CHUNKS * count):
-            chunk, j = divmod(at, count)
-            piece = pieces[at]
+        for at, piece in enumerate(pieces):
+            which, j = divmod(at, count)
+            cells = BACK[which]
             lanes = pl.ds(pl.multiple_of((place[0] ^ j) * width, width), width)
-            rows = pl.ds(chunk * CHUNK, CHUNK)
-            real = pl.ds(pl.multiple_of(block * CHUNK, CHUNK), CHUNK)
-            imag = pl.ds(pl.multiple_of((blocks + block) * CHUNK, CHUNK), CHUNK)
+            rows = pl.ds(which * BACK[0], cells)
+            real = pl.ds(pl.multiple_of(block * cells, cells), cells)
+            imag = pl.ds(pl.multiple_of((blocks + block) * cells, cells), cells)
             tile_real[block, rows, lanes], tile_imag[block, rows, lanes] = encode(
-                piece[real, :], piece[imag, :], top, cell_sign
+                piece[real, :], piece[imag, :], top, cell_sign[:cells]
             )
         for copy in copies_out(block):
             copy.start()
@@ -697,13 +699,13 @@
     lines = lines.reshape(RES, total_rows, width)
 
     piece_shapes = [
-        jax.ShapeDtypeStruct((2 * blocks * CHUNK + spare, width), jnp.float32)
-        for spare in (0,) * (CHUNKS - 1) + (SPARE,)
+        jax.ShapeDtypeStruct((2 * blocks * cells + spare, width), jnp.float32)
+        for cells, spare in zip(BACK, (0, SPARE))
     ]
     *near, peak_sq = pl.pallas_call(
         partial(column_inverse_kernel, row_total),
         in_specs=[whole(pltpu.SMEM), anywhere, whole(), whole()],
-        out_specs=[anywhere] * (CHUNKS * row_total) + [whole(pltpu.SMEM)],
+        out_specs=[anywhere] * (2 * row_total) + [whole(pltpu.SMEM)],
         out_shape=[shape for shape in piece_shapes for _ in range(row_total)]
         + [jax.ShapeDtypeStruct((1,), jnp.float32)],
         scratch_shapes=[
@@ -750,10 +752,13 @@
         peak_sq = jnp.maximum(*peaks)[0]
         for piece in near[1][1:]:
             peak_sq = jnp.maximum(peak_sq, piece[-1, 0])
-        near = jnp.stack([jnp.stack([piece[: 2 * blocks * CHUNK] for piece in pieces]) for pieces in near])
-        near = jnp.take(near, jnp.arange(row_total) ^ place_row[0], axis=1)
-        near = near.reshape(CHUNKS, row_total, 2, blocks, CHUNK, width)
-        near = near.transpose(2, 3, 0, 4, 1, 5).reshape(2, height, tile_width)
+        both = []
+        for cells, pieces in zip(BACK, near):
+            part = jnp.stack([piece[: 2 * blocks * cells] for piece in pieces])
+            part = jnp.take(part, jnp.arange(row_total) ^ place_row[0], axis=0)
+            both.append(part.reshape(row_total, 2, blocks, cells, width))
+        near = jnp.concatenate(both, axis=3)
+        near = near.transpose(1, 2, 3, 0, 4).reshape(2, height, tile_width)
         odd_cell = (jnp.arange(height)[:, None] + jnp.arange(tile_width)[None, :]) % 2
         cell_sign = (1 - 2 * odd_cell).astype(jnp.float32)
         return encode(near[0], near[1], peak_sq, cell_sign)
@@ -761,7 +766,7 @@
     tile = pltpu.VMEM((blocks, INNER, tile_width), jnp.float32)
     return pl.pallas_call(
         partial(encode_kernel, row_total),
-        in_specs=[whole(pltpu.SMEM)] * 3 + [whole()] * (CHUNKS * row_total),
+        in_specs=[whole(pltpu.SMEM)] * 3 + [whole()] * (2 * row_total),
         out_specs=[anywhere] * 2,
         out_shape=[tile_shape, tile_shape],
         scratch_shapes=[tile, tile, pltpu.SemaphoreType.DMA((2 * blocks,))],

time: 267 us -> 269 us (level)
  transfers between devices with their start and end apart: 15 -> 15, of which waited for: 9 -> 11; matrix products, arithmetic and copies ran while one was open for 0% -> 0% of each run, Pallas kernels for 5% -> 5%
where the time goes in v18:
time: 269 us
  blocking collectives  135 us (50%)
  waiting for transfers between devices  63.2 us (23%)
  Pallas kernels  46.4 us (17%)
  starting transfers between devices  21 us (8%)
  between operations  2.76 us (1%)
    all_to_all x2, blocking collectives, body(): lax.all_to_all(lines, ('row', 'col'), split_axis=0, concat_axis=0, tiled=...  135 us
    ppermute x12, waiting for transfers between devices, exchange(): lax.ppermute(pieces[j], axis, [(i, i ^ j) for i in range(total)])  56.4 us
    ppermute x12, starting transfers between devices, exchange(): lax.ppermute(pieces[j], axis, [(i, i ^ j) for i in range(total)])  18.3 us
    pallas_call x1, Pallas kernels, body(): pl.pallas_call(partial(line_kernel, order, own, tail), grid=(-(-own // at...  12 us
    pallas_call x2, Pallas kernels, body(): pl.pallas_call(partial(column_forward_kernel, row_total), in_specs=[whole...  10.5 us
    pallas_call x1, Pallas kernels, body(): pl.pallas_call(partial(column_inverse_kernel, row_total), in_specs=[whole...  9.79 us
    ppermute x3, waiting for transfers between devices, body(): peaks = [peak_sq, lax.ppermute(peak_sq, 'col', partner)]  6.81 us
    pallas_call x2, Pallas kernels, body(): pl.pallas_call(pack_kernel, grid=(1,), in_specs=[whole(pltpu.SMEM)] + [pl...  5.94 us
  transfers between devices with their start and end apart: 15, of which 11 were waited for; matrix products, arithmetic and copies ran while one was open for 0% of the time, Pallas kernels for 5%

profile of v18, /device:TPU:0, one launch (start us, length us, event | category | flops | bytes accessed | tf_op | source)
XLA Modules:
  0.0 268.5 jit_solution(14523643223796863821)
XLA Ops:
  0.6 3.0 %pack.3 = (f32[2,4,128,128]{3,2,1,0:T(8,128)}, f32[2,4,128,128]{3,2,1,0:T(8,128)}, f32[2,4,128,128]{3,2,1,0:T(8,128)}, f32[2,4,128,128]{3,2,1,0:T(8,128)}) custom-call(s32[1]{0:T(128)} %bitcast.place, f32[4,256,512]{2,1,0:T(8,128)} %bitcast.4, f32[4,256,512]{2,1,0:T(8,128)} %bitcast.6), custom_call_target="tpu_custom_call" | custom-call | bytes 4194304 | tf_op jit(solution)/shard_map/pack/pallas_call | solution.py:634
  3.6 3.0 %collective-permute-start.3 = (f32[2,4,128,128]{3,2,1,0:T(8,128)}, f32[2,4,128,128]{3,2,1,0:T(8,128)S(1)}, u32[]{:S(2)}, u32[]{:S(2)}) collective-permute-start(f32[2,4,128,128]{3,2,1,0:T(8,128)} %get-tuple-element.38), channel_id=1, source_target_pairs={{0,8},{8,0},{16,24},{24,16},{1,9},{9,1},{17,25},{25,17},{2,10},{10... | collective-permute-start | bytes 1572872 | tf_op jit(solution)/shard_map/ppermute | solution.py:573
  6.6 1.5 collective-permute-start.4
  8.1 0.1 collective-permute-start.5
  8.2 3.0 %pack.2 = (f32[2,4,128,128]{3,2,1,0:T(8,128)}, f32[2,4,128,128]{3,2,1,0:T(8,128)}, f32[2,4,128,128]{3,2,1,0:T(8,128)}, f32[2,4,128,128]{3,2,1,0:T(8,128)}) custom-call(s32[1]{0:T(128)} %bitcast.place, f32[4,256,512]{2,1,0:T(8,128)} %bitcast.5, f32[4,256,512]{2,1,0:T(8,128)} %bitcast.7), custom_call_target="tpu_custom_call" | custom-call | bytes 4194304 | tf_op jit(solution)/shard_map/pack/pallas_call | solution.py:634
  11.2 1.9 collective-permute-start
  13.1 1.5 collective-permute-start.1
  14.6 5.0 %collective-permute-done.3.refs_1_ = f32[2,4,128,128]{3,2,1,0:T(8,128)S(1)} collective-permute-done((f32[2,4,128,128]{3,2,1,0:T(8,128)}, f32[2,4,128,128]{3,2,1,0:T(8,128)S(1)}, u32[]{:S(2)}, u32[]{:S(2)}) %collective-permute-start.3) | collective-permute-done | bytes 524320 | tf_op jit(solution)/shard_map/ppermute | solution.py:573
  19.6 3.0 %collective-permute-start.2 = (f32[2,4,128,128]{3,2,1,0:T(8,128)}, f32[2,4,128,128]{3,2,1,0:T(8,128)S(1)}, u32[]{:S(2)}, u32[]{:S(2)}) collective-permute-start(f32[2,4,128,128]{3,2,1,0:T(8,128)} %get-tuple-element.36), channel_id=1, source_target_pairs={{0,24},{8,16},{16,8},{24,0},{1,25},{9,17},{17,9},{25,1},{2,26},{10... | collective-permute-start | bytes 1572872 | tf_op jit(solution)/shard_map/ppermute | solution.py:573
  22.6 0.1 pad_add_fusion.place
  22.7 4.1 %gain.1 = f32[2,11,256,128]{3,2,1,0:T(8,128)S(1)} custom-call(s32[2]{0:T(128)S(1)} %pad_add_fusion.place), custom_call_target="tpu_custom_call" | custom-call | tf_op jit(solution)/shard_map/gain/pallas_call | solution.py:613
  26.8 0.0 copy-start
  26.8 0.0 copy-start.8
  26.8 0.0 copy-start.11
  26.8 6.1 %collective-permute-done.4.refs_2_ = f32[2,4,128,128]{3,2,1,0:T(8,128)S(1)} collective-permute-done((f32[2,4,128,128]{3,2,1,0:T(8,128)}, f32[2,4,128,128]{3,2,1,0:T(8,128)S(1)}, u32[]{:S(2)}, u32[]{:S(2)}) %collective-permute-start.4) | collective-permute-done | bytes 524320 | tf_op jit(solution)/shard_map/ppermute | solution.py:573
  32.9 0.0 collective-permute-done.5.refs_3_
  32.9 0.0 copy-done.2
  32.9 0.0 copy-done.9
  32.9 0.0 copy-done.12
  32.9 5.8 %column_forward.2.refs_4_ = f32[32,168,128]{2,1,0:T(8,128)S(1)} custom-call(s32[1]{0:T(128)} %bitcast.place, f32[128,128]{1,0:T(8,128)S(1)} %copy-done.12, bf16[336,256]{1,0:T(8,128)(2,1)S(1)} %copy-done.9, f32[2,4,128,128]{3,2,1,0:T(8,128)S(1)} %copy-done.2, f32[2,4,128,128]{3,2,1,0:T(8,128)S(1)} %collective-permute-done.3.refs_1_, ...), custom_call_target="tpu_custom_call" | custom-call | bytes 20971520 | tf_op jit(solution)/shard_map/column_forward/pallas_call | solution.py:658
  38.7 3.4 %collective-permute-done.refs_1_ = f32[2,4,128,128]{3,2,1,0:T(8,128)S(1)} collective-permute-done((f32[2,4,128,128]{3,2,1,0:T(8,128)}, f32[2,4,128,128]{3,2,1,0:T(8,128)S(1)}, u32[]{:S(2)}, u32[]{:S(2)}) %collective-permute-start) | collective-permute-done | bytes 524320 | tf_op jit(solution)/shard_map/ppermute | solution.py:573
  42.1 11.8 %collective-permute-done.1.refs_2_ = f32[2,4,128,128]{3,2,1,0:T(8,128)S(1)} collective-permute-done((f32[2,4,128,128]{3,2,1,0:T(8,128)}, f32[2,4,128,128]{3,2,1,0:T(8,128)S(1)}, u32[]{:S(2)}, u32[]{:S(2)}) %collective-permute-start.1) | collective-permute-done | bytes 524320 | tf_op jit(solution)/shard_map/ppermute | solution.py:573
  53.9 0.0 collective-permute-done.2.refs_3_
  53.9 0.0 copy-done
  53.9 0.0 copy-done.8
  53.9 0.0 copy-done.11
  53.9 4.8 %column_forward.3 = f32[32,168,128]{2,1,0:T(8,128)S(1)} custom-call(s32[1]{0:T(128)} %bitcast.place, f32[128,128]{1,0:T(8,128)S(1)} %copy-done.11, bf16[336,256]{1,0:T(8,128)(2,1)S(1)} %copy-done.8, f32[2,4,128,128]{3,2,1,0:T(8,128)S(1)} %copy-done, f32[2,4,128,128]{3,2,1,0:T(8,128)S(1)} %collective-permute-done.refs_1_, ...), custom_call_target="tpu_custom_call" | custom-call | bytes 20971520 | tf_op jit(solution)/shard_map/column_forward/pallas_call | solution.py:658
  58.7 0.0 copy-start.3
  58.7 0.0 copy-start.4
  58.8 0.0 copy-start.5
  58.8 0.0 copy-start.6
  58.8 0.0 copy-start.7
  58.8 68.8 %all_to_all.10.lines = f32[32,168,128]{2,1,0:T(8,128)S(1)} all-to-all(f32[32,168,128]{2,1,0:T(8,128)S(1)} %column_forward.3), channel_id=1, replica_groups=mesh['row'=4,'col'=8] {'row','col'}, dimensions={0} | all-to-all | bytes 5505024 | tf_op jit(solution)/shard_map/all_to_all | solution.py:672
  127.6 0.0 copy-done.3
  127.6 0.0 copy-done.4
  127.6 0.0 copy-done.5
  127.6 0.0 copy-done.6
  127.6 0.0 copy-done.7
  127.7 12.0 %line.1 = f32[32,168,128]{2,1,0:T(8,128)S(1)} custom-call(f32[32,168,128]{2,1,0:T(8,128)S(1)} %all_to_all.10.lines, f32[2,11,256,128]{3,2,1,0:T(8,128)S(1)} %gain.1, f32[2,17,8,256]{3,2,1,0:T(8,128)S(1)} %copy-done.3, bf16[512,256]{1,0:T(8,128)(2,1)S(1)} %copy-done.7, bf16[512,256]{1,0:T(8,128)(2,1)S(1)} %copy-done.6, bf16[256,512]{1,0:T(8,128)(2,1)S(1)} %copy-done.5, ...), custom_call_target="tpu_custom_call" | custom-call | tf_op jit(solution)/shard_map/line/pallas_call | solution.py:683
  139.6 0.0 copy-start.1
  139.6 0.0 copy-start.10
  139.7 66.1 %all_to_all.11.source = f32[32,168,128]{2,1,0:T(8,128)S(1)} all-to-all(f32[32,168,128]{2,1,0:T(8,128)S(1)} %line.1), channel_id=1, replica_groups=mesh['row'=4,'col'=8] {'row','col'}, dimensions={0} | all-to-all | bytes 5505024 | tf_op jit(solution)/shard_map/all_to_all | solution.py:698
  205.8 0.0 copy-done.1
  205.8 9.8 %column_inverse.1 = (f32[1536,128]{1,0:T(8,128)S(1)}, f32[1536,128]{1,0:T(8,128)S(1)}, f32[1536,128]{1,0:T(8,128)S(1)}, f32[1536,128]{1,0:T(8,128)S(1)}, f32[520...) custom-call(s32[1]{0:T(128)} %bitcast.place, ...), custom_call_target="tpu_custom_call" | custom-call | tf_op jit(solution)/shard_map/column_inverse/pallas_call | solution.py:705
  215.6 0.1 collective-permute-start.9
  215.7 1.1 collective-permute-start.10
  216.8 2.4 collective-permute-start.11
  219.1 0.0 collective-permute-start.6
  219.1 1.2 collective-permute-done.6
  221.7 1.4 collective-permute-start.7
  223.1 2.3 collective-permute-done.7
  226.0 1.4 collective-permute-start.8
  227.4 3.2 %collective-permute-done.8.peak_two = f32[1]{0:T(128)} collective-permute-done((f32[1]{0:T(128)}, f32[1]{0:T(128)}, u32[]{:S(2)}, u32[]{:S(2)}) %collective-permute-start.8) | collective-permute-done | bytes 36 | tf_op jit(solution)/shard_map/ppermute | solution.py:729
  230.6 0.7 stamp.1
  231.3 0.6 collective-permute-start.13
  231.9 1.0 collective-permute-start.14
  232.9 3.2 %collective-permute-done.9.refs_1_ = f32[1536,128]{1,0:T(8,128)S(1)} collective-permute-done((f32[1536,128]{1,0:T(8,128)S(1)}, f32[1536,128]{1,0:T(8,128)S(1)}, u32[]{:S(2)}, u32[]{:S(2)}) %collective-permute-start.9) | collective-permute-done | bytes 786464 | tf_op jit(solution)/shard_map/ppermute | solution.py:573
  236.1 22.5 %collective-permute-done.10.refs_2_ = f32[1536,128]{1,0:T(8,128)S(1)} collective-permute-done((f32[1536,128]{1,0:T(8,128)S(1)}, f32[1536,128]{1,0:T(8,128)S(1)}, u32[]{:S(2)}, u32[]{:S(2)}) %collective-permute-start.10) | collective-permute-done | bytes 786464 | tf_op jit(solution)/shard_map/ppermute | solution.py:573
  258.6 0.0 collective-permute-done.11.refs_3_
  258.6 2.1 collective-permute-start.12
  260.7 3.2 %collective-permute-done.13.refs_6_ = f32[520,128]{1,0:T(8,128)S(1)} collective-permute-done((f32[520,128]{1,0:T(8,128)S(1)}, f32[520,128]{1,0:T(8,128)S(1)}, u32[]{:S(2)}, u32[]{:S(2)}) %collective-permute-start.13) | collective-permute-done | bytes 266272 | tf_op jit(solution)/shard_map/ppermute | solution.py:573
  263.9 0.0 collective-permute-done.14.refs_7_
  263.9 1.2 collective-permute-done.12.refs_5_
  265.1 3.4 %encode.1 = (f32[1024,512]{1,0:T(8,128)}, f32[1024,512]{1,0:T(8,128)}) custom-call(s32[1]{0:T(128)} %bitcast.place, f32[1]{0:T(128)} %max.7.peak_one, f32[1]{0:T(128)} %collective-permute-done.8.peak_two, f32[1536,128]{1,0:T(8,128)S(1)} %get-tuple-element.52.refs_0_, f32[1536,128]{1,0:T(8,128)S(1)} %collective-permute-done.9.refs_1_, ...), custom_call_target="tpu_custom_call" | custom-call | tf_op jit(solution)/shard_map/encode/pallas_call | solution.py:767
  (4 shorter events, 0.0 us)
Async XLA Ops:
  3.6 16.0 %collective-permute-start.3 = (f32[2,4,128,128]{3,2,1,0:T(8,128)}, f32[2,4,128,128]{3,2,1,0:T(8,128)S(1)}, u32[]{:S(2)}, u32[]{:S(2)}) collective-permute-start(f32[2,4,128,128]{3,2,1,0:T(8,128)} %get-tuple-element.38), channel_id=1, source_target_pairs={{0,8},{8,0},{16,24},{24,16},{1,9},{9,1},{17,25},{25,17},{2,10},{10... | collective-permute-start | bytes 1572872 | tf_op jit(solution)/shard_map/ppermute | solution.py:573
  6.6 26.3 %collective-permute-start.4 = (f32[2,4,128,128]{3,2,1,0:T(8,128)}, f32[2,4,128,128]{3,2,1,0:T(8,128)S(1)}, u32[]{:S(2)}, u32[]{:S(2)}) collective-permute-start(f32[2,4,128,128]{3,2,1,0:T(8,128)} %get-tuple-element.39), channel_id=1, source_target_pairs={{0,16},{8,24},{16,0},{24,8},{1,17},{9,25},{17,1},{25,9},{2,18},{10... | collective-permute-start | bytes 1572872 | tf_op jit(solution)/shard_map/ppermute | solution.py:573
  8.1 24.8 %copy-start.2 = (f32[2,4,128,128]{3,2,1,0:T(8,128)S(1)}, f32[2,4,128,128]{3,2,1,0:T(8,128)}, u32[]{:S(2)}) copy-start(f32[2,4,128,128]{3,2,1,0:T(8,128)} %get-tuple-element.41.refs_0_) | copy-start | bytes 1572868
  8.1 24.8 %copy-start.9 = (bf16[336,256]{1,0:T(8,128)(2,1)S(1)}, bf16[336,256]{1,0:T(8,128)(2,1)}, u32[]{:S(2)}) copy-start(bf16[336,256]{1,0:T(8,128)(2,1)} %constant.61.clone.matrix) | copy-start | bytes 516100
  8.1 24.8 %copy-start.12 = (f32[128,128]{1,0:T(8,128)S(1)}, f32[128,128]{1,0:T(8,128)}, u32[]{:S(2)}) copy-start(f32[128,128]{1,0:T(8,128)} %constant.60.clone.twist) | copy-start | bytes 196612
  8.1 24.8 %collective-permute-start.5 = (f32[2,4,128,128]{3,2,1,0:T(8,128)}, f32[2,4,128,128]{3,2,1,0:T(8,128)}, u32[]{:S(2)}, u32[]{:S(2)}) collective-permute-start(f32[2,4,128,128]{3,2,1,0:T(8,128)} %get-tuple-element.40), channel_id=1, source_target_pairs={{0,24},{8,16},{16,8},{24,0},{1,25},{9,17},{17,9},{25,1},{2,26},{10... | collective-permute-start | bytes 1572872 | tf_op jit(solution)/shard_map/ppermute | solution.py:573
  11.2 30.9 %collective-permute-start = (f32[2,4,128,128]{3,2,1,0:T(8,128)}, f32[2,4,128,128]{3,2,1,0:T(8,128)S(1)}, u32[]{:S(2)}, u32[]{:S(2)}) collective-permute-start(f32[2,4,128,128]{3,2,1,0:T(8,128)} %get-tuple-element.34), channel_id=1, source_target_pairs={{0,8},{8,0},{16,24},{24,16},{1,9},{9,1},{17,25},{25,17},{2,10},{10... | collective-permute-start | bytes 1572872 | tf_op jit(solution)/shard_map/ppermute | solution.py:573
  13.1 40.8 %collective-permute-start.1 = (f32[2,4,128,128]{3,2,1,0:T(8,128)}, f32[2,4,128,128]{3,2,1,0:T(8,128)S(1)}, u32[]{:S(2)}, u32[]{:S(2)}) collective-permute-start(f32[2,4,128,128]{3,2,1,0:T(8,128)} %get-tuple-element.35), channel_id=1, source_target_pairs={{0,16},{8,24},{16,0},{24,8},{1,17},{9,25},{17,1},{25,9},{2,18},{10... | collective-permute-start | bytes 1572872 | tf_op jit(solution)/shard_map/ppermute | solution.py:573
  19.6 34.3 %collective-permute-start.2 = (f32[2,4,128,128]{3,2,1,0:T(8,128)}, f32[2,4,128,128]{3,2,1,0:T(8,128)S(1)}, u32[]{:S(2)}, u32[]{:S(2)}) collective-permute-start(f32[2,4,128,128]{3,2,1,0:T(8,128)} %get-tuple-element.36), channel_id=1, source_target_pairs={{0,24},{8,16},{16,8},{24,0},{1,25},{9,17},{17,9},{25,1},{2,26},{10... | collective-permute-start | bytes 1572872 | tf_op jit(solution)/shard_map/ppermute | solution.py:573
  26.8 27.2 %copy-start = (f32[2,4,128,128]{3,2,1,0:T(8,128)S(1)}, f32[2,4,128,128]{3,2,1,0:T(8,128)}, u32[]{:S(2)}) copy-start(f32[2,4,128,128]{3,2,1,0:T(8,128)} %get-tuple-element.33.refs_0_) | copy-start | bytes 1572868
  26.8 27.1 %copy-start.8 = (bf16[336,256]{1,0:T(8,128)(2,1)S(1)}, bf16[336,256]{1,0:T(8,128)(2,1)}, u32[]{:S(2)}) copy-start(bf16[336,256]{1,0:T(8,128)(2,1)} %constant.63.clone.matrix) | copy-start | bytes 516100
  26.8 27.1 %copy-start.11 = (f32[128,128]{1,0:T(8,128)S(1)}, f32[128,128]{1,0:T(8,128)}, u32[]{:S(2)}) copy-start(f32[128,128]{1,0:T(8,128)} %constant.62.clone.twist) | copy-start | bytes 196612
  58.7 68.9 %copy-start.3 = (f32[2,17,8,256]{3,2,1,0:T(8,128)S(1)}, f32[2,17,8,256]{3,2,1,0:T(8,128)}, u32[]{:S(2)}) copy-start(f32[2,17,8,256]{3,2,1,0:T(8,128)} %constant.64.clone.twist) | copy-start | bytes 835588
  58.7 68.9 %copy-start.4 = (bf16[256,512]{1,0:T(8,128)(2,1)S(1)}, bf16[256,512]{1,0:T(8,128)(2,1)}, u32[]{:S(2)}) copy-start(bf16[256,512]{1,0:T(8,128)(2,1)} %constant.68.clone.inv_low) | copy-start | bytes 786436
  58.8 68.9 %copy-start.5 = (bf16[256,512]{1,0:T(8,128)(2,1)S(1)}, bf16[256,512]{1,0:T(8,128)(2,1)}, u32[]{:S(2)}) copy-start(bf16[256,512]{1,0:T(8,128)(2,1)} %constant.67.clone.inv_high) | copy-start | bytes 786436
  58.8 68.9 %copy-start.6 = (bf16[512,256]{1,0:T(8,128)(2,1)S(1)}, bf16[512,256]{1,0:T(8,128)(2,1)}, u32[]{:S(2)}) copy-start(bf16[512,256]{1,0:T(8,128)(2,1)} %constant.66.clone.fwd_low) | copy-start | bytes 786436
  58.8 68.9 %copy-start.7 = (bf16[512,256]{1,0:T(8,128)(2,1)S(1)}, bf16[512,256]{1,0:T(8,128)(2,1)}, u32[]{:S(2)}) copy-start(bf16[512,256]{1,0:T(8,128)(2,1)} %constant.65.clone.fwd_high) | copy-start | bytes 786436
  139.6 66.2 %copy-start.1 = (bf16[2,256,512]{2,1,0:T(8,128)(2,1)S(1)}, bf16[2,256,512]{2,1,0:T(8,128)(2,1)}, u32[]{:S(2)}) copy-start(bf16[2,256,512]{2,1,0:T(8,128)(2,1)} %constant.70.clone.matrix) | copy-start | bytes 1572868
  139.6 66.1 %copy-start.10 = (f32[256,128]{1,0:T(8,128)S(1)}, f32[256,128]{1,0:T(8,128)}, u32[]{:S(2)}) copy-start(f32[256,128]{1,0:T(8,128)} %constant.69.clone.twist) | copy-start | bytes 393220
  215.6 20.5 %collective-permute-start.9 = (f32[1536,128]{1,0:T(8,128)S(1)}, f32[1536,128]{1,0:T(8,128)S(1)}, u32[]{:S(2)}, u32[]{:S(2)}) collective-permute-start(f32[1536,128]{1,0:T(8,128)S(1)} %get-tuple-element.53), channel_id=1, source_target_pairs={{0,8},{8,0},{16,24},{24,16},{1,9},{9,1},{17,25},{25,17},{2,10},{10... | collective-permute-start | bytes 2359304 | tf_op jit(solution)/shard_map/ppermute | solution.py:573
  215.7 43.0 %collective-permute-start.10 = (f32[1536,128]{1,0:T(8,128)S(1)}, f32[1536,128]{1,0:T(8,128)S(1)}, u32[]{:S(2)}, u32[]{:S(2)}) collective-permute-start(f32[1536,128]{1,0:T(8,128)S(1)} %get-tuple-element.54), channel_id=1, source_target_pairs={{0,16},{8,24},{16,0},{24,8},{1,17},{9,25},{17,1},{25,9},{2,18},{10... | collective-permute-start | bytes 2359304 | tf_op jit(solution)/shard_map/ppermute | solution.py:573
  216.8 41.9 %collective-permute-start.11 = (f32[1536,128]{1,0:T(8,128)S(1)}, f32[1536,128]{1,0:T(8,128)S(1)}, u32[]{:S(2)}, u32[]{:S(2)}) collective-permute-start(f32[1536,128]{1,0:T(8,128)S(1)} %get-tuple-element.55), channel_id=1, source_target_pairs={{0,24},{8,16},{16,8},{24,0},{1,25},{9,17},{17,9},{25,1},{2,26},{10... | collective-permute-start | bytes 2359304 | tf_op jit(solution)/shard_map/ppermute | solution.py:573
  219.1 1.2 collective-permute-start.6
  221.7 3.7 %collective-permute-start.7 = (f32[1]{0:T(128)}, f32[1]{0:T(128)}, u32[]{:S(2)}, u32[]{:S(2)}) collective-permute-start(f32[1]{0:T(128)} %max.6), channel_id=1, source_target_pairs={{0,2},{1,3},{2,0},{3,1},{4,6},{5,7},{6,4},{7,5},{8,10},{9,11},{10,... | collective-permute-start | bytes 20 | tf_op jit(solution)/shard_map/ppermute | solution.py:729
  226.0 4.6 %collective-permute-start.8 = (f32[1]{0:T(128)}, f32[1]{0:T(128)}, u32[]{:S(2)}, u32[]{:S(2)}) collective-permute-start(f32[1]{0:T(128)} %max.7.peak_one), channel_id=1, source_target_pairs={{0,4},{1,5},{2,6},{3,7},{4,0},{5,1},{6,2},{7,3},{8,12},{9,13},{10,... | collective-permute-start | bytes 20 | tf_op jit(solution)/shard_map/ppermute | solution.py:729
  231.3 32.6 %collective-permute-start.13 = (f32[520,128]{1,0:T(8,128)S(1)}, f32[520,128]{1,0:T(8,128)S(1)}, u32[]{:S(2)}, u32[]{:S(2)}) collective-permute-start(f32[520,128]{1,0:T(8,128)S(1)} %get-tuple-element.62), channel_id=1, source_target_pairs={{0,16},{8,24},{16,0},{24,8},{1,17},{9,25},{17,1},{25,9},{2,18},{10... | collective-permute-start | bytes 798728 | tf_op jit(solution)/shard_map/ppermute | solution.py:573
  231.9 32.0 %collective-permute-start.14 = (f32[520,128]{1,0:T(8,128)S(1)}, f32[520,128]{1,0:T(8,128)S(1)}, u32[]{:S(2)}, u32[]{:S(2)}) collective-permute-start(f32[520,128]{1,0:T(8,128)S(1)} %get-tuple-element.63), channel_id=1, source_target_pairs={{0,24},{8,16},{16,8},{24,0},{1,25},{9,17},{17,9},{25,1},{2,26},{10... | collective-permute-start | bytes 798728 | tf_op jit(solution)/shard_map/ppermute | solution.py:573
  258.6 6.5 %collective-permute-start.12 = (f32[520,128]{1,0:T(8,128)S(1)}, f32[520,128]{1,0:T(8,128)S(1)}, u32[]{:S(2)}, u32[]{:S(2)}) collective-permute-start(f32[520,128]{1,0:T(8,128)S(1)} %get-tuple-element.61), channel_id=1, source_target_pairs={{0,8},{8,0},{16,24},{24,16},{1,9},{9,1},{17,25},{25,17},{2,10},{10... | collective-permute-start | bytes 798728 | tf_op jit(solution)/shard_map/ppermute | solution.py:573

commit v19 on v17

--- a/solution.py
+++ b/solution.py
@@ -520,10 +520,12 @@
     cell = cell + lax.broadcasted_iota(jnp.int32, (CHUNK, width), 1)
     cell_sign = (1 - 2 * (cell & 1)).astype(jnp.float32)
 
-    def copies_out(block):
-        rows = pl.ds(block * INNER, INNER)
+    def copies_out(block, chunk):
+        part_rows = pl.ds(chunk * CHUNK, CHUNK)
+        rows = pl.ds(block * INNER + chunk * CHUNK, CHUNK)
+        first = 2 * (CHUNKS * block + chunk)
         return [
-            pltpu.make_async_copy(tile.at[block], slm.at[rows], sems.at[2 * block + part])
+            pltpu.make_async_copy(tile.at[block, part_rows], slm.at[rows], sems.at[first + part])
             for part, (tile, slm) in enumerate(((tile_real, slm_real), (tile_imag, slm_imag)))
         ]
 
@@ -539,28 +541,36 @@
             tile_real[block, rows, lanes], tile_imag[block, rows, lanes] = encode(
                 piece[real, :], piece[imag, :], top, cell_sign
             )
-        for copy in copies_out(block):
+            if j == count - 1:
+                for copy in copies_out(block, chunk):
+                    copy.start()
+
+    for block in range(blocks):
+        for chunk in range(CHUNKS):
+            for copy in copies_out(block, chunk):
+                copy.wait()
+
+
+def pack_kernel(start, place, field_real, field_imag, *refs):
+    pieces, (rows_in, in_sems, sems) = refs[:-3], refs[-3:]
+    size, width = pieces[0].shape[2:]
+    rows = pl.ds(start, size)
+    fetches = [
+        pltpu.make_async_copy(field.at[:, rows], rows_in.at[part], in_sems.at[part])
+        for part, field in enumerate((field_real, field_imag))
+    ]
+    for fetch in fetches:
+        fetch.start()
+    copies = []
+    for part, fetch in enumerate(fetches):
+        fetch.wait()
+        for j in list(range(1, len(pieces))) + [0]:
+            lanes = pl.ds(pl.multiple_of((place[0] ^ j) * width, width), width)
+            copy = pltpu.make_async_copy(
+                rows_in.at[part, :, :, lanes], pieces[j].at[part], sems.at[2 * j + part]
+            )
             copy.start()
-
-    for block in range(blocks):
-        for copy in copies_out(block):
-            copy.wait()
-
-
-def pack_kernel(place, field_real, field_imag, *refs):
-    pieces, sems = refs[:-1], refs[-1]
-    width = pieces[0].shape[-1]
-    copies = []
-    for j in list(range(1, len(pieces))) + [0]:
-        lanes = pl.ds(pl.multiple_of((place[0] ^ j) * width, width), width)
-        for part, field in enumerate((field_real, field_imag)):
-            copies.append(
-                pltpu.make_async_copy(
-                    field.at[:, :, lanes], pieces[j].at[part], sems.at[2 * j + part]
-                )
-            )
-    for copy in copies:
-        copy.start()
+            copies.append(copy)
     for copy in copies:
         copy.wait()
 
@@ -627,16 +637,17 @@
     lines = []
     for chunk, (start, size) in enumerate(FRONT):
         piece_shape = jax.ShapeDtypeStruct((2, blocks, size, width), jnp.float32)
-        at = start // size
         if width == 128:
             pieces = pl.pallas_call(
-                pack_kernel,
-                grid=(1,),
-                in_specs=[whole(pltpu.SMEM)]
-                + [pl.BlockSpec((blocks, size, tile_width), lambda i: (0, at, 0))] * 2,
+                partial(pack_kernel, start),
+                in_specs=[whole(pltpu.SMEM), anywhere, anywhere],
                 out_specs=[anywhere] * row_total,
                 out_shape=[piece_shape] * row_total,
-                scratch_shapes=[pltpu.SemaphoreType.DMA((2 * row_total,))],
+                scratch_shapes=[
+                    pltpu.VMEM((2, blocks, size, tile_width), jnp.float32),
+                    pltpu.SemaphoreType.DMA((2,)),
+                    pltpu.SemaphoreType.DMA((2 * row_total,)),
+                ],
                 compiler_params=params(56),
                 cost_estimate=cost(4),
                 name="pack",
@@ -764,7 +775,7 @@
         in_specs=[whole(pltpu.SMEM)] * 3 + [whole()] * (CHUNKS * row_total),
         out_specs=[anywhere] * 2,
         out_shape=[tile_shape, tile_shape],
-        scratch_shapes=[tile, tile, pltpu.SemaphoreType.DMA((2 * blocks,))],
+        scratch_shapes=[tile, tile, pltpu.SemaphoreType.DMA((2 * CHUNKS * blocks,))],
         compiler_params=params(16),
         name="encode",
     )(place_row, *peaks, *near[0], *near[1])

time: 267 us -> 267 us (level)
  no operation moved by 1% of the time
where the time goes in v19:
time: 267 us
  blocking collectives  135 us (51%)
  waiting for transfers between devices  62.9 us (24%)
  Pallas kernels  45.5 us (17%)
  starting transfers between devices  20.4 us (8%)
  between operations  2.76 us (1%)
    all_to_all x2, blocking collectives, body(): lax.all_to_all(lines, ('row', 'col'), split_axis=0, concat_axis=0, tiled=...  135 us
    ppermute x12, waiting for transfers between devices, exchange(): lax.ppermute(pieces[j], axis, [(i, i ^ j) for i in range(total)])  56.1 us
    ppermute x12, starting transfers between devices, exchange(): lax.ppermute(pieces[j], axis, [(i, i ^ j) for i in range(total)])  17.7 us
    pallas_call x1, Pallas kernels, body(): pl.pallas_call(partial(line_kernel, order, own, tail), grid=(-(-own // at...  12 us
    pallas_call x2, Pallas kernels, body(): pl.pallas_call(partial(column_forward_kernel, row_total), in_specs=[whole...  10.5 us
    pallas_call x1, Pallas kernels, body(): pl.pallas_call(partial(column_inverse_kernel, row_total), in_specs=[whole...  9.78 us
    ppermute x3, waiting for transfers between devices, body(): peaks = [peak_sq, lax.ppermute(peak_sq, 'col', partner)]  6.81 us
  transfers between devices with their start and end apart: 15, of which 9 were waited for; matrix products, arithmetic and copies ran while one was open for 0% of the time, Pallas kernels for 5%

profile of v19, /device:TPU:0, one launch (start us, length us, event | category | flops | bytes accessed | tf_op | source)
XLA Modules:
  0.0 266.7 jit_solution(16022688397300043730)
XLA Ops:
  0.6 2.6 pack.3
  3.3 3.0 %collective-permute-start.3 = (f32[2,4,128,128]{3,2,1,0:T(8,128)}, f32[2,4,128,128]{3,2,1,0:T(8,128)S(1)}, u32[]{:S(2)}, u32[]{:S(2)}) collective-permute-start(f32[2,4,128,128]{3,2,1,0:T(8,128)} %get-tuple-element.38), channel_id=1, source_target_pairs={{0,8},{8,0},{16,24},{24,16},{1,9},{9,1},{17,25},{25,17},{2,10},{10... | collective-permute-start | bytes 1572872 | tf_op jit(solution)/shard_map/ppermute | solution.py:581
  6.3 1.5 collective-permute-start.4
  7.8 0.1 collective-permute-start.5
  7.9 2.7 %pack.2 = (f32[2,4,128,128]{3,2,1,0:T(8,128)}, f32[2,4,128,128]{3,2,1,0:T(8,128)}, f32[2,4,128,128]{3,2,1,0:T(8,128)}, f32[2,4,128,128]{3,2,1,0:T(8,128)}) custom-call(s32[1]{0:T(128)} %bitcast.place, f32[4,256,512]{2,1,0:T(8,128)} %bitcast.5, f32[4,256,512]{2,1,0:T(8,128)} %bitcast.7), custom_call_target="tpu_custom_call" | custom-call | bytes 4194304 | tf_op jit(solution)/shard_map/pack/pallas_call | solution.py:641
  10.5 1.9 collective-permute-start
  12.5 1.5 collective-permute-start.1
  14.0 5.3 %collective-permute-done.3.refs_1_ = f32[2,4,128,128]{3,2,1,0:T(8,128)S(1)} collective-permute-done((f32[2,4,128,128]{3,2,1,0:T(8,128)}, f32[2,4,128,128]{3,2,1,0:T(8,128)S(1)}, u32[]{:S(2)}, u32[]{:S(2)}) %collective-permute-start.3) | collective-permute-done | bytes 524320 | tf_op jit(solution)/shard_map/ppermute | solution.py:581
  19.2 3.0 %collective-permute-start.2 = (f32[2,4,128,128]{3,2,1,0:T(8,128)}, f32[2,4,128,128]{3,2,1,0:T(8,128)S(1)}, u32[]{:S(2)}, u32[]{:S(2)}) collective-permute-start(f32[2,4,128,128]{3,2,1,0:T(8,128)} %get-tuple-element.36), channel_id=1, source_target_pairs={{0,24},{8,16},{16,8},{24,0},{1,25},{9,17},{17,9},{25,1},{2,26},{10... | collective-permute-start | bytes 1572872 | tf_op jit(solution)/shard_map/ppermute | solution.py:581
  22.3 0.1 pad_add_fusion.place
  22.3 4.1 %gain.1 = f32[2,11,256,128]{3,2,1,0:T(8,128)S(1)} custom-call(s32[2]{0:T(128)S(1)} %pad_add_fusion.place), custom_call_target="tpu_custom_call" | custom-call | tf_op jit(solution)/shard_map/gain/pallas_call | solution.py:621
  26.4 0.0 copy-start
  26.4 0.0 copy-start.8
  26.5 0.0 copy-start.11
  26.5 6.1 %collective-permute-done.4.refs_2_ = f32[2,4,128,128]{3,2,1,0:T(8,128)S(1)} collective-permute-done((f32[2,4,128,128]{3,2,1,0:T(8,128)}, f32[2,4,128,128]{3,2,1,0:T(8,128)S(1)}, u32[]{:S(2)}, u32[]{:S(2)}) %collective-permute-start.4) | collective-permute-done | bytes 524320 | tf_op jit(solution)/shard_map/ppermute | solution.py:581
  32.6 0.0 collective-permute-done.5.refs_3_
  32.6 0.0 copy-done.2
  32.6 0.0 copy-done.9
  32.6 0.0 copy-done.12
  32.6 5.8 %column_forward.2.refs_4_ = f32[32,168,128]{2,1,0:T(8,128)S(1)} custom-call(s32[1]{0:T(128)} %bitcast.place, f32[128,128]{1,0:T(8,128)S(1)} %copy-done.12, bf16[336,256]{1,0:T(8,128)(2,1)S(1)} %copy-done.9, f32[2,4,128,128]{3,2,1,0:T(8,128)S(1)} %copy-done.2, f32[2,4,128,128]{3,2,1,0:T(8,128)S(1)} %collective-permute-done.3.refs_1_, ...), custom_call_target="tpu_custom_call" | custom-call | bytes 20971520 | tf_op jit(solution)/shard_map/column_forward/pallas_call | solution.py:667
  38.4 3.4 %collective-permute-done.refs_1_ = f32[2,4,128,128]{3,2,1,0:T(8,128)S(1)} collective-permute-done((f32[2,4,128,128]{3,2,1,0:T(8,128)}, f32[2,4,128,128]{3,2,1,0:T(8,128)S(1)}, u32[]{:S(2)}, u32[]{:S(2)}) %collective-permute-start) | collective-permute-done | bytes 524320 | tf_op jit(solution)/shard_map/ppermute | solution.py:581
  41.8 11.8 %collective-permute-done.1.refs_2_ = f32[2,4,128,128]{3,2,1,0:T(8,128)S(1)} collective-permute-done((f32[2,4,128,128]{3,2,1,0:T(8,128)}, f32[2,4,128,128]{3,2,1,0:T(8,128)S(1)}, u32[]{:S(2)}, u32[]{:S(2)}) %collective-permute-start.1) | collective-permute-done | bytes 524320 | tf_op jit(solution)/shard_map/ppermute | solution.py:581
  53.6 0.0 collective-permute-done.2.refs_3_
  53.6 0.0 copy-done
  53.6 0.0 copy-done.8
  53.6 0.0 copy-done.11
  53.6 4.8 %column_forward.3 = f32[32,168,128]{2,1,0:T(8,128)S(1)} custom-call(s32[1]{0:T(128)} %bitcast.place, f32[128,128]{1,0:T(8,128)S(1)} %copy-done.11, bf16[336,256]{1,0:T(8,128)(2,1)S(1)} %copy-done.8, f32[2,4,128,128]{3,2,1,0:T(8,128)S(1)} %copy-done, f32[2,4,128,128]{3,2,1,0:T(8,128)S(1)} %collective-permute-done.refs_1_, ...), custom_call_target="tpu_custom_call" | custom-call | bytes 20971520 | tf_op jit(solution)/shard_map/column_forward/pallas_call | solution.py:667
  58.4 0.0 copy-start.3
  58.4 0.0 copy-start.4
  58.4 0.0 copy-start.5
  58.4 0.0 copy-start.6
  58.4 0.0 copy-start.7
  58.5 68.8 %all_to_all.10.lines = f32[32,168,128]{2,1,0:T(8,128)S(1)} all-to-all(f32[32,168,128]{2,1,0:T(8,128)S(1)} %column_forward.3), channel_id=1, replica_groups=mesh['row'=4,'col'=8] {'row','col'}, dimensions={0} | all-to-all | bytes 5505024 | tf_op jit(solution)/shard_map/all_to_all | solution.py:681
  127.3 0.0 copy-done.3
  127.3 0.0 copy-done.4
  127.3 0.0 copy-done.5
  127.3 0.0 copy-done.6
  127.3 0.0 copy-done.7
  127.3 12.0 %line.1 = f32[32,168,128]{2,1,0:T(8,128)S(1)} custom-call(f32[32,168,128]{2,1,0:T(8,128)S(1)} %all_to_all.10.lines, f32[2,11,256,128]{3,2,1,0:T(8,128)S(1)} %gain.1, f32[2,17,8,256]{3,2,1,0:T(8,128)S(1)} %copy-done.3, bf16[512,256]{1,0:T(8,128)(2,1)S(1)} %copy-done.7, bf16[512,256]{1,0:T(8,128)(2,1)S(1)} %copy-done.6, bf16[256,512]{1,0:T(8,128)(2,1)S(1)} %copy-done.5, ...), custom_call_target="tpu_custom_call" | custom-call | tf_op jit(solution)/shard_map/line/pallas_call | solution.py:692
  139.3 0.0 copy-start.1
  139.3 0.0 copy-start.10
  139.3 66.1 %all_to_all.11.source = f32[32,168,128]{2,1,0:T(8,128)S(1)} all-to-all(f32[32,168,128]{2,1,0:T(8,128)S(1)} %line.1), channel_id=1, replica_groups=mesh['row'=4,'col'=8] {'row','col'}, dimensions={0} | all-to-all | bytes 5505024 | tf_op jit(solution)/shard_map/all_to_all | solution.py:707
  205.4 0.0 copy-done.1
  205.5 9.8 %column_inverse.1 = (f32[1024,128]{1,0:T(8,128)S(1)}, f32[1024,128]{1,0:T(8,128)S(1)}, f32[1024,128]{1,0:T(8,128)S(1)}, f32[1024,128]{1,0:T(8,128)S(1)}, f32[103...) custom-call(s32[1]{0:T(128)} %bitcast.place, ...), custom_call_target="tpu_custom_call" | custom-call | tf_op jit(solution)/shard_map/column_inverse/pallas_call | solution.py:714
  215.2 0.1 collective-permute-start.9
  215.3 1.1 collective-permute-start.10
  216.4 2.4 collective-permute-start.11
  218.8 0.0 collective-permute-start.6
  218.8 1.2 collective-permute-done.6
  221.4 1.4 collective-permute-start.7
  222.7 2.3 collective-permute-done.7
  225.7 1.4 collective-permute-start.8
  227.0 3.2 %collective-permute-done.8.peak_two = f32[1]{0:T(128)} collective-permute-done((f32[1]{0:T(128)}, f32[1]{0:T(128)}, u32[]{:S(2)}, u32[]{:S(2)}) %collective-permute-start.8) | collective-permute-done | bytes 36 | tf_op jit(solution)/shard_map/ppermute | solution.py:738
  230.3 0.7 stamp.1
  231.0 0.6 collective-permute-start.13
  231.6 1.0 collective-permute-start.14
  232.6 0.0 collective-permute-done.9.refs_1_
  232.6 19.6 %collective-permute-done.10.refs_2_ = f32[1024,128]{1,0:T(8,128)S(1)} collective-permute-done((f32[1024,128]{1,0:T(8,128)S(1)}, f32[1024,128]{1,0:T(8,128)S(1)}, u32[]{:S(2)}, u32[]{:S(2)}) %collective-permute-start.10) | collective-permute-done | bytes 524320 | tf_op jit(solution)/shard_map/ppermute | solution.py:581
  252.2 0.0 collective-permute-done.11.refs_3_
  252.2 1.5 collective-permute-start.12
  253.7 9.9 %collective-permute-done.13.refs_6_ = f32[1032,128]{1,0:T(8,128)S(1)} collective-permute-done((f32[1032,128]{1,0:T(8,128)S(1)}, f32[1032,128]{1,0:T(8,128)S(1)}, u32[]{:S(2)}, u32[]{:S(2)}) %collective-permute-start.13) | collective-permute-done | bytes 528416 | tf_op jit(solution)/shard_map/ppermute | solution.py:581
  263.6 0.0 collective-permute-done.14.refs_7_
  263.6 0.0 collective-permute-done.12.refs_5_
  263.6 3.1 %encode.1 = (f32[1024,512]{1,0:T(8,128)}, f32[1024,512]{1,0:T(8,128)}) custom-call(s32[1]{0:T(128)} %bitcast.place, f32[1]{0:T(128)} %max.7.peak_one, f32[1]{0:T(128)} %collective-permute-done.8.peak_two, f32[1024,128]{1,0:T(8,128)S(1)} %get-tuple-element.52.refs_0_, f32[1024,128]{1,0:T(8,128)S(1)} %collective-permute-done.9.refs_1_, ...), custom_call_target="tpu_custom_call" | custom-call | tf_op jit(solution)/shard_map/encode/pallas_call | solution.py:773
  (4 shorter events, 0.0 us)
Async XLA Ops:
  3.3 16.0 %collective-permute-start.3 = (f32[2,4,128,128]{3,2,1,0:T(8,128)}, f32[2,4,128,128]{3,2,1,0:T(8,128)S(1)}, u32[]{:S(2)}, u32[]{:S(2)}) collective-permute-start(f32[2,4,128,128]{3,2,1,0:T(8,128)} %get-tuple-element.38), channel_id=1, source_target_pairs={{0,8},{8,0},{16,24},{24,16},{1,9},{9,1},{17,25},{25,17},{2,10},{10... | collective-permute-start | bytes 1572872 | tf_op jit(solution)/shard_map/ppermute | solution.py:581
  6.3 26.3 %collective-permute-start.4 = (f32[2,4,128,128]{3,2,1,0:T(8,128)}, f32[2,4,128,128]{3,2,1,0:T(8,128)S(1)}, u32[]{:S(2)}, u32[]{:S(2)}) collective-permute-start(f32[2,4,128,128]{3,2,1,0:T(8,128)} %get-tuple-element.39), channel_id=1, source_target_pairs={{0,16},{8,24},{16,0},{24,8},{1,17},{9,25},{17,1},{25,9},{2,18},{10... | collective-permute-start | bytes 1572872 | tf_op jit(solution)/shard_map/ppermute | solution.py:581
  7.8 24.8 %copy-start.2 = (f32[2,4,128,128]{3,2,1,0:T(8,128)S(1)}, f32[2,4,128,128]{3,2,1,0:T(8,128)}, u32[]{:S(2)}) copy-start(f32[2,4,128,128]{3,2,1,0:T(8,128)} %get-tuple-element.41.refs_0_) | copy-start | bytes 1572868
  7.8 24.8 %copy-start.9 = (bf16[336,256]{1,0:T(8,128)(2,1)S(1)}, bf16[336,256]{1,0:T(8,128)(2,1)}, u32[]{:S(2)}) copy-start(bf16[336,256]{1,0:T(8,128)(2,1)} %constant.61.clone.matrix) | copy-start | bytes 516100
  7.8 24.8 %copy-start.12 = (f32[128,128]{1,0:T(8,128)S(1)}, f32[128,128]{1,0:T(8,128)}, u32[]{:S(2)}) copy-start(f32[128,128]{1,0:T(8,128)} %constant.60.clone.twist) | copy-start | bytes 196612
  7.8 24.8 %collective-permute-start.5 = (f32[2,4,128,128]{3,2,1,0:T(8,128)}, f32[2,4,128,128]{3,2,1,0:T(8,128)}, u32[]{:S(2)}, u32[]{:S(2)}) collective-permute-start(f32[2,4,128,128]{3,2,1,0:T(8,128)} %get-tuple-element.40), channel_id=1, source_target_pairs={{0,24},{8,16},{16,8},{24,0},{1,25},{9,17},{17,9},{25,1},{2,26},{10... | collective-permute-start | bytes 1572872 | tf_op jit(solution)/shard_map/ppermute | solution.py:581
  10.5 31.2 %collective-permute-start = (f32[2,4,128,128]{3,2,1,0:T(8,128)}, f32[2,4,128,128]{3,2,1,0:T(8,128)S(1)}, u32[]{:S(2)}, u32[]{:S(2)}) collective-permute-start(f32[2,4,128,128]{3,2,1,0:T(8,128)} %get-tuple-element.34), channel_id=1, source_target_pairs={{0,8},{8,0},{16,24},{24,16},{1,9},{9,1},{17,25},{25,17},{2,10},{10... | collective-permute-start | bytes 1572872 | tf_op jit(solution)/shard_map/ppermute | solution.py:581
  12.5 41.1 %collective-permute-start.1 = (f32[2,4,128,128]{3,2,1,0:T(8,128)}, f32[2,4,128,128]{3,2,1,0:T(8,128)S(1)}, u32[]{:S(2)}, u32[]{:S(2)}) collective-permute-start(f32[2,4,128,128]{3,2,1,0:T(8,128)} %get-tuple-element.35), channel_id=1, source_target_pairs={{0,16},{8,24},{16,0},{24,8},{1,17},{9,25},{17,1},{25,9},{2,18},{10... | collective-permute-start | bytes 1572872 | tf_op jit(solution)/shard_map/ppermute | solution.py:581
  19.2 34.3 %collective-permute-start.2 = (f32[2,4,128,128]{3,2,1,0:T(8,128)}, f32[2,4,128,128]{3,2,1,0:T(8,128)S(1)}, u32[]{:S(2)}, u32[]{:S(2)}) collective-permute-start(f32[2,4,128,128]{3,2,1,0:T(8,128)} %get-tuple-element.36), channel_id=1, source_target_pairs={{0,24},{8,16},{16,8},{24,0},{1,25},{9,17},{17,9},{25,1},{2,26},{10... | collective-permute-start | bytes 1572872 | tf_op jit(solution)/shard_map/ppermute | solution.py:581
  26.4 27.2 %copy-start = (f32[2,4,128,128]{3,2,1,0:T(8,128)S(1)}, f32[2,4,128,128]{3,2,1,0:T(8,128)}, u32[]{:S(2)}) copy-start(f32[2,4,128,128]{3,2,1,0:T(8,128)} %get-tuple-element.33.refs_0_) | copy-start | bytes 1572868
  26.4 27.1 %copy-start.8 = (bf16[336,256]{1,0:T(8,128)(2,1)S(1)}, bf16[336,256]{1,0:T(8,128)(2,1)}, u32[]{:S(2)}) copy-start(bf16[336,256]{1,0:T(8,128)(2,1)} %constant.63.clone.matrix) | copy-start | bytes 516100
  26.5 27.1 %copy-start.11 = (f32[128,128]{1,0:T(8,128)S(1)}, f32[128,128]{1,0:T(8,128)}, u32[]{:S(2)}) copy-start(f32[128,128]{1,0:T(8,128)} %constant.62.clone.twist) | copy-start | bytes 196612
  58.4 68.9 %copy-start.3 = (f32[2,17,8,256]{3,2,1,0:T(8,128)S(1)}, f32[2,17,8,256]{3,2,1,0:T(8,128)}, u32[]{:S(2)}) copy-start(f32[2,17,8,256]{3,2,1,0:T(8,128)} %constant.64.clone.twist) | copy-start | bytes 835588
  58.4 68.9 %copy-start.4 = (bf16[256,512]{1,0:T(8,128)(2,1)S(1)}, bf16[256,512]{1,0:T(8,128)(2,1)}, u32[]{:S(2)}) copy-start(bf16[256,512]{1,0:T(8,128)(2,1)} %constant.68.clone.inv_low) | copy-start | bytes 786436
  58.4 68.9 %copy-start.5 = (bf16[256,512]{1,0:T(8,128)(2,1)S(1)}, bf16[256,512]{1,0:T(8,128)(2,1)}, u32[]{:S(2)}) copy-start(bf16[256,512]{1,0:T(8,128)(2,1)} %constant.67.clone.inv_high) | copy-start | bytes 786436
  58.4 68.9 %copy-start.6 = (bf16[512,256]{1,0:T(8,128)(2,1)S(1)}, bf16[512,256]{1,0:T(8,128)(2,1)}, u32[]{:S(2)}) copy-start(bf16[512,256]{1,0:T(8,128)(2,1)} %constant.66.clone.fwd_low) | copy-start | bytes 786436
  58.4 68.9 %copy-start.7 = (bf16[512,256]{1,0:T(8,128)(2,1)S(1)}, bf16[512,256]{1,0:T(8,128)(2,1)}, u32[]{:S(2)}) copy-start(bf16[512,256]{1,0:T(8,128)(2,1)} %constant.65.clone.fwd_high) | copy-start | bytes 786436
  139.3 66.2 %copy-start.1 = (bf16[2,256,512]{2,1,0:T(8,128)(2,1)S(1)}, bf16[2,256,512]{2,1,0:T(8,128)(2,1)}, u32[]{:S(2)}) copy-start(bf16[2,256,512]{2,1,0:T(8,128)(2,1)} %constant.70.clone.matrix) | copy-start | bytes 1572868
  139.3 66.1 %copy-start.10 = (f32[256,128]{1,0:T(8,128)S(1)}, f32[256,128]{1,0:T(8,128)}, u32[]{:S(2)}) copy-start(f32[256,128]{1,0:T(8,128)} %constant.69.clone.twist) | copy-start | bytes 393220
  215.2 17.4 %collective-permute-start.9 = (f32[1024,128]{1,0:T(8,128)S(1)}, f32[1024,128]{1,0:T(8,128)S(1)}, u32[]{:S(2)}, u32[]{:S(2)}) collective-permute-start(f32[1024,128]{1,0:T(8,128)S(1)} %get-tuple-element.53), channel_id=1, source_target_pairs={{0,8},{8,0},{16,24},{24,16},{1,9},{9,1},{17,25},{25,17},{2,10},{10... | collective-permute-start | bytes 1572872 | tf_op jit(solution)/shard_map/ppermute | solution.py:581
  215.3 36.8 %collective-permute-start.10 = (f32[1024,128]{1,0:T(8,128)S(1)}, f32[1024,128]{1,0:T(8,128)S(1)}, u32[]{:S(2)}, u32[]{:S(2)}) collective-permute-start(f32[1024,128]{1,0:T(8,128)S(1)} %get-tuple-element.54), channel_id=1, source_target_pairs={{0,16},{8,24},{16,0},{24,8},{1,17},{9,25},{17,1},{25,9},{2,18},{10... | collective-permute-start | bytes 1572872 | tf_op jit(solution)/shard_map/ppermute | solution.py:581
  216.4 35.7 %collective-permute-start.11 = (f32[1024,128]{1,0:T(8,128)S(1)}, f32[1024,128]{1,0:T(8,128)S(1)}, u32[]{:S(2)}, u32[]{:S(2)}) collective-permute-start(f32[1024,128]{1,0:T(8,128)S(1)} %get-tuple-element.55), channel_id=1, source_target_pairs={{0,24},{8,16},{16,8},{24,0},{1,25},{9,17},{17,9},{25,1},{2,26},{10... | collective-permute-start | bytes 1572872 | tf_op jit(solution)/shard_map/ppermute | solution.py:581
  218.8 1.2 collective-permute-start.6
  221.4 3.7 %collective-permute-start.7 = (f32[1]{0:T(128)}, f32[1]{0:T(128)}, u32[]{:S(2)}, u32[]{:S(2)}) collective-permute-start(f32[1]{0:T(128)} %max.6), channel_id=1, source_target_pairs={{0,2},{1,3},{2,0},{3,1},{4,6},{5,7},{6,4},{7,5},{8,10},{9,11},{10,... | collective-permute-start | bytes 20 | tf_op jit(solution)/shard_map/ppermute | solution.py:738
  225.7 4.6 %collective-permute-start.8 = (f32[1]{0:T(128)}, f32[1]{0:T(128)}, u32[]{:S(2)}, u32[]{:S(2)}) collective-permute-start(f32[1]{0:T(128)} %max.7.peak_one), channel_id=1, source_target_pairs={{0,4},{1,5},{2,6},{3,7},{4,0},{5,1},{6,2},{7,3},{8,12},{9,13},{10,... | collective-permute-start | bytes 20 | tf_op jit(solution)/shard_map/ppermute | solution.py:738
  231.0 32.6 %collective-permute-start.13 = (f32[1032,128]{1,0:T(8,128)S(1)}, f32[1032,128]{1,0:T(8,128)S(1)}, u32[]{:S(2)}, u32[]{:S(2)}) collective-permute-start(f32[1032,128]{1,0:T(8,128)S(1)} %get-tuple-element.62), channel_id=1, source_target_pairs={{0,16},{8,24},{16,0},{24,8},{1,17},{9,25},{17,1},{25,9},{2,18},{10... | collective-permute-start | bytes 1585160 | tf_op jit(solution)/shard_map/ppermute | solution.py:581
  231.6 32.0 %collective-permute-start.14 = (f32[1032,128]{1,0:T(8,128)S(1)}, f32[1032,128]{1,0:T(8,128)S(1)}, u32[]{:S(2)}, u32[]{:S(2)}) collective-permute-start(f32[1032,128]{1,0:T(8,128)S(1)} %get-tuple-element.63), channel_id=1, source_target_pairs={{0,24},{8,16},{16,8},{24,0},{1,25},{9,17},{17,9},{25,1},{2,26},{10... | collective-permute-start | bytes 1585160 | tf_op jit(solution)/shard_map/ppermute | solution.py:581
  252.2 11.4 %collective-permute-start.12 = (f32[1032,128]{1,0:T(8,128)S(1)}, f32[1032,128]{1,0:T(8,128)S(1)}, u32[]{:S(2)}, u32[]{:S(2)}) collective-permute-start(f32[1032,128]{1,0:T(8,128)S(1)} %get-tuple-element.61), channel_id=1, source_target_pairs={{0,8},{8,0},{16,24},{24,16},{1,9},{9,1},{17,25},{25,17},{2,10},{10... | collective-permute-start | bytes 1585160 | tf_op jit(solution)/shard_map/ppermute | solution.py:581

commit v20 on v19

--- a/solution.py
+++ b/solution.py
@@ -310,10 +310,14 @@
         copy_in(p).start()
     top[...] = jnp.zeros_like(top)
 
-    @pl.loop(0, products)
+    prepare(0)
+
+    @pl.loop(1, products)
     def _(p):
+        product(p - 1, 0)
         prepare(p)
-        product(p, 0)
+
+    product(products - 1, 0)
 
     tiles = CHUNK // 16
     steps = min(tiles, products // 2)

time: 267 us -> 267 us (level)
  no operation moved by 1% of the time
where the time goes in v20:
time: 267 us
  blocking collectives  135 us (51%)
  waiting for transfers between devices  62.9 us (24%)
  Pallas kernels  45.7 us (17%)
  starting transfers between devices  20.4 us (8%)
  between operations  2.76 us (1%)
    all_to_all x2, blocking collectives, body(): lax.all_to_all(lines, ('row', 'col'), split_axis=0, concat_axis=0, tiled=...  135 us
    ppermute x12, waiting for transfers between devices, exchange(): lax.ppermute(pieces[j], axis, [(i, i ^ j) for i in range(total)])  56.1 us
    ppermute x12, starting transfers between devices, exchange(): lax.ppermute(pieces[j], axis, [(i, i ^ j) for i in range(total)])  17.7 us
    pallas_call x1, Pallas kernels, body(): pl.pallas_call(partial(line_kernel, order, own, tail), grid=(-(-own // at...  12 us
    pallas_call x2, Pallas kernels, body(): pl.pallas_call(partial(column_forward_kernel, row_total), in_specs=[whole...  10.5 us
    pallas_call x1, Pallas kernels, body(): pl.pallas_call(partial(column_inverse_kernel, row_total), in_specs=[whole...  10 us
    ppermute x3, waiting for transfers between devices, body(): peaks = [peak_sq, lax.ppermute(peak_sq, 'col', partner)]  6.81 us
  transfers between devices with their start and end apart: 15, of which 9 were waited for; matrix products, arithmetic and copies ran while one was open for 0% of the time, Pallas kernels for 5%

profile of v20, /device:TPU:0, one launch (start us, length us, event | category | flops | bytes accessed | tf_op | source)
XLA Modules:
  0.0 266.9 jit_solution(14677264802912463423)
XLA Ops:
  0.6 2.6 pack.3
  3.3 3.0 %collective-permute-start.3 = (f32[2,4,128,128]{3,2,1,0:T(8,128)}, f32[2,4,128,128]{3,2,1,0:T(8,128)S(1)}, u32[]{:S(2)}, u32[]{:S(2)}) collective-permute-start(f32[2,4,128,128]{3,2,1,0:T(8,128)} %get-tuple-element.38), channel_id=1, source_target_pairs={{0,8},{8,0},{16,24},{24,16},{1,9},{9,1},{17,25},{25,17},{2,10},{10... | collective-permute-start | bytes 1572872 | tf_op jit(solution)/shard_map/ppermute | solution.py:585
  6.3 1.5 collective-permute-start.4
  7.8 0.1 collective-permute-start.5
  7.9 2.7 %pack.2 = (f32[2,4,128,128]{3,2,1,0:T(8,128)}, f32[2,4,128,128]{3,2,1,0:T(8,128)}, f32[2,4,128,128]{3,2,1,0:T(8,128)}, f32[2,4,128,128]{3,2,1,0:T(8,128)}) custom-call(s32[1]{0:T(128)} %bitcast.place, f32[4,256,512]{2,1,0:T(8,128)} %bitcast.5, f32[4,256,512]{2,1,0:T(8,128)} %bitcast.7), custom_call_target="tpu_custom_call" | custom-call | bytes 4194304 | tf_op jit(solution)/shard_map/pack/pallas_call | solution.py:645
  10.5 1.9 collective-permute-start
  12.5 1.5 collective-permute-start.1
  14.0 5.3 %collective-permute-done.3.refs_1_ = f32[2,4,128,128]{3,2,1,0:T(8,128)S(1)} collective-permute-done((f32[2,4,128,128]{3,2,1,0:T(8,128)}, f32[2,4,128,128]{3,2,1,0:T(8,128)S(1)}, u32[]{:S(2)}, u32[]{:S(2)}) %collective-permute-start.3) | collective-permute-done | bytes 524320 | tf_op jit(solution)/shard_map/ppermute | solution.py:585
  19.2 3.0 %collective-permute-start.2 = (f32[2,4,128,128]{3,2,1,0:T(8,128)}, f32[2,4,128,128]{3,2,1,0:T(8,128)S(1)}, u32[]{:S(2)}, u32[]{:S(2)}) collective-permute-start(f32[2,4,128,128]{3,2,1,0:T(8,128)} %get-tuple-element.36), channel_id=1, source_target_pairs={{0,24},{8,16},{16,8},{24,0},{1,25},{9,17},{17,9},{25,1},{2,26},{10... | collective-permute-start | bytes 1572872 | tf_op jit(solution)/shard_map/ppermute | solution.py:585
  22.3 0.1 pad_add_fusion.place
  22.3 4.1 %gain.1 = f32[2,11,256,128]{3,2,1,0:T(8,128)S(1)} custom-call(s32[2]{0:T(128)S(1)} %pad_add_fusion.place), custom_call_target="tpu_custom_call" | custom-call | tf_op jit(solution)/shard_map/gain/pallas_call | solution.py:625
  26.4 0.0 copy-start
  26.4 0.0 copy-start.8
  26.5 0.0 copy-start.11
  26.5 6.1 %collective-permute-done.4.refs_2_ = f32[2,4,128,128]{3,2,1,0:T(8,128)S(1)} collective-permute-done((f32[2,4,128,128]{3,2,1,0:T(8,128)}, f32[2,4,128,128]{3,2,1,0:T(8,128)S(1)}, u32[]{:S(2)}, u32[]{:S(2)}) %collective-permute-start.4) | collective-permute-done | bytes 524320 | tf_op jit(solution)/shard_map/ppermute | solution.py:585
  32.6 0.0 collective-permute-done.5.refs_3_
  32.6 0.0 copy-done.2
  32.6 0.0 copy-done.9
  32.6 0.0 copy-done.12
  32.6 5.8 %column_forward.2.refs_4_ = f32[32,168,128]{2,1,0:T(8,128)S(1)} custom-call(s32[1]{0:T(128)} %bitcast.place, f32[128,128]{1,0:T(8,128)S(1)} %copy-done.12, bf16[336,256]{1,0:T(8,128)(2,1)S(1)} %copy-done.9, f32[2,4,128,128]{3,2,1,0:T(8,128)S(1)} %copy-done.2, f32[2,4,128,128]{3,2,1,0:T(8,128)S(1)} %collective-permute-done.3.refs_1_, ...), custom_call_target="tpu_custom_call" | custom-call | bytes 20971520 | tf_op jit(solution)/shard_map/column_forward/pallas_call | solution.py:671
  38.4 3.4 %collective-permute-done.refs_1_ = f32[2,4,128,128]{3,2,1,0:T(8,128)S(1)} collective-permute-done((f32[2,4,128,128]{3,2,1,0:T(8,128)}, f32[2,4,128,128]{3,2,1,0:T(8,128)S(1)}, u32[]{:S(2)}, u32[]{:S(2)}) %collective-permute-start) | collective-permute-done | bytes 524320 | tf_op jit(solution)/shard_map/ppermute | solution.py:585
  41.8 11.8 %collective-permute-done.1.refs_2_ = f32[2,4,128,128]{3,2,1,0:T(8,128)S(1)} collective-permute-done((f32[2,4,128,128]{3,2,1,0:T(8,128)}, f32[2,4,128,128]{3,2,1,0:T(8,128)S(1)}, u32[]{:S(2)}, u32[]{:S(2)}) %collective-permute-start.1) | collective-permute-done | bytes 524320 | tf_op jit(solution)/shard_map/ppermute | solution.py:585
  53.6 0.0 collective-permute-done.2.refs_3_
  53.6 0.0 copy-done
  53.6 0.0 copy-done.8
  53.6 0.0 copy-done.11
  53.6 4.8 %column_forward.3 = f32[32,168,128]{2,1,0:T(8,128)S(1)} custom-call(s32[1]{0:T(128)} %bitcast.place, f32[128,128]{1,0:T(8,128)S(1)} %copy-done.11, bf16[336,256]{1,0:T(8,128)(2,1)S(1)} %copy-done.8, f32[2,4,128,128]{3,2,1,0:T(8,128)S(1)} %copy-done, f32[2,4,128,128]{3,2,1,0:T(8,128)S(1)} %collective-permute-done.refs_1_, ...), custom_call_target="tpu_custom_call" | custom-call | bytes 20971520 | tf_op jit(solution)/shard_map/column_forward/pallas_call | solution.py:671
  58.4 0.0 copy-start.3
  58.4 0.0 copy-start.4
  58.4 0.0 copy-start.5
  58.4 0.0 copy-start.6
  58.4 0.0 copy-start.7
  58.5 68.8 %all_to_all.10.lines = f32[32,168,128]{2,1,0:T(8,128)S(1)} all-to-all(f32[32,168,128]{2,1,0:T(8,128)S(1)} %column_forward.3), channel_id=1, replica_groups=mesh['row'=4,'col'=8] {'row','col'}, dimensions={0} | all-to-all | bytes 5505024 | tf_op jit(solution)/shard_map/all_to_all | solution.py:685
  127.3 0.0 copy-done.3
  127.3 0.0 copy-done.4
  127.3 0.0 copy-done.5
  127.3 0.0 copy-done.6
  127.3 0.0 copy-done.7
  127.3 12.0 %line.1 = f32[32,168,128]{2,1,0:T(8,128)S(1)} custom-call(f32[32,168,128]{2,1,0:T(8,128)S(1)} %all_to_all.10.lines, f32[2,11,256,128]{3,2,1,0:T(8,128)S(1)} %gain.1, f32[2,17,8,256]{3,2,1,0:T(8,128)S(1)} %copy-done.3, bf16[512,256]{1,0:T(8,128)(2,1)S(1)} %copy-done.7, bf16[512,256]{1,0:T(8,128)(2,1)S(1)} %copy-done.6, bf16[256,512]{1,0:T(8,128)(2,1)S(1)} %copy-done.5, ...), custom_call_target="tpu_custom_call" | custom-call | tf_op jit(solution)/shard_map/line/pallas_call | solution.py:696
  139.3 0.0 copy-start.1
  139.3 0.0 copy-start.10
  139.3 66.1 %all_to_all.11.source = f32[32,168,128]{2,1,0:T(8,128)S(1)} all-to-all(f32[32,168,128]{2,1,0:T(8,128)S(1)} %line.1), channel_id=1, replica_groups=mesh['row'=4,'col'=8] {'row','col'}, dimensions={0} | all-to-all | bytes 5505024 | tf_op jit(solution)/shard_map/all_to_all | solution.py:711
  205.4 0.0 copy-done.1
  205.5 10.0 %column_inverse.1 = (f32[1024,128]{1,0:T(8,128)S(1)}, f32[1024,128]{1,0:T(8,128)S(1)}, f32[1024,128]{1,0:T(8,128)S(1)}, f32[1024,128]{1,0:T(8,128)S(1)}, f32[103...) custom-call(s32[1]{0:T(128)} %bitcast.place, ...), custom_call_target="tpu_custom_call" | custom-call | tf_op jit(solution)/shard_map/column_inverse/pallas_call | solution.py:718
  215.5 0.1 collective-permute-start.9
  215.6 1.1 collective-permute-start.10
  216.7 2.4 collective-permute-start.11
  219.0 0.0 collective-permute-start.6
  219.0 1.2 collective-permute-done.6
  221.6 1.4 collective-permute-start.7
  223.0 2.3 collective-permute-done.7
  225.9 1.4 collective-permute-start.8
  227.3 3.2 %collective-permute-done.8.peak_two = f32[1]{0:T(128)} collective-permute-done((f32[1]{0:T(128)}, f32[1]{0:T(128)}, u32[]{:S(2)}, u32[]{:S(2)}) %collective-permute-start.8) | collective-permute-done | bytes 36 | tf_op jit(solution)/shard_map/ppermute | solution.py:742
  230.5 0.7 stamp.1
  231.2 0.6 collective-permute-start.13
  231.8 1.0 collective-permute-start.14
  232.8 0.0 collective-permute-done.9.refs_1_
  232.8 19.6 %collective-permute-done.10.refs_2_ = f32[1024,128]{1,0:T(8,128)S(1)} collective-permute-done((f32[1024,128]{1,0:T(8,128)S(1)}, f32[1024,128]{1,0:T(8,128)S(1)}, u32[]{:S(2)}, u32[]{:S(2)}) %collective-permute-start.10) | collective-permute-done | bytes 524320 | tf_op jit(solution)/shard_map/ppermute | solution.py:585
  252.4 0.0 collective-permute-done.11.refs_3_
  252.4 1.5 collective-permute-start.12
  253.9 9.9 %collective-permute-done.13.refs_6_ = f32[1032,128]{1,0:T(8,128)S(1)} collective-permute-done((f32[1032,128]{1,0:T(8,128)S(1)}, f32[1032,128]{1,0:T(8,128)S(1)}, u32[]{:S(2)}, u32[]{:S(2)}) %collective-permute-start.13) | collective-permute-done | bytes 528416 | tf_op jit(solution)/shard_map/ppermute | solution.py:585
  263.8 0.0 collective-permute-done.14.refs_7_
  263.8 0.0 collective-permute-done.12.refs_5_
  263.9 3.1 %encode.1 = (f32[1024,512]{1,0:T(8,128)}, f32[1024,512]{1,0:T(8,128)}) custom-call(s32[1]{0:T(128)} %bitcast.place, f32[1]{0:T(128)} %max.7.peak_one, f32[1]{0:T(128)} %collective-permute-done.8.peak_two, f32[1024,128]{1,0:T(8,128)S(1)} %get-tuple-element.52.refs_0_, f32[1024,128]{1,0:T(8,128)S(1)} %collective-permute-done.9.refs_1_, ...), custom_call_target="tpu_custom_call" | custom-call | tf_op jit(solution)/shard_map/encode/pallas_call | solution.py:777
  (4 shorter events, 0.0 us)
Async XLA Ops:
  3.3 16.0 %collective-permute-start.3 = (f32[2,4,128,128]{3,2,1,0:T(8,128)}, f32[2,4,128,128]{3,2,1,0:T(8,128)S(1)}, u32[]{:S(2)}, u32[]{:S(2)}) collective-permute-start(f32[2,4,128,128]{3,2,1,0:T(8,128)} %get-tuple-element.38), channel_id=1, source_target_pairs={{0,8},{8,0},{16,24},{24,16},{1,9},{9,1},{17,25},{25,17},{2,10},{10... | collective-permute-start | bytes 1572872 | tf_op jit(solution)/shard_map/ppermute | solution.py:585
  6.3 26.3 %collective-permute-start.4 = (f32[2,4,128,128]{3,2,1,0:T(8,128)}, f32[2,4,128,128]{3,2,1,0:T(8,128)S(1)}, u32[]{:S(2)}, u32[]{:S(2)}) collective-permute-start(f32[2,4,128,128]{3,2,1,0:T(8,128)} %get-tuple-element.39), channel_id=1, source_target_pairs={{0,16},{8,24},{16,0},{24,8},{1,17},{9,25},{17,1},{25,9},{2,18},{10... | collective-permute-start | bytes 1572872 | tf_op jit(solution)/shard_map/ppermute | solution.py:585
  7.8 24.8 %copy-start.2 = (f32[2,4,128,128]{3,2,1,0:T(8,128)S(1)}, f32[2,4,128,128]{3,2,1,0:T(8,128)}, u32[]{:S(2)}) copy-start(f32[2,4,128,128]{3,2,1,0:T(8,128)} %get-tuple-element.41.refs_0_) | copy-start | bytes 1572868
  7.8 24.8 %copy-start.9 = (bf16[336,256]{1,0:T(8,128)(2,1)S(1)}, bf16[336,256]{1,0:T(8,128)(2,1)}, u32[]{:S(2)}) copy-start(bf16[336,256]{1,0:T(8,128)(2,1)} %constant.61.clone.matrix) | copy-start | bytes 516100
  7.8 24.8 %copy-start.12 = (f32[128,128]{1,0:T(8,128)S(1)}, f32[128,128]{1,0:T(8,128)}, u32[]{:S(2)}) copy-start(f32[128,128]{1,0:T(8,128)} %constant.60.clone.twist) | copy-start | bytes 196612
  7.8 24.8 %collective-permute-start.5 = (f32[2,4,128,128]{3,2,1,0:T(8,128)}, f32[2,4,128,128]{3,2,1,0:T(8,128)}, u32[]{:S(2)}, u32[]{:S(2)}) collective-permute-start(f32[2,4,128,128]{3,2,1,0:T(8,128)} %get-tuple-element.40), channel_id=1, source_target_pairs={{0,24},{8,16},{16,8},{24,0},{1,25},{9,17},{17,9},{25,1},{2,26},{10... | collective-permute-start | bytes 1572872 | tf_op jit(solution)/shard_map/ppermute | solution.py:585
  10.5 31.2 %collective-permute-start = (f32[2,4,128,128]{3,2,1,0:T(8,128)}, f32[2,4,128,128]{3,2,1,0:T(8,128)S(1)}, u32[]{:S(2)}, u32[]{:S(2)}) collective-permute-start(f32[2,4,128,128]{3,2,1,0:T(8,128)} %get-tuple-element.34), channel_id=1, source_target_pairs={{0,8},{8,0},{16,24},{24,16},{1,9},{9,1},{17,25},{25,17},{2,10},{10... | collective-permute-start | bytes 1572872 | tf_op jit(solution)/shard_map/ppermute | solution.py:585
  12.5 41.1 %collective-permute-start.1 = (f32[2,4,128,128]{3,2,1,0:T(8,128)}, f32[2,4,128,128]{3,2,1,0:T(8,128)S(1)}, u32[]{:S(2)}, u32[]{:S(2)}) collective-permute-start(f32[2,4,128,128]{3,2,1,0:T(8,128)} %get-tuple-element.35), channel_id=1, source_target_pairs={{0,16},{8,24},{16,0},{24,8},{1,17},{9,25},{17,1},{25,9},{2,18},{10... | collective-permute-start | bytes 1572872 | tf_op jit(solution)/shard_map/ppermute | solution.py:585
  19.2 34.3 %collective-permute-start.2 = (f32[2,4,128,128]{3,2,1,0:T(8,128)}, f32[2,4,128,128]{3,2,1,0:T(8,128)S(1)}, u32[]{:S(2)}, u32[]{:S(2)}) collective-permute-start(f32[2,4,128,128]{3,2,1,0:T(8,128)} %get-tuple-element.36), channel_id=1, source_target_pairs={{0,24},{8,16},{16,8},{24,0},{1,25},{9,17},{17,9},{25,1},{2,26},{10... | collective-permute-start | bytes 1572872 | tf_op jit(solution)/shard_map/ppermute | solution.py:585
  26.4 27.2 %copy-start = (f32[2,4,128,128]{3,2,1,0:T(8,128)S(1)}, f32[2,4,128,128]{3,2,1,0:T(8,128)}, u32[]{:S(2)}) copy-start(f32[2,4,128,128]{3,2,1,0:T(8,128)} %get-tuple-element.33.refs_0_) | copy-start | bytes 1572868
  26.4 27.1 %copy-start.8 = (bf16[336,256]{1,0:T(8,128)(2,1)S(1)}, bf16[336,256]{1,0:T(8,128)(2,1)}, u32[]{:S(2)}) copy-start(bf16[336,256]{1,0:T(8,128)(2,1)} %constant.63.clone.matrix) | copy-start | bytes 516100
  26.5 27.1 %copy-start.11 = (f32[128,128]{1,0:T(8,128)S(1)}, f32[128,128]{1,0:T(8,128)}, u32[]{:S(2)}) copy-start(f32[128,128]{1,0:T(8,128)} %constant.62.clone.twist) | copy-start | bytes 196612
  58.4 68.9 %copy-start.3 = (f32[2,17,8,256]{3,2,1,0:T(8,128)S(1)}, f32[2,17,8,256]{3,2,1,0:T(8,128)}, u32[]{:S(2)}) copy-start(f32[2,17,8,256]{3,2,1,0:T(8,128)} %constant.64.clone.twist) | copy-start | bytes 835588
  58.4 68.9 %copy-start.4 = (bf16[256,512]{1,0:T(8,128)(2,1)S(1)}, bf16[256,512]{1,0:T(8,128)(2,1)}, u32[]{:S(2)}) copy-start(bf16[256,512]{1,0:T(8,128)(2,1)} %constant.68.clone.inv_low) | copy-start | bytes 786436
  58.4 68.9 %copy-start.5 = (bf16[256,512]{1,0:T(8,128)(2,1)S(1)}, bf16[256,512]{1,0:T(8,128)(2,1)}, u32[]{:S(2)}) copy-start(bf16[256,512]{1,0:T(8,128)(2,1)} %constant.67.clone.inv_high) | copy-start | bytes 786436
  58.4 68.9 %copy-start.6 = (bf16[512,256]{1,0:T(8,128)(2,1)S(1)}, bf16[512,256]{1,0:T(8,128)(2,1)}, u32[]{:S(2)}) copy-start(bf16[512,256]{1,0:T(8,128)(2,1)} %constant.66.clone.fwd_low) | copy-start | bytes 786436
  58.4 68.9 %copy-start.7 = (bf16[512,256]{1,0:T(8,128)(2,1)S(1)}, bf16[512,256]{1,0:T(8,128)(2,1)}, u32[]{:S(2)}) copy-start(bf16[512,256]{1,0:T(8,128)(2,1)} %constant.65.clone.fwd_high) | copy-start | bytes 786436
  139.3 66.2 %copy-start.1 = (bf16[2,256,512]{2,1,0:T(8,128)(2,1)S(1)}, bf16[2,256,512]{2,1,0:T(8,128)(2,1)}, u32[]{:S(2)}) copy-start(bf16[2,256,512]{2,1,0:T(8,128)(2,1)} %constant.70.clone.matrix) | copy-start | bytes 1572868
  139.3 66.1 %copy-start.10 = (f32[256,128]{1,0:T(8,128)S(1)}, f32[256,128]{1,0:T(8,128)}, u32[]{:S(2)}) copy-start(f32[256,128]{1,0:T(8,128)} %constant.69.clone.twist) | copy-start | bytes 393220
  215.5 17.4 %collective-permute-start.9 = (f32[1024,128]{1,0:T(8,128)S(1)}, f32[1024,128]{1,0:T(8,128)S(1)}, u32[]{:S(2)}, u32[]{:S(2)}) collective-permute-start(f32[1024,128]{1,0:T(8,128)S(1)} %get-tuple-element.53), channel_id=1, source_target_pairs={{0,8},{8,0},{16,24},{24,16},{1,9},{9,1},{17,25},{25,17},{2,10},{10... | collective-permute-start | bytes 1572872 | tf_op jit(solution)/shard_map/ppermute | solution.py:585
  215.6 36.8 %collective-permute-start.10 = (f32[1024,128]{1,0:T(8,128)S(1)}, f32[1024,128]{1,0:T(8,128)S(1)}, u32[]{:S(2)}, u32[]{:S(2)}) collective-permute-start(f32[1024,128]{1,0:T(8,128)S(1)} %get-tuple-element.54), channel_id=1, source_target_pairs={{0,16},{8,24},{16,0},{24,8},{1,17},{9,25},{17,1},{25,9},{2,18},{10... | collective-permute-start | bytes 1572872 | tf_op jit(solution)/shard_map/ppermute | solution.py:585
  216.7 35.7 %collective-permute-start.11 = (f32[1024,128]{1,0:T(8,128)S(1)}, f32[1024,128]{1,0:T(8,128)S(1)}, u32[]{:S(2)}, u32[]{:S(2)}) collective-permute-start(f32[1024,128]{1,0:T(8,128)S(1)} %get-tuple-element.55), channel_id=1, source_target_pairs={{0,24},{8,16},{16,8},{24,0},{1,25},{9,17},{17,9},{25,1},{2,26},{10... | collective-permute-start | bytes 1572872 | tf_op jit(solution)/shard_map/ppermute | solution.py:585
  219.0 1.2 collective-permute-start.6
  221.6 3.7 %collective-permute-start.7 = (f32[1]{0:T(128)}, f32[1]{0:T(128)}, u32[]{:S(2)}, u32[]{:S(2)}) collective-permute-start(f32[1]{0:T(128)} %max.6), channel_id=1, source_target_pairs={{0,2},{1,3},{2,0},{3,1},{4,6},{5,7},{6,4},{7,5},{8,10},{9,11},{10,... | collective-permute-start | bytes 20 | tf_op jit(solution)/shard_map/ppermute | solution.py:742
  225.9 4.6 %collective-permute-start.8 = (f32[1]{0:T(128)}, f32[1]{0:T(128)}, u32[]{:S(2)}, u32[]{:S(2)}) collective-permute-start(f32[1]{0:T(128)} %max.7.peak_one), channel_id=1, source_target_pairs={{0,4},{1,5},{2,6},{3,7},{4,0},{5,1},{6,2},{7,3},{8,12},{9,13},{10,... | collective-permute-start | bytes 20 | tf_op jit(solution)/shard_map/ppermute | solution.py:742
  231.2 32.6 %collective-permute-start.13 = (f32[1032,128]{1,0:T(8,128)S(1)}, f32[1032,128]{1,0:T(8,128)S(1)}, u32[]{:S(2)}, u32[]{:S(2)}) collective-permute-start(f32[1032,128]{1,0:T(8,128)S(1)} %get-tuple-element.62), channel_id=1, source_target_pairs={{0,16},{8,24},{16,0},{24,8},{1,17},{9,25},{17,1},{25,9},{2,18},{10... | collective-permute-start | bytes 1585160 | tf_op jit(solution)/shard_map/ppermute | solution.py:585
  231.8 32.0 %collective-permute-start.14 = (f32[1032,128]{1,0:T(8,128)S(1)}, f32[1032,128]{1,0:T(8,128)S(1)}, u32[]{:S(2)}, u32[]{:S(2)}) collective-permute-start(f32[1032,128]{1,0:T(8,128)S(1)} %get-tuple-element.63), channel_id=1, source_target_pairs={{0,24},{8,16},{16,8},{24,0},{1,25},{9,17},{17,9},{25,1},{2,26},{10... | collective-permute-start | bytes 1585160 | tf_op jit(solution)/shard_map/ppermute | solution.py:585
  252.4 11.4 %collective-permute-start.12 = (f32[1032,128]{1,0:T(8,128)S(1)}, f32[1032,128]{1,0:T(8,128)S(1)}, u32[]{:S(2)}, u32[]{:S(2)}) collective-permute-start(f32[1032,128]{1,0:T(8,128)S(1)} %get-tuple-element.61), channel_id=1, source_target_pairs={{0,8},{8,0},{16,24},{24,16},{1,9},{9,1},{17,25},{25,17},{2,10},{10... | collective-permute-start | bytes 1585160 | tf_op jit(solution)/shard_map/ppermute | solution.py:585
